TPU v7x, 32 devices: a whole 2x2x4 slice. The times are simulated.
32 devices in a mesh: patch: 16 (over z, y, x), vec: 2 (over core).
Axes of the slice: x: 2, y: 2, z: 4, core: 2. Of those that a mesh axis runs over, the one named last changes fastest.
Arguments:
- vectors: float32 [8192, 512], P('patch', 'vec'), may hold values from -6 to 6
- blocks: bfloat16 [1024, 256, 256], P('patch'), may hold values from -0.075 to 0.075, as said below
- block_row: int32 [1024], P('patch'), may hold values from 0 to 31, as said below
- block_col: int32 [1024], P('patch'), may hold values from 0 to 31, as said below
- block_count: int32 [16], P('patch'), may hold values from 0 to 58, as said below
Outputs:
- subspace: float32 [8192, 512], P('patch', 'vec')
- residual: float32 [8192, 512], P('patch', 'vec')
Inputs may be any that keep to these rules, and one draw needn't show every extreme that they name: `block_row`: device p owns entries p * 64 to (p + 1) * 64 - 1. Its used slots come first and hold tiles of block rows 4 * (p // 2) to 4 * (p // 2) + 3 whose block column is at most the row and at least 4 * (p // 2) - 12; both devices of a pair p // 2 share these rows, tiles grouped by 4 x 4 patches each on one device. Every lower tile of the pattern stands in exactly one used slot, every diagonal tile is present, and unused slots name block row and column 4 * (p // 2). `block_col`: the block column of the tile in the same slot, as described for block_row. `block_count`: at most 58 used slots on a device, reached by some device in every draw; the loads are uneven. `blocks`: entries of unused slots are never read.
All inputs are finite; a program needn't handle non-finite values.
Results may differ from a plain program's by a relative error of at most 0.0038.
Values may be sent and summed in bfloat16 or wider, within the bound.
No kernel may reach another device: no remote copies, remote signals or barrier semaphores. Data moves between devices by JAX's collectives and lax.ppermute only.
A program may use at most 128 MiB of HBM per device.

v0:
```python
import jax
import jax.numpy as jnp
from jax import lax
from jax.sharding import PartitionSpec as P

STEPS = 2


step_rate = 0.25
exact_mode = lax.Precision.HIGHEST


def shifted(block, axis, distance):
    devices = range(lax.axis_size(axis))
    route = [(i - distance, i) for i in devices if i - distance in devices]
    return lax.ppermute(block, axis, route)


def accumulate(window_x, totals, block_tiles, row_ids, col_ids, used_slots, window_start):
    group_total = (used_slots + 7) // 8

    def one_turn(group_index, partial_value):
        first_slot = group_index * 8
        chosen = lax.dynamic_slice_in_dim(block_tiles, first_slot, 8, 0)
        rows_here = lax.dynamic_slice_in_dim(row_ids, first_slot, 8, 0) - window_start
        cols_here = lax.dynamic_slice_in_dim(col_ids, first_slot, 8, 0) - window_start
        alive_mask = (first_slot + jnp.arange(8, dtype=jnp.int32) < used_slots).astype(jnp.float32)
        weight = (jnp.where(rows_here == cols_here, 0.5, 1.0).astype(jnp.float32) * alive_mask)[
            :, None, None
        ]
        direct = (
            jnp.einsum(
                "sab,sbk->sak", chosen, window_x[cols_here], preferred_element_type=jnp.float32
            )
            * weight
        )
        mirror = (
            jnp.einsum(
                "sba,sbk->sak", chosen, window_x[rows_here], preferred_element_type=jnp.float32
            )
            * weight
        )
        return partial_value.at[rows_here].add(direct).at[cols_here].add(mirror)

    return lax.fori_loop(0, group_total, one_turn, totals)


def shards(vectors, blocks, block_row, block_col, block_count):
    dev_rows, col_width = vectors.shape
    tile_size = blocks.shape[1]
    total_rows = dev_rows * lax.axis_size("patch")
    position = lax.axis_index("patch")
    parity = position % 2
    window_start = 2 * (position - 6 - parity)
    column_start = lax.axis_index("vec") * col_width
    used_slots = block_count[0]
    current = vectors
    residual = vectors
    for iteration in range(STEPS):
        rounded = current.astype(jnp.bfloat16)
        pieces = {0: rounded}
        for offset in (7, 6, 5, 4, 3, 2, 1, -1):
            pieces[offset] = shifted(rounded, "patch", offset)
        lower_side = jnp.concatenate([pieces[6 - segment] for segment in range(8)], axis=0)
        upper_side = jnp.concatenate([pieces[7 - segment] for segment in range(8)], axis=0)
        window_x = jnp.where(parity == 0, lower_side, upper_side).reshape(16, tile_size, col_width)
        totals = jnp.zeros((16, tile_size, col_width), jnp.float32)
        totals = accumulate(
            window_x, totals, blocks, block_row, block_col, used_slots, window_start
        )
        segments = totals.reshape(8, dev_rows, col_width)
        zero_rows = jnp.zeros((dev_rows, col_width), jnp.float32)
        applied = jnp.where(parity == 0, segments[6], segments[7])
        for offset in (1, -1, -2, -3, -4, -5, -6, -7):
            lower_seg = segments[offset + 6] if 0 <= offset + 6 <= 7 else zero_rows
            upper_seg = segments[offset + 7] if 0 <= offset + 7 <= 7 else zero_rows
            outgoing = jnp.where(parity == 0, lower_seg, upper_seg)
            applied = applied + shifted(outgoing, "patch", offset)
        current_all = lax.all_gather(current, "vec", axis=1, tiled=True)
        applied_all = lax.all_gather(applied, "vec", axis=1, tiled=True)
        cross_xx, cross_xy, cross_yy = lax.psum(
            (
                jnp.dot(
                    current_all.T,
                    current_all,
                    precision=exact_mode,
                    preferred_element_type=jnp.float32,
                )
                / total_rows,
                jnp.dot(
                    current_all.T,
                    applied_all,
                    precision=exact_mode,
                    preferred_element_type=jnp.float32,
                )
                / total_rows,
                jnp.dot(
                    applied_all.T,
                    applied_all,
                    precision=exact_mode,
                    preferred_element_type=jnp.float32,
                )
                / total_rows,
            ),
            "patch",
        )
        rayleigh = lax.dynamic_slice_in_dim(cross_xy, column_start, col_width, 1)
        residual = applied - jnp.dot(
            current_all, rayleigh, precision=exact_mode, preferred_element_type=jnp.float32
        )
        update_all = current_all - step_rate * (
            applied_all
            - jnp.dot(
                current_all, cross_xy, precision=exact_mode, preferred_element_type=jnp.float32
            )
        )
        amplify = jnp.eye(cross_xy.shape[0], dtype=jnp.float32) + step_rate * cross_xy
        mixed = jnp.dot(
            amplify.T, cross_xy, precision=exact_mode, preferred_element_type=jnp.float32
        )
        gram_matrix = jnp.dot(
            jnp.dot(amplify.T, cross_xx, precision=exact_mode, preferred_element_type=jnp.float32),
            amplify,
            precision=exact_mode,
            preferred_element_type=jnp.float32,
        )
        gram_matrix = gram_matrix - step_rate * (mixed + mixed.T) + step_rate * step_rate * cross_yy
        factor = jnp.linalg.cholesky(gram_matrix)
        solved = lax.linalg.triangular_solve(
            factor, update_all, left_side=False, lower=True, transpose_a=True
        )
        current = lax.dynamic_slice_in_dim(solved, column_start, col_width, 1)
    return (current, residual)


def solution(mesh):
    in_specs = (P("patch", "vec"), P("patch", None, None), P("patch"), P("patch"), P("patch"))
    out_specs = (P("patch", "vec"), P("patch", "vec"))
    return jax.shard_map(shards, mesh=mesh, in_specs=in_specs, out_specs=out_specs, check_vma=False)
```

profile of v0, /device:TPU:0, one launch (start us, length us, event | category | flops | bytes accessed | tf_op | source)
XLA Modules:
  0.0 1395.1 jit_solution(3274318994700956580)
XLA Ops:
  8.5 6.8 collective-permute-start.7
  15.3 4.5 collective-permute-start
  40.1 4.4 collective-permute-done.6
  49.7 34.0 %while.24 = (s32[]{:T(128)}, f32[16,256,256]{2,1,0:T(8,128)}, s32[]{:T(128)}, s32[64]{0:T(128)S(1)}, s32[]{:T(128)}, /*index=5*/bf16[64,256,256]{2,1,0:T(8,128)(...) while((s32[]{:T(128)}, f32[16,256,256]{2,1,0:T(8,128)}, ...), condition=%wide.region_3.4_spmd, body=%wide.region_0.3_spmd.sunk | while | flops 538970240 | bytes 25174700 | solution.py:45
  105.0 20.7 %collective-permute-done.10 = f32[512,256]{0,1:T(8,128)} collective-permute-done((f32[512,256]{0,1:T(8,128)}, f32[512,256]{0,1:T(8,128)}, u32[]{:S(2)}, u32[]{:S(2)}) %collective-permute-start.10) | collective-permute-done | bytes 524320 | tf_op jit(solution)/shard_map/ppermute | solution.py:16
  127.0 16.6 %collective-permute-start.8 = (f32[512,256]{0,1:T(8,128)}, f32[512,256]{0,1:T(8,128)S(1)}, u32[]{:S(2)}, u32[]{:S(2)}) collective-permute-start(f32[512,256]{0,1:T(8,128)} %copy.52), channel_id=1, source_target_pairs={{0,2},{2,4},{4,6},{6,8},{8,10},{10,12},{12,14},{14,16},{16,18},{18... | collective-permute-start | bytes 1572872 | tf_op jit(solution)/shard_map/ppermute | solution.py:16
  143.6 5.8 collective-permute-done.12
  150.8 77.3 %collective-permute-done.13 = f32[512,256]{0,1:T(8,128)S(1)} collective-permute-done((f32[512,256]{0,1:T(8,128)}, f32[512,256]{0,1:T(8,128)S(1)}, u32[]{:S(2)}, u32[]{:S(2)}) %collective-permute-start.13) | collective-permute-done | bytes 524320 | tf_op jit(solution)/shard_map/ppermute | solution.py:16
  228.1 5.6 collective-permute-done.9
  236.9 9.0 all-gather.7.cloned.1.call-done
  246.0 4.4 convolution_multiply_fusion.8
  250.3 101.7 %all-gather.5.cloned.1.call-done = f32[512,512]{0,1:T(8,128)} async-done(((f32[512,256]{0,1:T(8,128)}), f32[512,512]{0,1:T(8,128)}) %all-gather.5.cloned.1.call-update) | async-done | bytes 1048592 | tf_op jit(solution)/shard_map/all_gather | solution.py:80
  352.0 4.5 convolution_multiply_fusion.7
  359.9 148.6 %all-reduce.8.cloned.1.call-done = (f32[512,512]{0,1:T(8,128)}, f32[512,512]{1,0:T(8,128)}, f32[512,512]{1,0:T(8,128)}) async-done(((f32[512,512]{0,1:T(8,128)}, f32[512,512]{1,0:T(8,128)}, f32[512,512]{1,0:T(8,128)}), (f32[512,512]{0,1:T(8,128)}, f32[512,512]{1,0:T(8,128)}, f32[512,512]{1,0:T(8,128)})) %all-reduce.8.cloned.1.call-update) | async-done | bytes 3145744 | tf_op jit(solution)/shard_map/psum | solution.py:81
  508.5 4.5 fusion.20
  521.1 5.2 fusion.14
  531.5 11.7 cholesky.286
  544.4 9.9 custom-call.27
  557.6 11.7 cholesky.305
  569.9 9.8 custom-call.28
  582.1 11.7 cholesky.326
  595.1 10.2 custom-call.29
  607.5 11.7 cholesky.343
  626.1 11.9 while.26
  638.0 39.9 %custom-call.30 = f32[4,128,128]{1,2,0:T(8,128)} custom-call(f32[4,128,128]{2,1,0:T(8,128)S(1)} %get-tuple-element.116), custom_call_target="InvertDiagBlocksLowerTriangular" | custom-call | tf_op jit(solution)/shard_map/triangular_solve/custom-call.3 | solution.py:129
  686.9 4.3 collective-permute-start.23
  714.3 4.4 collective-permute-done.22
  723.8 34.0 %while.25 = (s32[]{:T(128)}, f32[16,256,256]{2,1,0:T(8,128)}, s32[]{:T(128)}, s32[64]{0:T(128)S(1)}, s32[]{:T(128)}, /*index=5*/bf16[64,256,256]{2,1,0:T(8,128)(...) while((s32[]{:T(128)}, f32[16,256,256]{2,1,0:T(8,128)}, ...), condition=%wide.region_18.21_spmd, body=%wide.region_15.20_spmd.sunk | while | flops 538970240 | bytes 25174700 | solution.py:45
  781.3 32.7 %collective-permute-done.25 = f32[512,256]{0,1:T(8,128)} collective-permute-done((f32[512,256]{0,1:T(8,128)}, f32[512,256]{0,1:T(8,128)}, u32[]{:S(2)}, u32[]{:S(2)}) %collective-permute-start.25) | collective-permute-done | bytes 524320 | tf_op jit(solution)/shard_map/ppermute | solution.py:16
  815.2 7.8 collective-permute-done.26
  824.5 57.9 %collective-permute-done.28 = f32[512,256]{0,1:T(8,128)S(1)} collective-permute-done((f32[512,256]{0,1:T(8,128)}, f32[512,256]{0,1:T(8,128)S(1)}, u32[]{:S(2)}, u32[]{:S(2)}) %collective-permute-start.28) | collective-permute-done | bytes 524320 | tf_op jit(solution)/shard_map/ppermute | solution.py:16
  882.5 12.0 collective-permute-done.29
  894.5 38.1 %collective-permute-done.30 = f32[512,256]{0,1:T(8,128)S(1)} collective-permute-done((f32[512,256]{0,1:T(8,128)}, f32[512,256]{0,1:T(8,128)S(1)}, u32[]{:S(2)}, u32[]{:S(2)}) %collective-permute-start.30) | collective-permute-done | bytes 524320 | tf_op jit(solution)/shard_map/ppermute | solution.py:16
  932.6 30.5 %collective-permute-done.31 = f32[512,256]{0,1:T(8,128)} collective-permute-done((f32[512,256]{0,1:T(8,128)}, f32[512,256]{0,1:T(8,128)}, u32[]{:S(2)}, u32[]{:S(2)}) %collective-permute-start.31) | collective-permute-done | bytes 524320 | tf_op jit(solution)/shard_map/ppermute | solution.py:16
  966.2 4.4 convolution_multiply_fusion.5
  970.6 76.7 %all-gather.11.cloned.1.call-done = f32[512,512]{0,1:T(8,128)} async-done(((f32[512,256]{0,1:T(8,128)}), f32[512,512]{0,1:T(8,128)}) %all-gather.11.cloned.1.call-update) | async-done | bytes 1048592 | tf_op jit(solution)/shard_map/all_gather | solution.py:80
  1047.3 4.5 convolution_multiply_fusion.4
  1054.7 149.1 %all-reduce.6.cloned.1.call-done = (f32[512,512]{1,0:T(8,128)}, f32[512,512]{1,0:T(8,128)}, f32[512,512]{1,0:T(8,128)}) async-done(((f32[512,512]{1,0:T(8,128)}, f32[512,512]{1,0:T(8,128)}, f32[512,512]{1,0:T(8,128)}), (f32[512,512]{1,0:T(8,128)}, f32[512,512]{1,0:T(8,128)}, f32[512,512]{1,0:T(8,128)})) %all-reduce.6.cloned.1.call-update) | async-done | bytes 3145744 | tf_op jit(solution)/shard_map/psum | solution.py:81
  1223.9 5.4 fusion.10
  1234.3 11.7 cholesky.358
  1246.2 9.8 custom-call.31
  1258.6 12.1 cholesky.377
  1272.0 9.8 custom-call.32
  1284.3 11.7 cholesky.398
  1297.4 9.8 custom-call.33
  1309.5 11.9 cholesky.415
  1327.7 11.3 while.27
  1339.0 39.9 %custom-call.34 = f32[4,128,128]{1,2,0:T(8,128)} custom-call(f32[4,128,128]{2,1,0:T(8,128)S(1)} %get-tuple-element.117), custom_call_target="InvertDiagBlocksLowerTriangular" | custom-call | tf_op jit(solution)/shard_map/triangular_solve/custom-call.3 | solution.py:129
  (281 shorter events, 293.1 us)
Async XLA Ops:
  7.2 238.8 %all-gather.7.cloned.1.call-start = ((), (), s32[]{:S(2)}) async-start(), calls=%async_computation.1 | async-start | bytes 1572864 | tf_op jit(solution)/shard_map/all_gather | solution.py:79
  8.5 31.6 %copy-start.7 = (f32[512,256]{0,1:T(8,128)}, f32[512,256]{0,1:T(8,128)S(1)}, u32[]{:S(2)}) copy-start(f32[512,256]{0,1:T(8,128)S(1)} %copy.9) | copy-start | bytes 1572868
  8.5 19.6 %collective-permute-start.7 = (bf16[512,256]{0,1:T(8,128)(2,1)S(1)}, bf16[512,256]{0,1:T(8,128)(2,1)S(1)}, u32[]{:S(2)}, u32[]{:S(2)}) collective-permute-start(bf16[512,256]{0,1:T(8,128)(2,1)S(1)} %convert_element_type.15), channel_id=1, source_target_pairs={{0,14},{2,16},{4,18},{6,20},{8,22},{10,24},{12,26},{14,28},{16,30}... | collective-permute-start | bytes 786440 | tf_op jit(solution)/shard_map/ppermute | solution.py:16
  15.3 14.3 %collective-permute-start = (bf16[512,256]{0,1:T(8,128)(2,1)S(1)}, bf16[512,256]{0,1:T(8,128)(2,1)S(1)}, u32[]{:S(2)}, u32[]{:S(2)}) collective-permute-start(bf16[512,256]{0,1:T(8,128)(2,1)S(1)} %convert_element_type.15), channel_id=1, source_target_pairs={{0,12},{2,14},{4,16},{6,18},{8,20},{10,22},{12,24},{14,26},{16,28}... | collective-permute-start | bytes 786440 | tf_op jit(solution)/shard_map/ppermute | solution.py:16
  19.8 13.5 collective-permute-start.1
  21.1 16.7 %collective-permute-start.2 = (bf16[512,256]{0,1:T(8,128)(2,1)S(1)}, bf16[512,256]{0,1:T(8,128)(2,1)S(1)}, u32[]{:S(2)}, u32[]{:S(2)}) collective-permute-start(bf16[512,256]{0,1:T(8,128)(2,1)S(1)} %convert_element_type.15), channel_id=1, source_target_pairs={{0,8},{2,10},{4,12},{6,14},{8,16},{10,18},{12,20},{14,22},{16,24},... | collective-permute-start | bytes 786440 | tf_op jit(solution)/shard_map/ppermute | solution.py:16
  23.6 14.2 %collective-permute-start.3 = (bf16[512,256]{0,1:T(8,128)(2,1)S(1)}, bf16[512,256]{0,1:T(8,128)(2,1)S(1)}, u32[]{:S(2)}, u32[]{:S(2)}) collective-permute-start(bf16[512,256]{0,1:T(8,128)(2,1)S(1)} %convert_element_type.15), channel_id=1, source_target_pairs={{0,6},{2,8},{4,10},{6,12},{8,14},{10,16},{12,18},{14,20},{16,22},{... | collective-permute-start | bytes 786440 | tf_op jit(solution)/shard_map/ppermute | solution.py:16
  28.1 11.9 collective-permute-start.4
  29.7 10.3 collective-permute-start.5
  33.3 11.2 collective-permute-start.6
  47.3 2.4 copy-start.15
  89.4 36.3 %collective-permute-start.10 = (f32[512,256]{0,1:T(8,128)}, f32[512,256]{0,1:T(8,128)}, u32[]{:S(2)}, u32[]{:S(2)}) collective-permute-start(f32[512,256]{0,1:T(8,128)} %copy.54), channel_id=1, source_target_pairs={{4,0},{6,2},{8,4},{10,6},{12,8},{14,10},{16,12},{18,14},{20,16},{2... | collective-permute-start | bytes 1572872 | tf_op jit(solution)/shard_map/ppermute | solution.py:16
  92.7 34.3 %collective-permute-start.11 = (f32[512,256]{0,1:T(8,128)}, f32[512,256]{0,1:T(8,128)}, u32[]{:S(2)}, u32[]{:S(2)}) collective-permute-start(f32[512,256]{0,1:T(8,128)} %copy.55), channel_id=1, source_target_pairs={{6,0},{8,2},{10,4},{12,6},{14,8},{16,10},{18,12},{20,14},{22,16},{... | collective-permute-start | bytes 1572872 | tf_op jit(solution)/shard_map/ppermute | solution.py:16
  96.1 53.3 %collective-permute-start.12 = (f32[512,256]{0,1:T(8,128)}, f32[512,256]{0,1:T(8,128)}, u32[]{:S(2)}, u32[]{:S(2)}) collective-permute-start(f32[512,256]{0,1:T(8,128)} %copy.56), channel_id=1, source_target_pairs={{8,0},{10,2},{12,4},{14,6},{16,8},{18,10},{20,12},{22,14},{24,16},... | collective-permute-start | bytes 1572872 | tf_op jit(solution)/shard_map/ppermute | solution.py:16
  97.4 254.6 %all-gather.5.cloned.1.call-start = ((), (), s32[]{:S(2)}) async-start(), calls=%async_computation | async-start | bytes 1572864 | tf_op jit(solution)/shard_map/all_gather | solution.py:80
  98.5 129.7 %collective-permute-start.13 = (f32[512,256]{0,1:T(8,128)}, f32[512,256]{0,1:T(8,128)S(1)}, u32[]{:S(2)}, u32[]{:S(2)}) collective-permute-start(f32[512,256]{0,1:T(8,128)} %copy.57), channel_id=1, source_target_pairs={{10,0},{12,2},{14,4},{16,6},{18,8},{20,10},{22,12},{24,14},{26,16}... | collective-permute-start | bytes 1572872 | tf_op jit(solution)/shard_map/ppermute | solution.py:16
  100.8 127.4 %collective-permute-start.14 = (f32[512,256]{0,1:T(8,128)}, f32[512,256]{0,1:T(8,128)S(1)}, u32[]{:S(2)}, u32[]{:S(2)}) collective-permute-start(f32[512,256]{0,1:T(8,128)} %copy.58), channel_id=1, source_target_pairs={{12,0},{14,2},{16,4},{18,6},{20,8},{22,10},{24,12},{26,14},{28,16}... | collective-permute-start | bytes 1572872 | tf_op jit(solution)/shard_map/ppermute | solution.py:16
  125.7 102.4 %collective-permute-start.15 = (f32[512,256]{0,1:T(8,128)}, f32[512,256]{0,1:T(8,128)S(1)}, u32[]{:S(2)}, u32[]{:S(2)}) collective-permute-start(f32[512,256]{0,1:T(8,128)} %copy.59), channel_id=1, source_target_pairs={{14,0},{16,2},{18,4},{20,6},{22,8},{24,10},{26,12},{28,14},{30,16}... | collective-permute-start | bytes 1572872 | tf_op jit(solution)/shard_map/ppermute | solution.py:16
  127.0 101.1 %collective-permute-start.8 = (f32[512,256]{0,1:T(8,128)}, f32[512,256]{0,1:T(8,128)S(1)}, u32[]{:S(2)}, u32[]{:S(2)}) collective-permute-start(f32[512,256]{0,1:T(8,128)} %copy.52), channel_id=1, source_target_pairs={{0,2},{2,4},{4,6},{6,8},{8,10},{10,12},{12,14},{14,16},{16,18},{18... | collective-permute-start | bytes 1572872 | tf_op jit(solution)/shard_map/ppermute | solution.py:16
  149.4 84.4 %collective-permute-start.9 = (f32[512,256]{0,1:T(8,128)}, f32[512,256]{0,1:T(8,128)}, u32[]{:S(2)}, u32[]{:S(2)}) collective-permute-start(f32[512,256]{0,1:T(8,128)} %copy.53), channel_id=1, source_target_pairs={{2,0},{4,2},{6,4},{8,6},{10,8},{12,10},{14,12},{16,14},{18,16},{20... | collective-permute-start | bytes 1572872 | tf_op jit(solution)/shard_map/ppermute | solution.py:16
  236.7 271.8 %all-reduce.8.cloned.1.call-start = ((), (), s32[]{:S(2)}) async-start(), calls=%async_computation.5 | async-start | bytes 6291456 | tf_op jit(solution)/shard_map/psum | solution.py:81
  250.3 106.2 %copy-start.2 = (f32[512,512]{0,1:T(8,128)S(1)}, f32[512,512]{0,1:T(8,128)}, u32[]{:S(2)}) copy-start(f32[512,512]{0,1:T(8,128)} %all-gather.7.cloned.1.call-done) | copy-start | bytes 3145732
  352.0 4.5 copy-start.3
  359.4 606.8 %all-gather.9.cloned.1.call-start = ((), (), s32[]{:S(2)}) async-start(), calls=%async_computation.2 | async-start | bytes 1572864 | tf_op jit(solution)/shard_map/all_gather | solution.py:79
  508.5 4.6 copy-start.1
  508.5 4.6 copy-start.11
  686.9 15.1 %collective-permute-start.23 = (bf16[512,256]{0,1:T(8,128)(2,1)S(1)}, bf16[512,256]{0,1:T(8,128)(2,1)S(1)}, u32[]{:S(2)}, u32[]{:S(2)}) collective-permute-start(bf16[512,256]{0,1:T(8,128)(2,1)S(1)} %get-tuple-element.196), channel_id=1, source_target_pairs={{0,14},{2,16},{4,18},{6,20},{8,22},{10,24},{12,26},{14,28},{16,30}... | collective-permute-start | bytes 786440 | tf_op jit(solution)/shard_map/ppermute | solution.py:16
  691.2 12.5 collective-permute-start.16
  694.5 14.6 %collective-permute-start.17 = (bf16[512,256]{0,1:T(8,128)(2,1)S(1)}, bf16[512,256]{0,1:T(8,128)(2,1)S(1)}, u32[]{:S(2)}, u32[]{:S(2)}) collective-permute-start(bf16[512,256]{0,1:T(8,128)(2,1)S(1)} %get-tuple-element.196), channel_id=1, source_target_pairs={{0,10},{2,12},{4,14},{6,16},{8,18},{10,20},{12,22},{14,24},{16,26}... | collective-permute-start | bytes 786440 | tf_op jit(solution)/shard_map/ppermute | solution.py:16
  695.9 17.5 %collective-permute-start.18 = (bf16[512,256]{0,1:T(8,128)(2,1)S(1)}, bf16[512,256]{0,1:T(8,128)(2,1)S(1)}, u32[]{:S(2)}, u32[]{:S(2)}) collective-permute-start(bf16[512,256]{0,1:T(8,128)(2,1)S(1)} %get-tuple-element.196), channel_id=1, source_target_pairs={{0,8},{2,10},{4,12},{6,14},{8,16},{10,18},{12,20},{14,22},{16,24},... | collective-permute-start | bytes 786440 | tf_op jit(solution)/shard_map/ppermute | solution.py:16
  698.3 15.1 %collective-permute-start.19 = (bf16[512,256]{0,1:T(8,128)(2,1)S(1)}, bf16[512,256]{0,1:T(8,128)(2,1)S(1)}, u32[]{:S(2)}, u32[]{:S(2)}) collective-permute-start(bf16[512,256]{0,1:T(8,128)(2,1)S(1)} %get-tuple-element.196), channel_id=1, source_target_pairs={{0,6},{2,8},{4,10},{6,12},{8,14},{10,16},{12,18},{14,20},{16,22},{... | collective-permute-start | bytes 786440 | tf_op jit(solution)/shard_map/ppermute | solution.py:16
  702.1 12.1 collective-permute-start.20
  703.7 10.5 collective-permute-start.21
  709.1 9.5 collective-permute-start.22
  763.6 16.4 %collective-permute-start.24 = (f32[512,256]{0,1:T(8,128)}, f32[512,256]{0,1:T(8,128)}, u32[]{:S(2)}, u32[]{:S(2)}) collective-permute-start(f32[512,256]{0,1:T(8,128)} %copy.62), channel_id=1, source_target_pairs={{0,2},{2,4},{4,6},{6,8},{8,10},{10,12},{12,14},{14,16},{16,18},{18... | collective-permute-start | bytes 1572872 | tf_op jit(solution)/shard_map/ppermute | solution.py:16
  767.7 46.3 %collective-permute-start.25 = (f32[512,256]{0,1:T(8,128)}, f32[512,256]{0,1:T(8,128)}, u32[]{:S(2)}, u32[]{:S(2)}) collective-permute-start(f32[512,256]{0,1:T(8,128)} %copy.63), channel_id=1, source_target_pairs={{2,0},{4,2},{6,4},{8,6},{10,8},{12,10},{14,12},{16,14},{18,16},{20... | collective-permute-start | bytes 1572872 | tf_op jit(solution)/shard_map/ppermute | solution.py:16
  771.0 52.0 %collective-permute-start.26 = (f32[512,256]{0,1:T(8,128)}, f32[512,256]{0,1:T(8,128)}, u32[]{:S(2)}, u32[]{:S(2)}) collective-permute-start(f32[512,256]{0,1:T(8,128)} %copy.64), channel_id=1, source_target_pairs={{4,0},{6,2},{8,4},{10,6},{12,8},{14,10},{16,12},{18,14},{20,16},{2... | collective-permute-start | bytes 1572872 | tf_op jit(solution)/shard_map/ppermute | solution.py:16
  772.3 275.0 %all-gather.11.cloned.1.call-start = ((), (), s32[]{:S(2)}) async-start(), calls=%async_computation.3 | async-start | bytes 1572864 | tf_op jit(solution)/shard_map/all_gather | solution.py:80
  773.4 51.1 %collective-permute-start.27 = (f32[512,256]{0,1:T(8,128)}, f32[512,256]{0,1:T(8,128)S(1)}, u32[]{:S(2)}, u32[]{:S(2)}) collective-permute-start(f32[512,256]{0,1:T(8,128)} %copy.65), channel_id=1, source_target_pairs={{6,0},{8,2},{10,4},{12,6},{14,8},{16,10},{18,12},{20,14},{22,16},{... | collective-permute-start | bytes 1572872 | tf_op jit(solution)/shard_map/ppermute | solution.py:16
  775.7 106.8 %collective-permute-start.28 = (f32[512,256]{0,1:T(8,128)}, f32[512,256]{0,1:T(8,128)S(1)}, u32[]{:S(2)}, u32[]{:S(2)}) collective-permute-start(f32[512,256]{0,1:T(8,128)} %copy.66), channel_id=1, source_target_pairs={{8,0},{10,2},{12,4},{14,6},{16,8},{18,10},{20,12},{22,14},{24,16},... | collective-permute-start | bytes 1572872 | tf_op jit(solution)/shard_map/ppermute | solution.py:16
  780.0 114.5 %collective-permute-start.29 = (f32[512,256]{0,1:T(8,128)}, f32[512,256]{0,1:T(8,128)S(1)}, u32[]{:S(2)}, u32[]{:S(2)}) collective-permute-start(f32[512,256]{0,1:T(8,128)} %copy.67), channel_id=1, source_target_pairs={{10,0},{12,2},{14,4},{16,6},{18,8},{20,10},{22,12},{24,14},{26,16}... | collective-permute-start | bytes 1572872 | tf_op jit(solution)/shard_map/ppermute | solution.py:16
  813.9 118.6 %collective-permute-start.30 = (f32[512,256]{0,1:T(8,128)}, f32[512,256]{0,1:T(8,128)S(1)}, u32[]{:S(2)}, u32[]{:S(2)}) collective-permute-start(f32[512,256]{0,1:T(8,128)} %copy.68), channel_id=1, source_target_pairs={{12,0},{14,2},{16,4},{18,6},{20,8},{22,10},{24,12},{26,14},{28,16}... | collective-permute-start | bytes 1572872 | tf_op jit(solution)/shard_map/ppermute | solution.py:16
  823.0 140.0 %collective-permute-start.31 = (f32[512,256]{0,1:T(8,128)}, f32[512,256]{0,1:T(8,128)}, u32[]{:S(2)}, u32[]{:S(2)}) collective-permute-start(f32[512,256]{0,1:T(8,128)} %copy.69), channel_id=1, source_target_pairs={{14,0},{16,2},{18,4},{20,6},{22,8},{24,10},{26,12},{28,14},{30,16}... | collective-permute-start | bytes 1572872 | tf_op jit(solution)/shard_map/ppermute | solution.py:16
  966.0 237.9 %all-reduce.6.cloned.1.call-start = ((), (), s32[]{:S(2)}) async-start(), calls=%async_computation.4 | async-start | bytes 6291456 | tf_op jit(solution)/shard_map/psum | solution.py:81
  970.6 81.2 %copy-start = (f32[512,512]{0,1:T(8,128)S(1)}, f32[512,512]{0,1:T(8,128)}, u32[]{:S(2)}) copy-start(f32[512,512]{0,1:T(8,128)} %all-gather.9.cloned.1.call-done) | copy-start | bytes 3145732
  1047.3 4.5 copy-start.4
  1229.3 2.6 copy-start.6
  1284.3 94.6 %copy-start.5 = (f32[512,512]{1,0:T(8,128)S(1)}, f32[512,512]{1,0:T(8,128)}, u32[]{:S(2)}) copy-start(f32[512,512]{1,0:T(8,128)} %get-tuple-element.190) | copy-start | bytes 3145732
  (6 other events, 9.3 us)
Sparse Core Ops, SparseCore 0:
  97.5 148.4 all-gather.6
  248.1 103.9 all-gather.4
  359.5 148.9 all-reduce.7
  772.4 147.5 all-gather.8
  966.1 81.2 all-gather.10
  1054.9 148.9 all-reduce.5
where the time goes:
time: 1400 us
  waiting for transfers between devices  794 us (57%)
  other arithmetic  301 us (22%)
  local copies, waits for them, and re-layouts  99.2 us (7%)
  matrix products  96.4 us (7%)
  starting transfers between devices  83.7 us (6%)
  between operations  21.1 us (2%)
    ppermute x32, waiting for transfers between devices, shifted(): return lax.ppermute(block, axis, route)  308 us
    psum x2, waiting for transfers between devices, shards(): lax.psum((jnp.dot(current_all.T, current_all, precision=exact_mode, prefe...  298 us
    all_gather x2, waiting for transfers between devices, shards(): applied_all = lax.all_gather(applied, 'vec', axis=1, tiled=True)  178 us
    another operation x29, other arithmetic, shards(): factor = jnp.linalg.cholesky(gram_matrix)  162 us
    another operation x6, other arithmetic, shards(): lax.linalg.triangular_solve(factor, update_all, left_side=False, lower=Tr...  84.9 us
    ppermute x32, starting transfers between devices, shifted(): return lax.ppermute(block, axis, route)  82.7 us
    scatter-add x8, other arithmetic, one_turn(): return partial_value.at[rows_here].add(direct).at[cols_here].add(mirror)  33.2 us
  transfers between devices with their start and end apart: 38, of which 23 were waited for; matrix products, arithmetic and copies ran while one was open for 2% of the time, Pallas kernels for 0%

commit v1 on v0

v1 whole, which is shorter than its diff:
```python
import jax
import jax.numpy as jnp
from jax import lax
from jax.experimental import pallas as pl
from jax.experimental.pallas import tpu as pltpu
from jax.sharding import PartitionSpec as P

STEPS = 2
STEP_RATE = 0.25
GROUP = 8
REACH = 4

f32, bf16 = jnp.float32, jnp.bfloat16
VMEM, SMEM = pltpu.VMEM, pltpu.SMEM


def dot_nn(a, b):
    return lax.dot_general(a, b, (((1,), (0,)), ((), ())), preferred_element_type=f32)


def dot_nt(a, b):
    return lax.dot_general(a, b, (((1,), (1,)), ((), ())), preferred_element_type=f32)


def split(a):
    high = a.astype(bf16)
    return high, (a - high.astype(f32)).astype(bf16)


def dot3(dot, a, b):
    (ah, al), (bh, bl) = a, b
    return dot(ah, bh) + (dot(ah, bl) + dot(al, bh))


def call(kernel, out, args, scratch=(), smem=0, flops=1 << 28):
    moved = sum(a.size * a.dtype.itemsize for a in args) + sum(o.size * o.dtype.itemsize for o in out)
    return pl.pallas_call(
        kernel,
        out_shape=out,
        in_specs=[pl.BlockSpec(memory_space=SMEM)] * smem + [pl.BlockSpec(memory_space=VMEM)] * (len(args) - smem),
        out_specs=[pl.BlockSpec(memory_space=VMEM)] * len(out),
        scratch_shapes=list(scratch),
        compiler_params=pltpu.CompilerParams(vmem_limit_bytes=48 << 20),
        cost_estimate=pl.CostEstimate(flops=flops, bytes_accessed=moved, transcendentals=0),
    )(*args)


def shape(dtype, *dims):
    return jax.ShapeDtypeStruct(dims, dtype)


def pack_kernel(vectors, columns, chunk):
    size = chunk.shape[2]
    for t in range(chunk.shape[0]):
        turned = vectors[pl.ds(t * size, size), :].T
        columns[:, pl.ds(t * size, size)] = turned
        chunk[t] = turned.astype(bf16)


def apply_kernel(meta, rows, cols, *refs):
    pieces, tiles = refs[: 2 * REACH], refs[2 * REACH]
    same, cross = refs[2 * REACH + 1 : 3 * REACH + 1], refs[3 * REACH + 1 : 4 * REACH + 1]
    everything, window, total, sems = refs[4 * REACH + 1 :]
    step = pl.program_id(0)
    used, start, odd = meta[0], meta[1], meta[2]

    @pl.when(step == 0)
    def _():
        copies = [
            pltpu.make_async_copy(piece, window.at[pl.ds(2 * s, 2)], sems.at[s]) for s, piece in enumerate(pieces)
        ]
        for copy in copies:
            copy.start()
        total[...] = jnp.zeros_like(total)
        for copy in copies:
            copy.wait()

    def place(tile):
        w = tile - start
        return (REACH - 1 - w // 4) * 4 + 2 * (((w % 4) // 2) ^ odd) + w % 2

    @pl.when(step * GROUP < used)
    def _():
        found = []
        for k in range(GROUP):
            slot = step * GROUP + k
            row, col = rows[slot], cols[slot]
            weight = jnp.where(row == col, 0.5, 1.0).astype(f32)
            r, c = place(row), place(col)
            tile = jnp.where(slot < used, tiles[k], jnp.zeros_like(tiles[k]))
            found.append((r, dot_nt(window[c], tile), weight))
            found.append((c, dot_nn(window[r], tile), weight))
        for at, part, weight in found:
            total[at] += part * weight

    @pl.when(step == pl.num_programs(0) - 1)
    def _():
        for d in range(REACH):
            for s in range(2):
                same[d][s] = total[4 * d + s]
                cross[d][s] = total[4 * d + 2 + s].astype(bf16)
        everything[...] = total[...].astype(bf16)


def apply_tiles(pieces, blocks, rows, cols, meta):
    slots, size, _ = blocks.shape
    width = pieces[0].shape[1]

    def tile_map(i, meta, rows, cols):
        last = jnp.maximum((meta[0] + GROUP - 1) // GROUP - 1, 0)
        return (jnp.minimum(i, last), 0, 0)

    def whole(dims):
        return pl.BlockSpec(dims, lambda i, *_: (0,) * len(dims))

    segment, window = (2, width, size), (4 * REACH, width, size)
    out = pl.pallas_call(
        apply_kernel,
        grid_spec=pltpu.PrefetchScalarGridSpec(
            num_scalar_prefetch=3,
            grid=(slots // GROUP,),
            in_specs=[pl.BlockSpec(memory_space=pl.ANY)] * (2 * REACH)
            + [pl.BlockSpec((GROUP, size, size), tile_map)],
            out_specs=[whole(segment)] * (2 * REACH) + [whole(window)],
            scratch_shapes=[VMEM(window, bf16), VMEM(window, f32), pltpu.SemaphoreType.DMA((2 * REACH,))],
        ),
        out_shape=[shape(f32, *segment)] * REACH + [shape(bf16, *segment)] * REACH + [shape(bf16, *window)],
        compiler_params=pltpu.CompilerParams(vmem_limit_bytes=48 << 20),
        cost_estimate=pl.CostEstimate(flops=4 << 30, bytes_accessed=16 << 20, transcendentals=0),
    )(meta, rows, cols, *pieces, blocks)
    return out[:REACH], out[REACH : 2 * REACH], out[2 * REACH]


def inner_kernel(*refs):
    pieces, mine, theirs, out = refs[: 2 * REACH], refs[2 * REACH], refs[2 * REACH + 1], refs[-1]
    size = out.shape[1]
    own = jnp.zeros((size, size), f32)
    other = jnp.zeros((size, size), f32)
    for s, piece in enumerate(pieces):
        for t in range(2):
            own += dot_nt(mine[2 * s + t], piece[t])
            other += dot_nt(piece[t], theirs[2 * s + t])
    out[pl.ds(0, size), :] = own
    out[pl.ds(size, size), :] = other


def update_kernel(rows_total, x, x_other, kept, near, far1, far2, far3, inner, update, *residual):
    width, count = x.shape
    size = kept.shape[2]
    own = split(inner[pl.ds(0, width), :] / rows_total)
    other = split(inner[pl.ds(width, width), :] / rows_total)
    for t in range(count // size):
        part = pl.ds(t * size, size)
        applied = kept[t] + near[t].astype(f32)
        applied += far1[t].astype(f32) + far2[t].astype(f32) + far3[t].astype(f32)
        now = x[:, part]
        rest = applied - (dot3(dot_nn, own, split(now)) + dot3(dot_nn, other, split(x_other[:, part])))
        update[:, part] = now - STEP_RATE * rest
        if residual:
            residual[0][part, :] = rest.T


def gram_kernel(core, mine, theirs, out):
    width = mine.shape[0]
    half = width // 2
    own, other = split(mine[...]), split(theirs[...])
    out[pl.ds(0, width), :] = dot3(dot_nt, own, own)
    ahead = core[0] == 0
    high = jnp.where(ahead, theirs[pl.ds(0, half), :], mine[pl.ds(half, half), :])
    low = [jnp.where(ahead, a, b) for a, b in zip(own, other)]
    out[pl.ds(width, half), :] = dot3(dot_nt, split(high), low)


def inverse_factor(g, w, high, low):
    n = g.shape[0]
    at_row = lax.broadcasted_iota(jnp.int32, (n, n), 0)
    at_col = lax.broadcasted_iota(jnp.int32, (n, n), 1)
    eye = jnp.where(at_row == at_col, 1.0, 0.0).astype(f32)
    diagonal = eye * g[...]
    by_row = lax.rsqrt(jnp.sum(diagonal, axis=1, keepdims=True))
    by_col = lax.rsqrt(jnp.sum(diagonal, axis=0, keepdims=True))
    unit = g[...] * by_row * by_col
    rounded = unit.astype(bf16)
    square = dot_nn(rounded, rounded).astype(bf16)
    fourth = dot_nn(square, square)
    scale = 1.9 / jnp.sqrt(jnp.sqrt(jnp.sqrt(jnp.sum(fourth * fourth, keepdims=True))))
    scaled = unit * scale
    high[...], low[...] = split(scaled)

    def lower(e):
        return jnp.where(at_row > at_col, e, 0.5 * eye * e)

    p = lower(scaled - eye)
    pb = p.astype(bf16)
    w[...] = eye - p + dot_nn(pb, pb)

    def improve(e):
        p = lower(e)
        pb = p.astype(bf16)
        first = dot_nn(pb, w[...].astype(bf16))
        w[...] = w[...] - first + dot_nn(pb, first.astype(bf16))
        return jnp.sqrt(jnp.sum(p * p))

    def rough(state):
        wb = w[...].astype(bf16)
        e = dot_nt(dot_nn(wb, high[...]).astype(bf16), wb) - eye
        return state[0] + 1, improve(e)

    def fine(state):
        ws = split(w[...])
        e = dot3(dot_nt, split(dot3(dot_nn, ws, (high[...], low[...]))), ws) - eye
        return state[0] + 1, improve(e)

    def until(bound, most):
        return lambda state: (state[0] < most) & jnp.logical_not(state[1] <= bound)

    lax.while_loop(until(0.4, 16), rough, (0, jnp.float32(1e9)))
    _, error = lax.while_loop(until(2e-3, 6), fine, (0, jnp.float32(1e9)))
    done = error <= 2e-3

    @pl.when(done)
    def _():
        w[...] = w[...] * (by_col * jnp.sqrt(scale))

    @pl.when(jnp.logical_not(done))
    def _():
        w[...] = eye

        def eliminate(k, carry):
            lane = lax.broadcasted_iota(jnp.int32, (1, n), 1)
            below = lax.broadcasted_iota(jnp.int32, (n, 1), 0)
            row = g[pl.ds(k, 1), :]
            pivot = jnp.sum(jnp.where(lane == k, row, 0.0), axis=1, keepdims=True)
            column = jnp.sum(jnp.where(at_col == k, g[...], 0.0), axis=1, keepdims=True)
            ratio = jnp.where(below > k, column / pivot, 0.0)
            solved = w[pl.ds(k, 1), :]
            g[...] = g[...] - ratio * row
            w[...] = w[...] - ratio * solved
            w[pl.ds(k, 1), :] = solved * lax.rsqrt(pivot)
            return carry

        lax.fori_loop(0, n, eliminate, 0)


def factor_kernel(rows_total, last, core, mine, theirs, gram, gram_other, *refs):
    out, (g, w, high, low, update) = refs[:-5], refs[-5:]
    width = mine.shape[0]
    half = width // 2
    ahead = core[0] == 0
    first = jnp.where(ahead, gram[...], gram_other[...]) / rows_total
    second = jnp.where(ahead, gram_other[...], gram[...]) / rows_total
    g[pl.ds(0, width), pl.ds(0, width)] = first[:width]
    g[pl.ds(width, width), pl.ds(width, width)] = second[:width]
    below = jnp.concatenate([first[width:], second[width:]], axis=0)
    g[pl.ds(width, width), pl.ds(0, width)] = below
    g[pl.ds(0, width), pl.ds(width, width)] = below.T
    inverse_factor(g, w, high, low)
    start = pl.multiple_of(core[0] * width, width)
    update[pl.ds(start, width), :] = mine[...]
    update[pl.ds(width - start, width), :] = theirs[...]
    mix = split(w[pl.ds(start, width), :])
    size = width
    for t in range(mine.shape[1] // size):
        part = pl.ds(t * size, size)
        solved = dot3(dot_nn, mix, split(update[:, part]))
        if last:
            out[0][part, :] = solved.T
        else:
            out[0][:, part] = solved
            out[1][t] = solved.astype(bf16)


def swap_cores(a):
    return lax.ppermute(a, "vec", [(0, 1), (1, 0)])


def flip(a, mask):
    return lax.ppermute(a, "patch", [(i, i ^ mask) for i in range(lax.axis_size("patch"))])


def shift(a, pairs):
    devices = range(lax.axis_size("patch"))
    return lax.ppermute(a, "patch", [(i - 2 * pairs, i) for i in devices if i - 2 * pairs in devices])


def summed(a):
    position = lax.axis_index("patch")
    left, stride, stages = lax.axis_size("patch"), 1, []
    while left > 1:
        radix = 4 if left % 4 == 0 else 2
        stages.append((radix, stride))
        left, stride = left // radix, stride * radix
    for radix, stride in stages:
        place = (position // stride) % radix
        parts = a.reshape(radix, a.shape[0] // radix, a.shape[1])
        a = lax.dynamic_index_in_dim(parts, place, 0, False)
        for m in range(1, radix):
            a = a + flip(lax.dynamic_index_in_dim(parts, place ^ m, 0, False), m * stride)
    for radix, stride in stages[::-1]:
        place = (position // stride) % radix
        parts = jnp.stack([a] + [flip(a, m * stride) for m in range(1, radix)])
        a = parts[jnp.arange(radix) ^ place].reshape(radix * a.shape[0], a.shape[1])
    return a


def shards(vectors, blocks, block_row, block_col, block_count):
    count, width = vectors.shape
    size = blocks.shape[1]
    rows_total = float(count * lax.axis_size("patch"))
    position = lax.axis_index("patch")
    odd = position % 2
    meta = jnp.stack([block_count[0], 2 * (position - odd) - 4 * (REACH - 1), odd]).astype(jnp.int32)
    core = lax.axis_index("vec").astype(jnp.int32).reshape(1)
    flat, chunk = shape(f32, width, count), shape(bf16, count // size, width, size)
    x, u = call(pack_kernel, [flat, chunk], [vectors])
    for step in range(STEPS):
        last = step == STEPS - 1
        reached = [u] + [shift(u, d) for d in range(1, REACH)]
        pieces = [a for own in reached for a in (own, flip(own, 1))]
        x_other = swap_cores(x)
        same, cross, everything = apply_tiles(pieces, blocks, block_row, block_col, meta)
        joined = [None] * REACH
        for d in range(REACH - 1, 0, -1):
            joined[d] = shift((same[d] + flip(cross[d], 1).astype(f32)).astype(bf16), -d)
        joined[0] = flip(cross[0], 1)
        (inner,) = call(inner_kernel, [shape(f32, 2 * width, width)], pieces + [everything, swap_cores(everything)])
        inner = summed(inner)
        out = [flat] + ([shape(f32, count, width)] if last else [])
        update, *residual = call(
            lambda *refs: update_kernel(rows_total, *refs), out, [x, x_other, same[0], *joined, inner]
        )
        update_other = swap_cores(update)
        (gram,) = call(
            gram_kernel, [shape(f32, width + width // 2, width)], [core, update, update_other], smem=1
        )
        gram = summed(gram)
        full = (2 * width, 2 * width)
        out = call(
            lambda *refs: factor_kernel(rows_total, last, *refs),
            [shape(f32, count, width)] if last else [flat, chunk],
            [core, update, update_other, gram, swap_cores(gram)],
            scratch=[VMEM(full, f32), VMEM(full, f32), VMEM(full, bf16), VMEM(full, bf16), VMEM((2 * width, count), f32)],
            smem=1,
            flops=16 << 30,
        )
        if last:
            return out[0], residual[0]
        x, u = out


def solution(mesh):
    in_specs = (P("patch", "vec"), P("patch", None, None), P("patch"), P("patch"), P("patch"))
    out_specs = (P("patch", "vec"), P("patch", "vec"))
    return jax.shard_map(shards, mesh=mesh, in_specs=in_specs, out_specs=out_specs, check_vma=False)
```

time: 1400 us -> 351 us (0.25)
  waiting for transfers between devices: 794 us -> 119 us
  other arithmetic: 301 us -> 8.59 us
  matrix products: 96.4 us -> 0 us
  local copies, waits for them, and re-layouts: 99.2 us -> 35.6 us
  starting transfers between devices: 83.7 us -> 137 us
  Pallas kernels: 0 us -> 47.1 us
  between operations: 21.1 us -> 1.89 us
    psum x2 -> x0, waiting for transfers between devices: 298 us -> none  [shards(): lax.psum((jnp.dot(current_all.T, current_all, precision=exact_mode, prefe...]
    another operation x35 -> x9, other arithmetic: 246 us -> 1.83 us  [the longest x8 1.76 us: summed(): parts = jnp.stack([a] + [flip(a, m * stride) for m in range(1, radix)])]
    ppermute x32 -> x84, waiting for transfers between devices: 308 us -> 119 us  [the longest x64 80.3 us: flip(): lax.ppermute(a, 'patch', [(i, i ^ mask) for i in range(lax.axis_size('pat...]
    all_gather x4 -> x0, waiting for transfers between devices: 187 us -> none  [the longest x2 178 us: shards(): applied_all = lax.all_gather(applied, 'vec', axis=1, tiled=True)]
    dot_general x23 -> x0, matrix products: 70.6 us -> none  [the longest x2 10.6 us: shards(): jnp.dot(jnp.dot(amplify.T, cross_xx, precision=exact_mode, preferred_elem...]
    ppermute x32 -> x84, starting transfers between devices: 82.7 us -> 137 us  [the longest x64 106 us: flip(): lax.ppermute(a, 'patch', [(i, i ^ mask) for i in range(lax.axis_size('pat...]
    pallas_call x0 -> x11, Pallas kernels: none -> 47.1 us  [the longest x9 36.2 us: call(): pl.pallas_call(kernel, out_shape=out, in_specs=[pl.BlockSpec(memory_space...]
    scatter-add x8 -> x0, other arithmetic: 33.2 us -> none  [one_turn(): return partial_value.at[rows_here].add(direct).at[cols_here].add(mirror)]
  transfers between devices with their start and end apart: 38 -> 84, of which waited for: 23 -> 60; matrix products, arithmetic and copies ran while one was open for 2% -> 4% of each run, Pallas kernels for 0% -> 1%
where the time goes in v1:
time: 351 us; the launch traced here: 349 us
  starting transfers between devices  137 us (39%)
  waiting for transfers between devices  119 us (34%)
  Pallas kernels  47.1 us (13%)
  local copies, waits for them, and re-layouts  35.6 us (10%)
  other arithmetic  8.59 us (2%)
    ppermute x64, starting transfers between devices, flip(): lax.ppermute(a, 'patch', [(i, i ^ mask) for i in range(lax.axis_size('pat...  106 us
    ppermute x64, waiting for transfers between devices, flip(): lax.ppermute(a, 'patch', [(i, i ^ mask) for i in range(lax.axis_size('pat...  80.3 us
    pallas_call x9, Pallas kernels, call(): pl.pallas_call(kernel, out_shape=out, in_specs=[pl.BlockSpec(memory_space...  36.2 us
    ppermute x12, starting transfers between devices, shift(): lax.ppermute(a, 'patch', [(i - 2 * pairs, i) for i in devices if i - 2 *...  30.2 us
    unnamed x72, local copies, waits for them, and re-layouts  28.1 us
    ppermute x12, waiting for transfers between devices, shift(): lax.ppermute(a, 'patch', [(i - 2 * pairs, i) for i in devices if i - 2 *...  22.4 us
    ppermute x8, waiting for transfers between devices, swap_cores(): return lax.ppermute(a, 'vec', [(0, 1), (1, 0)])  16.3 us
    pallas_call x2, Pallas kernels, apply_tiles(): pl.pallas_call(apply_kernel, grid_spec=pltpu.PrefetchScalarGridSpec(num_s...  10.9 us
  transfers between devices with their start and end apart: 84, of which 60 were waited for; matrix products, arithmetic and copies ran while one was open for 4% of the time, Pallas kernels for 1%

profile of v1, /device:TPU:0, one launch (start us, length us, event | category | flops | bytes accessed | tf_op | source)
XLA Modules:
  0.0 349.1 jit_solution(12411198753505185927)
XLA Ops:
  1.9 4.9 %collective-permute-start.2 = (bf16[2,256,256]{2,1,0:T(8,128)(2,1)S(1)}, bf16[2,256,256]{2,1,0:T(8,128)(2,1)S(1)}, u32[]{:S(2)}, u32[]{:S(2)}) collective-permute-start(bf16[2,256,256]{2,1,0:T(8,128)(2,1)S(1)} %get-tuple-element.27.refs_0_), channel_id=1, source_target_pairs={{0,4},{2,6},{4,8},{6,10},{8,12},{10,14},{12,16},{14,18},{16,20},{1... | collective-permute-start | bytes 786440 | tf_op jit(solution)/shard_map/ppermute | solution.py:283
  6.8 3.5 collective-permute-start.4
  10.3 4.4 %collective-permute-start.6 = (bf16[2,256,256]{2,1,0:T(8,128)(2,1)S(1)}, bf16[2,256,256]{2,1,0:T(8,128)(2,1)S(1)}, u32[]{:S(2)}, u32[]{:S(2)}) collective-permute-start(bf16[2,256,256]{2,1,0:T(8,128)(2,1)S(1)} %get-tuple-element.27.refs_0_), channel_id=1, source_target_pairs={{0,12},{2,14},{4,16},{6,18},{8,20},{10,22},{12,24},{14,26},{16,28}... | collective-permute-start | bytes 786440 | tf_op jit(solution)/shard_map/ppermute | solution.py:283
  18.4 2.7 collective-permute-done.6.refs_6_
  24.8 4.9 %collective-permute-done.3.refs_3_ = bf16[2,256,256]{2,1,0:T(8,128)(2,1)S(1)} collective-permute-done((bf16[2,256,256]{2,1,0:T(8,128)(2,1)S(1)}, bf16[2,256,256]{2,1,0:T(8,128)(2,1)S(1)}, u32[]{:S(2)}, u32[]{:S(2)}) %collective-permute-start.3) | collective-permute-done | bytes 262176 | tf_op jit(solution)/shard_map/ppermute | solution.py:278
  30.3 4.9 %collective-permute-done.5.refs_5_ = bf16[2,256,256]{2,1,0:T(8,128)(2,1)S(1)} collective-permute-done((bf16[2,256,256]{2,1,0:T(8,128)(2,1)S(1)}, bf16[2,256,256]{2,1,0:T(8,128)(2,1)S(1)}, u32[]{:S(2)}, u32[]{:S(2)}) %collective-permute-start.5) | collective-permute-done | bytes 262176 | tf_op jit(solution)/shard_map/ppermute | solution.py:278
  36.0 2.9 collective-permute-done.7.refs_7_
  45.6 5.5 %shard_map.69 = (f32[2,256,256]{2,1,0:T(8,128)S(1)}, f32[2,256,256]{2,1,0:T(8,128)S(1)}, f32[2,256,256]{2,1,0:T(8,128)S(1)}, f32[2,256,256]{2,1,0:T(8,128)S(1)},...) custom-call(s32[3]{0:T(128)S(1)} %pad_add_fusion.meta, ...), custom_call_target="tpu_custom_call" | custom-call | flops 4294967296 | bytes 16777216 | tf_op jit(solution)/shard_map/pallas_call | solution.py:117
  54.6 4.7 %collective-permute-done.15.refs_9_ = bf16[16,256,256]{2,1,0:T(8,128)(2,1)} collective-permute-done((bf16[16,256,256]{2,1,0:T(8,128)(2,1)}, bf16[16,256,256]{2,1,0:T(8,128)(2,1)}, u32[]{:S(2)}, u32[]{:S(2)}) %collective-permute-start.15) | collective-permute-done | bytes 2097184 | tf_op jit(solution)/shard_map/ppermute | solution.py:274
  67.6 2.9 shard_map.70
  71.2 3.4 collective-permute-start.18
  76.7 2.1 collective-permute-done.18
  78.8 2.7 collective-permute-done.17
  82.7 5.3 %collective-permute-start.21 = (f32[32,256]{1,0:T(8,128)S(1)}, f32[32,256]{1,0:T(8,128)S(1)}, u32[]{:S(2)}, u32[]{:S(2)}) collective-permute-start(f32[32,256]{1,0:T(8,128)S(1)} %get-tuple-element.66), channel_id=1, source_target_pairs={{0,24},{2,26},{4,28},{6,30},{8,16},{10,18},{12,20},{14,22},{16,8},... | collective-permute-start | bytes 98312 | tf_op jit(solution)/shard_map/ppermute | solution.py:278
  93.1 3.5 collective-permute-start.24
  106.4 3.7 %collective-permute-done.27 = f32[128,256]{1,0:T(8,128)S(1)} collective-permute-done((f32[128,256]{1,0:T(8,128)S(1)}, f32[128,256]{1,0:T(8,128)S(1)}, u32[]{:S(2)}, u32[]{:S(2)}) %collective-permute-start.27) | collective-permute-done | bytes 131104 | tf_op jit(solution)/shard_map/ppermute | solution.py:278
  117.2 4.2 %collective-permute-done.10.refs_4_ = bf16[2,256,256]{2,1,0:T(8,128)(2,1)S(1)} collective-permute-done((bf16[2,256,256]{2,1,0:T(8,128)(2,1)}, bf16[2,256,256]{2,1,0:T(8,128)(2,1)S(1)}, u32[]{:S(2)}, u32[]{:S(2)}) %collective-permute-start.10) | collective-permute-done | bytes 262176 | tf_op jit(solution)/shard_map/ppermute | solution.py:283
  121.3 2.4 collective-permute-done.12.refs_5_
  130.1 11.3 %collective-permute-start.31 = (f32[96,256]{1,0:T(8,128)S(1)}, f32[96,256]{1,0:T(8,128)S(1)}, u32[]{:S(2)}, u32[]{:S(2)}) collective-permute-start(f32[96,256]{1,0:T(8,128)S(1)} %get-tuple-element.60), channel_id=1, source_target_pairs={{0,6},{2,4},{4,2},{6,0},{8,14},{10,12},{12,10},{14,8},{16,22},{18,... | collective-permute-start | bytes 294920 | tf_op jit(solution)/shard_map/ppermute | solution.py:278
  142.0 2.6 collective-permute-done.31
  147.2 3.9 %collective-permute-start.32 = (f32[24,256]{1,0:T(8,128)S(1)}, f32[24,256]{1,0:T(8,128)S(1)}, u32[]{:S(2)}, u32[]{:S(2)}) collective-permute-start(f32[24,256]{1,0:T(8,128)S(1)} %get-tuple-element.71), channel_id=1, source_target_pairs={{0,8},{2,10},{4,12},{6,14},{8,0},{10,2},{12,4},{14,6},{16,24},{18,... | collective-permute-start | bytes 73736 | tf_op jit(solution)/shard_map/ppermute | solution.py:278
  152.9 2.4 collective-permute-start.37
  171.2 14.3 %shard_map.73 = (f32[256,512]{1,0:T(8,128)S(1)}, bf16[2,256,256]{2,1,0:T(8,128)(2,1)S(1)}) custom-call(s32[1]{0:T(128)} %bitcast.core.refs_0_, f32[256,512]{1,0:T(8,128)S(1)} %shard_map.71.mine.refs_1_, f32[256,512]{1,0:T(8,128)S(1)} %collective-permute-done.28.theirs.refs_2_, f32[384,256]{1,0:T(8,128)S(1)} %bitcast.162, ...), custom_call_target="tpu_custom_call" | custom-call | flops 17179869184 | bytes 2621444 | tf_op jit(solution)/shard_map/pallas_call | solution.py:37
  185.5 2.5 collective-permute-start.44
  188.1 2.8 collective-permute-start.46
  190.9 4.2 %collective-permute-start.48 = (bf16[2,256,256]{2,1,0:T(8,128)(2,1)S(1)}, bf16[2,256,256]{2,1,0:T(8,128)(2,1)S(1)}, u32[]{:S(2)}, u32[]{:S(2)}) collective-permute-start(bf16[2,256,256]{2,1,0:T(8,128)(2,1)S(1)} %get-tuple-element.38.refs_0_), channel_id=1, source_target_pairs={{0,12},{2,14},{4,16},{6,18},{8,20},{10,22},{12,24},{14,26},{16,28}... | collective-permute-start | bytes 786440 | tf_op jit(solution)/shard_map/ppermute | solution.py:283
  198.6 3.4 collective-permute-done.48.refs_6_
  204.3 5.6 %collective-permute-done.45.refs_3_ = bf16[2,256,256]{2,1,0:T(8,128)(2,1)S(1)} collective-permute-done((bf16[2,256,256]{2,1,0:T(8,128)(2,1)S(1)}, bf16[2,256,256]{2,1,0:T(8,128)(2,1)S(1)}, u32[]{:S(2)}, u32[]{:S(2)}) %collective-permute-start.45) | collective-permute-done | bytes 262176 | tf_op jit(solution)/shard_map/ppermute | solution.py:278
  210.0 5.6 %collective-permute-done.47.refs_5_ = bf16[2,256,256]{2,1,0:T(8,128)(2,1)S(1)} collective-permute-done((bf16[2,256,256]{2,1,0:T(8,128)(2,1)S(1)}, bf16[2,256,256]{2,1,0:T(8,128)(2,1)S(1)}, u32[]{:S(2)}, u32[]{:S(2)}) %collective-permute-start.47) | collective-permute-done | bytes 262176 | tf_op jit(solution)/shard_map/ppermute | solution.py:278
  215.6 3.9 %collective-permute-done.49.refs_7_ = bf16[2,256,256]{2,1,0:T(8,128)(2,1)S(1)} collective-permute-done((bf16[2,256,256]{2,1,0:T(8,128)(2,1)S(1)}, bf16[2,256,256]{2,1,0:T(8,128)(2,1)S(1)}, u32[]{:S(2)}, u32[]{:S(2)}) %collective-permute-start.49) | collective-permute-done | bytes 262176 | tf_op jit(solution)/shard_map/ppermute | solution.py:278
  219.5 5.4 %shard_map.74 = (f32[2,256,256]{2,1,0:T(8,128)S(1)}, f32[2,256,256]{2,1,0:T(8,128)S(1)}, f32[2,256,256]{2,1,0:T(8,128)S(1)}, f32[2,256,256]{2,1,0:T(8,128)S(1)},...) custom-call(s32[3]{0:T(128)S(1)} %pad_add_fusion.meta, ...), custom_call_target="tpu_custom_call" | custom-call | flops 4294967296 | bytes 16777216 | tf_op jit(solution)/shard_map/pallas_call | solution.py:117
  225.0 4.4 %collective-permute-done.57.refs_9_ = bf16[16,256,256]{2,1,0:T(8,128)(2,1)S(1)} collective-permute-done((bf16[16,256,256]{2,1,0:T(8,128)(2,1)}, bf16[16,256,256]{2,1,0:T(8,128)(2,1)S(1)}, u32[]{:S(2)}, u32[]{:S(2)}) %collective-permute-start.57) | collective-permute-done | bytes 2097184 | tf_op jit(solution)/shard_map/ppermute | solution.py:274
  232.3 2.9 shard_map.75
  235.2 2.1 collective-permute-start.60
  239.4 3.0 collective-permute-done.60
  242.4 2.1 collective-permute-done.59
  244.6 6.5 %collective-permute-start.63 = (f32[32,256]{1,0:T(8,128)S(1)}, f32[32,256]{1,0:T(8,128)S(1)}, u32[]{:S(2)}, u32[]{:S(2)}) collective-permute-start(f32[32,256]{1,0:T(8,128)S(1)} %get-tuple-element.63), channel_id=1, source_target_pairs={{0,24},{2,26},{4,28},{6,30},{8,16},{10,18},{12,20},{14,22},{16,8},... | collective-permute-start | bytes 98312 | tf_op jit(solution)/shard_map/ppermute | solution.py:278
  252.3 2.4 collective-permute-start.61
  256.6 4.6 %collective-permute-start.66 = (f32[32,256]{1,0:T(8,128)S(1)}, f32[32,256]{1,0:T(8,128)S(1)}, u32[]{:S(2)}, u32[]{:S(2)}) collective-permute-start(f32[32,256]{1,0:T(8,128)S(1)} %fusion.9), channel_id=1, source_target_pairs={{0,24},{2,26},{4,28},{6,30},{8,16},{10,18},{12,20},{14,22},{16,8},... | collective-permute-start | bytes 98312 | tf_op jit(solution)/shard_map/ppermute | solution.py:278
  264.0 2.1 collective-permute-done.65
  271.0 2.8 collective-permute-done.69
  281.1 3.9 %collective-permute-done.52.refs_4_ = bf16[2,256,256]{2,1,0:T(8,128)(2,1)S(1)} collective-permute-done((bf16[2,256,256]{2,1,0:T(8,128)(2,1)}, bf16[2,256,256]{2,1,0:T(8,128)(2,1)S(1)}, u32[]{:S(2)}, u32[]{:S(2)}) %collective-permute-start.52) | collective-permute-done | bytes 262176 | tf_op jit(solution)/shard_map/ppermute | solution.py:283
  285.0 2.8 collective-permute-done.54.refs_5_
  294.7 12.1 %collective-permute-start.73 = (f32[96,256]{1,0:T(8,128)S(1)}, f32[96,256]{1,0:T(8,128)S(1)}, u32[]{:S(2)}, u32[]{:S(2)}) collective-permute-start(f32[96,256]{1,0:T(8,128)S(1)} %get-tuple-element.57), channel_id=1, source_target_pairs={{0,6},{2,4},{4,2},{6,0},{8,14},{10,12},{12,10},{14,8},{16,22},{18,... | collective-permute-start | bytes 294920 | tf_op jit(solution)/shard_map/ppermute | solution.py:278
  307.4 2.6 collective-permute-done.73
  312.6 3.9 %collective-permute-start.74 = (f32[24,256]{1,0:T(8,128)S(1)}, f32[24,256]{1,0:T(8,128)S(1)}, u32[]{:S(2)}, u32[]{:S(2)}) collective-permute-start(f32[24,256]{1,0:T(8,128)S(1)} %get-tuple-element.68), channel_id=1, source_target_pairs={{0,8},{2,10},{4,12},{6,14},{8,0},{10,2},{12,4},{14,6},{16,24},{18,... | collective-permute-start | bytes 73736 | tf_op jit(solution)/shard_map/ppermute | solution.py:278
  318.3 2.4 collective-permute-start.79
  336.6 12.5 %shard_map.78 = f32[512,256]{1,0:T(8,128)} custom-call(s32[1]{0:T(128)} %bitcast.core.refs_0_, f32[256,512]{1,0:T(8,128)S(1)} %get-tuple-element.48.mine.refs_1_, f32[256,512]{1,0:T(8,128)S(1)} %collective-permute-done.70.theirs.refs_2_, f32[384,256]{1,0:T(8,128)S(1)} %bitcast.164, f32[384,256]{1,0:T(8,128)S(1)} %collective-permute-done.83.refs_4_), custom_call_target="tpu_custom_call" | custom-call | flops 17179869184 | bytes 2359300 | tf_op jit(solution)/shard_map/pallas_call | solution.py:37
  (246 shorter events, 137.7 us)
Async XLA Ops:
  1.9 14.4 %collective-permute-start.2 = (bf16[2,256,256]{2,1,0:T(8,128)(2,1)S(1)}, bf16[2,256,256]{2,1,0:T(8,128)(2,1)S(1)}, u32[]{:S(2)}, u32[]{:S(2)}) collective-permute-start(bf16[2,256,256]{2,1,0:T(8,128)(2,1)S(1)} %get-tuple-element.27.refs_0_), channel_id=1, source_target_pairs={{0,4},{2,6},{4,8},{6,10},{8,12},{10,14},{12,16},{14,18},{16,20},{1... | collective-permute-start | bytes 786440 | tf_op jit(solution)/shard_map/ppermute | solution.py:283
  6.8 10.1 %collective-permute-start.4 = (bf16[2,256,256]{2,1,0:T(8,128)(2,1)S(1)}, bf16[2,256,256]{2,1,0:T(8,128)(2,1)S(1)}, u32[]{:S(2)}, u32[]{:S(2)}) collective-permute-start(bf16[2,256,256]{2,1,0:T(8,128)(2,1)S(1)} %get-tuple-element.27.refs_0_), channel_id=1, source_target_pairs={{0,8},{2,10},{4,12},{6,14},{8,16},{10,18},{12,20},{14,22},{16,24},... | collective-permute-start | bytes 786440 | tf_op jit(solution)/shard_map/ppermute | solution.py:283
  10.3 10.9 %collective-permute-start.6 = (bf16[2,256,256]{2,1,0:T(8,128)(2,1)S(1)}, bf16[2,256,256]{2,1,0:T(8,128)(2,1)S(1)}, u32[]{:S(2)}, u32[]{:S(2)}) collective-permute-start(bf16[2,256,256]{2,1,0:T(8,128)(2,1)S(1)} %get-tuple-element.27.refs_0_), channel_id=1, source_target_pairs={{0,12},{2,14},{4,16},{6,18},{8,20},{10,22},{12,24},{14,26},{16,28}... | collective-permute-start | bytes 786440 | tf_op jit(solution)/shard_map/ppermute | solution.py:283
  14.7 9.3 %collective-permute-start.1 = (bf16[2,256,256]{2,1,0:T(8,128)(2,1)S(1)}, bf16[2,256,256]{2,1,0:T(8,128)(2,1)S(1)}, u32[]{:S(2)}, u32[]{:S(2)}) collective-permute-start(bf16[2,256,256]{2,1,0:T(8,128)(2,1)S(1)} %get-tuple-element.27.refs_0_), channel_id=1, source_target_pairs={{0,2},{2,0},{4,6},{6,4},{8,10},{10,8},{12,14},{14,12},{16,18},{18,... | collective-permute-start | bytes 786440 | tf_op jit(solution)/shard_map/ppermute | solution.py:278
  16.3 13.4 %collective-permute-start.3 = (bf16[2,256,256]{2,1,0:T(8,128)(2,1)S(1)}, bf16[2,256,256]{2,1,0:T(8,128)(2,1)S(1)}, u32[]{:S(2)}, u32[]{:S(2)}) collective-permute-start(bf16[2,256,256]{2,1,0:T(8,128)(2,1)S(1)} %collective-permute-done.2.refs_2_), channel_id=1, source_target_pairs={{0,2},{2,0},{4,6},{6,4},{8,10},{10,8},{12,14},{14,12},{16,18},{18,... | collective-permute-start | bytes 786440 | tf_op jit(solution)/shard_map/ppermute | solution.py:278
  16.9 18.4 %collective-permute-start.5 = (bf16[2,256,256]{2,1,0:T(8,128)(2,1)S(1)}, bf16[2,256,256]{2,1,0:T(8,128)(2,1)S(1)}, u32[]{:S(2)}, u32[]{:S(2)}) collective-permute-start(bf16[2,256,256]{2,1,0:T(8,128)(2,1)S(1)} %collective-permute-done.4.refs_4_), channel_id=1, source_target_pairs={{0,2},{2,0},{4,6},{6,4},{8,10},{10,8},{12,14},{14,12},{16,18},{18,... | collective-permute-start | bytes 786440 | tf_op jit(solution)/shard_map/ppermute | solution.py:278
  21.1 17.7 %collective-permute-start.7 = (bf16[2,256,256]{2,1,0:T(8,128)(2,1)S(1)}, bf16[2,256,256]{2,1,0:T(8,128)(2,1)S(1)}, u32[]{:S(2)}, u32[]{:S(2)}) collective-permute-start(bf16[2,256,256]{2,1,0:T(8,128)(2,1)S(1)} %collective-permute-done.6.refs_6_), channel_id=1, source_target_pairs={{0,2},{2,0},{4,6},{6,4},{8,10},{10,8},{12,14},{14,12},{16,18},{18,... | collective-permute-start | bytes 786440 | tf_op jit(solution)/shard_map/ppermute | solution.py:278
  54.1 63.1 %collective-permute-start = (f32[256,512]{1,0:T(8,128)S(1)}, f32[256,512]{1,0:T(8,128)S(1)}, u32[]{:S(2)}, u32[]{:S(2)}) collective-permute-start(f32[256,512]{1,0:T(8,128)S(1)} %get-tuple-element.26.refs_0_), channel_id=1, source_target_pairs={{0,1},{1,0},{2,3},{3,2},{4,5},{5,4},{6,7},{7,6},{8,9},{9,8},{10,11... | collective-permute-start | bytes 1572872 | tf_op jit(solution)/shard_map/ppermute | solution.py:274
  71.2 7.6 %collective-permute-start.18 = (f32[128,256]{1,0:T(8,128)}, f32[128,256]{1,0:T(8,128)S(1)}, u32[]{:S(2)}, u32[]{:S(2)}) collective-permute-start(f32[128,256]{1,0:T(8,128)} %get-tuple-element.54), channel_id=1, source_target_pairs={{0,6},{2,4},{4,2},{6,0},{8,14},{10,12},{12,10},{14,8},{16,22},{18,... | collective-permute-start | bytes 393224 | tf_op jit(solution)/shard_map/ppermute | solution.py:278
  74.6 6.9 %collective-permute-start.17 = (f32[128,256]{1,0:T(8,128)}, f32[128,256]{1,0:T(8,128)}, u32[]{:S(2)}, u32[]{:S(2)}) collective-permute-start(f32[128,256]{1,0:T(8,128)} %get-tuple-element.55), channel_id=1, source_target_pairs={{0,4},{2,6},{4,0},{6,2},{8,12},{10,14},{12,8},{14,10},{16,20},{18,... | collective-permute-start | bytes 393224 | tf_op jit(solution)/shard_map/ppermute | solution.py:278
  74.6 7.0 %collective-permute-start.16 = (f32[128,256]{1,0:T(8,128)}, f32[128,256]{1,0:T(8,128)}, u32[]{:S(2)}, u32[]{:S(2)}) collective-permute-start(f32[128,256]{1,0:T(8,128)} %get-tuple-element.53), channel_id=1, source_target_pairs={{0,2},{2,0},{4,6},{6,4},{8,10},{10,8},{12,14},{14,12},{16,18},{18,... | collective-permute-start | bytes 393224 | tf_op jit(solution)/shard_map/ppermute | solution.py:278
  75.2 13.6 %collective-permute-start.9 = (bf16[2,256,256]{2,1,0:T(8,128)(2,1)}, bf16[2,256,256]{2,1,0:T(8,128)(2,1)S(1)}, u32[]{:S(2)}, u32[]{:S(2)}) collective-permute-start(bf16[2,256,256]{2,1,0:T(8,128)(2,1)} %copy-done.30), channel_id=1, source_target_pairs={{0,2},{2,0},{4,6},{6,4},{8,10},{10,8},{12,14},{14,12},{16,18},{18,... | collective-permute-start | bytes 786440 | tf_op jit(solution)/shard_map/ppermute | solution.py:278
  78.8 18.4 %collective-permute-start.11 = (bf16[2,256,256]{2,1,0:T(8,128)(2,1)}, bf16[2,256,256]{2,1,0:T(8,128)(2,1)S(1)}, u32[]{:S(2)}, u32[]{:S(2)}) collective-permute-start(bf16[2,256,256]{2,1,0:T(8,128)(2,1)} %copy-done.29), channel_id=1, source_target_pairs={{0,2},{2,0},{4,6},{6,4},{8,10},{10,8},{12,14},{14,12},{16,18},{18,... | collective-permute-start | bytes 786440 | tf_op jit(solution)/shard_map/ppermute | solution.py:278
  82.7 9.1 %collective-permute-start.21 = (f32[32,256]{1,0:T(8,128)S(1)}, f32[32,256]{1,0:T(8,128)S(1)}, u32[]{:S(2)}, u32[]{:S(2)}) collective-permute-start(f32[32,256]{1,0:T(8,128)S(1)} %get-tuple-element.66), channel_id=1, source_target_pairs={{0,24},{2,26},{4,28},{6,30},{8,16},{10,18},{12,20},{14,22},{16,8},... | collective-permute-start | bytes 98312 | tf_op jit(solution)/shard_map/ppermute | solution.py:278
  91.8 13.7 %collective-permute-start.13 = (bf16[2,256,256]{2,1,0:T(8,128)(2,1)S(1)}, bf16[2,256,256]{2,1,0:T(8,128)(2,1)S(1)}, u32[]{:S(2)}, u32[]{:S(2)}) collective-permute-start(bf16[2,256,256]{2,1,0:T(8,128)(2,1)S(1)} %copy-done.28), channel_id=1, source_target_pairs={{0,2},{2,0},{4,6},{6,4},{8,10},{10,8},{12,14},{14,12},{16,18},{18,... | collective-permute-start | bytes 786440 | tf_op jit(solution)/shard_map/ppermute | solution.py:278
  93.1 5.8 %collective-permute-start.24 = (f32[32,256]{1,0:T(8,128)S(1)}, f32[32,256]{1,0:T(8,128)S(1)}, u32[]{:S(2)}, u32[]{:S(2)}) collective-permute-start(f32[32,256]{1,0:T(8,128)S(1)} %fusion.11), channel_id=1, source_target_pairs={{0,24},{2,26},{4,28},{6,30},{8,16},{10,18},{12,20},{14,22},{16,8},... | collective-permute-start | bytes 98312 | tf_op jit(solution)/shard_map/ppermute | solution.py:278
  98.9 18.3 %collective-permute-start.8 = (bf16[2,256,256]{2,1,0:T(8,128)(2,1)}, bf16[2,256,256]{2,1,0:T(8,128)(2,1)S(1)}, u32[]{:S(2)}, u32[]{:S(2)}) collective-permute-start(bf16[2,256,256]{2,1,0:T(8,128)(2,1)} %get-tuple-element.29), channel_id=1, source_target_pairs={{0,2},{2,0},{4,6},{6,4},{8,10},{10,8},{12,14},{14,12},{16,18},{18,... | collective-permute-start | bytes 786440 | tf_op jit(solution)/shard_map/ppermute | solution.py:278
  102.1 8.0 %collective-permute-start.27 = (f32[128,256]{1,0:T(8,128)S(1)}, f32[128,256]{1,0:T(8,128)S(1)}, u32[]{:S(2)}, u32[]{:S(2)}) collective-permute-start(f32[128,256]{1,0:T(8,128)S(1)} %bitcast.169), channel_id=1, source_target_pairs={{0,6},{2,4},{4,2},{6,0},{8,14},{10,12},{12,10},{14,8},{16,22},{18,... | collective-permute-start | bytes 393224 | tf_op jit(solution)/shard_map/ppermute | solution.py:278
  104.0 7.9 %collective-permute-start.26 = (f32[128,256]{1,0:T(8,128)S(1)}, f32[128,256]{1,0:T(8,128)S(1)}, u32[]{:S(2)}, u32[]{:S(2)}) collective-permute-start(f32[128,256]{1,0:T(8,128)S(1)} %bitcast.170), channel_id=1, source_target_pairs={{0,4},{2,6},{4,0},{6,2},{8,12},{10,14},{12,8},{14,10},{16,20},{18,... | collective-permute-start | bytes 393224 | tf_op jit(solution)/shard_map/ppermute | solution.py:278
  105.5 7.7 %collective-permute-start.25 = (f32[128,256]{1,0:T(8,128)S(1)}, f32[128,256]{1,0:T(8,128)S(1)}, u32[]{:S(2)}, u32[]{:S(2)}) collective-permute-start(f32[128,256]{1,0:T(8,128)S(1)} %bitcast.171), channel_id=1, source_target_pairs={{0,2},{2,0},{4,6},{6,4},{8,10},{10,8},{12,14},{14,12},{16,18},{18,... | collective-permute-start | bytes 393224 | tf_op jit(solution)/shard_map/ppermute | solution.py:278
  110.1 11.3 %collective-permute-start.10 = (bf16[2,256,256]{2,1,0:T(8,128)(2,1)}, bf16[2,256,256]{2,1,0:T(8,128)(2,1)S(1)}, u32[]{:S(2)}, u32[]{:S(2)}) collective-permute-start(bf16[2,256,256]{2,1,0:T(8,128)(2,1)} %add_convert_fusion.5), channel_id=1, source_target_pairs={{4,0},{6,2},{8,4},{10,6},{12,8},{14,10},{16,12},{18,14},{20,16},{2... | collective-permute-start | bytes 786440 | tf_op jit(solution)/shard_map/ppermute | solution.py:283
  111.9 11.9 %collective-permute-start.12 = (bf16[2,256,256]{2,1,0:T(8,128)(2,1)}, bf16[2,256,256]{2,1,0:T(8,128)(2,1)S(1)}, u32[]{:S(2)}, u32[]{:S(2)}) collective-permute-start(bf16[2,256,256]{2,1,0:T(8,128)(2,1)} %add_convert_fusion.4), channel_id=1, source_target_pairs={{8,0},{10,2},{12,4},{14,6},{16,8},{18,10},{20,12},{22,14},{24,16},... | collective-permute-start | bytes 786440 | tf_op jit(solution)/shard_map/ppermute | solution.py:283
  113.2 11.9 %collective-permute-start.14 = (bf16[2,256,256]{2,1,0:T(8,128)(2,1)}, bf16[2,256,256]{2,1,0:T(8,128)(2,1)S(1)}, u32[]{:S(2)}, u32[]{:S(2)}) collective-permute-start(bf16[2,256,256]{2,1,0:T(8,128)(2,1)} %add_convert_fusion.3), channel_id=1, source_target_pairs={{12,0},{14,2},{16,4},{18,6},{20,8},{22,10},{24,12},{26,14},{28,16}... | collective-permute-start | bytes 786440 | tf_op jit(solution)/shard_map/ppermute | solution.py:283
  130.1 14.5 %collective-permute-start.31 = (f32[96,256]{1,0:T(8,128)S(1)}, f32[96,256]{1,0:T(8,128)S(1)}, u32[]{:S(2)}, u32[]{:S(2)}) collective-permute-start(f32[96,256]{1,0:T(8,128)S(1)} %get-tuple-element.60), channel_id=1, source_target_pairs={{0,6},{2,4},{4,2},{6,0},{8,14},{10,12},{12,10},{14,8},{16,22},{18,... | collective-permute-start | bytes 294920 | tf_op jit(solution)/shard_map/ppermute | solution.py:278
  185.5 10.1 %collective-permute-start.44 = (bf16[2,256,256]{2,1,0:T(8,128)(2,1)S(1)}, bf16[2,256,256]{2,1,0:T(8,128)(2,1)S(1)}, u32[]{:S(2)}, u32[]{:S(2)}) collective-permute-start(bf16[2,256,256]{2,1,0:T(8,128)(2,1)S(1)} %get-tuple-element.38.refs_0_), channel_id=1, source_target_pairs={{0,4},{2,6},{4,8},{6,10},{8,12},{10,14},{12,16},{14,18},{16,20},{1... | collective-permute-start | bytes 786440 | tf_op jit(solution)/shard_map/ppermute | solution.py:283
  188.1 9.5 %collective-permute-start.46 = (bf16[2,256,256]{2,1,0:T(8,128)(2,1)S(1)}, bf16[2,256,256]{2,1,0:T(8,128)(2,1)S(1)}, u32[]{:S(2)}, u32[]{:S(2)}) collective-permute-start(bf16[2,256,256]{2,1,0:T(8,128)(2,1)S(1)} %get-tuple-element.38.refs_0_), channel_id=1, source_target_pairs={{0,8},{2,10},{4,12},{6,14},{8,16},{10,18},{12,20},{14,22},{16,24},... | collective-permute-start | bytes 786440 | tf_op jit(solution)/shard_map/ppermute | solution.py:283
  190.9 11.2 %collective-permute-start.48 = (bf16[2,256,256]{2,1,0:T(8,128)(2,1)S(1)}, bf16[2,256,256]{2,1,0:T(8,128)(2,1)S(1)}, u32[]{:S(2)}, u32[]{:S(2)}) collective-permute-start(bf16[2,256,256]{2,1,0:T(8,128)(2,1)S(1)} %get-tuple-element.38.refs_0_), channel_id=1, source_target_pairs={{0,12},{2,14},{4,16},{6,18},{8,20},{10,22},{12,24},{14,26},{16,28}... | collective-permute-start | bytes 786440 | tf_op jit(solution)/shard_map/ppermute | solution.py:283
  195.0 9.3 %collective-permute-start.43 = (bf16[2,256,256]{2,1,0:T(8,128)(2,1)S(1)}, bf16[2,256,256]{2,1,0:T(8,128)(2,1)S(1)}, u32[]{:S(2)}, u32[]{:S(2)}) collective-permute-start(bf16[2,256,256]{2,1,0:T(8,128)(2,1)S(1)} %get-tuple-element.38.refs_0_), channel_id=1, source_target_pairs={{0,2},{2,0},{4,6},{6,4},{8,10},{10,8},{12,14},{14,12},{16,18},{18,... | collective-permute-start | bytes 786440 | tf_op jit(solution)/shard_map/ppermute | solution.py:278
  195.6 14.4 %collective-permute-start.45 = (bf16[2,256,256]{2,1,0:T(8,128)(2,1)S(1)}, bf16[2,256,256]{2,1,0:T(8,128)(2,1)S(1)}, u32[]{:S(2)}, u32[]{:S(2)}) collective-permute-start(bf16[2,256,256]{2,1,0:T(8,128)(2,1)S(1)} %collective-permute-done.44.refs_2_), channel_id=1, source_target_pairs={{0,2},{2,0},{4,6},{6,4},{8,10},{10,8},{12,14},{14,12},{16,18},{18,... | collective-permute-start | bytes 786440 | tf_op jit(solution)/shard_map/ppermute | solution.py:278
  197.5 18.0 %collective-permute-start.47 = (bf16[2,256,256]{2,1,0:T(8,128)(2,1)S(1)}, bf16[2,256,256]{2,1,0:T(8,128)(2,1)S(1)}, u32[]{:S(2)}, u32[]{:S(2)}) collective-permute-start(bf16[2,256,256]{2,1,0:T(8,128)(2,1)S(1)} %collective-permute-done.46.refs_4_), channel_id=1, source_target_pairs={{0,2},{2,0},{4,6},{6,4},{8,10},{10,8},{12,14},{14,12},{16,18},{18,... | collective-permute-start | bytes 786440 | tf_op jit(solution)/shard_map/ppermute | solution.py:278
  202.0 17.4 %collective-permute-start.49 = (bf16[2,256,256]{2,1,0:T(8,128)(2,1)S(1)}, bf16[2,256,256]{2,1,0:T(8,128)(2,1)S(1)}, u32[]{:S(2)}, u32[]{:S(2)}) collective-permute-start(bf16[2,256,256]{2,1,0:T(8,128)(2,1)S(1)} %collective-permute-done.48.refs_6_), channel_id=1, source_target_pairs={{0,2},{2,0},{4,6},{6,4},{8,10},{10,8},{12,14},{14,12},{16,18},{18,... | collective-permute-start | bytes 786440 | tf_op jit(solution)/shard_map/ppermute | solution.py:278
  235.2 7.2 %collective-permute-start.60 = (f32[128,256]{1,0:T(8,128)S(1)}, f32[128,256]{1,0:T(8,128)S(1)}, u32[]{:S(2)}, u32[]{:S(2)}) collective-permute-start(f32[128,256]{1,0:T(8,128)S(1)} %get-tuple-element.51), channel_id=1, source_target_pairs={{0,6},{2,4},{4,2},{6,0},{8,14},{10,12},{12,10},{14,8},{16,22},{18,... | collective-permute-start | bytes 393224 | tf_op jit(solution)/shard_map/ppermute | solution.py:278
  237.3 7.2 %collective-permute-start.59 = (f32[128,256]{1,0:T(8,128)S(1)}, f32[128,256]{1,0:T(8,128)S(1)}, u32[]{:S(2)}, u32[]{:S(2)}) collective-permute-start(f32[128,256]{1,0:T(8,128)S(1)} %get-tuple-element.52), channel_id=1, source_target_pairs={{0,4},{2,6},{4,0},{6,2},{8,12},{10,14},{12,8},{14,10},{16,20},{18,... | collective-permute-start | bytes 393224 | tf_op jit(solution)/shard_map/ppermute | solution.py:278
  237.3 7.2 %collective-permute-start.58 = (f32[128,256]{1,0:T(8,128)S(1)}, f32[128,256]{1,0:T(8,128)S(1)}, u32[]{:S(2)}, u32[]{:S(2)}) collective-permute-start(f32[128,256]{1,0:T(8,128)S(1)} %get-tuple-element.50), channel_id=1, source_target_pairs={{0,2},{2,0},{4,6},{6,4},{8,10},{10,8},{12,14},{14,12},{16,18},{18,... | collective-permute-start | bytes 393224 | tf_op jit(solution)/shard_map/ppermute | solution.py:278
  238.8 42.3 %collective-permute-start.42 = (f32[256,512]{1,0:T(8,128)S(1)}, f32[256,512]{1,0:T(8,128)S(1)}, u32[]{:S(2)}, u32[]{:S(2)}) collective-permute-start(f32[256,512]{1,0:T(8,128)S(1)} %get-tuple-element.37.refs_0_), channel_id=1, source_target_pairs={{0,1},{1,0},{2,3},{3,2},{4,5},{5,4},{6,7},{7,6},{8,9},{9,8},{10,11... | collective-permute-start | bytes 1572872 | tf_op jit(solution)/shard_map/ppermute | solution.py:274
  238.8 13.5 %collective-permute-start.51 = (bf16[2,256,256]{2,1,0:T(8,128)(2,1)S(1)}, bf16[2,256,256]{2,1,0:T(8,128)(2,1)S(1)}, u32[]{:S(2)}, u32[]{:S(2)}) collective-permute-start(bf16[2,256,256]{2,1,0:T(8,128)(2,1)S(1)} %get-tuple-element.42), channel_id=1, source_target_pairs={{0,2},{2,0},{4,6},{6,4},{8,10},{10,8},{12,14},{14,12},{16,18},{18,... | collective-permute-start | bytes 786440 | tf_op jit(solution)/shard_map/ppermute | solution.py:278
  242.4 19.4 %collective-permute-start.53 = (bf16[2,256,256]{2,1,0:T(8,128)(2,1)S(1)}, bf16[2,256,256]{2,1,0:T(8,128)(2,1)S(1)}, u32[]{:S(2)}, u32[]{:S(2)}) collective-permute-start(bf16[2,256,256]{2,1,0:T(8,128)(2,1)S(1)} %get-tuple-element.44), channel_id=1, source_target_pairs={{0,2},{2,0},{4,6},{6,4},{8,10},{10,8},{12,14},{14,12},{16,18},{18,... | collective-permute-start | bytes 786440 | tf_op jit(solution)/shard_map/ppermute | solution.py:278
  244.6 10.9 %collective-permute-start.63 = (f32[32,256]{1,0:T(8,128)S(1)}, f32[32,256]{1,0:T(8,128)S(1)}, u32[]{:S(2)}, u32[]{:S(2)}) collective-permute-start(f32[32,256]{1,0:T(8,128)S(1)} %get-tuple-element.63), channel_id=1, source_target_pairs={{0,24},{2,26},{4,28},{6,30},{8,16},{10,18},{12,20},{14,22},{16,8},... | collective-permute-start | bytes 98312 | tf_op jit(solution)/shard_map/ppermute | solution.py:278
  255.4 13.5 %collective-permute-start.55 = (bf16[2,256,256]{2,1,0:T(8,128)(2,1)S(1)}, bf16[2,256,256]{2,1,0:T(8,128)(2,1)S(1)}, u32[]{:S(2)}, u32[]{:S(2)}) collective-permute-start(bf16[2,256,256]{2,1,0:T(8,128)(2,1)S(1)} %get-tuple-element.46), channel_id=1, source_target_pairs={{0,2},{2,0},{4,6},{6,4},{8,10},{10,8},{12,14},{14,12},{16,18},{18,... | collective-permute-start | bytes 786440 | tf_op jit(solution)/shard_map/ppermute | solution.py:278
  256.6 6.8 %collective-permute-start.66 = (f32[32,256]{1,0:T(8,128)S(1)}, f32[32,256]{1,0:T(8,128)S(1)}, u32[]{:S(2)}, u32[]{:S(2)}) collective-permute-start(f32[32,256]{1,0:T(8,128)S(1)} %fusion.9), channel_id=1, source_target_pairs={{0,24},{2,26},{4,28},{6,30},{8,16},{10,18},{12,20},{14,22},{16,8},... | collective-permute-start | bytes 98312 | tf_op jit(solution)/shard_map/ppermute | solution.py:278
  263.3 17.7 %collective-permute-start.50 = (bf16[2,256,256]{2,1,0:T(8,128)(2,1)}, bf16[2,256,256]{2,1,0:T(8,128)(2,1)S(1)}, u32[]{:S(2)}, u32[]{:S(2)}) collective-permute-start(bf16[2,256,256]{2,1,0:T(8,128)(2,1)} %get-tuple-element.40), channel_id=1, source_target_pairs={{0,2},{2,0},{4,6},{6,4},{8,10},{10,8},{12,14},{14,12},{16,18},{18,... | collective-permute-start | bytes 786440 | tf_op jit(solution)/shard_map/ppermute | solution.py:278
  266.6 7.1 %collective-permute-start.69 = (f32[128,256]{1,0:T(8,128)S(1)}, f32[128,256]{1,0:T(8,128)S(1)}, u32[]{:S(2)}, u32[]{:S(2)}) collective-permute-start(f32[128,256]{1,0:T(8,128)S(1)} %bitcast.173), channel_id=1, source_target_pairs={{0,6},{2,4},{4,2},{6,0},{8,14},{10,12},{12,10},{14,8},{16,22},{18,... | collective-permute-start | bytes 393224 | tf_op jit(solution)/shard_map/ppermute | solution.py:278
  268.5 7.5 %collective-permute-start.68 = (f32[128,256]{1,0:T(8,128)S(1)}, f32[128,256]{1,0:T(8,128)S(1)}, u32[]{:S(2)}, u32[]{:S(2)}) collective-permute-start(f32[128,256]{1,0:T(8,128)S(1)} %bitcast.174), channel_id=1, source_target_pairs={{0,4},{2,6},{4,0},{6,2},{8,12},{10,14},{12,8},{14,10},{16,20},{18,... | collective-permute-start | bytes 393224 | tf_op jit(solution)/shard_map/ppermute | solution.py:278
  269.0 8.3 %collective-permute-start.67 = (f32[128,256]{1,0:T(8,128)S(1)}, f32[128,256]{1,0:T(8,128)S(1)}, u32[]{:S(2)}, u32[]{:S(2)}) collective-permute-start(f32[128,256]{1,0:T(8,128)S(1)} %bitcast.175), channel_id=1, source_target_pairs={{0,2},{2,0},{4,6},{6,4},{8,10},{10,8},{12,14},{14,12},{16,18},{18,... | collective-permute-start | bytes 393224 | tf_op jit(solution)/shard_map/ppermute | solution.py:278
  273.7 11.3 %collective-permute-start.52 = (bf16[2,256,256]{2,1,0:T(8,128)(2,1)}, bf16[2,256,256]{2,1,0:T(8,128)(2,1)S(1)}, u32[]{:S(2)}, u32[]{:S(2)}) collective-permute-start(bf16[2,256,256]{2,1,0:T(8,128)(2,1)} %add_convert_fusion.2), channel_id=1, source_target_pairs={{4,0},{6,2},{8,4},{10,6},{12,8},{14,10},{16,12},{18,14},{20,16},{2... | collective-permute-start | bytes 786440 | tf_op jit(solution)/shard_map/ppermute | solution.py:283
  276.0 11.9 %collective-permute-start.54 = (bf16[2,256,256]{2,1,0:T(8,128)(2,1)}, bf16[2,256,256]{2,1,0:T(8,128)(2,1)S(1)}, u32[]{:S(2)}, u32[]{:S(2)}) collective-permute-start(bf16[2,256,256]{2,1,0:T(8,128)(2,1)} %add_convert_fusion.1), channel_id=1, source_target_pairs={{8,0},{10,2},{12,4},{14,6},{16,8},{18,10},{20,12},{22,14},{24,16},... | collective-permute-start | bytes 786440 | tf_op jit(solution)/shard_map/ppermute | solution.py:283
  277.3 11.6 %collective-permute-start.56 = (bf16[2,256,256]{2,1,0:T(8,128)(2,1)}, bf16[2,256,256]{2,1,0:T(8,128)(2,1)S(1)}, u32[]{:S(2)}, u32[]{:S(2)}) collective-permute-start(bf16[2,256,256]{2,1,0:T(8,128)(2,1)} %add_convert_fusion), channel_id=1, source_target_pairs={{12,0},{14,2},{16,4},{18,6},{20,8},{22,10},{24,12},{26,14},{28,16}... | collective-permute-start | bytes 786440 | tf_op jit(solution)/shard_map/ppermute | solution.py:283
  294.7 15.3 %collective-permute-start.73 = (f32[96,256]{1,0:T(8,128)S(1)}, f32[96,256]{1,0:T(8,128)S(1)}, u32[]{:S(2)}, u32[]{:S(2)}) collective-permute-start(f32[96,256]{1,0:T(8,128)S(1)} %get-tuple-element.57), channel_id=1, source_target_pairs={{0,6},{2,4},{4,2},{6,0},{8,14},{10,12},{12,10},{14,8},{16,22},{18,... | collective-permute-start | bytes 294920 | tf_op jit(solution)/shard_map/ppermute | solution.py:278
  (72 other events, 385.6 us)

commit v2 on v1

--- a/solution.py
+++ b/solution.py
@@ -32,7 +32,7 @@
     return dot(ah, bh) + (dot(ah, bl) + dot(al, bh))
 
 
-def call(kernel, out, args, scratch=(), smem=0, flops=1 << 28):
+def call(kernel, out, args, scratch=(), smem=0, flops=1 << 28, vmem=16):
     moved = sum(a.size * a.dtype.itemsize for a in args) + sum(o.size * o.dtype.itemsize for o in out)
     return pl.pallas_call(
         kernel,
@@ -40,7 +40,7 @@
         in_specs=[pl.BlockSpec(memory_space=SMEM)] * smem + [pl.BlockSpec(memory_space=VMEM)] * (len(args) - smem),
         out_specs=[pl.BlockSpec(memory_space=VMEM)] * len(out),
         scratch_shapes=list(scratch),
-        compiler_params=pltpu.CompilerParams(vmem_limit_bytes=48 << 20),
+        compiler_params=pltpu.CompilerParams(vmem_limit_bytes=vmem << 20),
         cost_estimate=pl.CostEstimate(flops=flops, bytes_accessed=moved, transcendentals=0),
     )(*args)
 
@@ -62,7 +62,7 @@
     same, cross = refs[2 * REACH + 1 : 3 * REACH + 1], refs[3 * REACH + 1 : 4 * REACH + 1]
     everything, window, total, sems = refs[4 * REACH + 1 :]
     step = pl.program_id(0)
-    used, start, odd = meta[0], meta[1], meta[2]
+    used, start, odd, pair_odd = meta[0], meta[1], meta[2], meta[3]
 
     @pl.when(step == 0)
     def _():
@@ -77,7 +77,9 @@
 
     def place(tile):
         w = tile - start
-        return (REACH - 1 - w // 4) * 4 + 2 * (((w % 4) // 2) ^ odd) + w % 2
+        back = REACH - 1 - w // 4
+        role = jnp.where(back % 2 == 1, 2 + ((back // 2) ^ pair_odd ^ 1), back // 2)
+        return role * 4 + 2 * (((w % 4) // 2) ^ odd) + w % 2
 
     @pl.when(step * GROUP < used)
     def _():
@@ -125,7 +127,7 @@
             scratch_shapes=[VMEM(window, bf16), VMEM(window, f32), pltpu.SemaphoreType.DMA((2 * REACH,))],
         ),
         out_shape=[shape(f32, *segment)] * REACH + [shape(bf16, *segment)] * REACH + [shape(bf16, *window)],
-        compiler_params=pltpu.CompilerParams(vmem_limit_bytes=48 << 20),
+        compiler_params=pltpu.CompilerParams(vmem_limit_bytes=32 << 20),
         cost_estimate=pl.CostEstimate(flops=4 << 30, bytes_accessed=16 << 20, transcendentals=0),
     )(meta, rows, cols, *pieces, blocks)
     return out[:REACH], out[REACH : 2 * REACH], out[2 * REACH]
@@ -144,15 +146,14 @@
     out[pl.ds(size, size), :] = other
 
 
-def update_kernel(rows_total, x, x_other, kept, near, far1, far2, far3, inner, update, *residual):
+def update_kernel(rows_total, x, x_other, kept, near, far, two, inner, update, *residual):
     width, count = x.shape
     size = kept.shape[2]
     own = split(inner[pl.ds(0, width), :] / rows_total)
     other = split(inner[pl.ds(width, width), :] / rows_total)
     for t in range(count // size):
         part = pl.ds(t * size, size)
-        applied = kept[t] + near[t].astype(f32)
-        applied += far1[t].astype(f32) + far2[t].astype(f32) + far3[t].astype(f32)
+        applied = kept[t] + near[t].astype(f32) + (far[t].astype(f32) + two[t].astype(f32))
         now = x[:, part]
         rest = applied - (dot3(dot_nn, own, split(now)) + dot3(dot_nn, other, split(x_other[:, part])))
         update[:, part] = now - STEP_RATE * rest
@@ -283,23 +284,62 @@
     return lax.ppermute(a, "patch", [(i - 2 * pairs, i) for i in devices if i - 2 * pairs in devices])
 
 
-def summed(a):
+def stride(a, back=False):
+    devices = range(lax.axis_size("patch"))
+    route = [(i - (2 if i // 2 % 2 else 6), i) for i in devices]
+    return lax.ppermute(a, "patch", [(d, s) if back else (s, d) for s, d in route if s in devices])
+
+
+def together(*arrays):
+    return lax.optimization_barrier(arrays)
+
+
+def reach(u):
+    two = shift(u, 2)
+    own = flip(u, 1)
+    far = stride(u)
+    two, own = together(two, own)
+    side, two_x = flip(two, 2), flip(two, 1)
+    far, two_x = together(far, two_x)
+    return [u, own, two, two_x, far, flip(far, 1), side, flip(side, 1)]
+
+
+def place_order(parts, place):
+    radix = len(parts)
+    bit = 1
+    while bit < radix:
+        swapped = [parts[j ^ bit] for j in range(radix)]
+        parts = [jnp.where(place & bit, b, a) for a, b in zip(parts, swapped)]
+        bit *= 2
+    return parts
+
+
+def summed(a, gates=()):
     position = lax.axis_index("patch")
-    left, stride, stages = lax.axis_size("patch"), 1, []
+    left, step, stages = lax.axis_size("patch"), 1, []
     while left > 1:
         radix = 4 if left % 4 == 0 else 2
-        stages.append((radix, stride))
-        left, stride = left // radix, stride * radix
-    for radix, stride in stages:
-        place = (position // stride) % radix
-        parts = a.reshape(radix, a.shape[0] // radix, a.shape[1])
+        stages.append((radix, step))
+        left, step = left // radix, step * radix
+    gates = list(gates)
+
+    def gated(x):
+        return together(x, *gates.pop(0))[0] if gates else x
+
+    for radix, step in stages[:-1]:
+        place = (position // step) % radix
+        parts = gated(a).reshape(radix, a.shape[0] // radix, a.shape[1])
         a = lax.dynamic_index_in_dim(parts, place, 0, False)
         for m in range(1, radix):
-            a = a + flip(lax.dynamic_index_in_dim(parts, place ^ m, 0, False), m * stride)
-    for radix, stride in stages[::-1]:
-        place = (position // stride) % radix
-        parts = jnp.stack([a] + [flip(a, m * stride) for m in range(1, radix)])
-        a = parts[jnp.arange(radix) ^ place].reshape(radix * a.shape[0], a.shape[1])
+            a = a + flip(lax.dynamic_index_in_dim(parts, place ^ m, 0, False), m * step)
+    radix, step = stages[-1]
+    a = gated(a)
+    a = sum([flip(a, m * step) for m in range(1, radix)], a)
+    for radix, step in stages[-2::-1]:
+        place = (position // step) % radix
+        a = gated(a)
+        parts = place_order([a] + [flip(a, m * step) for m in range(1, radix)], place)
+        a = jnp.concatenate(parts, axis=0)
     return a
 
 
@@ -309,22 +349,24 @@
     rows_total = float(count * lax.axis_size("patch"))
     position = lax.axis_index("patch")
     odd = position % 2
-    meta = jnp.stack([block_count[0], 2 * (position - odd) - 4 * (REACH - 1), odd]).astype(jnp.int32)
+    meta = jnp.stack([block_count[0], 2 * (position - odd) - 4 * (REACH - 1), odd, position // 2 % 2]).astype(jnp.int32)
     core = lax.axis_index("vec").astype(jnp.int32).reshape(1)
     flat, chunk = shape(f32, width, count), shape(bf16, count // size, width, size)
     x, u = call(pack_kernel, [flat, chunk], [vectors])
     for step in range(STEPS):
         last = step == STEPS - 1
-        reached = [u] + [shift(u, d) for d in range(1, REACH)]
-        pieces = [a for own in reached for a in (own, flip(own, 1))]
+        pieces = reach(u)
         x_other = swap_cores(x)
         same, cross, everything = apply_tiles(pieces, blocks, block_row, block_col, meta)
-        joined = [None] * REACH
-        for d in range(REACH - 1, 0, -1):
-            joined[d] = shift((same[d] + flip(cross[d], 1).astype(f32)).astype(bf16), -d)
-        joined[0] = flip(cross[0], 1)
-        (inner,) = call(inner_kernel, [shape(f32, 2 * width, width)], pieces + [everything, swap_cores(everything)])
-        inner = summed(inner)
+        side_x, two_x = flip(cross[3], 1), flip(cross[1], 1)
+        side = flip((same[3] + side_x.astype(f32)).astype(bf16), 2)
+        theirs, _ = together(swap_cores(everything), side_x)
+        (inner,) = call(inner_kernel, [shape(f32, 2 * width, width)], pieces + [everything, theirs])
+        far_x, own_x = flip(cross[2], 1), flip(cross[0], 1)
+        far = (same[2] + far_x.astype(f32)).astype(bf16)
+        two = (same[1] + (two_x.astype(f32) + side.astype(f32))).astype(bf16)
+        joined = [own_x, stride(far, True), shift(two, -2)]
+        inner = summed(inner, [(two_x,), (far, two, own_x), joined[1:]])
         out = [flat] + ([shape(f32, count, width)] if last else [])
         update, *residual = call(
             lambda *refs: update_kernel(rows_total, *refs), out, [x, x_other, same[0], *joined, inner]
@@ -342,6 +384,7 @@
             scratch=[VMEM(full, f32), VMEM(full, f32), VMEM(full, bf16), VMEM(full, bf16), VMEM((2 * width, count), f32)],
             smem=1,
             flops=16 << 30,
+            vmem=40,
         )
         if last:
             return out[0], residual[0]

time: 351 us -> 335 us (0.954)
  waiting for transfers between devices: 119 us -> 144 us
  starting transfers between devices: 137 us -> 116 us
  local copies, waits for them, and re-layouts: 35.6 us -> 27 us
  other arithmetic: 8.59 us -> 3.09 us
  Pallas kernels: 47.1 us -> 43 us
    ppermute x64 -> x56, waiting for transfers between devices: 80.3 us -> 129 us  [flip(): lax.ppermute(a, 'patch', [(i, i ^ mask) for i in range(lax.axis_size('pat...]
    ppermute x12 -> x4, starting transfers between devices: 30.2 us -> 9.33 us  [shift(): lax.ppermute(a, 'patch', [(i - 2 * pairs, i) for i in devices if i - 2 *...]
    ppermute x12 -> x4, waiting for transfers between devices: 22.4 us -> 7.62 us  [shift(): lax.ppermute(a, 'patch', [(i - 2 * pairs, i) for i in devices if i - 2 *...]
    ppermute x8, waiting for transfers between devices: 16.3 us -> 7.23 us  [swap_cores(): return lax.ppermute(a, 'vec', [(0, 1), (1, 0)])]
    ppermute x0 -> x4, starting transfers between devices: none -> 8.71 us  [stride(): lax.ppermute(a, 'patch', [(d, s) if back else (s, d) for s, d in route if...]
    ppermute x64 -> x56, starting transfers between devices: 106 us -> 97.5 us  [flip(): lax.ppermute(a, 'patch', [(i, i ^ mask) for i in range(lax.axis_size('pat...]
    gather x8 -> x0, local copies, waits for them, and re-layouts: 6.61 us -> none  [summed(): a = parts[jnp.arange(radix) ^ place].reshape(radix * a.shape[0], a.shape[1])]
    unnamed x72 -> x76, local copies, waits for them, and re-layouts: 28.1 us -> 26.8 us
  transfers between devices with their start and end apart: 84 -> 72, of which waited for: 60 -> 47; matrix products, arithmetic and copies ran while one was open for 4% -> 1% of each run, Pallas kernels for 1% -> 1%
where the time goes in v2:
time: 335 us
  waiting for transfers between devices  144 us (43%)
  starting transfers between devices  116 us (35%)
  Pallas kernels  43 us (13%)
  local copies, waits for them, and re-layouts  27 us (8%)
    ppermute x56, waiting for transfers between devices, flip(): lax.ppermute(a, 'patch', [(i, i ^ mask) for i in range(lax.axis_size('pat...  129 us
    ppermute x56, starting transfers between devices, flip(): lax.ppermute(a, 'patch', [(i, i ^ mask) for i in range(lax.axis_size('pat...  97.5 us
    pallas_call x9, Pallas kernels, call(): pl.pallas_call(kernel, out_shape=out, in_specs=[pl.BlockSpec(memory_space...  34.5 us
    unnamed x76, local copies, waits for them, and re-layouts  26.8 us
    ppermute x4, starting transfers between devices, shift(): lax.ppermute(a, 'patch', [(i - 2 * pairs, i) for i in devices if i - 2 *...  9.33 us
    ppermute x4, starting transfers between devices, stride(): lax.ppermute(a, 'patch', [(d, s) if back else (s, d) for s, d in route if...  8.71 us
    pallas_call x2, Pallas kernels, apply_tiles(): pl.pallas_call(apply_kernel, grid_spec=pltpu.PrefetchScalarGridSpec(num_s...  8.51 us
    ppermute x4, waiting for transfers between devices, shift(): lax.ppermute(a, 'patch', [(i - 2 * pairs, i) for i in devices if i - 2 *...  7.62 us
  transfers between devices with their start and end apart: 72, of which 47 were waited for; matrix products, arithmetic and copies ran while one was open for 1% of the time, Pallas kernels for 1%

profile of v2, /device:TPU:0, one launch (start us, length us, event | category | flops | bytes accessed | tf_op | source)
XLA Modules:
  0.0 334.7 jit_solution(5072681992599633059)
XLA Ops:
  2.7 4.9 %collective-permute-start.1 = (bf16[2,256,256]{2,1,0:T(8,128)(2,1)S(1)}, bf16[2,256,256]{2,1,0:T(8,128)(2,1)S(1)}, u32[]{:S(2)}, u32[]{:S(2)}) collective-permute-start(bf16[2,256,256]{2,1,0:T(8,128)(2,1)S(1)} %get-tuple-element.43.refs_0_), channel_id=1, source_target_pairs={{0,8},{2,10},{4,12},{6,14},{8,16},{10,18},{12,20},{14,22},{16,24},... | collective-permute-start | bytes 786440 | tf_op jit(solution)/shard_map/ppermute | solution.py:284
  9.2 3.4 %collective-permute-start.3 = (bf16[2,256,256]{2,1,0:T(8,128)(2,1)S(1)}, bf16[2,256,256]{2,1,0:T(8,128)(2,1)S(1)}, u32[]{:S(2)}, u32[]{:S(2)}) collective-permute-start(bf16[2,256,256]{2,1,0:T(8,128)(2,1)S(1)} %get-tuple-element.43.refs_0_), channel_id=1, source_target_pairs={{0,4},{2,6},{8,12},{10,14},{4,16},{6,18},{16,20},{18,22},{12,24},{... | collective-permute-start | bytes 786440 | tf_op jit(solution)/shard_map/ppermute | solution.py:290
  13.1 2.3 collective-permute-done.2.refs_1_
  19.9 3.1 collective-permute-done.4.refs_3_
  27.9 4.6 %collective-permute-done.5.refs_5_ = bf16[2,256,256]{2,1,0:T(8,128)(2,1)S(1)} collective-permute-done((bf16[2,256,256]{2,1,0:T(8,128)(2,1)S(1)}, bf16[2,256,256]{2,1,0:T(8,128)(2,1)S(1)}, u32[]{:S(2)}, u32[]{:S(2)}) %collective-permute-start.5) | collective-permute-done | bytes 262176 | tf_op jit(solution)/shard_map/ppermute | solution.py:279
  33.2 2.1 collective-permute-done.7.refs_7_
  42.7 3.4 %copy-done.28 = bf16[64,256,256]{2,1,0:T(8,128)(2,1)S(1)} copy-done((bf16[64,256,256]{2,1,0:T(8,128)(2,1)S(1)}, bf16[64,256,256]{2,1,0:T(8,128)(2,1)}, u32[]{:S(2)}) %copy-start.28) | copy-done | bytes 8388632
  47.3 4.7 %shard_map.69 = (f32[2,256,256]{2,1,0:T(8,128)S(1)}, f32[2,256,256]{2,1,0:T(8,128)S(1)}, f32[2,256,256]{2,1,0:T(8,128)S(1)}, f32[2,256,256]{2,1,0:T(8,128)S(1)},...) custom-call(s32[4]{0:T(128)S(1)} %pad_add_fusion.meta, ...), custom_call_target="tpu_custom_call" | custom-call | flops 4294967296 | bytes 16777216 | tf_op jit(solution)/shard_map/pallas_call | solution.py:119
  55.0 2.0 collective-permute-start.9
  57.1 2.0 collective-permute-start.11
  59.1 5.4 %collective-permute-done.12 = bf16[2,256,256]{2,1,0:T(8,128)(2,1)} collective-permute-done((bf16[2,256,256]{2,1,0:T(8,128)(2,1)}, bf16[2,256,256]{2,1,0:T(8,128)(2,1)}, u32[]{:S(2)}, u32[]{:S(2)}) %collective-permute-start.12) | collective-permute-done | bytes 262176 | tf_op jit(solution)/shard_map/ppermute | solution.py:279
  67.2 2.9 collective-permute-done.9
  76.8 2.9 shard_map.70
  80.8 2.5 collective-permute-start.18
  84.5 2.8 collective-permute-done.18
  87.3 2.5 collective-permute-done.17
  89.8 10.9 %collective-permute-start.21 = (f32[128,256]{1,0:T(8,128)S(1)}, f32[128,256]{1,0:T(8,128)S(1)}, u32[]{:S(2)}, u32[]{:S(2)}) collective-permute-start(f32[128,256]{1,0:T(8,128)S(1)} %fusion.3), channel_id=1, source_target_pairs={{0,24},{2,26},{4,28},{6,30},{8,16},{10,18},{12,20},{14,22},{16,8},... | collective-permute-start | bytes 393224 | tf_op jit(solution)/shard_map/ppermute | solution.py:279
  105.3 13.2 %collective-permute-done.20 = f32[128,256]{1,0:T(8,128)S(1)} collective-permute-done((f32[128,256]{1,0:T(8,128)S(1)}, f32[128,256]{1,0:T(8,128)S(1)}, u32[]{:S(2)}, u32[]{:S(2)}) %collective-permute-start.20) | collective-permute-done | bytes 131104 | tf_op jit(solution)/shard_map/ppermute | solution.py:279
  118.6 6.4 %collective-permute-start.22 = (f32[128,256]{1,0:T(8,128)S(1)}, f32[128,256]{1,0:T(8,128)S(1)}, u32[]{:S(2)}, u32[]{:S(2)}) collective-permute-start(f32[128,256]{1,0:T(8,128)S(1)} %add_add_fusion.1), channel_id=1, source_target_pairs={{0,6},{2,4},{4,2},{6,0},{8,14},{10,12},{12,10},{14,8},{16,22},{18,... | collective-permute-start | bytes 393224 | tf_op jit(solution)/shard_map/ppermute | solution.py:279
  128.7 2.6 collective-permute-done.23
  131.3 2.0 collective-permute-done.24
  140.2 3.1 collective-permute-done.28
  144.2 7.3 %collective-permute-start.30 = (f32[96,256]{1,0:T(8,128)S(1)}, f32[96,256]{1,0:T(8,128)S(1)}, u32[]{:S(2)}, u32[]{:S(2)}) collective-permute-start(f32[96,256]{1,0:T(8,128)S(1)} %fusion.7), channel_id=1, source_target_pairs={{0,16},{2,18},{4,20},{6,22},{8,24},{10,26},{12,28},{14,30},{16,0},... | collective-permute-start | bytes 294920 | tf_op jit(solution)/shard_map/ppermute | solution.py:279
  151.4 6.8 %collective-permute-done.30 = f32[96,256]{1,0:T(8,128)S(1)} collective-permute-done((f32[96,256]{1,0:T(8,128)S(1)}, f32[96,256]{1,0:T(8,128)S(1)}, u32[]{:S(2)}, u32[]{:S(2)}) %collective-permute-start.30) | collective-permute-done | bytes 98336 | tf_op jit(solution)/shard_map/ppermute | solution.py:279
  161.8 2.5 collective-permute-done.32
  167.1 14.3 %shard_map.73 = (f32[256,512]{1,0:T(8,128)S(1)}, bf16[2,256,256]{2,1,0:T(8,128)(2,1)S(1)}) custom-call(s32[1]{0:T(128)} %bitcast.core.refs_0_, f32[256,512]{1,0:T(8,128)S(1)} %shard_map.71.mine.refs_1_, f32[256,512]{1,0:T(8,128)S(1)} %collective-permute-done.25.theirs.refs_2_, f32[384,256]{1,0:T(8,128)S(1)} %pad_maximum_fusion.2.refs_3_, ...), custom_call_target="tpu_custom_call" | custom-call | flops 17179869184 | bytes 2621444 | tf_op jit(solution)/shard_map/pallas_call | solution.py:37
  184.3 2.7 collective-permute-start.39
  188.8 2.3 collective-permute-done.38.refs_1_
  193.0 5.3 %collective-permute-done.40.refs_3_ = bf16[2,256,256]{2,1,0:T(8,128)(2,1)S(1)} collective-permute-done((bf16[2,256,256]{2,1,0:T(8,128)(2,1)S(1)}, bf16[2,256,256]{2,1,0:T(8,128)(2,1)S(1)}, u32[]{:S(2)}, u32[]{:S(2)}) %collective-permute-start.40) | collective-permute-done | bytes 262176 | tf_op jit(solution)/shard_map/ppermute | solution.py:279
  200.3 7.0 %collective-permute-done.41.refs_5_ = bf16[2,256,256]{2,1,0:T(8,128)(2,1)S(1)} collective-permute-done((bf16[2,256,256]{2,1,0:T(8,128)(2,1)S(1)}, bf16[2,256,256]{2,1,0:T(8,128)(2,1)S(1)}, u32[]{:S(2)}, u32[]{:S(2)}) %collective-permute-start.41) | collective-permute-done | bytes 262176 | tf_op jit(solution)/shard_map/ppermute | solution.py:279
  207.4 2.8 collective-permute-done.43.refs_7_
  210.2 3.8 %shard_map.74 = (f32[2,256,256]{2,1,0:T(8,128)S(1)}, f32[2,256,256]{2,1,0:T(8,128)S(1)}, f32[2,256,256]{2,1,0:T(8,128)S(1)}, f32[2,256,256]{2,1,0:T(8,128)S(1)},...) custom-call(s32[4]{0:T(128)S(1)} %pad_add_fusion.meta, ...), custom_call_target="tpu_custom_call" | custom-call | flops 4294967296 | bytes 16777216 | tf_op jit(solution)/shard_map/pallas_call | solution.py:119
  214.2 2.0 collective-permute-start.45
  216.3 1.9 collective-permute-start.47
  218.3 5.1 %collective-permute-done.48 = bf16[2,256,256]{2,1,0:T(8,128)(2,1)S(1)} collective-permute-done((bf16[2,256,256]{2,1,0:T(8,128)(2,1)S(1)}, bf16[2,256,256]{2,1,0:T(8,128)(2,1)S(1)}, u32[]{:S(2)}, u32[]{:S(2)}) %collective-permute-start.48) | collective-permute-done | bytes 262176 | tf_op jit(solution)/shard_map/ppermute | solution.py:279
  224.5 4.5 %collective-permute-done.45 = bf16[2,256,256]{2,1,0:T(8,128)(2,1)S(1)} collective-permute-done((bf16[2,256,256]{2,1,0:T(8,128)(2,1)S(1)}, bf16[2,256,256]{2,1,0:T(8,128)(2,1)S(1)}, u32[]{:S(2)}, u32[]{:S(2)}) %collective-permute-start.45) | collective-permute-done | bytes 262176 | tf_op jit(solution)/shard_map/ppermute | solution.py:279
  230.3 9.4 %collective-permute-done.47 = bf16[2,256,256]{2,1,0:T(8,128)(2,1)S(1)} collective-permute-done((bf16[2,256,256]{2,1,0:T(8,128)(2,1)S(1)}, bf16[2,256,256]{2,1,0:T(8,128)(2,1)S(1)}, u32[]{:S(2)}, u32[]{:S(2)}) %collective-permute-start.47) | collective-permute-done | bytes 262176 | tf_op jit(solution)/shard_map/ppermute | solution.py:279
  243.4 3.7 %collective-permute-done.54 = f32[128,256]{1,0:T(8,128)S(1)} collective-permute-done((f32[128,256]{1,0:T(8,128)S(1)}, f32[128,256]{1,0:T(8,128)S(1)}, u32[]{:S(2)}, u32[]{:S(2)}) %collective-permute-start.54) | collective-permute-done | bytes 131104 | tf_op jit(solution)/shard_map/ppermute | solution.py:279
  248.6 9.1 %collective-permute-start.57 = (f32[128,256]{1,0:T(8,128)S(1)}, f32[128,256]{1,0:T(8,128)S(1)}, u32[]{:S(2)}, u32[]{:S(2)}) collective-permute-start(f32[128,256]{1,0:T(8,128)S(1)} %fusion.1), channel_id=1, source_target_pairs={{0,24},{2,26},{4,28},{6,30},{8,16},{10,18},{12,20},{14,22},{16,8},... | collective-permute-start | bytes 393224 | tf_op jit(solution)/shard_map/ppermute | solution.py:279
  262.1 5.7 %collective-permute-done.56 = f32[128,256]{1,0:T(8,128)S(1)} collective-permute-done((f32[128,256]{1,0:T(8,128)S(1)}, f32[128,256]{1,0:T(8,128)S(1)}, u32[]{:S(2)}, u32[]{:S(2)}) %collective-permute-start.56) | collective-permute-done | bytes 131104 | tf_op jit(solution)/shard_map/ppermute | solution.py:279
  267.9 5.3 %collective-permute-done.50.refs_5_ = bf16[2,256,256]{2,1,0:T(8,128)(2,1)S(1)} collective-permute-done((bf16[2,256,256]{2,1,0:T(8,128)(2,1)S(1)}, bf16[2,256,256]{2,1,0:T(8,128)(2,1)S(1)}, u32[]{:S(2)}, u32[]{:S(2)}) %collective-permute-start.50) | collective-permute-done | bytes 262176 | tf_op jit(solution)/shard_map/ppermute | solution.py:284
  273.3 6.8 %collective-permute-start.58 = (f32[128,256]{1,0:T(8,128)S(1)}, f32[128,256]{1,0:T(8,128)S(1)}, u32[]{:S(2)}, u32[]{:S(2)}) collective-permute-start(f32[128,256]{1,0:T(8,128)S(1)} %add_add_fusion), channel_id=1, source_target_pairs={{0,6},{2,4},{4,2},{6,0},{8,14},{10,12},{12,10},{14,8},{16,22},{18,... | collective-permute-start | bytes 393224 | tf_op jit(solution)/shard_map/ppermute | solution.py:279
  281.3 2.6 collective-permute-done.58
  295.2 3.1 collective-permute-done.64
  299.4 7.1 %collective-permute-start.66 = (f32[96,256]{1,0:T(8,128)S(1)}, f32[96,256]{1,0:T(8,128)S(1)}, u32[]{:S(2)}, u32[]{:S(2)}) collective-permute-start(f32[96,256]{1,0:T(8,128)S(1)} %fusion.5), channel_id=1, source_target_pairs={{0,16},{2,18},{4,20},{6,22},{8,24},{10,26},{12,28},{14,30},{16,0},... | collective-permute-start | bytes 294920 | tf_op jit(solution)/shard_map/ppermute | solution.py:279
  306.5 6.8 %collective-permute-done.66 = f32[96,256]{1,0:T(8,128)S(1)} collective-permute-done((f32[96,256]{1,0:T(8,128)S(1)}, f32[96,256]{1,0:T(8,128)S(1)}, u32[]{:S(2)}, u32[]{:S(2)}) %collective-permute-start.66) | collective-permute-done | bytes 98336 | tf_op jit(solution)/shard_map/ppermute | solution.py:279
  316.9 2.5 collective-permute-done.68
  322.2 12.5 %shard_map.78 = f32[512,256]{1,0:T(8,128)} custom-call(s32[1]{0:T(128)} %bitcast.core.refs_0_, f32[256,512]{1,0:T(8,128)S(1)} %get-tuple-element.80.mine.refs_1_, f32[256,512]{1,0:T(8,128)S(1)} %collective-permute-done.61.theirs.refs_2_, f32[384,256]{1,0:T(8,128)S(1)} %pad_maximum_fusion.3.refs_3_, f32[384,256]{1,0:T(8,128)S(1)} %collective-permute-done.71.refs_4_), custom_call_target="tpu_custom_call" | custom-call | flops 17179869184 | bytes 2359300 | tf_op jit(solution)/shard_map/pallas_call | solution.py:37
  (211 shorter events, 100.3 us)
Async XLA Ops:
  2.7 10.5 %collective-permute-start.1 = (bf16[2,256,256]{2,1,0:T(8,128)(2,1)S(1)}, bf16[2,256,256]{2,1,0:T(8,128)(2,1)S(1)}, u32[]{:S(2)}, u32[]{:S(2)}) collective-permute-start(bf16[2,256,256]{2,1,0:T(8,128)(2,1)S(1)} %get-tuple-element.43.refs_0_), channel_id=1, source_target_pairs={{0,8},{2,10},{4,12},{6,14},{8,16},{10,18},{12,20},{14,22},{16,24},... | collective-permute-start | bytes 786440 | tf_op jit(solution)/shard_map/ppermute | solution.py:284
  7.6 7.8 %collective-permute-start.2 = (bf16[2,256,256]{2,1,0:T(8,128)(2,1)S(1)}, bf16[2,256,256]{2,1,0:T(8,128)(2,1)S(1)}, u32[]{:S(2)}, u32[]{:S(2)}) collective-permute-start(bf16[2,256,256]{2,1,0:T(8,128)(2,1)S(1)} %get-tuple-element.43.refs_0_), channel_id=1, source_target_pairs={{0,2},{2,0},{4,6},{6,4},{8,10},{10,8},{12,14},{14,12},{16,18},{18,... | collective-permute-start | bytes 786440 | tf_op jit(solution)/shard_map/ppermute | solution.py:279
  9.2 10.7 %collective-permute-start.3 = (bf16[2,256,256]{2,1,0:T(8,128)(2,1)S(1)}, bf16[2,256,256]{2,1,0:T(8,128)(2,1)S(1)}, u32[]{:S(2)}, u32[]{:S(2)}) collective-permute-start(bf16[2,256,256]{2,1,0:T(8,128)(2,1)S(1)} %get-tuple-element.43.refs_0_), channel_id=1, source_target_pairs={{0,4},{2,6},{8,12},{10,14},{4,16},{6,18},{16,20},{18,22},{12,24},{... | collective-permute-start | bytes 786440 | tf_op jit(solution)/shard_map/ppermute | solution.py:290
  17.6 8.3 %collective-permute-start.6 = (bf16[2,256,256]{2,1,0:T(8,128)(2,1)S(1)}, bf16[2,256,256]{2,1,0:T(8,128)(2,1)S(1)}, u32[]{:S(2)}, u32[]{:S(2)}) collective-permute-start(bf16[2,256,256]{2,1,0:T(8,128)(2,1)S(1)} %collective-permute-done.1.refs_2_), channel_id=1, source_target_pairs={{0,4},{2,6},{4,0},{6,2},{8,12},{10,14},{12,8},{14,10},{16,20},{18,... | collective-permute-start | bytes 786440 | tf_op jit(solution)/shard_map/ppermute | solution.py:279
  23.7 8.7 %collective-permute-start.5 = (bf16[2,256,256]{2,1,0:T(8,128)(2,1)S(1)}, bf16[2,256,256]{2,1,0:T(8,128)(2,1)S(1)}, u32[]{:S(2)}, u32[]{:S(2)}) collective-permute-start(bf16[2,256,256]{2,1,0:T(8,128)(2,1)S(1)} %collective-permute-done.3.refs_4_), channel_id=1, source_target_pairs={{0,2},{2,0},{4,6},{6,4},{8,10},{10,8},{12,14},{14,12},{16,18},{18,... | collective-permute-start | bytes 786440 | tf_op jit(solution)/shard_map/ppermute | solution.py:279
  26.0 9.3 %collective-permute-start.7 = (bf16[2,256,256]{2,1,0:T(8,128)(2,1)S(1)}, bf16[2,256,256]{2,1,0:T(8,128)(2,1)S(1)}, u32[]{:S(2)}, u32[]{:S(2)}) collective-permute-start(bf16[2,256,256]{2,1,0:T(8,128)(2,1)S(1)} %collective-permute-done.6.refs_6_), channel_id=1, source_target_pairs={{0,2},{2,0},{4,6},{6,4},{8,10},{10,8},{12,14},{14,12},{16,18},{18,... | collective-permute-start | bytes 786440 | tf_op jit(solution)/shard_map/ppermute | solution.py:279
  55.0 16.1 %collective-permute-start.15 = (bf16[16,256,256]{2,1,0:T(8,128)(2,1)S(1)}, bf16[16,256,256]{2,1,0:T(8,128)(2,1)}, u32[]{:S(2)}, u32[]{:S(2)}) collective-permute-start(bf16[16,256,256]{2,1,0:T(8,128)(2,1)S(1)} %get-tuple-element.56.refs_8_), channel_id=1, source_target_pairs={{0,1},{1,0},{2,3},{3,2},{4,5},{5,4},{6,7},{7,6},{8,9},{9,8},{10,11... | collective-permute-start | bytes 6291464 | tf_op jit(solution)/shard_map/ppermute | solution.py:275
  55.0 9.4 %collective-permute-start.12 = (bf16[2,256,256]{2,1,0:T(8,128)(2,1)}, bf16[2,256,256]{2,1,0:T(8,128)(2,1)}, u32[]{:S(2)}, u32[]{:S(2)}) collective-permute-start(bf16[2,256,256]{2,1,0:T(8,128)(2,1)} %get-tuple-element.55), channel_id=1, source_target_pairs={{0,2},{2,0},{4,6},{6,4},{8,10},{10,8},{12,14},{14,12},{16,18},{18,... | collective-permute-start | bytes 786440 | tf_op jit(solution)/shard_map/ppermute | solution.py:279
  55.0 15.0 %collective-permute-start.9 = (bf16[2,256,256]{2,1,0:T(8,128)(2,1)}, bf16[2,256,256]{2,1,0:T(8,128)(2,1)}, u32[]{:S(2)}, u32[]{:S(2)}) collective-permute-start(bf16[2,256,256]{2,1,0:T(8,128)(2,1)} %get-tuple-element.51), channel_id=1, source_target_pairs={{0,2},{2,0},{4,6},{6,4},{8,10},{10,8},{12,14},{14,12},{16,18},{18,... | collective-permute-start | bytes 786440 | tf_op jit(solution)/shard_map/ppermute | solution.py:279
  57.0 32.8 %collective-permute-start.8 = (bf16[2,256,256]{2,1,0:T(8,128)(2,1)}, bf16[2,256,256]{2,1,0:T(8,128)(2,1)S(1)}, u32[]{:S(2)}, u32[]{:S(2)}) collective-permute-start(bf16[2,256,256]{2,1,0:T(8,128)(2,1)} %copy-done.30), channel_id=1, source_target_pairs={{0,2},{2,0},{4,6},{6,4},{8,10},{10,8},{12,14},{14,12},{16,18},{18,... | collective-permute-start | bytes 786440 | tf_op jit(solution)/shard_map/ppermute | solution.py:279
  57.1 23.7 %collective-permute-start.11 = (bf16[2,256,256]{2,1,0:T(8,128)(2,1)}, bf16[2,256,256]{2,1,0:T(8,128)(2,1)S(1)}, u32[]{:S(2)}, u32[]{:S(2)}) collective-permute-start(bf16[2,256,256]{2,1,0:T(8,128)(2,1)} %copy-done.31), channel_id=1, source_target_pairs={{0,2},{2,0},{4,6},{6,4},{8,10},{10,8},{12,14},{14,12},{16,18},{18,... | collective-permute-start | bytes 786440 | tf_op jit(solution)/shard_map/ppermute | solution.py:279
  65.6 18.8 %collective-permute-start.13 = (bf16[2,256,256]{2,1,0:T(8,128)(2,1)S(1)}, bf16[2,256,256]{2,1,0:T(8,128)(2,1)S(1)}, u32[]{:S(2)}, u32[]{:S(2)}) collective-permute-start(bf16[2,256,256]{2,1,0:T(8,128)(2,1)S(1)} %add_convert_fusion.4), channel_id=1, source_target_pairs={{0,4},{2,6},{4,0},{6,2},{8,12},{10,14},{12,8},{14,10},{16,20},{18,... | collective-permute-start | bytes 786440 | tf_op jit(solution)/shard_map/ppermute | solution.py:279
  89.8 15.4 %collective-permute-start.21 = (f32[128,256]{1,0:T(8,128)S(1)}, f32[128,256]{1,0:T(8,128)S(1)}, u32[]{:S(2)}, u32[]{:S(2)}) collective-permute-start(f32[128,256]{1,0:T(8,128)S(1)} %fusion.3), channel_id=1, source_target_pairs={{0,24},{2,26},{4,28},{6,30},{8,16},{10,18},{12,20},{14,22},{16,8},... | collective-permute-start | bytes 393224 | tf_op jit(solution)/shard_map/ppermute | solution.py:279
  100.7 17.8 %collective-permute-start.20 = (f32[128,256]{1,0:T(8,128)S(1)}, f32[128,256]{1,0:T(8,128)S(1)}, u32[]{:S(2)}, u32[]{:S(2)}) collective-permute-start(f32[128,256]{1,0:T(8,128)S(1)} %fusion.3), channel_id=1, source_target_pairs={{0,16},{2,18},{4,20},{6,22},{8,24},{10,26},{12,28},{14,30},{16,0},... | collective-permute-start | bytes 393224 | tf_op jit(solution)/shard_map/ppermute | solution.py:279
  101.9 16.6 %collective-permute-start.19 = (f32[128,256]{1,0:T(8,128)S(1)}, f32[128,256]{1,0:T(8,128)S(1)}, u32[]{:S(2)}, u32[]{:S(2)}) collective-permute-start(f32[128,256]{1,0:T(8,128)S(1)} %fusion.3), channel_id=1, source_target_pairs={{0,8},{2,10},{4,12},{6,14},{8,0},{10,2},{12,4},{14,6},{16,24},{18,... | collective-permute-start | bytes 393224 | tf_op jit(solution)/shard_map/ppermute | solution.py:279
  102.4 16.1 %collective-permute-start.10 = (bf16[2,256,256]{2,1,0:T(8,128)(2,1)S(1)}, bf16[2,256,256]{2,1,0:T(8,128)(2,1)S(1)}, u32[]{:S(2)}, u32[]{:S(2)}) collective-permute-start(bf16[2,256,256]{2,1,0:T(8,128)(2,1)S(1)} %add_convert_fusion.5), channel_id=1, source_target_pairs={{4,0},{6,2},{12,8},{14,10},{16,4},{18,6},{20,16},{22,18},{24,12},{... | collective-permute-start | bytes 786440 | tf_op jit(solution)/shard_map/ppermute | solution.py:290
  103.7 14.9 %collective-permute-start.14 = (bf16[2,256,256]{2,1,0:T(8,128)(2,1)S(1)}, bf16[2,256,256]{2,1,0:T(8,128)(2,1)S(1)}, u32[]{:S(2)}, u32[]{:S(2)}) collective-permute-start(bf16[2,256,256]{2,1,0:T(8,128)(2,1)S(1)} %add_convert_fusion.3), channel_id=1, source_target_pairs={{8,0},{10,2},{12,4},{14,6},{16,8},{18,10},{20,12},{22,14},{24,16},... | collective-permute-start | bytes 786440 | tf_op jit(solution)/shard_map/ppermute | solution.py:284
  105.2 28.1 %collective-permute-start = (f32[256,512]{1,0:T(8,128)S(1)}, f32[256,512]{1,0:T(8,128)S(1)}, u32[]{:S(2)}, u32[]{:S(2)}) collective-permute-start(f32[256,512]{1,0:T(8,128)S(1)} %copy-done.2), channel_id=1, source_target_pairs={{0,1},{1,0},{2,3},{3,2},{4,5},{5,4},{6,7},{7,6},{8,9},{9,8},{10,11... | collective-permute-start | bytes 1572872 | tf_op jit(solution)/shard_map/ppermute | solution.py:275
  118.6 10.1 %collective-permute-start.22 = (f32[128,256]{1,0:T(8,128)S(1)}, f32[128,256]{1,0:T(8,128)S(1)}, u32[]{:S(2)}, u32[]{:S(2)}) collective-permute-start(f32[128,256]{1,0:T(8,128)S(1)} %add_add_fusion.1), channel_id=1, source_target_pairs={{0,6},{2,4},{4,2},{6,0},{8,14},{10,12},{12,10},{14,8},{16,22},{18,... | collective-permute-start | bytes 393224 | tf_op jit(solution)/shard_map/ppermute | solution.py:279
  125.6 7.6 %collective-permute-start.24 = (f32[128,256]{1,0:T(8,128)S(1)}, f32[128,256]{1,0:T(8,128)S(1)}, u32[]{:S(2)}, u32[]{:S(2)}) collective-permute-start(f32[128,256]{1,0:T(8,128)S(1)} %add_add_fusion.1), channel_id=1, source_target_pairs={{0,2},{2,0},{4,6},{6,4},{8,10},{10,8},{12,14},{14,12},{16,18},{18,... | collective-permute-start | bytes 393224 | tf_op jit(solution)/shard_map/ppermute | solution.py:279
  144.1 7.3 %collective-permute-start.31 = (f32[96,256]{1,0:T(8,128)S(1)}, f32[96,256]{1,0:T(8,128)S(1)}, u32[]{:S(2)}, u32[]{:S(2)}) collective-permute-start(f32[96,256]{1,0:T(8,128)S(1)} %fusion.7), channel_id=1, source_target_pairs={{0,24},{2,26},{4,28},{6,30},{8,16},{10,18},{12,20},{14,22},{16,8},... | collective-permute-start | bytes 294920 | tf_op jit(solution)/shard_map/ppermute | solution.py:279
  144.2 14.1 %collective-permute-start.30 = (f32[96,256]{1,0:T(8,128)S(1)}, f32[96,256]{1,0:T(8,128)S(1)}, u32[]{:S(2)}, u32[]{:S(2)}) collective-permute-start(f32[96,256]{1,0:T(8,128)S(1)} %fusion.7), channel_id=1, source_target_pairs={{0,16},{2,18},{4,20},{6,22},{8,24},{10,26},{12,28},{14,30},{16,0},... | collective-permute-start | bytes 294920 | tf_op jit(solution)/shard_map/ppermute | solution.py:279
  181.3 7.5 %collective-permute-start.37 = (bf16[2,256,256]{2,1,0:T(8,128)(2,1)S(1)}, bf16[2,256,256]{2,1,0:T(8,128)(2,1)S(1)}, u32[]{:S(2)}, u32[]{:S(2)}) collective-permute-start(bf16[2,256,256]{2,1,0:T(8,128)(2,1)S(1)} %get-tuple-element.62.refs_0_), channel_id=1, source_target_pairs={{0,8},{2,10},{4,12},{6,14},{8,16},{10,18},{12,20},{14,22},{16,24},... | collective-permute-start | bytes 786440 | tf_op jit(solution)/shard_map/ppermute | solution.py:284
  183.0 8.1 %collective-permute-start.38 = (bf16[2,256,256]{2,1,0:T(8,128)(2,1)S(1)}, bf16[2,256,256]{2,1,0:T(8,128)(2,1)S(1)}, u32[]{:S(2)}, u32[]{:S(2)}) collective-permute-start(bf16[2,256,256]{2,1,0:T(8,128)(2,1)S(1)} %get-tuple-element.62.refs_0_), channel_id=1, source_target_pairs={{0,2},{2,0},{4,6},{6,4},{8,10},{10,8},{12,14},{14,12},{16,18},{18,... | collective-permute-start | bytes 786440 | tf_op jit(solution)/shard_map/ppermute | solution.py:279
  184.3 8.7 %collective-permute-start.39 = (bf16[2,256,256]{2,1,0:T(8,128)(2,1)S(1)}, bf16[2,256,256]{2,1,0:T(8,128)(2,1)S(1)}, u32[]{:S(2)}, u32[]{:S(2)}) collective-permute-start(bf16[2,256,256]{2,1,0:T(8,128)(2,1)S(1)} %get-tuple-element.62.refs_0_), channel_id=1, source_target_pairs={{0,4},{2,6},{8,12},{10,14},{4,16},{6,18},{16,20},{18,22},{12,24},{... | collective-permute-start | bytes 786440 | tf_op jit(solution)/shard_map/ppermute | solution.py:290
  191.1 7.2 %collective-permute-start.40 = (bf16[2,256,256]{2,1,0:T(8,128)(2,1)S(1)}, bf16[2,256,256]{2,1,0:T(8,128)(2,1)S(1)}, u32[]{:S(2)}, u32[]{:S(2)}) collective-permute-start(bf16[2,256,256]{2,1,0:T(8,128)(2,1)S(1)} %collective-permute-done.37.refs_2_), channel_id=1, source_target_pairs={{0,2},{2,0},{4,6},{6,4},{8,10},{10,8},{12,14},{14,12},{16,18},{18,... | collective-permute-start | bytes 786440 | tf_op jit(solution)/shard_map/ppermute | solution.py:279
  192.4 7.2 %collective-permute-start.42 = (bf16[2,256,256]{2,1,0:T(8,128)(2,1)S(1)}, bf16[2,256,256]{2,1,0:T(8,128)(2,1)S(1)}, u32[]{:S(2)}, u32[]{:S(2)}) collective-permute-start(bf16[2,256,256]{2,1,0:T(8,128)(2,1)S(1)} %collective-permute-done.37.refs_2_), channel_id=1, source_target_pairs={{0,4},{2,6},{4,0},{6,2},{8,12},{10,14},{12,8},{14,10},{16,20},{18,... | collective-permute-start | bytes 786440 | tf_op jit(solution)/shard_map/ppermute | solution.py:279
  198.3 9.1 %collective-permute-start.41 = (bf16[2,256,256]{2,1,0:T(8,128)(2,1)S(1)}, bf16[2,256,256]{2,1,0:T(8,128)(2,1)S(1)}, u32[]{:S(2)}, u32[]{:S(2)}) collective-permute-start(bf16[2,256,256]{2,1,0:T(8,128)(2,1)S(1)} %collective-permute-done.39.refs_4_), channel_id=1, source_target_pairs={{0,2},{2,0},{4,6},{6,4},{8,10},{10,8},{12,14},{14,12},{16,18},{18,... | collective-permute-start | bytes 786440 | tf_op jit(solution)/shard_map/ppermute | solution.py:279
  199.6 10.6 %collective-permute-start.43 = (bf16[2,256,256]{2,1,0:T(8,128)(2,1)S(1)}, bf16[2,256,256]{2,1,0:T(8,128)(2,1)S(1)}, u32[]{:S(2)}, u32[]{:S(2)}) collective-permute-start(bf16[2,256,256]{2,1,0:T(8,128)(2,1)S(1)} %collective-permute-done.42.refs_6_), channel_id=1, source_target_pairs={{0,2},{2,0},{4,6},{6,4},{8,10},{10,8},{12,14},{14,12},{16,18},{18,... | collective-permute-start | bytes 786440 | tf_op jit(solution)/shard_map/ppermute | solution.py:279
  214.1 14.9 %collective-permute-start.51 = (bf16[16,256,256]{2,1,0:T(8,128)(2,1)S(1)}, bf16[16,256,256]{2,1,0:T(8,128)(2,1)S(1)}, u32[]{:S(2)}, u32[]{:S(2)}) collective-permute-start(bf16[16,256,256]{2,1,0:T(8,128)(2,1)S(1)} %get-tuple-element.75.refs_8_), channel_id=1, source_target_pairs={{0,1},{1,0},{2,3},{3,2},{4,5},{5,4},{6,7},{7,6},{8,9},{9,8},{10,11... | collective-permute-start | bytes 6291464 | tf_op jit(solution)/shard_map/ppermute | solution.py:275
  214.2 9.2 %collective-permute-start.48 = (bf16[2,256,256]{2,1,0:T(8,128)(2,1)S(1)}, bf16[2,256,256]{2,1,0:T(8,128)(2,1)S(1)}, u32[]{:S(2)}, u32[]{:S(2)}) collective-permute-start(bf16[2,256,256]{2,1,0:T(8,128)(2,1)S(1)} %get-tuple-element.74), channel_id=1, source_target_pairs={{0,2},{2,0},{4,6},{6,4},{8,10},{10,8},{12,14},{14,12},{16,18},{18,... | collective-permute-start | bytes 786440 | tf_op jit(solution)/shard_map/ppermute | solution.py:279
  214.2 14.7 %collective-permute-start.45 = (bf16[2,256,256]{2,1,0:T(8,128)(2,1)S(1)}, bf16[2,256,256]{2,1,0:T(8,128)(2,1)S(1)}, u32[]{:S(2)}, u32[]{:S(2)}) collective-permute-start(bf16[2,256,256]{2,1,0:T(8,128)(2,1)S(1)} %get-tuple-element.70), channel_id=1, source_target_pairs={{0,2},{2,0},{4,6},{6,4},{8,10},{10,8},{12,14},{14,12},{16,18},{18,... | collective-permute-start | bytes 786440 | tf_op jit(solution)/shard_map/ppermute | solution.py:279
  216.2 32.4 %collective-permute-start.44 = (bf16[2,256,256]{2,1,0:T(8,128)(2,1)S(1)}, bf16[2,256,256]{2,1,0:T(8,128)(2,1)S(1)}, u32[]{:S(2)}, u32[]{:S(2)}) collective-permute-start(bf16[2,256,256]{2,1,0:T(8,128)(2,1)S(1)} %get-tuple-element.68), channel_id=1, source_target_pairs={{0,2},{2,0},{4,6},{6,4},{8,10},{10,8},{12,14},{14,12},{16,18},{18,... | collective-permute-start | bytes 786440 | tf_op jit(solution)/shard_map/ppermute | solution.py:279
  216.3 23.4 %collective-permute-start.47 = (bf16[2,256,256]{2,1,0:T(8,128)(2,1)S(1)}, bf16[2,256,256]{2,1,0:T(8,128)(2,1)S(1)}, u32[]{:S(2)}, u32[]{:S(2)}) collective-permute-start(bf16[2,256,256]{2,1,0:T(8,128)(2,1)S(1)} %get-tuple-element.72), channel_id=1, source_target_pairs={{0,2},{2,0},{4,6},{6,4},{8,10},{10,8},{12,14},{14,12},{16,18},{18,... | collective-permute-start | bytes 786440 | tf_op jit(solution)/shard_map/ppermute | solution.py:279
  223.4 19.9 %collective-permute-start.49 = (bf16[2,256,256]{2,1,0:T(8,128)(2,1)S(1)}, bf16[2,256,256]{2,1,0:T(8,128)(2,1)S(1)}, u32[]{:S(2)}, u32[]{:S(2)}) collective-permute-start(bf16[2,256,256]{2,1,0:T(8,128)(2,1)S(1)} %add_convert_fusion.1), channel_id=1, source_target_pairs={{0,4},{2,6},{4,0},{6,2},{8,12},{10,14},{12,8},{14,10},{16,20},{18,... | collective-permute-start | bytes 786440 | tf_op jit(solution)/shard_map/ppermute | solution.py:279
  239.8 7.4 %collective-permute-start.54 = (f32[128,256]{1,0:T(8,128)S(1)}, f32[128,256]{1,0:T(8,128)S(1)}, u32[]{:S(2)}, u32[]{:S(2)}) collective-permute-start(f32[128,256]{1,0:T(8,128)S(1)} %get-tuple-element.87), channel_id=1, source_target_pairs={{0,6},{2,4},{4,2},{6,0},{8,14},{10,12},{12,10},{14,8},{16,22},{18,... | collective-permute-start | bytes 393224 | tf_op jit(solution)/shard_map/ppermute | solution.py:279
  241.3 7.3 %collective-permute-start.53 = (f32[128,256]{1,0:T(8,128)S(1)}, f32[128,256]{1,0:T(8,128)S(1)}, u32[]{:S(2)}, u32[]{:S(2)}) collective-permute-start(f32[128,256]{1,0:T(8,128)S(1)} %get-tuple-element.88), channel_id=1, source_target_pairs={{0,4},{2,6},{4,0},{6,2},{8,12},{10,14},{12,8},{14,10},{16,20},{18,... | collective-permute-start | bytes 393224 | tf_op jit(solution)/shard_map/ppermute | solution.py:279
  241.6 7.0 %collective-permute-start.52 = (f32[128,256]{1,0:T(8,128)S(1)}, f32[128,256]{1,0:T(8,128)S(1)}, u32[]{:S(2)}, u32[]{:S(2)}) collective-permute-start(f32[128,256]{1,0:T(8,128)S(1)} %get-tuple-element.86), channel_id=1, source_target_pairs={{0,2},{2,0},{4,6},{6,4},{8,10},{10,8},{12,14},{14,12},{16,18},{18,... | collective-permute-start | bytes 393224 | tf_op jit(solution)/shard_map/ppermute | solution.py:279
  248.6 13.5 %collective-permute-start.57 = (f32[128,256]{1,0:T(8,128)S(1)}, f32[128,256]{1,0:T(8,128)S(1)}, u32[]{:S(2)}, u32[]{:S(2)}) collective-permute-start(f32[128,256]{1,0:T(8,128)S(1)} %fusion.1), channel_id=1, source_target_pairs={{0,24},{2,26},{4,28},{6,30},{8,16},{10,18},{12,20},{14,22},{16,8},... | collective-permute-start | bytes 393224 | tf_op jit(solution)/shard_map/ppermute | solution.py:279
  257.7 10.1 %collective-permute-start.56 = (f32[128,256]{1,0:T(8,128)S(1)}, f32[128,256]{1,0:T(8,128)S(1)}, u32[]{:S(2)}, u32[]{:S(2)}) collective-permute-start(f32[128,256]{1,0:T(8,128)S(1)} %fusion.1), channel_id=1, source_target_pairs={{0,16},{2,18},{4,20},{6,22},{8,24},{10,26},{12,28},{14,30},{16,0},... | collective-permute-start | bytes 393224 | tf_op jit(solution)/shard_map/ppermute | solution.py:279
  257.7 10.1 %collective-permute-start.55 = (f32[128,256]{1,0:T(8,128)S(1)}, f32[128,256]{1,0:T(8,128)S(1)}, u32[]{:S(2)}, u32[]{:S(2)}) collective-permute-start(f32[128,256]{1,0:T(8,128)S(1)} %fusion.1), channel_id=1, source_target_pairs={{0,8},{2,10},{4,12},{6,14},{8,0},{10,2},{12,4},{14,6},{16,24},{18,... | collective-permute-start | bytes 393224 | tf_op jit(solution)/shard_map/ppermute | solution.py:279
  258.4 9.5 %collective-permute-start.46 = (bf16[2,256,256]{2,1,0:T(8,128)(2,1)S(1)}, bf16[2,256,256]{2,1,0:T(8,128)(2,1)S(1)}, u32[]{:S(2)}, u32[]{:S(2)}) collective-permute-start(bf16[2,256,256]{2,1,0:T(8,128)(2,1)S(1)} %add_convert_fusion.2), channel_id=1, source_target_pairs={{4,0},{6,2},{12,8},{14,10},{16,4},{18,6},{20,16},{22,18},{24,12},{... | collective-permute-start | bytes 786440 | tf_op jit(solution)/shard_map/ppermute | solution.py:290
  259.7 13.6 %collective-permute-start.50 = (bf16[2,256,256]{2,1,0:T(8,128)(2,1)S(1)}, bf16[2,256,256]{2,1,0:T(8,128)(2,1)S(1)}, u32[]{:S(2)}, u32[]{:S(2)}) collective-permute-start(bf16[2,256,256]{2,1,0:T(8,128)(2,1)S(1)} %add_convert_fusion), channel_id=1, source_target_pairs={{8,0},{10,2},{12,4},{14,6},{16,8},{18,10},{20,12},{22,14},{24,16},... | collective-permute-start | bytes 786440 | tf_op jit(solution)/shard_map/ppermute | solution.py:284
  262.1 25.5 %collective-permute-start.36 = (f32[256,512]{1,0:T(8,128)S(1)}, f32[256,512]{1,0:T(8,128)S(1)}, u32[]{:S(2)}, u32[]{:S(2)}) collective-permute-start(f32[256,512]{1,0:T(8,128)S(1)} %get-tuple-element.61.refs_0_), channel_id=1, source_target_pairs={{0,1},{1,0},{2,3},{3,2},{4,5},{5,4},{6,7},{7,6},{8,9},{9,8},{10,11... | collective-permute-start | bytes 1572872 | tf_op jit(solution)/shard_map/ppermute | solution.py:275
  273.3 10.6 %collective-permute-start.58 = (f32[128,256]{1,0:T(8,128)S(1)}, f32[128,256]{1,0:T(8,128)S(1)}, u32[]{:S(2)}, u32[]{:S(2)}) collective-permute-start(f32[128,256]{1,0:T(8,128)S(1)} %add_add_fusion), channel_id=1, source_target_pairs={{0,6},{2,4},{4,2},{6,0},{8,14},{10,12},{12,10},{14,8},{16,22},{18,... | collective-permute-start | bytes 393224 | tf_op jit(solution)/shard_map/ppermute | solution.py:279
  280.1 7.4 %collective-permute-start.60 = (f32[128,256]{1,0:T(8,128)S(1)}, f32[128,256]{1,0:T(8,128)S(1)}, u32[]{:S(2)}, u32[]{:S(2)}) collective-permute-start(f32[128,256]{1,0:T(8,128)S(1)} %add_add_fusion), channel_id=1, source_target_pairs={{0,2},{2,0},{4,6},{6,4},{8,10},{10,8},{12,14},{14,12},{16,18},{18,... | collective-permute-start | bytes 393224 | tf_op jit(solution)/shard_map/ppermute | solution.py:279
  299.3 7.2 %collective-permute-start.67 = (f32[96,256]{1,0:T(8,128)S(1)}, f32[96,256]{1,0:T(8,128)S(1)}, u32[]{:S(2)}, u32[]{:S(2)}) collective-permute-start(f32[96,256]{1,0:T(8,128)S(1)} %fusion.5), channel_id=1, source_target_pairs={{0,24},{2,26},{4,28},{6,30},{8,16},{10,18},{12,20},{14,22},{16,8},... | collective-permute-start | bytes 294920 | tf_op jit(solution)/shard_map/ppermute | solution.py:279
  299.4 13.9 %collective-permute-start.66 = (f32[96,256]{1,0:T(8,128)S(1)}, f32[96,256]{1,0:T(8,128)S(1)}, u32[]{:S(2)}, u32[]{:S(2)}) collective-permute-start(f32[96,256]{1,0:T(8,128)S(1)} %fusion.5), channel_id=1, source_target_pairs={{0,16},{2,18},{4,20},{6,22},{8,24},{10,26},{12,28},{14,30},{16,0},... | collective-permute-start | bytes 294920 | tf_op jit(solution)/shard_map/ppermute | solution.py:279
  (62 other events, 488.3 us)

commit v3 on v2

--- a/solution.py
+++ b/solution.py
@@ -11,6 +11,7 @@
 REACH = 4
 
 f32, bf16 = jnp.float32, jnp.bfloat16
+SEGMENT_KINDS = (f32, bf16, f32, f32, f32, bf16, bf16, bf16)
 VMEM, SMEM = pltpu.VMEM, pltpu.SMEM
 
 
@@ -59,7 +60,7 @@
 
 def apply_kernel(meta, rows, cols, *refs):
     pieces, tiles = refs[: 2 * REACH], refs[2 * REACH]
-    same, cross = refs[2 * REACH + 1 : 3 * REACH + 1], refs[3 * REACH + 1 : 4 * REACH + 1]
+    out = refs[2 * REACH + 1 : 4 * REACH + 1]
     everything, window, total, sems = refs[4 * REACH + 1 :]
     step = pl.program_id(0)
     used, start, odd, pair_odd = meta[0], meta[1], meta[2], meta[3]
@@ -97,10 +98,8 @@
 
     @pl.when(step == pl.num_programs(0) - 1)
     def _():
-        for d in range(REACH):
-            for s in range(2):
-                same[d][s] = total[4 * d + s]
-                cross[d][s] = total[4 * d + 2 + s].astype(bf16)
+        for s, segment in enumerate(out):
+            segment[...] = total[pl.ds(2 * s, 2)].astype(segment.dtype)
         everything[...] = total[...].astype(bf16)
 
 
@@ -126,11 +125,11 @@
             out_specs=[whole(segment)] * (2 * REACH) + [whole(window)],
             scratch_shapes=[VMEM(window, bf16), VMEM(window, f32), pltpu.SemaphoreType.DMA((2 * REACH,))],
         ),
-        out_shape=[shape(f32, *segment)] * REACH + [shape(bf16, *segment)] * REACH + [shape(bf16, *window)],
-        compiler_params=pltpu.CompilerParams(vmem_limit_bytes=32 << 20),
+        out_shape=[shape(kind, *segment) for kind in SEGMENT_KINDS] + [shape(bf16, *window)],
+        compiler_params=pltpu.CompilerParams(vmem_limit_bytes=24 << 20),
         cost_estimate=pl.CostEstimate(flops=4 << 30, bytes_accessed=16 << 20, transcendentals=0),
     )(meta, rows, cols, *pieces, blocks)
-    return out[:REACH], out[REACH : 2 * REACH], out[2 * REACH]
+    return out[: 2 * REACH : 2], out[1 : 2 * REACH : 2], out[2 * REACH]
 
 
 def inner_kernel(*refs):
@@ -296,12 +295,12 @@
 
 def reach(u):
     two = shift(u, 2)
-    own = flip(u, 1)
     far = stride(u)
-    two, own = together(two, own)
-    side, two_x = flip(two, 2), flip(two, 1)
-    far, two_x = together(far, two_x)
-    return [u, own, two, two_x, far, flip(far, 1), side, flip(side, 1)]
+    own_x = flip(u, 1)
+    two, own_x = together(two, own_x)
+    two_x, side = flip(two, 1), flip(two, 2)
+    far, two_x, side = together(far, two_x, side)
+    return [u, own_x, two, two_x, far, flip(far, 1), side, flip(two_x, 2)]
 
 
 def place_order(parts, place):
@@ -358,15 +357,14 @@
         pieces = reach(u)
         x_other = swap_cores(x)
         same, cross, everything = apply_tiles(pieces, blocks, block_row, block_col, meta)
-        side_x, two_x = flip(cross[3], 1), flip(cross[1], 1)
-        side = flip((same[3] + side_x.astype(f32)).astype(bf16), 2)
-        theirs, _ = together(swap_cores(everything), side_x)
+        side_x, far_x, side, own_x = flip(cross[3], 2), flip(cross[2], 1), flip(same[3], 2), flip(cross[0], 1)
+        theirs, side_x, far_x = together(swap_cores(everything), side_x, far_x)
+        two_x = (cross[1] + side_x.astype(f32)).astype(bf16)
+        far = (same[2] + far_x.astype(f32)).astype(bf16)
         (inner,) = call(inner_kernel, [shape(f32, 2 * width, width)], pieces + [everything, theirs])
-        far_x, own_x = flip(cross[2], 1), flip(cross[0], 1)
-        far = (same[2] + far_x.astype(f32)).astype(bf16)
-        two = (same[1] + (two_x.astype(f32) + side.astype(f32))).astype(bf16)
+        two = (same[1] + (flip(two_x, 1).astype(f32) + side.astype(f32))).astype(bf16)
         joined = [own_x, stride(far, True), shift(two, -2)]
-        inner = summed(inner, [(two_x,), (far, two, own_x), joined[1:]])
+        inner = summed(inner, [(two_x, far), (joined[1], two), (joined[2], own_x)])
         out = [flat] + ([shape(f32, count, width)] if last else [])
         update, *residual = call(
             lambda *refs: update_kernel(rows_total, *refs), out, [x, x_other, same[0], *joined, inner]
@@ -384,7 +382,7 @@
             scratch=[VMEM(full, f32), VMEM(full, f32), VMEM(full, bf16), VMEM(full, bf16), VMEM((2 * width, count), f32)],
             smem=1,
             flops=16 << 30,
-            vmem=40,
+            vmem=28,
         )
         if last:
             return out[0], residual[0]

time: 335 us -> 314 us (0.937)
  waiting for transfers between devices: 144 us -> 133 us
  local copies, waits for them, and re-layouts: 27 us -> 20.6 us
  Pallas kernels: 43 us -> 39.3 us
    ppermute x56, waiting for transfers between devices: 129 us -> 110 us  [flip(): lax.ppermute(a, 'patch', [(i, i ^ mask) for i in range(lax.axis_size('pat...]
    ppermute x4, waiting for transfers between devices: 0.09 us -> 9.09 us  [stride(): lax.ppermute(a, 'patch', [(d, s) if back else (s, d) for s, d in route if...]
    unnamed x76 -> x72, local copies, waits for them, and re-layouts: 26.8 us -> 20.5 us
    pallas_call x2, Pallas kernels: 8.51 us -> 4.66 us  [apply_tiles(): pl.pallas_call(apply_kernel, grid_spec=pltpu.PrefetchScalarGridSpec(num_s...]
    ppermute x56, starting transfers between devices: 97.5 us -> 94.1 us  [flip(): lax.ppermute(a, 'patch', [(i, i ^ mask) for i in range(lax.axis_size('pat...]
  transfers between devices with their start and end apart: 72 -> 72, of which waited for: 47 -> 52; matrix products, arithmetic and copies ran while one was open for 1% -> 0% of each run, Pallas kernels for 1% -> 0%
where the time goes in v3:
time: 314 us
  waiting for transfers between devices  133 us (42%)
  starting transfers between devices  115 us (37%)
  Pallas kernels  39.3 us (13%)
  local copies, waits for them, and re-layouts  20.6 us (7%)
  other arithmetic  4.48 us (1%)
    ppermute x56, waiting for transfers between devices, flip(): lax.ppermute(a, 'patch', [(i, i ^ mask) for i in range(lax.axis_size('pat...  110 us
    ppermute x56, starting transfers between devices, flip(): lax.ppermute(a, 'patch', [(i, i ^ mask) for i in range(lax.axis_size('pat...  94.1 us
    pallas_call x9, Pallas kernels, call(): pl.pallas_call(kernel, out_shape=out, in_specs=[pl.BlockSpec(memory_space...  34.6 us
    unnamed x72, local copies, waits for them, and re-layouts  20.5 us
    ppermute x4, starting transfers between devices, shift(): lax.ppermute(a, 'patch', [(i - 2 * pairs, i) for i in devices if i - 2 *...  11.3 us
    ppermute x4, waiting for transfers between devices, stride(): lax.ppermute(a, 'patch', [(d, s) if back else (s, d) for s, d in route if...  9.09 us
    ppermute x4, starting transfers between devices, stride(): lax.ppermute(a, 'patch', [(d, s) if back else (s, d) for s, d in route if...  8.72 us
    ppermute x8, waiting for transfers between devices, swap_cores(): return lax.ppermute(a, 'vec', [(0, 1), (1, 0)])  7.23 us
  transfers between devices with their start and end apart: 72, of which 52 were waited for; matrix products, arithmetic and copies ran while one was open for 0% of the time, Pallas kernels for 0%

profile of v3, /device:TPU:0, one launch (start us, length us, event | category | flops | bytes accessed | tf_op | source)
XLA Modules:
  0.0 313.8 jit_solution(8426528919373978923)
XLA Ops:
  2.7 4.9 %collective-permute-start.1 = (bf16[2,256,256]{2,1,0:T(8,128)(2,1)S(1)}, bf16[2,256,256]{2,1,0:T(8,128)(2,1)S(1)}, u32[]{:S(2)}, u32[]{:S(2)}) collective-permute-start(bf16[2,256,256]{2,1,0:T(8,128)(2,1)S(1)} %get-tuple-element.49.refs_0_), channel_id=1, source_target_pairs={{0,8},{2,10},{4,12},{6,14},{8,16},{10,18},{12,20},{14,22},{16,24},... | collective-permute-start | bytes 786440 | tf_op jit(solution)/shard_map/ppermute | solution.py:283
  9.2 3.4 %collective-permute-start.3 = (bf16[2,256,256]{2,1,0:T(8,128)(2,1)S(1)}, bf16[2,256,256]{2,1,0:T(8,128)(2,1)S(1)}, u32[]{:S(2)}, u32[]{:S(2)}) collective-permute-start(bf16[2,256,256]{2,1,0:T(8,128)(2,1)S(1)} %get-tuple-element.49.refs_0_), channel_id=1, source_target_pairs={{0,4},{2,6},{8,12},{10,14},{4,16},{6,18},{16,20},{18,22},{12,24},{... | collective-permute-start | bytes 786440 | tf_op jit(solution)/shard_map/ppermute | solution.py:289
  13.1 2.3 collective-permute-done.2.refs_1_
  19.9 3.1 %collective-permute-done.4.refs_3_ = bf16[2,256,256]{2,1,0:T(8,128)(2,1)S(1)} collective-permute-done((bf16[2,256,256]{2,1,0:T(8,128)(2,1)S(1)}, bf16[2,256,256]{2,1,0:T(8,128)(2,1)S(1)}, u32[]{:S(2)}, u32[]{:S(2)}) %collective-permute-start.4) | collective-permute-done | bytes 262176 | tf_op jit(solution)/shard_map/ppermute | solution.py:278
  29.2 2.1 collective-permute-done.6.refs_5_
  39.9 3.4 %copy-done.26 = bf16[64,256,256]{2,1,0:T(8,128)(2,1)S(1)} copy-done((bf16[64,256,256]{2,1,0:T(8,128)(2,1)S(1)}, bf16[64,256,256]{2,1,0:T(8,128)(2,1)}, u32[]{:S(2)}) %copy-start.26) | copy-done | bytes 8388632
  44.6 2.8 shard_map.69
  49.7 4.5 %collective-permute-start.10 = (bf16[2,256,256]{2,1,0:T(8,128)(2,1)}, bf16[2,256,256]{2,1,0:T(8,128)(2,1)}, u32[]{:S(2)}, u32[]{:S(2)}) collective-permute-start(bf16[2,256,256]{2,1,0:T(8,128)(2,1)} %get-tuple-element.59), channel_id=1, source_target_pairs={{0,4},{2,6},{4,0},{6,2},{8,12},{10,14},{12,8},{14,10},{16,20},{18,... | collective-permute-start | bytes 786440 | tf_op jit(solution)/shard_map/ppermute | solution.py:278
  54.2 7.2 %collective-permute-done.10 = bf16[2,256,256]{2,1,0:T(8,128)(2,1)} collective-permute-done((bf16[2,256,256]{2,1,0:T(8,128)(2,1)}, bf16[2,256,256]{2,1,0:T(8,128)(2,1)}, u32[]{:S(2)}, u32[]{:S(2)}) %collective-permute-start.10) | collective-permute-done | bytes 262176 | tf_op jit(solution)/shard_map/ppermute | solution.py:278
  66.5 2.9 shard_map.70
  70.1 2.9 collective-permute-start.18
  73.6 2.3 collective-permute-done.16
  78.5 5.5 %collective-permute-done.14 = bf16[2,256,256]{2,1,0:T(8,128)(2,1)S(1)} collective-permute-done((bf16[2,256,256]{2,1,0:T(8,128)(2,1)}, bf16[2,256,256]{2,1,0:T(8,128)(2,1)S(1)}, u32[]{:S(2)}, u32[]{:S(2)}) %collective-permute-start.14) | collective-permute-done | bytes 262176 | tf_op jit(solution)/shard_map/ppermute | solution.py:278
  84.1 4.6 %collective-permute-done.12.refs_4_ = bf16[2,256,256]{2,1,0:T(8,128)(2,1)S(1)} collective-permute-done((bf16[2,256,256]{2,1,0:T(8,128)(2,1)}, bf16[2,256,256]{2,1,0:T(8,128)(2,1)S(1)}, u32[]{:S(2)}, u32[]{:S(2)}) %collective-permute-start.12) | collective-permute-done | bytes 262176 | tf_op jit(solution)/shard_map/ppermute | solution.py:289
  88.7 9.8 %collective-permute-start.19 = (f32[128,256]{1,0:T(8,128)S(1)}, f32[128,256]{1,0:T(8,128)S(1)}, u32[]{:S(2)}, u32[]{:S(2)}) collective-permute-start(f32[128,256]{1,0:T(8,128)S(1)} %fusion.3), channel_id=1, source_target_pairs={{0,8},{2,10},{4,12},{6,14},{8,0},{10,2},{12,4},{14,6},{16,24},{18,... | collective-permute-start | bytes 393224 | tf_op jit(solution)/shard_map/ppermute | solution.py:278
  98.5 3.5 %collective-permute-start.20 = (f32[128,256]{1,0:T(8,128)S(1)}, f32[128,256]{1,0:T(8,128)S(1)}, u32[]{:S(2)}, u32[]{:S(2)}) collective-permute-start(f32[128,256]{1,0:T(8,128)S(1)} %fusion.3), channel_id=1, source_target_pairs={{0,16},{2,18},{4,20},{6,22},{8,24},{10,26},{12,28},{14,30},{16,0},... | collective-permute-start | bytes 393224 | tf_op jit(solution)/shard_map/ppermute | solution.py:278
  106.7 6.8 %collective-permute-done.21 = f32[128,256]{1,0:T(8,128)S(1)} collective-permute-done((f32[128,256]{1,0:T(8,128)S(1)}, f32[128,256]{1,0:T(8,128)S(1)}, u32[]{:S(2)}, u32[]{:S(2)}) %collective-permute-start.21) | collective-permute-done | bytes 131104 | tf_op jit(solution)/shard_map/ppermute | solution.py:278
  113.5 2.3 collective-permute-done.15.refs_5_
  119.3 3.8 %collective-permute-done.22 = f32[128,256]{1,0:T(8,128)S(1)} collective-permute-done((f32[128,256]{1,0:T(8,128)S(1)}, f32[128,256]{1,0:T(8,128)S(1)}, u32[]{:S(2)}, u32[]{:S(2)}) %collective-permute-start.22) | collective-permute-done | bytes 131104 | tf_op jit(solution)/shard_map/ppermute | solution.py:278
  129.6 2.1 collective-permute-start.28
  131.7 2.2 collective-permute-done.26
  135.3 4.6 %collective-permute-start.29 = (f32[96,256]{1,0:T(8,128)S(1)}, f32[96,256]{1,0:T(8,128)S(1)}, u32[]{:S(2)}, u32[]{:S(2)}) collective-permute-start(f32[96,256]{1,0:T(8,128)S(1)} %fusion.7), channel_id=1, source_target_pairs={{0,8},{2,10},{4,12},{6,14},{8,0},{10,2},{12,4},{14,6},{16,24},{18,... | collective-permute-start | bytes 294920 | tf_op jit(solution)/shard_map/ppermute | solution.py:278
  139.9 2.4 collective-permute-start.31
  143.2 6.3 %collective-permute-done.30 = f32[96,256]{1,0:T(8,128)S(1)} collective-permute-done((f32[96,256]{1,0:T(8,128)S(1)}, f32[96,256]{1,0:T(8,128)S(1)}, u32[]{:S(2)}, u32[]{:S(2)}) %collective-permute-start.30) | collective-permute-done | bytes 98336 | tf_op jit(solution)/shard_map/ppermute | solution.py:278
  153.0 2.1 collective-permute-done.32
  158.0 14.3 %shard_map.73 = (f32[256,512]{1,0:T(8,128)S(1)}, bf16[2,256,256]{2,1,0:T(8,128)(2,1)S(1)}) custom-call(s32[1]{0:T(128)} %bitcast.core.refs_0_, f32[256,512]{1,0:T(8,128)S(1)} %shard_map.71.mine.refs_1_, f32[256,512]{1,0:T(8,128)S(1)} %collective-permute-done.25.theirs.refs_2_, f32[384,256]{1,0:T(8,128)S(1)} %pad_maximum_fusion.2.refs_3_, ...), custom_call_target="tpu_custom_call" | custom-call | flops 17179869184 | bytes 2621444 | tf_op jit(solution)/shard_map/pallas_call | solution.py:38
  172.3 3.7 %collective-permute-start.37 = (bf16[2,256,256]{2,1,0:T(8,128)(2,1)S(1)}, bf16[2,256,256]{2,1,0:T(8,128)(2,1)S(1)}, u32[]{:S(2)}, u32[]{:S(2)}) collective-permute-start(bf16[2,256,256]{2,1,0:T(8,128)(2,1)S(1)} %get-tuple-element.71.refs_0_), channel_id=1, source_target_pairs={{0,8},{2,10},{4,12},{6,14},{8,16},{10,18},{12,20},{14,22},{16,24},... | collective-permute-start | bytes 786440 | tf_op jit(solution)/shard_map/ppermute | solution.py:283
  177.5 2.5 collective-permute-start.39
  181.8 2.3 collective-permute-done.38.refs_1_
  186.1 5.2 %collective-permute-done.40.refs_3_ = bf16[2,256,256]{2,1,0:T(8,128)(2,1)S(1)} collective-permute-done((bf16[2,256,256]{2,1,0:T(8,128)(2,1)S(1)}, bf16[2,256,256]{2,1,0:T(8,128)(2,1)S(1)}, u32[]{:S(2)}, u32[]{:S(2)}) %collective-permute-start.40) | collective-permute-done | bytes 262176 | tf_op jit(solution)/shard_map/ppermute | solution.py:278
  194.4 4.5 %collective-permute-done.42.refs_5_ = bf16[2,256,256]{2,1,0:T(8,128)(2,1)S(1)} collective-permute-done((bf16[2,256,256]{2,1,0:T(8,128)(2,1)S(1)}, bf16[2,256,256]{2,1,0:T(8,128)(2,1)S(1)}, u32[]{:S(2)}, u32[]{:S(2)}) %collective-permute-start.42) | collective-permute-done | bytes 262176 | tf_op jit(solution)/shard_map/ppermute | solution.py:278
  201.4 4.4 %collective-permute-start.46 = (bf16[2,256,256]{2,1,0:T(8,128)(2,1)S(1)}, bf16[2,256,256]{2,1,0:T(8,128)(2,1)S(1)}, u32[]{:S(2)}, u32[]{:S(2)}) collective-permute-start(bf16[2,256,256]{2,1,0:T(8,128)(2,1)S(1)} %get-tuple-element.81), channel_id=1, source_target_pairs={{0,4},{2,6},{4,0},{6,2},{8,12},{10,14},{12,8},{14,10},{16,20},{18,... | collective-permute-start | bytes 786440 | tf_op jit(solution)/shard_map/ppermute | solution.py:278
  205.8 6.9 %collective-permute-done.46 = bf16[2,256,256]{2,1,0:T(8,128)(2,1)S(1)} collective-permute-done((bf16[2,256,256]{2,1,0:T(8,128)(2,1)S(1)}, bf16[2,256,256]{2,1,0:T(8,128)(2,1)S(1)}, u32[]{:S(2)}, u32[]{:S(2)}) %collective-permute-start.46) | collective-permute-done | bytes 262176 | tf_op jit(solution)/shard_map/ppermute | solution.py:278
  216.2 2.9 collective-permute-start.54
  219.7 2.3 collective-permute-done.52
  224.7 5.6 %collective-permute-done.50 = bf16[2,256,256]{2,1,0:T(8,128)(2,1)S(1)} collective-permute-done((bf16[2,256,256]{2,1,0:T(8,128)(2,1)S(1)}, bf16[2,256,256]{2,1,0:T(8,128)(2,1)S(1)}, u32[]{:S(2)}, u32[]{:S(2)}) %collective-permute-start.50) | collective-permute-done | bytes 262176 | tf_op jit(solution)/shard_map/ppermute | solution.py:278
  230.3 4.5 %collective-permute-done.48.refs_4_ = bf16[2,256,256]{2,1,0:T(8,128)(2,1)S(1)} collective-permute-done((bf16[2,256,256]{2,1,0:T(8,128)(2,1)S(1)}, bf16[2,256,256]{2,1,0:T(8,128)(2,1)S(1)}, u32[]{:S(2)}, u32[]{:S(2)}) %collective-permute-start.48) | collective-permute-done | bytes 262176 | tf_op jit(solution)/shard_map/ppermute | solution.py:289
  234.8 5.5 %collective-permute-start.55 = (f32[128,256]{1,0:T(8,128)S(1)}, f32[128,256]{1,0:T(8,128)S(1)}, u32[]{:S(2)}, u32[]{:S(2)}) collective-permute-start(f32[128,256]{1,0:T(8,128)S(1)} %fusion.1), channel_id=1, source_target_pairs={{0,8},{2,10},{4,12},{6,14},{8,0},{10,2},{12,4},{14,6},{16,24},{18,... | collective-permute-start | bytes 393224 | tf_op jit(solution)/shard_map/ppermute | solution.py:278
  240.3 5.0 %collective-permute-start.56 = (f32[128,256]{1,0:T(8,128)S(1)}, f32[128,256]{1,0:T(8,128)S(1)}, u32[]{:S(2)}, u32[]{:S(2)}) collective-permute-start(f32[128,256]{1,0:T(8,128)S(1)} %fusion.1), channel_id=1, source_target_pairs={{0,16},{2,18},{4,20},{6,22},{8,24},{10,26},{12,28},{14,30},{16,0},... | collective-permute-start | bytes 393224 | tf_op jit(solution)/shard_map/ppermute | solution.py:278
  249.8 7.1 %collective-permute-done.57 = f32[128,256]{1,0:T(8,128)S(1)} collective-permute-done((f32[128,256]{1,0:T(8,128)S(1)}, f32[128,256]{1,0:T(8,128)S(1)}, u32[]{:S(2)}, u32[]{:S(2)}) %collective-permute-start.57) | collective-permute-done | bytes 131104 | tf_op jit(solution)/shard_map/ppermute | solution.py:278
  256.9 2.0 collective-permute-done.51.refs_5_
  262.4 2.8 collective-permute-done.58
  276.0 2.8 collective-permute-done.63
  278.8 4.4 %collective-permute-start.65 = (f32[96,256]{1,0:T(8,128)S(1)}, f32[96,256]{1,0:T(8,128)S(1)}, u32[]{:S(2)}, u32[]{:S(2)}) collective-permute-start(f32[96,256]{1,0:T(8,128)S(1)} %fusion.5), channel_id=1, source_target_pairs={{0,8},{2,10},{4,12},{6,14},{8,0},{10,2},{12,4},{14,6},{16,24},{18,... | collective-permute-start | bytes 294920 | tf_op jit(solution)/shard_map/ppermute | solution.py:278
  283.2 2.4 collective-permute-start.67
  286.5 5.7 %collective-permute-done.66 = f32[96,256]{1,0:T(8,128)S(1)} collective-permute-done((f32[96,256]{1,0:T(8,128)S(1)}, f32[96,256]{1,0:T(8,128)S(1)}, u32[]{:S(2)}, u32[]{:S(2)}) %collective-permute-start.66) | collective-permute-done | bytes 98336 | tf_op jit(solution)/shard_map/ppermute | solution.py:278
  295.7 2.1 collective-permute-done.68
  301.3 12.5 %shard_map.78 = f32[512,256]{1,0:T(8,128)} custom-call(s32[1]{0:T(128)} %bitcast.core.refs_0_, f32[256,512]{1,0:T(8,128)S(1)} %get-tuple-element.92.mine.refs_1_, f32[256,512]{1,0:T(8,128)S(1)} %collective-permute-done.61.theirs.refs_2_, f32[384,256]{1,0:T(8,128)S(1)} %pad_maximum_fusion.3.refs_3_, f32[384,256]{1,0:T(8,128)S(1)} %collective-permute-done.71.refs_4_), custom_call_target="tpu_custom_call" | custom-call | flops 17179869184 | bytes 2359300 | tf_op jit(solution)/shard_map/pallas_call | solution.py:38
  (207 shorter events, 102.8 us)
Async XLA Ops:
  2.7 10.5 %collective-permute-start.1 = (bf16[2,256,256]{2,1,0:T(8,128)(2,1)S(1)}, bf16[2,256,256]{2,1,0:T(8,128)(2,1)S(1)}, u32[]{:S(2)}, u32[]{:S(2)}) collective-permute-start(bf16[2,256,256]{2,1,0:T(8,128)(2,1)S(1)} %get-tuple-element.49.refs_0_), channel_id=1, source_target_pairs={{0,8},{2,10},{4,12},{6,14},{8,16},{10,18},{12,20},{14,22},{16,24},... | collective-permute-start | bytes 786440 | tf_op jit(solution)/shard_map/ppermute | solution.py:283
  7.6 7.8 %collective-permute-start.2 = (bf16[2,256,256]{2,1,0:T(8,128)(2,1)S(1)}, bf16[2,256,256]{2,1,0:T(8,128)(2,1)S(1)}, u32[]{:S(2)}, u32[]{:S(2)}) collective-permute-start(bf16[2,256,256]{2,1,0:T(8,128)(2,1)S(1)} %get-tuple-element.49.refs_0_), channel_id=1, source_target_pairs={{0,2},{2,0},{4,6},{6,4},{8,10},{10,8},{12,14},{14,12},{16,18},{18,... | collective-permute-start | bytes 786440 | tf_op jit(solution)/shard_map/ppermute | solution.py:278
  9.2 10.7 %collective-permute-start.3 = (bf16[2,256,256]{2,1,0:T(8,128)(2,1)S(1)}, bf16[2,256,256]{2,1,0:T(8,128)(2,1)S(1)}, u32[]{:S(2)}, u32[]{:S(2)}) collective-permute-start(bf16[2,256,256]{2,1,0:T(8,128)(2,1)S(1)} %get-tuple-element.49.refs_0_), channel_id=1, source_target_pairs={{0,4},{2,6},{8,12},{10,14},{4,16},{6,18},{16,20},{18,22},{12,24},{... | collective-permute-start | bytes 786440 | tf_op jit(solution)/shard_map/ppermute | solution.py:289
  16.2 6.9 %collective-permute-start.4 = (bf16[2,256,256]{2,1,0:T(8,128)(2,1)S(1)}, bf16[2,256,256]{2,1,0:T(8,128)(2,1)S(1)}, u32[]{:S(2)}, u32[]{:S(2)}) collective-permute-start(bf16[2,256,256]{2,1,0:T(8,128)(2,1)S(1)} %collective-permute-done.1.refs_2_), channel_id=1, source_target_pairs={{0,2},{2,0},{4,6},{6,4},{8,10},{10,8},{12,14},{14,12},{16,18},{18,... | collective-permute-start | bytes 786440 | tf_op jit(solution)/shard_map/ppermute | solution.py:278
  17.6 6.6 %collective-permute-start.5 = (bf16[2,256,256]{2,1,0:T(8,128)(2,1)S(1)}, bf16[2,256,256]{2,1,0:T(8,128)(2,1)S(1)}, u32[]{:S(2)}, u32[]{:S(2)}) collective-permute-start(bf16[2,256,256]{2,1,0:T(8,128)(2,1)S(1)} %collective-permute-done.1.refs_2_), channel_id=1, source_target_pairs={{0,4},{2,6},{4,0},{6,2},{8,12},{10,14},{12,8},{14,10},{16,20},{18,... | collective-permute-start | bytes 786440 | tf_op jit(solution)/shard_map/ppermute | solution.py:278
  49.7 13.2 %collective-permute-start.9 = (bf16[16,256,256]{2,1,0:T(8,128)(2,1)S(1)}, bf16[16,256,256]{2,1,0:T(8,128)(2,1)}, u32[]{:S(2)}, u32[]{:S(2)}) collective-permute-start(bf16[16,256,256]{2,1,0:T(8,128)(2,1)S(1)} %get-tuple-element.58.refs_8_), channel_id=1, source_target_pairs={{0,1},{1,0},{2,3},{3,2},{4,5},{5,4},{6,7},{7,6},{8,9},{9,8},{10,11... | collective-permute-start | bytes 6291464 | tf_op jit(solution)/shard_map/ppermute | solution.py:274
  49.7 11.8 %collective-permute-start.10 = (bf16[2,256,256]{2,1,0:T(8,128)(2,1)}, bf16[2,256,256]{2,1,0:T(8,128)(2,1)}, u32[]{:S(2)}, u32[]{:S(2)}) collective-permute-start(bf16[2,256,256]{2,1,0:T(8,128)(2,1)} %get-tuple-element.59), channel_id=1, source_target_pairs={{0,4},{2,6},{4,0},{6,2},{8,12},{10,14},{12,8},{14,10},{16,20},{18,... | collective-permute-start | bytes 786440 | tf_op jit(solution)/shard_map/ppermute | solution.py:278
  54.2 8.8 %collective-permute-start.11 = (bf16[2,256,256]{2,1,0:T(8,128)(2,1)}, bf16[2,256,256]{2,1,0:T(8,128)(2,1)}, u32[]{:S(2)}, u32[]{:S(2)}) collective-permute-start(bf16[2,256,256]{2,1,0:T(8,128)(2,1)} %get-tuple-element.60), channel_id=1, source_target_pairs={{0,2},{2,0},{4,6},{6,4},{8,10},{10,8},{12,14},{14,12},{16,18},{18,... | collective-permute-start | bytes 786440 | tf_op jit(solution)/shard_map/ppermute | solution.py:278
  69.5 6.4 %collective-permute-start.16 = (f32[128,256]{1,0:T(8,128)S(1)}, f32[128,256]{1,0:T(8,128)S(1)}, u32[]{:S(2)}, u32[]{:S(2)}) collective-permute-start(f32[128,256]{1,0:T(8,128)S(1)} %get-tuple-element.105), channel_id=1, source_target_pairs={{0,2},{2,0},{4,6},{6,4},{8,10},{10,8},{12,14},{14,12},{16,18},{18,... | collective-permute-start | bytes 393224 | tf_op jit(solution)/shard_map/ppermute | solution.py:278
  69.8 8.5 %collective-permute-start.17 = (f32[128,256]{1,0:T(8,128)S(1)}, f32[128,256]{1,0:T(8,128)S(1)}, u32[]{:S(2)}, u32[]{:S(2)}) collective-permute-start(f32[128,256]{1,0:T(8,128)S(1)} %get-tuple-element.107), channel_id=1, source_target_pairs={{0,4},{2,6},{4,0},{6,2},{8,12},{10,14},{12,8},{14,10},{16,20},{18,... | collective-permute-start | bytes 393224 | tf_op jit(solution)/shard_map/ppermute | solution.py:278
  70.1 8.4 %collective-permute-start.18 = (f32[128,256]{1,0:T(8,128)S(1)}, f32[128,256]{1,0:T(8,128)S(1)}, u32[]{:S(2)}, u32[]{:S(2)}) collective-permute-start(f32[128,256]{1,0:T(8,128)S(1)} %get-tuple-element.106), channel_id=1, source_target_pairs={{0,6},{2,4},{4,2},{6,0},{8,14},{10,12},{12,10},{14,8},{16,22},{18,... | collective-permute-start | bytes 393224 | tf_op jit(solution)/shard_map/ppermute | solution.py:278
  73.0 11.0 %collective-permute-start.14 = (bf16[2,256,256]{2,1,0:T(8,128)(2,1)}, bf16[2,256,256]{2,1,0:T(8,128)(2,1)S(1)}, u32[]{:S(2)}, u32[]{:S(2)}) collective-permute-start(bf16[2,256,256]{2,1,0:T(8,128)(2,1)} %get-tuple-element.65), channel_id=1, source_target_pairs={{0,4},{2,6},{4,0},{6,2},{8,12},{10,14},{12,8},{14,10},{16,20},{18,... | collective-permute-start | bytes 786440 | tf_op jit(solution)/shard_map/ppermute | solution.py:278
  73.3 10.7 %collective-permute-start.13 = (bf16[2,256,256]{2,1,0:T(8,128)(2,1)}, bf16[2,256,256]{2,1,0:T(8,128)(2,1)S(1)}, u32[]{:S(2)}, u32[]{:S(2)}) collective-permute-start(bf16[2,256,256]{2,1,0:T(8,128)(2,1)} %add_convert_fusion.4), channel_id=1, source_target_pairs={{0,2},{2,0},{4,6},{6,4},{8,10},{10,8},{12,14},{14,12},{16,18},{18,... | collective-permute-start | bytes 786440 | tf_op jit(solution)/shard_map/ppermute | solution.py:278
  75.9 12.8 %collective-permute-start.12 = (bf16[2,256,256]{2,1,0:T(8,128)(2,1)}, bf16[2,256,256]{2,1,0:T(8,128)(2,1)S(1)}, u32[]{:S(2)}, u32[]{:S(2)}) collective-permute-start(bf16[2,256,256]{2,1,0:T(8,128)(2,1)} %add_convert_fusion.5), channel_id=1, source_target_pairs={{4,0},{6,2},{12,8},{14,10},{16,4},{18,6},{20,16},{22,18},{24,12},{... | collective-permute-start | bytes 786440 | tf_op jit(solution)/shard_map/ppermute | solution.py:289
  88.7 17.9 %collective-permute-start.19 = (f32[128,256]{1,0:T(8,128)S(1)}, f32[128,256]{1,0:T(8,128)S(1)}, u32[]{:S(2)}, u32[]{:S(2)}) collective-permute-start(f32[128,256]{1,0:T(8,128)S(1)} %fusion.3), channel_id=1, source_target_pairs={{0,8},{2,10},{4,12},{6,14},{8,0},{10,2},{12,4},{14,6},{16,24},{18,... | collective-permute-start | bytes 393224 | tf_op jit(solution)/shard_map/ppermute | solution.py:278
  98.5 8.2 %collective-permute-start.20 = (f32[128,256]{1,0:T(8,128)S(1)}, f32[128,256]{1,0:T(8,128)S(1)}, u32[]{:S(2)}, u32[]{:S(2)}) collective-permute-start(f32[128,256]{1,0:T(8,128)S(1)} %fusion.3), channel_id=1, source_target_pairs={{0,16},{2,18},{4,20},{6,22},{8,24},{10,26},{12,28},{14,30},{16,0},... | collective-permute-start | bytes 393224 | tf_op jit(solution)/shard_map/ppermute | solution.py:278
  102.0 11.5 %collective-permute-start.21 = (f32[128,256]{1,0:T(8,128)S(1)}, f32[128,256]{1,0:T(8,128)S(1)}, u32[]{:S(2)}, u32[]{:S(2)}) collective-permute-start(f32[128,256]{1,0:T(8,128)S(1)} %fusion.3), channel_id=1, source_target_pairs={{0,24},{2,26},{4,28},{6,30},{8,16},{10,18},{12,20},{14,22},{16,8},... | collective-permute-start | bytes 393224 | tf_op jit(solution)/shard_map/ppermute | solution.py:278
  103.5 10.1 %collective-permute-start.8 = (bf16[2,256,256]{2,1,0:T(8,128)(2,1)S(1)}, bf16[2,256,256]{2,1,0:T(8,128)(2,1)S(1)}, u32[]{:S(2)}, u32[]{:S(2)}) collective-permute-start(bf16[2,256,256]{2,1,0:T(8,128)(2,1)S(1)} %copy-done.29), channel_id=1, source_target_pairs={{0,2},{2,0},{4,6},{6,4},{8,10},{10,8},{12,14},{14,12},{16,18},{18,... | collective-permute-start | bytes 786440 | tf_op jit(solution)/shard_map/ppermute | solution.py:278
  105.2 10.6 %collective-permute-start.15 = (bf16[2,256,256]{2,1,0:T(8,128)(2,1)S(1)}, bf16[2,256,256]{2,1,0:T(8,128)(2,1)S(1)}, u32[]{:S(2)}, u32[]{:S(2)}) collective-permute-start(bf16[2,256,256]{2,1,0:T(8,128)(2,1)S(1)} %add_convert_fusion.3), channel_id=1, source_target_pairs={{8,0},{10,2},{12,4},{14,6},{16,8},{18,10},{20,12},{22,14},{24,16},... | collective-permute-start | bytes 786440 | tf_op jit(solution)/shard_map/ppermute | solution.py:283
  106.6 18.2 %collective-permute-start = (f32[256,512]{1,0:T(8,128)S(1)}, f32[256,512]{1,0:T(8,128)S(1)}, u32[]{:S(2)}, u32[]{:S(2)}) collective-permute-start(f32[256,512]{1,0:T(8,128)S(1)} %copy-done.2), channel_id=1, source_target_pairs={{0,1},{1,0},{2,3},{3,2},{4,5},{5,4},{6,7},{7,6},{8,9},{9,8},{10,11... | collective-permute-start | bytes 1572872 | tf_op jit(solution)/shard_map/ppermute | solution.py:274
  115.8 7.2 %collective-permute-start.22 = (f32[128,256]{1,0:T(8,128)S(1)}, f32[128,256]{1,0:T(8,128)S(1)}, u32[]{:S(2)}, u32[]{:S(2)}) collective-permute-start(f32[128,256]{1,0:T(8,128)S(1)} %add_add_fusion.1), channel_id=1, source_target_pairs={{0,6},{2,4},{4,2},{6,0},{8,14},{10,12},{12,10},{14,8},{16,22},{18,... | collective-permute-start | bytes 393224 | tf_op jit(solution)/shard_map/ppermute | solution.py:278
  128.6 6.7 %collective-permute-start.27 = (f32[96,256]{1,0:T(8,128)S(1)}, f32[96,256]{1,0:T(8,128)S(1)}, u32[]{:S(2)}, u32[]{:S(2)}) collective-permute-start(f32[96,256]{1,0:T(8,128)S(1)} %get-tuple-element.121), channel_id=1, source_target_pairs={{0,4},{2,6},{4,0},{6,2},{8,12},{10,14},{12,8},{14,10},{16,20},{18,... | collective-permute-start | bytes 294920 | tf_op jit(solution)/shard_map/ppermute | solution.py:278
  135.3 7.8 %collective-permute-start.29 = (f32[96,256]{1,0:T(8,128)S(1)}, f32[96,256]{1,0:T(8,128)S(1)}, u32[]{:S(2)}, u32[]{:S(2)}) collective-permute-start(f32[96,256]{1,0:T(8,128)S(1)} %fusion.7), channel_id=1, source_target_pairs={{0,8},{2,10},{4,12},{6,14},{8,0},{10,2},{12,4},{14,6},{16,24},{18,... | collective-permute-start | bytes 294920 | tf_op jit(solution)/shard_map/ppermute | solution.py:278
  139.9 9.5 %collective-permute-start.30 = (f32[96,256]{1,0:T(8,128)S(1)}, f32[96,256]{1,0:T(8,128)S(1)}, u32[]{:S(2)}, u32[]{:S(2)}) collective-permute-start(f32[96,256]{1,0:T(8,128)S(1)} %fusion.7), channel_id=1, source_target_pairs={{0,16},{2,18},{4,20},{6,22},{8,24},{10,26},{12,28},{14,30},{16,0},... | collective-permute-start | bytes 294920 | tf_op jit(solution)/shard_map/ppermute | solution.py:278
  139.9 9.5 %collective-permute-start.31 = (f32[96,256]{1,0:T(8,128)S(1)}, f32[96,256]{1,0:T(8,128)S(1)}, u32[]{:S(2)}, u32[]{:S(2)}) collective-permute-start(f32[96,256]{1,0:T(8,128)S(1)} %fusion.7), channel_id=1, source_target_pairs={{0,24},{2,26},{4,28},{6,30},{8,16},{10,18},{12,20},{14,22},{16,8},... | collective-permute-start | bytes 294920 | tf_op jit(solution)/shard_map/ppermute | solution.py:278
  172.3 9.5 %collective-permute-start.37 = (bf16[2,256,256]{2,1,0:T(8,128)(2,1)S(1)}, bf16[2,256,256]{2,1,0:T(8,128)(2,1)S(1)}, u32[]{:S(2)}, u32[]{:S(2)}) collective-permute-start(bf16[2,256,256]{2,1,0:T(8,128)(2,1)S(1)} %get-tuple-element.71.refs_0_), channel_id=1, source_target_pairs={{0,8},{2,10},{4,12},{6,14},{8,16},{10,18},{12,20},{14,22},{16,24},... | collective-permute-start | bytes 786440 | tf_op jit(solution)/shard_map/ppermute | solution.py:283
  176.0 8.1 %collective-permute-start.38 = (bf16[2,256,256]{2,1,0:T(8,128)(2,1)S(1)}, bf16[2,256,256]{2,1,0:T(8,128)(2,1)S(1)}, u32[]{:S(2)}, u32[]{:S(2)}) collective-permute-start(bf16[2,256,256]{2,1,0:T(8,128)(2,1)S(1)} %get-tuple-element.71.refs_0_), channel_id=1, source_target_pairs={{0,2},{2,0},{4,6},{6,4},{8,10},{10,8},{12,14},{14,12},{16,18},{18,... | collective-permute-start | bytes 786440 | tf_op jit(solution)/shard_map/ppermute | solution.py:278
  177.5 8.6 %collective-permute-start.39 = (bf16[2,256,256]{2,1,0:T(8,128)(2,1)S(1)}, bf16[2,256,256]{2,1,0:T(8,128)(2,1)S(1)}, u32[]{:S(2)}, u32[]{:S(2)}) collective-permute-start(bf16[2,256,256]{2,1,0:T(8,128)(2,1)S(1)} %get-tuple-element.71.refs_0_), channel_id=1, source_target_pairs={{0,4},{2,6},{8,12},{10,14},{4,16},{6,18},{16,20},{18,22},{12,24},{... | collective-permute-start | bytes 786440 | tf_op jit(solution)/shard_map/ppermute | solution.py:289
  184.1 7.2 %collective-permute-start.40 = (bf16[2,256,256]{2,1,0:T(8,128)(2,1)S(1)}, bf16[2,256,256]{2,1,0:T(8,128)(2,1)S(1)}, u32[]{:S(2)}, u32[]{:S(2)}) collective-permute-start(bf16[2,256,256]{2,1,0:T(8,128)(2,1)S(1)} %collective-permute-done.37.refs_2_), channel_id=1, source_target_pairs={{0,2},{2,0},{4,6},{6,4},{8,10},{10,8},{12,14},{14,12},{16,18},{18,... | collective-permute-start | bytes 786440 | tf_op jit(solution)/shard_map/ppermute | solution.py:278
  185.5 6.9 %collective-permute-start.41 = (bf16[2,256,256]{2,1,0:T(8,128)(2,1)S(1)}, bf16[2,256,256]{2,1,0:T(8,128)(2,1)S(1)}, u32[]{:S(2)}, u32[]{:S(2)}) collective-permute-start(bf16[2,256,256]{2,1,0:T(8,128)(2,1)S(1)} %collective-permute-done.37.refs_2_), channel_id=1, source_target_pairs={{0,4},{2,6},{4,0},{6,2},{8,12},{10,14},{12,8},{14,10},{16,20},{18,... | collective-permute-start | bytes 786440 | tf_op jit(solution)/shard_map/ppermute | solution.py:278
  201.3 12.8 %collective-permute-start.45 = (bf16[16,256,256]{2,1,0:T(8,128)(2,1)S(1)}, bf16[16,256,256]{2,1,0:T(8,128)(2,1)S(1)}, u32[]{:S(2)}, u32[]{:S(2)}) collective-permute-start(bf16[16,256,256]{2,1,0:T(8,128)(2,1)S(1)} %get-tuple-element.80.refs_8_), channel_id=1, source_target_pairs={{0,1},{1,0},{2,3},{3,2},{4,5},{5,4},{6,7},{7,6},{8,9},{9,8},{10,11... | collective-permute-start | bytes 6291464 | tf_op jit(solution)/shard_map/ppermute | solution.py:274
  201.4 11.3 %collective-permute-start.46 = (bf16[2,256,256]{2,1,0:T(8,128)(2,1)S(1)}, bf16[2,256,256]{2,1,0:T(8,128)(2,1)S(1)}, u32[]{:S(2)}, u32[]{:S(2)}) collective-permute-start(bf16[2,256,256]{2,1,0:T(8,128)(2,1)S(1)} %get-tuple-element.81), channel_id=1, source_target_pairs={{0,4},{2,6},{4,0},{6,2},{8,12},{10,14},{12,8},{14,10},{16,20},{18,... | collective-permute-start | bytes 786440 | tf_op jit(solution)/shard_map/ppermute | solution.py:278
  205.8 8.4 %collective-permute-start.47 = (bf16[2,256,256]{2,1,0:T(8,128)(2,1)S(1)}, bf16[2,256,256]{2,1,0:T(8,128)(2,1)S(1)}, u32[]{:S(2)}, u32[]{:S(2)}) collective-permute-start(bf16[2,256,256]{2,1,0:T(8,128)(2,1)S(1)} %get-tuple-element.82), channel_id=1, source_target_pairs={{0,2},{2,0},{4,6},{6,4},{8,10},{10,8},{12,14},{14,12},{16,18},{18,... | collective-permute-start | bytes 786440 | tf_op jit(solution)/shard_map/ppermute | solution.py:278
  216.0 8.6 %collective-permute-start.53 = (f32[128,256]{1,0:T(8,128)S(1)}, f32[128,256]{1,0:T(8,128)S(1)}, u32[]{:S(2)}, u32[]{:S(2)}) collective-permute-start(f32[128,256]{1,0:T(8,128)S(1)} %get-tuple-element.100), channel_id=1, source_target_pairs={{0,4},{2,6},{4,0},{6,2},{8,12},{10,14},{12,8},{14,10},{16,20},{18,... | collective-permute-start | bytes 393224 | tf_op jit(solution)/shard_map/ppermute | solution.py:278
  216.2 8.4 %collective-permute-start.54 = (f32[128,256]{1,0:T(8,128)S(1)}, f32[128,256]{1,0:T(8,128)S(1)}, u32[]{:S(2)}, u32[]{:S(2)}) collective-permute-start(f32[128,256]{1,0:T(8,128)S(1)} %get-tuple-element.99), channel_id=1, source_target_pairs={{0,6},{2,4},{4,2},{6,0},{8,14},{10,12},{12,10},{14,8},{16,22},{18,... | collective-permute-start | bytes 393224 | tf_op jit(solution)/shard_map/ppermute | solution.py:278
  219.2 11.1 %collective-permute-start.50 = (bf16[2,256,256]{2,1,0:T(8,128)(2,1)S(1)}, bf16[2,256,256]{2,1,0:T(8,128)(2,1)S(1)}, u32[]{:S(2)}, u32[]{:S(2)}) collective-permute-start(bf16[2,256,256]{2,1,0:T(8,128)(2,1)S(1)} %get-tuple-element.87), channel_id=1, source_target_pairs={{0,4},{2,6},{4,0},{6,2},{8,12},{10,14},{12,8},{14,10},{16,20},{18,... | collective-permute-start | bytes 786440 | tf_op jit(solution)/shard_map/ppermute | solution.py:278
  219.5 10.8 %collective-permute-start.49 = (bf16[2,256,256]{2,1,0:T(8,128)(2,1)S(1)}, bf16[2,256,256]{2,1,0:T(8,128)(2,1)S(1)}, u32[]{:S(2)}, u32[]{:S(2)}) collective-permute-start(bf16[2,256,256]{2,1,0:T(8,128)(2,1)S(1)} %add_convert_fusion.1), channel_id=1, source_target_pairs={{0,2},{2,0},{4,6},{6,4},{8,10},{10,8},{12,14},{14,12},{16,18},{18,... | collective-permute-start | bytes 786440 | tf_op jit(solution)/shard_map/ppermute | solution.py:278
  222.1 12.7 %collective-permute-start.48 = (bf16[2,256,256]{2,1,0:T(8,128)(2,1)S(1)}, bf16[2,256,256]{2,1,0:T(8,128)(2,1)S(1)}, u32[]{:S(2)}, u32[]{:S(2)}) collective-permute-start(bf16[2,256,256]{2,1,0:T(8,128)(2,1)S(1)} %add_convert_fusion.2), channel_id=1, source_target_pairs={{4,0},{6,2},{12,8},{14,10},{16,4},{18,6},{20,16},{22,18},{24,12},{... | collective-permute-start | bytes 786440 | tf_op jit(solution)/shard_map/ppermute | solution.py:289
  234.8 14.9 %collective-permute-start.55 = (f32[128,256]{1,0:T(8,128)S(1)}, f32[128,256]{1,0:T(8,128)S(1)}, u32[]{:S(2)}, u32[]{:S(2)}) collective-permute-start(f32[128,256]{1,0:T(8,128)S(1)} %fusion.1), channel_id=1, source_target_pairs={{0,8},{2,10},{4,12},{6,14},{8,0},{10,2},{12,4},{14,6},{16,24},{18,... | collective-permute-start | bytes 393224 | tf_op jit(solution)/shard_map/ppermute | solution.py:278
  240.3 9.5 %collective-permute-start.56 = (f32[128,256]{1,0:T(8,128)S(1)}, f32[128,256]{1,0:T(8,128)S(1)}, u32[]{:S(2)}, u32[]{:S(2)}) collective-permute-start(f32[128,256]{1,0:T(8,128)S(1)} %fusion.1), channel_id=1, source_target_pairs={{0,16},{2,18},{4,20},{6,22},{8,24},{10,26},{12,28},{14,30},{16,0},... | collective-permute-start | bytes 393224 | tf_op jit(solution)/shard_map/ppermute | solution.py:278
  245.3 11.5 %collective-permute-start.57 = (f32[128,256]{1,0:T(8,128)S(1)}, f32[128,256]{1,0:T(8,128)S(1)}, u32[]{:S(2)}, u32[]{:S(2)}) collective-permute-start(f32[128,256]{1,0:T(8,128)S(1)} %fusion.1), channel_id=1, source_target_pairs={{0,24},{2,26},{4,28},{6,30},{8,16},{10,18},{12,20},{14,22},{16,8},... | collective-permute-start | bytes 393224 | tf_op jit(solution)/shard_map/ppermute | solution.py:278
  246.8 10.1 %collective-permute-start.44 = (bf16[2,256,256]{2,1,0:T(8,128)(2,1)S(1)}, bf16[2,256,256]{2,1,0:T(8,128)(2,1)S(1)}, u32[]{:S(2)}, u32[]{:S(2)}) collective-permute-start(bf16[2,256,256]{2,1,0:T(8,128)(2,1)S(1)} %get-tuple-element.78), channel_id=1, source_target_pairs={{0,2},{2,0},{4,6},{6,4},{8,10},{10,8},{12,14},{14,12},{16,18},{18,... | collective-permute-start | bytes 786440 | tf_op jit(solution)/shard_map/ppermute | solution.py:278
  248.4 10.5 %collective-permute-start.51 = (bf16[2,256,256]{2,1,0:T(8,128)(2,1)S(1)}, bf16[2,256,256]{2,1,0:T(8,128)(2,1)S(1)}, u32[]{:S(2)}, u32[]{:S(2)}) collective-permute-start(bf16[2,256,256]{2,1,0:T(8,128)(2,1)S(1)} %add_convert_fusion), channel_id=1, source_target_pairs={{8,0},{10,2},{12,4},{14,6},{16,8},{18,10},{20,12},{22,14},{24,16},... | collective-permute-start | bytes 786440 | tf_op jit(solution)/shard_map/ppermute | solution.py:283
  249.7 17.2 %collective-permute-start.36 = (f32[256,512]{1,0:T(8,128)S(1)}, f32[256,512]{1,0:T(8,128)S(1)}, u32[]{:S(2)}, u32[]{:S(2)}) collective-permute-start(f32[256,512]{1,0:T(8,128)S(1)} %get-tuple-element.70.refs_0_), channel_id=1, source_target_pairs={{0,1},{1,0},{2,3},{3,2},{4,5},{5,4},{6,7},{7,6},{8,9},{9,8},{10,11... | collective-permute-start | bytes 1572872 | tf_op jit(solution)/shard_map/ppermute | solution.py:274
  272.1 6.7 %collective-permute-start.63 = (f32[96,256]{1,0:T(8,128)S(1)}, f32[96,256]{1,0:T(8,128)S(1)}, u32[]{:S(2)}, u32[]{:S(2)}) collective-permute-start(f32[96,256]{1,0:T(8,128)S(1)} %get-tuple-element.114), channel_id=1, source_target_pairs={{0,4},{2,6},{4,0},{6,2},{8,12},{10,14},{12,8},{14,10},{16,20},{18,... | collective-permute-start | bytes 294920 | tf_op jit(solution)/shard_map/ppermute | solution.py:278
  278.8 7.7 %collective-permute-start.65 = (f32[96,256]{1,0:T(8,128)S(1)}, f32[96,256]{1,0:T(8,128)S(1)}, u32[]{:S(2)}, u32[]{:S(2)}) collective-permute-start(f32[96,256]{1,0:T(8,128)S(1)} %fusion.5), channel_id=1, source_target_pairs={{0,8},{2,10},{4,12},{6,14},{8,0},{10,2},{12,4},{14,6},{16,24},{18,... | collective-permute-start | bytes 294920 | tf_op jit(solution)/shard_map/ppermute | solution.py:278
  283.2 8.9 %collective-permute-start.66 = (f32[96,256]{1,0:T(8,128)S(1)}, f32[96,256]{1,0:T(8,128)S(1)}, u32[]{:S(2)}, u32[]{:S(2)}) collective-permute-start(f32[96,256]{1,0:T(8,128)S(1)} %fusion.5), channel_id=1, source_target_pairs={{0,16},{2,18},{4,20},{6,22},{8,24},{10,26},{12,28},{14,30},{16,0},... | collective-permute-start | bytes 294920 | tf_op jit(solution)/shard_map/ppermute | solution.py:278
  283.2 8.9 %collective-permute-start.67 = (f32[96,256]{1,0:T(8,128)S(1)}, f32[96,256]{1,0:T(8,128)S(1)}, u32[]{:S(2)}, u32[]{:S(2)}) collective-permute-start(f32[96,256]{1,0:T(8,128)S(1)} %fusion.5), channel_id=1, source_target_pairs={{0,24},{2,26},{4,28},{6,30},{8,16},{10,18},{12,20},{14,22},{16,8},... | collective-permute-start | bytes 294920 | tf_op jit(solution)/shard_map/ppermute | solution.py:278
  (60 other events, 520.0 us)

commit v4 on v3

--- a/solution.py
+++ b/solution.py
@@ -59,22 +59,27 @@
 
 
 def apply_kernel(meta, rows, cols, *refs):
-    pieces, tiles = refs[: 2 * REACH], refs[2 * REACH]
-    out = refs[2 * REACH + 1 : 4 * REACH + 1]
-    everything, window, total, sems = refs[4 * REACH + 1 :]
-    step = pl.program_id(0)
+    pieces, blocks, out = refs[: 2 * REACH], refs[2 * REACH], refs[2 * REACH + 1 : 4 * REACH + 1]
+    everything, window, total, tiles, piece_sems, tile_sems = refs[4 * REACH + 1 :]
     used, start, odd, pair_odd = meta[0], meta[1], meta[2], meta[3]
-
-    @pl.when(step == 0)
+    groups = (used + GROUP - 1) // GROUP
+
+    def fetch(group):
+        at = group % 2
+        return pltpu.make_async_copy(blocks.at[pl.ds(group * GROUP, GROUP)], tiles.at[at], tile_sems.at[at])
+
+    @pl.when(groups > 0)
     def _():
-        copies = [
-            pltpu.make_async_copy(piece, window.at[pl.ds(2 * s, 2)], sems.at[s]) for s, piece in enumerate(pieces)
-        ]
-        for copy in copies:
-            copy.start()
-        total[...] = jnp.zeros_like(total)
-        for copy in copies:
-            copy.wait()
+        fetch(0).start()
+
+    copies = [
+        pltpu.make_async_copy(piece, window.at[pl.ds(2 * s, 2)], piece_sems.at[s]) for s, piece in enumerate(pieces)
+    ]
+    for copy in copies:
+        copy.start()
+    total[...] = jnp.zeros_like(total)
+    for copy in copies:
+        copy.wait()
 
     def place(tile):
         w = tile - start
@@ -82,65 +87,66 @@
         role = jnp.where(back % 2 == 1, 2 + ((back // 2) ^ pair_odd ^ 1), back // 2)
         return role * 4 + 2 * (((w % 4) // 2) ^ odd) + w % 2
 
-    @pl.when(step * GROUP < used)
-    def _():
+    def multiply(group, carry):
+        @pl.when(group + 1 < groups)
+        def _():
+            fetch(group + 1).start()
+
+        fetch(group).wait()
         found = []
         for k in range(GROUP):
-            slot = step * GROUP + k
+            slot = group * GROUP + k
             row, col = rows[slot], cols[slot]
             weight = jnp.where(row == col, 0.5, 1.0).astype(f32)
             r, c = place(row), place(col)
-            tile = jnp.where(slot < used, tiles[k], jnp.zeros_like(tiles[k]))
+            tile = tiles[group % 2, k]
+            tile = jnp.where(slot < used, tile, jnp.zeros_like(tile))
             found.append((r, dot_nt(window[c], tile), weight))
             found.append((c, dot_nn(window[r], tile), weight))
         for at, part, weight in found:
             total[at] += part * weight
-
-    @pl.when(step == pl.num_programs(0) - 1)
-    def _():
-        for s, segment in enumerate(out):
-            segment[...] = total[pl.ds(2 * s, 2)].astype(segment.dtype)
-        everything[...] = total[...].astype(bf16)
+        return carry
+
+    lax.fori_loop(0, groups, multiply, 0)
+    for s, segment in enumerate(out):
+        segment[...] = total[pl.ds(2 * s, 2)].astype(segment.dtype)
+    everything[...] = total[...].astype(bf16)
 
 
 def apply_tiles(pieces, blocks, rows, cols, meta):
-    slots, size, _ = blocks.shape
+    size = blocks.shape[1]
     width = pieces[0].shape[1]
-
-    def tile_map(i, meta, rows, cols):
-        last = jnp.maximum((meta[0] + GROUP - 1) // GROUP - 1, 0)
-        return (jnp.minimum(i, last), 0, 0)
-
-    def whole(dims):
-        return pl.BlockSpec(dims, lambda i, *_: (0,) * len(dims))
-
     segment, window = (2, width, size), (4 * REACH, width, size)
     out = pl.pallas_call(
         apply_kernel,
-        grid_spec=pltpu.PrefetchScalarGridSpec(
-            num_scalar_prefetch=3,
-            grid=(slots // GROUP,),
-            in_specs=[pl.BlockSpec(memory_space=pl.ANY)] * (2 * REACH)
-            + [pl.BlockSpec((GROUP, size, size), tile_map)],
-            out_specs=[whole(segment)] * (2 * REACH) + [whole(window)],
-            scratch_shapes=[VMEM(window, bf16), VMEM(window, f32), pltpu.SemaphoreType.DMA((2 * REACH,))],
-        ),
+        in_specs=[pl.BlockSpec(memory_space=SMEM)] * 3
+        + [pl.BlockSpec(memory_space=pl.ANY)] * (2 * REACH)
+        + [pl.BlockSpec(memory_space=pltpu.HBM)],
+        out_specs=[pl.BlockSpec(memory_space=VMEM)] * (2 * REACH + 1),
+        scratch_shapes=[
+            VMEM(window, bf16),
+            VMEM(window, f32),
+            VMEM((2, GROUP, size, size), bf16),
+            pltpu.SemaphoreType.DMA((2 * REACH,)),
+            pltpu.SemaphoreType.DMA((2,)),
+        ],
         out_shape=[shape(kind, *segment) for kind in SEGMENT_KINDS] + [shape(bf16, *window)],
-        compiler_params=pltpu.CompilerParams(vmem_limit_bytes=24 << 20),
+        compiler_params=pltpu.CompilerParams(vmem_limit_bytes=50 << 20),
         cost_estimate=pl.CostEstimate(flops=4 << 30, bytes_accessed=16 << 20, transcendentals=0),
     )(meta, rows, cols, *pieces, blocks)
     return out[: 2 * REACH : 2], out[1 : 2 * REACH : 2], out[2 * REACH]
 
 
 def inner_kernel(*refs):
-    pieces, mine, theirs, out = refs[: 2 * REACH], refs[2 * REACH], refs[2 * REACH + 1], refs[-1]
+    pieces, theirs, mine, out = refs[: 2 * REACH], refs[2 * REACH : -2], refs[-2], refs[-1]
     size = out.shape[1]
     own = jnp.zeros((size, size), f32)
     other = jnp.zeros((size, size), f32)
     for s, piece in enumerate(pieces):
+        group, start = GROUPED[s]
         for t in range(2):
             own += dot_nt(mine[2 * s + t], piece[t])
-            other += dot_nt(piece[t], theirs[2 * s + t])
+            other += dot_nt(mine[2 * s + t], theirs[group][start + t])
     out[pl.ds(0, size), :] = own
     out[pl.ds(size, size), :] = other
 
@@ -299,8 +305,15 @@
     own_x = flip(u, 1)
     two, own_x = together(two, own_x)
     two_x, side = flip(two, 1), flip(two, 2)
+    first = swap_cores(jnp.concatenate([u, own_x, two]))
     far, two_x, side = together(far, two_x, side)
-    return [u, own_x, two, two_x, far, flip(far, 1), side, flip(two_x, 2)]
+    second = swap_cores(jnp.concatenate([far, two_x, side]))
+    far_x, side_x = flip(far, 1), flip(two_x, 2)
+    third = swap_cores(jnp.concatenate([far_x, side_x]))
+    return [u, own_x, two, two_x, far, far_x, side, side_x], [first, second, third]
+
+
+GROUPED = ((0, 0), (0, 2), (0, 4), (1, 2), (1, 0), (2, 0), (1, 4), (2, 2))
 
 
 def place_order(parts, place):
@@ -354,17 +367,19 @@
     x, u = call(pack_kernel, [flat, chunk], [vectors])
     for step in range(STEPS):
         last = step == STEPS - 1
-        pieces = reach(u)
+        pieces, others = reach(u)
         x_other = swap_cores(x)
         same, cross, everything = apply_tiles(pieces, blocks, block_row, block_col, meta)
         side_x, far_x, side, own_x = flip(cross[3], 2), flip(cross[2], 1), flip(same[3], 2), flip(cross[0], 1)
-        theirs, side_x, far_x = together(swap_cores(everything), side_x, far_x)
-        two_x = (cross[1] + side_x.astype(f32)).astype(bf16)
-        far = (same[2] + far_x.astype(f32)).astype(bf16)
-        (inner,) = call(inner_kernel, [shape(f32, 2 * width, width)], pieces + [everything, theirs])
-        two = (same[1] + (flip(two_x, 1).astype(f32) + side.astype(f32))).astype(bf16)
-        joined = [own_x, stride(far, True), shift(two, -2)]
-        inner = summed(inner, [(two_x, far), (joined[1], two), (joined[2], own_x)])
+        (inner,) = call(
+            inner_kernel, [shape(f32, 2 * width, width)], pieces + others + [everything], flops=1 << 30
+        )
+        side_x, far_x, inner = together(side_x, far_x, inner)
+        two_x = flip((cross[1] + side_x.astype(f32)).astype(bf16), 1)
+        far = stride((same[2] + far_x.astype(f32)).astype(bf16), True)
+        two = (same[1] + (two_x.astype(f32) + side.astype(f32))).astype(bf16)
+        joined = [own_x, far, shift(two, -2)]
+        inner = summed(inner, [(two_x, far), (joined[2],), (own_x,)])
         out = [flat] + ([shape(f32, count, width)] if last else [])
         update, *residual = call(
             lambda *refs: update_kernel(rows_total, *refs), out, [x, x_other, same[0], *joined, inner]

time: 314 us -> 304 us (0.968); the launches traced: 314 us -> 309 us
  starting transfers between devices: 115 us -> 140 us
  waiting for transfers between devices: 133 us -> 117 us
  local copies, waits for them, and re-layouts: 20.6 us -> 5.05 us
    ppermute x56, starting transfers between devices: 94.1 us -> 118 us  [flip(): lax.ppermute(a, 'patch', [(i, i ^ mask) for i in range(lax.axis_size('pat...]
    ppermute x56, waiting for transfers between devices: 110 us -> 92.5 us  [flip(): lax.ppermute(a, 'patch', [(i, i ^ mask) for i in range(lax.axis_size('pat...]
    unnamed x72 -> x22, local copies, waits for them, and re-layouts: 20.5 us -> 4.24 us
    pallas_call x2, Pallas kernels: 4.66 us -> 9.8 us  [apply_tiles(): pl.pallas_call(apply_kernel, in_specs=[pl.BlockSpec(memory_space=SMEM)] *...]
    ppermute x8 -> x12, waiting for transfers between devices: 7.23 us -> 7.24 us  [swap_cores(): return lax.ppermute(a, 'vec', [(0, 1), (1, 0)])]
  transfers between devices with their start and end apart: 72 -> 76, of which waited for: 52 -> 54; matrix products, arithmetic and copies ran while one was open for 0% -> 1% of each run, Pallas kernels for 0% -> 4%
where the time goes in v4:
time: 304 us; the launch traced here: 309 us
  starting transfers between devices  140 us (46%)
  waiting for transfers between devices  117 us (38%)
  Pallas kernels  41.4 us (14%)
  local copies, waits for them, and re-layouts  5.05 us (2%)
  other arithmetic  3.77 us (1%)
    ppermute x56, starting transfers between devices, flip(): lax.ppermute(a, 'patch', [(i, i ^ mask) for i in range(lax.axis_size('pat...  118 us
    ppermute x56, waiting for transfers between devices, flip(): lax.ppermute(a, 'patch', [(i, i ^ mask) for i in range(lax.axis_size('pat...  92.5 us
    pallas_call x9, Pallas kernels, call(): pl.pallas_call(kernel, out_shape=out, in_specs=[pl.BlockSpec(memory_space...  31.6 us
    ppermute x4, starting transfers between devices, shift(): lax.ppermute(a, 'patch', [(i - 2 * pairs, i) for i in devices if i - 2 *...  11.8 us
    pallas_call x2, Pallas kernels, apply_tiles(): pl.pallas_call(apply_kernel, in_specs=[pl.BlockSpec(memory_space=SMEM)] *...  9.8 us
    ppermute x4, waiting for transfers between devices, stride(): lax.ppermute(a, 'patch', [(d, s) if back else (s, d) for s, d in route if...  9.61 us
    ppermute x4, starting transfers between devices, stride(): lax.ppermute(a, 'patch', [(d, s) if back else (s, d) for s, d in route if...  8.93 us
    ppermute x4, waiting for transfers between devices, shift(): lax.ppermute(a, 'patch', [(i - 2 * pairs, i) for i in devices if i - 2 *...  7.95 us
  transfers between devices with their start and end apart: 76, of which 54 were waited for; matrix products, arithmetic and copies ran while one was open for 1% of the time, Pallas kernels for 4%

profile of v4, /device:TPU:0, one launch (start us, length us, event | category | flops | bytes accessed | tf_op | source)
XLA Modules:
  0.0 309.4 jit_solution(16429372593105131589)
XLA Ops:
  1.9 4.9 %collective-permute-start.1 = (bf16[2,256,256]{2,1,0:T(8,128)(2,1)S(1)}, bf16[2,256,256]{2,1,0:T(8,128)(2,1)S(1)}, u32[]{:S(2)}, u32[]{:S(2)}) collective-permute-start(bf16[2,256,256]{2,1,0:T(8,128)(2,1)S(1)} %get-tuple-element.49.refs_0_), channel_id=1, source_target_pairs={{0,8},{2,10},{4,12},{6,14},{8,16},{10,18},{12,20},{14,22},{16,24},... | collective-permute-start | bytes 786440 | tf_op jit(solution)/shard_map/ppermute | solution.py:289
  8.4 3.4 %collective-permute-start.3 = (bf16[2,256,256]{2,1,0:T(8,128)(2,1)S(1)}, bf16[2,256,256]{2,1,0:T(8,128)(2,1)S(1)}, u32[]{:S(2)}, u32[]{:S(2)}) collective-permute-start(bf16[2,256,256]{2,1,0:T(8,128)(2,1)S(1)} %get-tuple-element.49.refs_0_), channel_id=1, source_target_pairs={{0,4},{2,6},{8,12},{10,14},{4,16},{6,18},{16,20},{18,22},{12,24},{... | collective-permute-start | bytes 786440 | tf_op jit(solution)/shard_map/ppermute | solution.py:295
  12.4 2.3 collective-permute-done.2.refs_1_
  18.4 3.2 %collective-permute-done.4.refs_3_ = bf16[2,256,256]{2,1,0:T(8,128)(2,1)S(1)} collective-permute-done((bf16[2,256,256]{2,1,0:T(8,128)(2,1)S(1)}, bf16[2,256,256]{2,1,0:T(8,128)(2,1)S(1)}, u32[]{:S(2)}, u32[]{:S(2)}) %collective-permute-start.4) | collective-permute-done | bytes 262176 | tf_op jit(solution)/shard_map/ppermute | solution.py:284
  23.3 2.2 collective-permute-start.7
  26.3 2.8 collective-permute-done.6.refs_5_
  29.9 4.8 %shard_map.69 = (f32[2,256,256]{2,1,0:T(8,128)S(1)}, bf16[2,256,256]{2,1,0:T(8,128)(2,1)S(1)}, f32[2,256,256]{2,1,0:T(8,128)}, f32[2,256,256]{2,1,0:T(8,128)}, f...) custom-call(s32[4]{0:T(128)S(1)} %pad_add_fusion.meta, ...), custom_call_target="tpu_custom_call" | custom-call | flops 4294967296 | bytes 16777216 | tf_op jit(solution)/shard_map/pallas_call | solution.py:120
  34.8 5.7 %collective-permute-start.9 = (bf16[2,256,256]{2,1,0:T(8,128)(2,1)S(1)}, bf16[2,256,256]{2,1,0:T(8,128)(2,1)S(1)}, u32[]{:S(2)}, u32[]{:S(2)}) collective-permute-start(bf16[2,256,256]{2,1,0:T(8,128)(2,1)S(1)} %get-tuple-element.58), channel_id=1, source_target_pairs={{0,4},{2,6},{4,0},{6,2},{8,12},{10,14},{12,8},{14,10},{16,20},{18,... | collective-permute-start | bytes 786440 | tf_op jit(solution)/shard_map/ppermute | solution.py:284
  43.5 3.7 %collective-permute-done.9 = bf16[2,256,256]{2,1,0:T(8,128)(2,1)S(1)} collective-permute-done((bf16[2,256,256]{2,1,0:T(8,128)(2,1)S(1)}, bf16[2,256,256]{2,1,0:T(8,128)(2,1)S(1)}, u32[]{:S(2)}, u32[]{:S(2)}) %collective-permute-start.9) | collective-permute-done | bytes 262176 | tf_op jit(solution)/shard_map/ppermute | solution.py:284
  49.8 2.7 collective-permute-start.16
  52.5 2.8 collective-permute-done.15
  55.2 4.6 %collective-permute-done.14.refs_4_ = bf16[2,256,256]{2,1,0:T(8,128)(2,1)S(1)} collective-permute-done((bf16[2,256,256]{2,1,0:T(8,128)(2,1)}, bf16[2,256,256]{2,1,0:T(8,128)(2,1)S(1)}, u32[]{:S(2)}, u32[]{:S(2)}) %collective-permute-start.14) | collective-permute-done | bytes 262176 | tf_op jit(solution)/shard_map/ppermute | solution.py:295
  62.2 12.6 %collective-permute-start.19 = (f32[128,256]{1,0:T(8,128)}, f32[128,256]{1,0:T(8,128)S(1)}, u32[]{:S(2)}, u32[]{:S(2)}) collective-permute-start(f32[128,256]{1,0:T(8,128)} %get-tuple-element.107), channel_id=1, source_target_pairs={{0,4},{2,6},{4,0},{6,2},{8,12},{10,14},{12,8},{14,10},{16,20},{18,... | collective-permute-start | bytes 393224 | tf_op jit(solution)/shard_map/ppermute | solution.py:284
  82.0 3.0 collective-permute-done.17.refs_5_
  85.0 7.8 %collective-permute-start.21 = (f32[128,256]{1,0:T(8,128)S(1)}, f32[128,256]{1,0:T(8,128)S(1)}, u32[]{:S(2)}, u32[]{:S(2)}) collective-permute-start(f32[128,256]{1,0:T(8,128)S(1)} %fusion.3), channel_id=1, source_target_pairs={{0,8},{2,10},{4,12},{6,14},{8,0},{10,2},{12,4},{14,6},{16,24},{18,... | collective-permute-start | bytes 393224 | tf_op jit(solution)/shard_map/ppermute | solution.py:284
  92.9 2.8 collective-permute-start.22
  98.7 4.3 %collective-permute-done.23 = f32[128,256]{1,0:T(8,128)S(1)} collective-permute-done((f32[128,256]{1,0:T(8,128)S(1)}, f32[128,256]{1,0:T(8,128)S(1)}, u32[]{:S(2)}, u32[]{:S(2)}) %collective-permute-start.23) | collective-permute-done | bytes 131104 | tf_op jit(solution)/shard_map/ppermute | solution.py:284
  103.0 3.2 %collective-permute-done.8.refs_3_ = bf16[2,256,256]{2,1,0:T(8,128)(2,1)S(1)} collective-permute-done((bf16[2,256,256]{2,1,0:T(8,128)(2,1)S(1)}, bf16[2,256,256]{2,1,0:T(8,128)(2,1)S(1)}, u32[]{:S(2)}, u32[]{:S(2)}) %collective-permute-start.8) | collective-permute-done | bytes 262176 | tf_op jit(solution)/shard_map/ppermute | solution.py:284
  109.8 2.5 collective-permute-done.24
  121.3 3.5 %collective-permute-done.29 = f32[96,256]{1,0:T(8,128)S(1)} collective-permute-done((f32[96,256]{1,0:T(8,128)S(1)}, f32[96,256]{1,0:T(8,128)S(1)}, u32[]{:S(2)}, u32[]{:S(2)}) %collective-permute-start.29) | collective-permute-done | bytes 98336 | tf_op jit(solution)/shard_map/ppermute | solution.py:284
  125.5 2.4 collective-permute-start.32
  129.6 5.3 %collective-permute-done.32 = f32[96,256]{1,0:T(8,128)S(1)} collective-permute-done((f32[96,256]{1,0:T(8,128)S(1)}, f32[96,256]{1,0:T(8,128)S(1)}, u32[]{:S(2)}, u32[]{:S(2)}) %collective-permute-start.32) | collective-permute-done | bytes 98336 | tf_op jit(solution)/shard_map/ppermute | solution.py:284
  134.9 2.1 collective-permute-start.34
  143.4 12.9 %shard_map.73 = (f32[256,512]{1,0:T(8,128)S(1)}, bf16[2,256,256]{2,1,0:T(8,128)(2,1)S(1)}) custom-call(s32[1]{0:T(128)} %bitcast.core.refs_0_, f32[256,512]{1,0:T(8,128)S(1)} %shard_map.71.mine.refs_1_, f32[256,512]{1,0:T(8,128)S(1)} %collective-permute-done.27.theirs.refs_2_, f32[384,256]{1,0:T(8,128)S(1)} %pad_maximum_fusion.8.refs_3_, ...), custom_call_target="tpu_custom_call" | custom-call | flops 17179869184 | bytes 2621444 | tf_op jit(solution)/shard_map/pallas_call | solution.py:38
  156.4 4.1 %collective-permute-start.39 = (bf16[2,256,256]{2,1,0:T(8,128)(2,1)S(1)}, bf16[2,256,256]{2,1,0:T(8,128)(2,1)S(1)}, u32[]{:S(2)}, u32[]{:S(2)}) collective-permute-start(bf16[2,256,256]{2,1,0:T(8,128)(2,1)S(1)} %get-tuple-element.71.refs_0_), channel_id=1, source_target_pairs={{0,8},{2,10},{4,12},{6,14},{8,16},{10,18},{12,20},{14,22},{16,24},... | collective-permute-start | bytes 786440 | tf_op jit(solution)/shard_map/ppermute | solution.py:289
  161.5 2.9 collective-permute-start.41
  166.3 2.3 collective-permute-done.40.refs_1_
  170.6 5.2 %collective-permute-done.42.refs_3_ = bf16[2,256,256]{2,1,0:T(8,128)(2,1)S(1)} collective-permute-done((bf16[2,256,256]{2,1,0:T(8,128)(2,1)S(1)}, bf16[2,256,256]{2,1,0:T(8,128)(2,1)S(1)}, u32[]{:S(2)}, u32[]{:S(2)}) %collective-permute-start.42) | collective-permute-done | bytes 262176 | tf_op jit(solution)/shard_map/ppermute | solution.py:284
  180.2 2.7 collective-permute-done.44.refs_5_
  184.0 5.0 %shard_map.74 = (f32[2,256,256]{2,1,0:T(8,128)S(1)}, bf16[2,256,256]{2,1,0:T(8,128)(2,1)S(1)}, f32[2,256,256]{2,1,0:T(8,128)}, f32[2,256,256]{2,1,0:T(8,128)}, f...) custom-call(s32[4]{0:T(128)S(1)} %pad_add_fusion.meta, ...), custom_call_target="tpu_custom_call" | custom-call | flops 4294967296 | bytes 16777216 | tf_op jit(solution)/shard_map/pallas_call | solution.py:120
  189.1 4.5 %collective-permute-start.48 = (bf16[2,256,256]{2,1,0:T(8,128)(2,1)S(1)}, bf16[2,256,256]{2,1,0:T(8,128)(2,1)S(1)}, u32[]{:S(2)}, u32[]{:S(2)}) collective-permute-start(bf16[2,256,256]{2,1,0:T(8,128)(2,1)S(1)} %get-tuple-element.81), channel_id=1, source_target_pairs={{0,2},{2,0},{4,6},{6,4},{8,10},{10,8},{12,14},{14,12},{16,18},{18,... | collective-permute-start | bytes 786440 | tf_op jit(solution)/shard_map/ppermute | solution.py:284
  197.8 2.5 collective-permute-done.48
  203.5 2.7 collective-permute-start.54
  206.2 2.1 collective-permute-done.53
  208.3 5.0 %collective-permute-done.52.refs_4_ = bf16[2,256,256]{2,1,0:T(8,128)(2,1)S(1)} collective-permute-done((bf16[2,256,256]{2,1,0:T(8,128)(2,1)S(1)}, bf16[2,256,256]{2,1,0:T(8,128)(2,1)S(1)}, u32[]{:S(2)}, u32[]{:S(2)}) %collective-permute-start.52) | collective-permute-done | bytes 262176 | tf_op jit(solution)/shard_map/ppermute | solution.py:295
  213.7 14.2 %collective-permute-start.57 = (f32[128,256]{1,0:T(8,128)S(1)}, f32[128,256]{1,0:T(8,128)S(1)}, u32[]{:S(2)}, u32[]{:S(2)}) collective-permute-start(f32[128,256]{1,0:T(8,128)S(1)} %get-tuple-element.100), channel_id=1, source_target_pairs={{0,4},{2,6},{4,0},{6,2},{8,12},{10,14},{12,8},{14,10},{16,20},{18,... | collective-permute-start | bytes 393224 | tf_op jit(solution)/shard_map/ppermute | solution.py:284
  229.4 2.7 collective-permute-done.57
  233.8 2.6 collective-permute-done.55.refs_5_
  236.4 8.4 %collective-permute-start.59 = (f32[128,256]{1,0:T(8,128)S(1)}, f32[128,256]{1,0:T(8,128)S(1)}, u32[]{:S(2)}, u32[]{:S(2)}) collective-permute-start(f32[128,256]{1,0:T(8,128)S(1)} %fusion.1), channel_id=1, source_target_pairs={{0,8},{2,10},{4,12},{6,14},{8,0},{10,2},{12,4},{14,6},{16,24},{18,... | collective-permute-start | bytes 393224 | tf_op jit(solution)/shard_map/ppermute | solution.py:284
  244.8 2.9 collective-permute-start.60
  250.7 4.3 %collective-permute-done.61 = f32[128,256]{1,0:T(8,128)S(1)} collective-permute-done((f32[128,256]{1,0:T(8,128)S(1)}, f32[128,256]{1,0:T(8,128)S(1)}, u32[]{:S(2)}, u32[]{:S(2)}) %collective-permute-start.61) | collective-permute-done | bytes 131104 | tf_op jit(solution)/shard_map/ppermute | solution.py:284
  255.0 3.3 %collective-permute-done.46.refs_3_ = bf16[2,256,256]{2,1,0:T(8,128)(2,1)S(1)} collective-permute-done((bf16[2,256,256]{2,1,0:T(8,128)(2,1)S(1)}, bf16[2,256,256]{2,1,0:T(8,128)(2,1)S(1)}, u32[]{:S(2)}, u32[]{:S(2)}) %collective-permute-start.46) | collective-permute-done | bytes 262176 | tf_op jit(solution)/shard_map/ppermute | solution.py:284
  258.3 2.8 collective-permute-start.63
  261.8 2.5 collective-permute-done.62
  275.7 2.1 collective-permute-done.67
  278.5 2.4 collective-permute-start.70
  282.5 4.9 %collective-permute-done.70 = f32[96,256]{1,0:T(8,128)S(1)} collective-permute-done((f32[96,256]{1,0:T(8,128)S(1)}, f32[96,256]{1,0:T(8,128)S(1)}, u32[]{:S(2)}, u32[]{:S(2)}) %collective-permute-start.70) | collective-permute-done | bytes 98336 | tf_op jit(solution)/shard_map/ppermute | solution.py:284
  296.9 12.5 %shard_map.78 = f32[512,256]{1,0:T(8,128)} custom-call(s32[1]{0:T(128)} %bitcast.core.refs_0_, f32[256,512]{1,0:T(8,128)S(1)} %get-tuple-element.92.mine.refs_1_, f32[256,512]{1,0:T(8,128)S(1)} %collective-permute-done.65.theirs.refs_2_, f32[384,256]{1,0:T(8,128)S(1)} %pad_maximum_fusion.9.refs_3_, f32[384,256]{1,0:T(8,128)S(1)} %collective-permute-done.75.refs_4_), custom_call_target="tpu_custom_call" | custom-call | flops 17179869184 | bytes 2359300 | tf_op jit(solution)/shard_map/pallas_call | solution.py:38
  (170 shorter events, 97.6 us)
Async XLA Ops:
  1.9 10.5 %collective-permute-start.1 = (bf16[2,256,256]{2,1,0:T(8,128)(2,1)S(1)}, bf16[2,256,256]{2,1,0:T(8,128)(2,1)S(1)}, u32[]{:S(2)}, u32[]{:S(2)}) collective-permute-start(bf16[2,256,256]{2,1,0:T(8,128)(2,1)S(1)} %get-tuple-element.49.refs_0_), channel_id=1, source_target_pairs={{0,8},{2,10},{4,12},{6,14},{8,16},{10,18},{12,20},{14,22},{16,24},... | collective-permute-start | bytes 786440 | tf_op jit(solution)/shard_map/ppermute | solution.py:289
  6.8 7.8 %collective-permute-start.2 = (bf16[2,256,256]{2,1,0:T(8,128)(2,1)S(1)}, bf16[2,256,256]{2,1,0:T(8,128)(2,1)S(1)}, u32[]{:S(2)}, u32[]{:S(2)}) collective-permute-start(bf16[2,256,256]{2,1,0:T(8,128)(2,1)S(1)} %get-tuple-element.49.refs_0_), channel_id=1, source_target_pairs={{0,2},{2,0},{4,6},{6,4},{8,10},{10,8},{12,14},{14,12},{16,18},{18,... | collective-permute-start | bytes 786440 | tf_op jit(solution)/shard_map/ppermute | solution.py:284
  8.4 10.0 %collective-permute-start.3 = (bf16[2,256,256]{2,1,0:T(8,128)(2,1)S(1)}, bf16[2,256,256]{2,1,0:T(8,128)(2,1)S(1)}, u32[]{:S(2)}, u32[]{:S(2)}) collective-permute-start(bf16[2,256,256]{2,1,0:T(8,128)(2,1)S(1)} %get-tuple-element.49.refs_0_), channel_id=1, source_target_pairs={{0,4},{2,6},{8,12},{10,14},{4,16},{6,18},{16,20},{18,22},{12,24},{... | collective-permute-start | bytes 786440 | tf_op jit(solution)/shard_map/ppermute | solution.py:295
  14.7 6.9 %collective-permute-start.4 = (bf16[2,256,256]{2,1,0:T(8,128)(2,1)S(1)}, bf16[2,256,256]{2,1,0:T(8,128)(2,1)S(1)}, u32[]{:S(2)}, u32[]{:S(2)}) collective-permute-start(bf16[2,256,256]{2,1,0:T(8,128)(2,1)S(1)} %collective-permute-done.1.refs_2_), channel_id=1, source_target_pairs={{0,2},{2,0},{4,6},{6,4},{8,10},{10,8},{12,14},{14,12},{16,18},{18,... | collective-permute-start | bytes 786440 | tf_op jit(solution)/shard_map/ppermute | solution.py:284
  16.1 6.6 %collective-permute-start.5 = (bf16[2,256,256]{2,1,0:T(8,128)(2,1)S(1)}, bf16[2,256,256]{2,1,0:T(8,128)(2,1)S(1)}, u32[]{:S(2)}, u32[]{:S(2)}) collective-permute-start(bf16[2,256,256]{2,1,0:T(8,128)(2,1)S(1)} %collective-permute-done.1.refs_2_), channel_id=1, source_target_pairs={{0,4},{2,6},{4,0},{6,2},{8,12},{10,14},{12,8},{14,10},{16,20},{18,... | collective-permute-start | bytes 786440 | tf_op jit(solution)/shard_map/ppermute | solution.py:284
  25.5 15.1 %collective-permute-start.11 = (bf16[6,256,256]{2,1,0:T(8,128)(2,1)S(1)}, bf16[6,256,256]{2,1,0:T(8,128)(2,1)S(1)}, u32[]{:S(2)}, u32[]{:S(2)}) collective-permute-start(bf16[6,256,256]{2,1,0:T(8,128)(2,1)S(1)} %pad_maximum_fusion), channel_id=1, source_target_pairs={{0,1},{1,0},{2,3},{3,2},{4,5},{5,4},{6,7},{7,6},{8,9},{9,8},{10,11... | collective-permute-start | bytes 2359304 | tf_op jit(solution)/shard_map/ppermute | solution.py:280
  25.7 14.9 %collective-permute-start.12 = (bf16[6,256,256]{2,1,0:T(8,128)(2,1)S(1)}, bf16[6,256,256]{2,1,0:T(8,128)(2,1)S(1)}, u32[]{:S(2)}, u32[]{:S(2)}) collective-permute-start(bf16[6,256,256]{2,1,0:T(8,128)(2,1)S(1)} %pad_maximum_fusion.1), channel_id=1, source_target_pairs={{0,1},{1,0},{2,3},{3,2},{4,5},{5,4},{6,7},{7,6},{8,9},{9,8},{10,11... | collective-permute-start | bytes 2359304 | tf_op jit(solution)/shard_map/ppermute | solution.py:280
  29.8 10.7 %collective-permute-start.13 = (bf16[4,256,256]{2,1,0:T(8,128)(2,1)S(1)}, bf16[4,256,256]{2,1,0:T(8,128)(2,1)S(1)}, u32[]{:S(2)}, u32[]{:S(2)}) collective-permute-start(bf16[4,256,256]{2,1,0:T(8,128)(2,1)S(1)} %pad_maximum_fusion.4), channel_id=1, source_target_pairs={{0,1},{1,0},{2,3},{3,2},{4,5},{5,4},{6,7},{7,6},{8,9},{9,8},{10,11... | collective-permute-start | bytes 1572872 | tf_op jit(solution)/shard_map/ppermute | solution.py:280
  34.8 8.7 %collective-permute-start.10 = (bf16[2,256,256]{2,1,0:T(8,128)(2,1)S(1)}, bf16[2,256,256]{2,1,0:T(8,128)(2,1)S(1)}, u32[]{:S(2)}, u32[]{:S(2)}) collective-permute-start(bf16[2,256,256]{2,1,0:T(8,128)(2,1)S(1)} %get-tuple-element.59), channel_id=1, source_target_pairs={{0,2},{2,0},{4,6},{6,4},{8,10},{10,8},{12,14},{14,12},{16,18},{18,... | collective-permute-start | bytes 786440 | tf_op jit(solution)/shard_map/ppermute | solution.py:284
  34.8 12.4 %collective-permute-start.9 = (bf16[2,256,256]{2,1,0:T(8,128)(2,1)S(1)}, bf16[2,256,256]{2,1,0:T(8,128)(2,1)S(1)}, u32[]{:S(2)}, u32[]{:S(2)}) collective-permute-start(bf16[2,256,256]{2,1,0:T(8,128)(2,1)S(1)} %get-tuple-element.58), channel_id=1, source_target_pairs={{0,4},{2,6},{4,0},{6,2},{8,12},{10,14},{12,8},{14,10},{16,20},{18,... | collective-permute-start | bytes 786440 | tf_op jit(solution)/shard_map/ppermute | solution.py:284
  47.3 8.0 %collective-permute-start.15 = (bf16[2,256,256]{2,1,0:T(8,128)(2,1)S(1)}, bf16[2,256,256]{2,1,0:T(8,128)(2,1)S(1)}, u32[]{:S(2)}, u32[]{:S(2)}) collective-permute-start(bf16[2,256,256]{2,1,0:T(8,128)(2,1)S(1)} %add_convert_fusion.4), channel_id=1, source_target_pairs={{0,2},{2,0},{4,6},{6,4},{8,10},{10,8},{12,14},{14,12},{16,18},{18,... | collective-permute-start | bytes 786440 | tf_op jit(solution)/shard_map/ppermute | solution.py:284
  48.5 11.3 %collective-permute-start.14 = (bf16[2,256,256]{2,1,0:T(8,128)(2,1)}, bf16[2,256,256]{2,1,0:T(8,128)(2,1)S(1)}, u32[]{:S(2)}, u32[]{:S(2)}) collective-permute-start(bf16[2,256,256]{2,1,0:T(8,128)(2,1)} %add_convert_fusion.5), channel_id=1, source_target_pairs={{4,0},{6,2},{12,8},{14,10},{16,4},{18,6},{20,16},{22,18},{24,12},{... | collective-permute-start | bytes 786440 | tf_op jit(solution)/shard_map/ppermute | solution.py:295
  49.8 26.0 %collective-permute-start.16 = (bf16[2,256,256]{2,1,0:T(8,128)(2,1)}, bf16[2,256,256]{2,1,0:T(8,128)(2,1)S(1)}, u32[]{:S(2)}, u32[]{:S(2)}) collective-permute-start(bf16[2,256,256]{2,1,0:T(8,128)(2,1)} %get-tuple-element.65), channel_id=1, source_target_pairs={{0,4},{2,6},{4,0},{6,2},{8,12},{10,14},{12,8},{14,10},{16,20},{18,... | collective-permute-start | bytes 786440 | tf_op jit(solution)/shard_map/ppermute | solution.py:284
  60.5 17.5 %collective-permute-start.18 = (f32[128,256]{1,0:T(8,128)}, f32[128,256]{1,0:T(8,128)S(1)}, u32[]{:S(2)}, u32[]{:S(2)}) collective-permute-start(f32[128,256]{1,0:T(8,128)} %get-tuple-element.105), channel_id=1, source_target_pairs={{0,2},{2,0},{4,6},{6,4},{8,10},{10,8},{12,14},{14,12},{16,18},{18,... | collective-permute-start | bytes 393224 | tf_op jit(solution)/shard_map/ppermute | solution.py:284
  62.2 17.4 %collective-permute-start.19 = (f32[128,256]{1,0:T(8,128)}, f32[128,256]{1,0:T(8,128)S(1)}, u32[]{:S(2)}, u32[]{:S(2)}) collective-permute-start(f32[128,256]{1,0:T(8,128)} %get-tuple-element.107), channel_id=1, source_target_pairs={{0,4},{2,6},{4,0},{6,2},{8,12},{10,14},{12,8},{14,10},{16,20},{18,... | collective-permute-start | bytes 393224 | tf_op jit(solution)/shard_map/ppermute | solution.py:284
  76.5 8.5 %collective-permute-start.17 = (bf16[2,256,256]{2,1,0:T(8,128)(2,1)}, bf16[2,256,256]{2,1,0:T(8,128)(2,1)S(1)}, u32[]{:S(2)}, u32[]{:S(2)}) collective-permute-start(bf16[2,256,256]{2,1,0:T(8,128)(2,1)} %add_convert_fusion.3), channel_id=1, source_target_pairs={{8,0},{10,2},{12,4},{14,6},{16,8},{18,10},{20,12},{22,14},{24,16},... | collective-permute-start | bytes 786440 | tf_op jit(solution)/shard_map/ppermute | solution.py:289
  85.0 12.6 %collective-permute-start.21 = (f32[128,256]{1,0:T(8,128)S(1)}, f32[128,256]{1,0:T(8,128)S(1)}, u32[]{:S(2)}, u32[]{:S(2)}) collective-permute-start(f32[128,256]{1,0:T(8,128)S(1)} %fusion.3), channel_id=1, source_target_pairs={{0,8},{2,10},{4,12},{6,14},{8,0},{10,2},{12,4},{14,6},{16,24},{18,... | collective-permute-start | bytes 393224 | tf_op jit(solution)/shard_map/ppermute | solution.py:284
  95.7 7.3 %collective-permute-start.23 = (f32[128,256]{1,0:T(8,128)S(1)}, f32[128,256]{1,0:T(8,128)S(1)}, u32[]{:S(2)}, u32[]{:S(2)}) collective-permute-start(f32[128,256]{1,0:T(8,128)S(1)} %fusion.3), channel_id=1, source_target_pairs={{0,24},{2,26},{4,28},{6,30},{8,16},{10,18},{12,20},{14,22},{16,8},... | collective-permute-start | bytes 393224 | tf_op jit(solution)/shard_map/ppermute | solution.py:284
  97.2 9.1 %collective-permute-start.8 = (bf16[2,256,256]{2,1,0:T(8,128)(2,1)S(1)}, bf16[2,256,256]{2,1,0:T(8,128)(2,1)S(1)}, u32[]{:S(2)}, u32[]{:S(2)}) collective-permute-start(bf16[2,256,256]{2,1,0:T(8,128)(2,1)S(1)} %get-tuple-element.56), channel_id=1, source_target_pairs={{0,2},{2,0},{4,6},{6,4},{8,10},{10,8},{12,14},{14,12},{16,18},{18,... | collective-permute-start | bytes 786440 | tf_op jit(solution)/shard_map/ppermute | solution.py:284
  97.6 15.4 %collective-permute-start = (f32[256,512]{1,0:T(8,128)S(1)}, f32[256,512]{1,0:T(8,128)S(1)}, u32[]{:S(2)}, u32[]{:S(2)}) collective-permute-start(f32[256,512]{1,0:T(8,128)S(1)} %get-tuple-element.48.refs_0_), channel_id=1, source_target_pairs={{0,1},{1,0},{2,3},{3,2},{4,5},{5,4},{6,7},{7,6},{8,9},{9,8},{10,11... | collective-permute-start | bytes 1572872 | tf_op jit(solution)/shard_map/ppermute | solution.py:280
  118.2 6.7 %collective-permute-start.29 = (f32[96,256]{1,0:T(8,128)S(1)}, f32[96,256]{1,0:T(8,128)S(1)}, u32[]{:S(2)}, u32[]{:S(2)}) collective-permute-start(f32[96,256]{1,0:T(8,128)S(1)} %get-tuple-element.121), channel_id=1, source_target_pairs={{0,4},{2,6},{4,0},{6,2},{8,12},{10,14},{12,8},{14,10},{16,20},{18,... | collective-permute-start | bytes 294920 | tf_op jit(solution)/shard_map/ppermute | solution.py:284
  118.2 6.7 %collective-permute-start.30 = (f32[96,256]{1,0:T(8,128)S(1)}, f32[96,256]{1,0:T(8,128)S(1)}, u32[]{:S(2)}, u32[]{:S(2)}) collective-permute-start(f32[96,256]{1,0:T(8,128)S(1)} %get-tuple-element.120), channel_id=1, source_target_pairs={{0,6},{2,4},{4,2},{6,0},{8,14},{10,12},{12,10},{14,8},{16,22},{18,... | collective-permute-start | bytes 294920 | tf_op jit(solution)/shard_map/ppermute | solution.py:284
  125.5 9.3 %collective-permute-start.32 = (f32[96,256]{1,0:T(8,128)S(1)}, f32[96,256]{1,0:T(8,128)S(1)}, u32[]{:S(2)}, u32[]{:S(2)}) collective-permute-start(f32[96,256]{1,0:T(8,128)S(1)} %fusion.7), channel_id=1, source_target_pairs={{0,16},{2,18},{4,20},{6,22},{8,24},{10,26},{12,28},{14,30},{16,0},... | collective-permute-start | bytes 294920 | tf_op jit(solution)/shard_map/ppermute | solution.py:284
  127.9 7.0 %collective-permute-start.33 = (f32[96,256]{1,0:T(8,128)S(1)}, f32[96,256]{1,0:T(8,128)S(1)}, u32[]{:S(2)}, u32[]{:S(2)}) collective-permute-start(f32[96,256]{1,0:T(8,128)S(1)} %fusion.7), channel_id=1, source_target_pairs={{0,24},{2,26},{4,28},{6,30},{8,16},{10,18},{12,20},{14,22},{16,8},... | collective-permute-start | bytes 294920 | tf_op jit(solution)/shard_map/ppermute | solution.py:284
  156.4 9.9 %collective-permute-start.39 = (bf16[2,256,256]{2,1,0:T(8,128)(2,1)S(1)}, bf16[2,256,256]{2,1,0:T(8,128)(2,1)S(1)}, u32[]{:S(2)}, u32[]{:S(2)}) collective-permute-start(bf16[2,256,256]{2,1,0:T(8,128)(2,1)S(1)} %get-tuple-element.71.refs_0_), channel_id=1, source_target_pairs={{0,8},{2,10},{4,12},{6,14},{8,16},{10,18},{12,20},{14,22},{16,24},... | collective-permute-start | bytes 786440 | tf_op jit(solution)/shard_map/ppermute | solution.py:289
  160.5 8.1 %collective-permute-start.40 = (bf16[2,256,256]{2,1,0:T(8,128)(2,1)S(1)}, bf16[2,256,256]{2,1,0:T(8,128)(2,1)S(1)}, u32[]{:S(2)}, u32[]{:S(2)}) collective-permute-start(bf16[2,256,256]{2,1,0:T(8,128)(2,1)S(1)} %get-tuple-element.71.refs_0_), channel_id=1, source_target_pairs={{0,2},{2,0},{4,6},{6,4},{8,10},{10,8},{12,14},{14,12},{16,18},{18,... | collective-permute-start | bytes 786440 | tf_op jit(solution)/shard_map/ppermute | solution.py:284
  161.5 9.1 %collective-permute-start.41 = (bf16[2,256,256]{2,1,0:T(8,128)(2,1)S(1)}, bf16[2,256,256]{2,1,0:T(8,128)(2,1)S(1)}, u32[]{:S(2)}, u32[]{:S(2)}) collective-permute-start(bf16[2,256,256]{2,1,0:T(8,128)(2,1)S(1)} %get-tuple-element.71.refs_0_), channel_id=1, source_target_pairs={{0,4},{2,6},{8,12},{10,14},{4,16},{6,18},{16,20},{18,22},{12,24},{... | collective-permute-start | bytes 786440 | tf_op jit(solution)/shard_map/ppermute | solution.py:295
  168.6 7.2 %collective-permute-start.42 = (bf16[2,256,256]{2,1,0:T(8,128)(2,1)S(1)}, bf16[2,256,256]{2,1,0:T(8,128)(2,1)S(1)}, u32[]{:S(2)}, u32[]{:S(2)}) collective-permute-start(bf16[2,256,256]{2,1,0:T(8,128)(2,1)S(1)} %collective-permute-done.39.refs_2_), channel_id=1, source_target_pairs={{0,2},{2,0},{4,6},{6,4},{8,10},{10,8},{12,14},{14,12},{16,18},{18,... | collective-permute-start | bytes 786440 | tf_op jit(solution)/shard_map/ppermute | solution.py:284
  169.6 6.9 %collective-permute-start.43 = (bf16[2,256,256]{2,1,0:T(8,128)(2,1)S(1)}, bf16[2,256,256]{2,1,0:T(8,128)(2,1)S(1)}, u32[]{:S(2)}, u32[]{:S(2)}) collective-permute-start(bf16[2,256,256]{2,1,0:T(8,128)(2,1)S(1)} %collective-permute-done.39.refs_2_), channel_id=1, source_target_pairs={{0,4},{2,6},{4,0},{6,2},{8,12},{10,14},{12,8},{14,10},{16,20},{18,... | collective-permute-start | bytes 786440 | tf_op jit(solution)/shard_map/ppermute | solution.py:284
  179.4 14.1 %collective-permute-start.49 = (bf16[6,256,256]{2,1,0:T(8,128)(2,1)S(1)}, bf16[6,256,256]{2,1,0:T(8,128)(2,1)S(1)}, u32[]{:S(2)}, u32[]{:S(2)}) collective-permute-start(bf16[6,256,256]{2,1,0:T(8,128)(2,1)S(1)} %pad_maximum_fusion.2), channel_id=1, source_target_pairs={{0,1},{1,0},{2,3},{3,2},{4,5},{5,4},{6,7},{7,6},{8,9},{9,8},{10,11... | collective-permute-start | bytes 2359304 | tf_op jit(solution)/shard_map/ppermute | solution.py:280
  179.6 14.0 %collective-permute-start.50 = (bf16[6,256,256]{2,1,0:T(8,128)(2,1)S(1)}, bf16[6,256,256]{2,1,0:T(8,128)(2,1)S(1)}, u32[]{:S(2)}, u32[]{:S(2)}) collective-permute-start(bf16[6,256,256]{2,1,0:T(8,128)(2,1)S(1)} %pad_maximum_fusion.3), channel_id=1, source_target_pairs={{0,1},{1,0},{2,3},{3,2},{4,5},{5,4},{6,7},{7,6},{8,9},{9,8},{10,11... | collective-permute-start | bytes 2359304 | tf_op jit(solution)/shard_map/ppermute | solution.py:280
  183.9 9.6 %collective-permute-start.51 = (bf16[4,256,256]{2,1,0:T(8,128)(2,1)S(1)}, bf16[4,256,256]{2,1,0:T(8,128)(2,1)S(1)}, u32[]{:S(2)}, u32[]{:S(2)}) collective-permute-start(bf16[4,256,256]{2,1,0:T(8,128)(2,1)S(1)} %pad_maximum_fusion.6), channel_id=1, source_target_pairs={{0,1},{1,0},{2,3},{3,2},{4,5},{5,4},{6,7},{7,6},{8,9},{9,8},{10,11... | collective-permute-start | bytes 1572872 | tf_op jit(solution)/shard_map/ppermute | solution.py:280
  189.0 8.8 %collective-permute-start.47 = (bf16[2,256,256]{2,1,0:T(8,128)(2,1)S(1)}, bf16[2,256,256]{2,1,0:T(8,128)(2,1)S(1)}, u32[]{:S(2)}, u32[]{:S(2)}) collective-permute-start(bf16[2,256,256]{2,1,0:T(8,128)(2,1)S(1)} %get-tuple-element.80), channel_id=1, source_target_pairs={{0,4},{2,6},{4,0},{6,2},{8,12},{10,14},{12,8},{14,10},{16,20},{18,... | collective-permute-start | bytes 786440 | tf_op jit(solution)/shard_map/ppermute | solution.py:284
  189.1 11.1 %collective-permute-start.48 = (bf16[2,256,256]{2,1,0:T(8,128)(2,1)S(1)}, bf16[2,256,256]{2,1,0:T(8,128)(2,1)S(1)}, u32[]{:S(2)}, u32[]{:S(2)}) collective-permute-start(bf16[2,256,256]{2,1,0:T(8,128)(2,1)S(1)} %get-tuple-element.81), channel_id=1, source_target_pairs={{0,2},{2,0},{4,6},{6,4},{8,10},{10,8},{12,14},{14,12},{16,18},{18,... | collective-permute-start | bytes 786440 | tf_op jit(solution)/shard_map/ppermute | solution.py:284
  200.3 8.0 %collective-permute-start.53 = (bf16[2,256,256]{2,1,0:T(8,128)(2,1)S(1)}, bf16[2,256,256]{2,1,0:T(8,128)(2,1)S(1)}, u32[]{:S(2)}, u32[]{:S(2)}) collective-permute-start(bf16[2,256,256]{2,1,0:T(8,128)(2,1)S(1)} %add_convert_fusion.1), channel_id=1, source_target_pairs={{0,2},{2,0},{4,6},{6,4},{8,10},{10,8},{12,14},{14,12},{16,18},{18,... | collective-permute-start | bytes 786440 | tf_op jit(solution)/shard_map/ppermute | solution.py:284
  202.2 11.1 %collective-permute-start.52 = (bf16[2,256,256]{2,1,0:T(8,128)(2,1)S(1)}, bf16[2,256,256]{2,1,0:T(8,128)(2,1)S(1)}, u32[]{:S(2)}, u32[]{:S(2)}) collective-permute-start(bf16[2,256,256]{2,1,0:T(8,128)(2,1)S(1)} %add_convert_fusion.2), channel_id=1, source_target_pairs={{4,0},{6,2},{12,8},{14,10},{16,4},{18,6},{20,16},{22,18},{24,12},{... | collective-permute-start | bytes 786440 | tf_op jit(solution)/shard_map/ppermute | solution.py:295
  203.5 24.5 %collective-permute-start.54 = (bf16[2,256,256]{2,1,0:T(8,128)(2,1)S(1)}, bf16[2,256,256]{2,1,0:T(8,128)(2,1)S(1)}, u32[]{:S(2)}, u32[]{:S(2)}) collective-permute-start(bf16[2,256,256]{2,1,0:T(8,128)(2,1)S(1)} %get-tuple-element.87), channel_id=1, source_target_pairs={{0,4},{2,6},{4,0},{6,2},{8,12},{10,14},{12,8},{14,10},{16,20},{18,... | collective-permute-start | bytes 786440 | tf_op jit(solution)/shard_map/ppermute | solution.py:284
  213.4 16.0 %collective-permute-start.56 = (f32[128,256]{1,0:T(8,128)S(1)}, f32[128,256]{1,0:T(8,128)S(1)}, u32[]{:S(2)}, u32[]{:S(2)}) collective-permute-start(f32[128,256]{1,0:T(8,128)S(1)} %get-tuple-element.98), channel_id=1, source_target_pairs={{0,2},{2,0},{4,6},{6,4},{8,10},{10,8},{12,14},{14,12},{16,18},{18,... | collective-permute-start | bytes 393224 | tf_op jit(solution)/shard_map/ppermute | solution.py:284
  213.7 18.4 %collective-permute-start.57 = (f32[128,256]{1,0:T(8,128)S(1)}, f32[128,256]{1,0:T(8,128)S(1)}, u32[]{:S(2)}, u32[]{:S(2)}) collective-permute-start(f32[128,256]{1,0:T(8,128)S(1)} %get-tuple-element.100), channel_id=1, source_target_pairs={{0,4},{2,6},{4,0},{6,2},{8,12},{10,14},{12,8},{14,10},{16,20},{18,... | collective-permute-start | bytes 393224 | tf_op jit(solution)/shard_map/ppermute | solution.py:284
  228.1 8.3 %collective-permute-start.55 = (bf16[2,256,256]{2,1,0:T(8,128)(2,1)S(1)}, bf16[2,256,256]{2,1,0:T(8,128)(2,1)S(1)}, u32[]{:S(2)}, u32[]{:S(2)}) collective-permute-start(bf16[2,256,256]{2,1,0:T(8,128)(2,1)S(1)} %add_convert_fusion), channel_id=1, source_target_pairs={{8,0},{10,2},{12,4},{14,6},{16,8},{18,10},{20,12},{22,14},{24,16},... | collective-permute-start | bytes 786440 | tf_op jit(solution)/shard_map/ppermute | solution.py:289
  236.4 14.1 %collective-permute-start.59 = (f32[128,256]{1,0:T(8,128)S(1)}, f32[128,256]{1,0:T(8,128)S(1)}, u32[]{:S(2)}, u32[]{:S(2)}) collective-permute-start(f32[128,256]{1,0:T(8,128)S(1)} %fusion.1), channel_id=1, source_target_pairs={{0,8},{2,10},{4,12},{6,14},{8,0},{10,2},{12,4},{14,6},{16,24},{18,... | collective-permute-start | bytes 393224 | tf_op jit(solution)/shard_map/ppermute | solution.py:284
  247.7 7.3 %collective-permute-start.61 = (f32[128,256]{1,0:T(8,128)S(1)}, f32[128,256]{1,0:T(8,128)S(1)}, u32[]{:S(2)}, u32[]{:S(2)}) collective-permute-start(f32[128,256]{1,0:T(8,128)S(1)} %fusion.1), channel_id=1, source_target_pairs={{0,24},{2,26},{4,28},{6,30},{8,16},{10,18},{12,20},{14,22},{16,8},... | collective-permute-start | bytes 393224 | tf_op jit(solution)/shard_map/ppermute | solution.py:284
  249.1 9.2 %collective-permute-start.46 = (bf16[2,256,256]{2,1,0:T(8,128)(2,1)S(1)}, bf16[2,256,256]{2,1,0:T(8,128)(2,1)S(1)}, u32[]{:S(2)}, u32[]{:S(2)}) collective-permute-start(bf16[2,256,256]{2,1,0:T(8,128)(2,1)S(1)} %get-tuple-element.78), channel_id=1, source_target_pairs={{0,2},{2,0},{4,6},{6,4},{8,10},{10,8},{12,14},{14,12},{16,18},{18,... | collective-permute-start | bytes 786440 | tf_op jit(solution)/shard_map/ppermute | solution.py:284
  250.5 15.7 %collective-permute-start.38 = (f32[256,512]{1,0:T(8,128)S(1)}, f32[256,512]{1,0:T(8,128)S(1)}, u32[]{:S(2)}, u32[]{:S(2)}) collective-permute-start(f32[256,512]{1,0:T(8,128)S(1)} %get-tuple-element.70.refs_0_), channel_id=1, source_target_pairs={{0,1},{1,0},{2,3},{3,2},{4,5},{5,4},{6,7},{7,6},{8,9},{9,8},{10,11... | collective-permute-start | bytes 1572872 | tf_op jit(solution)/shard_map/ppermute | solution.py:280
  258.3 7.1 %collective-permute-start.63 = (f32[128,256]{1,0:T(8,128)S(1)}, f32[128,256]{1,0:T(8,128)S(1)}, u32[]{:S(2)}, u32[]{:S(2)}) collective-permute-start(f32[128,256]{1,0:T(8,128)S(1)} %add_add_fusion), channel_id=1, source_target_pairs={{0,4},{2,6},{4,0},{6,2},{8,12},{10,14},{12,8},{14,10},{16,20},{18,... | collective-permute-start | bytes 393224 | tf_op jit(solution)/shard_map/ppermute | solution.py:284
  271.1 6.7 %collective-permute-start.67 = (f32[96,256]{1,0:T(8,128)S(1)}, f32[96,256]{1,0:T(8,128)S(1)}, u32[]{:S(2)}, u32[]{:S(2)}) collective-permute-start(f32[96,256]{1,0:T(8,128)S(1)} %get-tuple-element.114), channel_id=1, source_target_pairs={{0,4},{2,6},{4,0},{6,2},{8,12},{10,14},{12,8},{14,10},{16,20},{18,... | collective-permute-start | bytes 294920 | tf_op jit(solution)/shard_map/ppermute | solution.py:284
  278.5 8.9 %collective-permute-start.70 = (f32[96,256]{1,0:T(8,128)S(1)}, f32[96,256]{1,0:T(8,128)S(1)}, u32[]{:S(2)}, u32[]{:S(2)}) collective-permute-start(f32[96,256]{1,0:T(8,128)S(1)} %fusion.5), channel_id=1, source_target_pairs={{0,16},{2,18},{4,20},{6,22},{8,24},{10,26},{12,28},{14,30},{16,0},... | collective-permute-start | bytes 294920 | tf_op jit(solution)/shard_map/ppermute | solution.py:284
  280.8 6.6 %collective-permute-start.71 = (f32[96,256]{1,0:T(8,128)S(1)}, f32[96,256]{1,0:T(8,128)S(1)}, u32[]{:S(2)}, u32[]{:S(2)}) collective-permute-start(f32[96,256]{1,0:T(8,128)S(1)} %fusion.5), channel_id=1, source_target_pairs={{0,24},{2,26},{4,28},{6,30},{8,16},{10,18},{12,20},{14,22},{16,8},... | collective-permute-start | bytes 294920 | tf_op jit(solution)/shard_map/ppermute | solution.py:284
  (39 other events, 254.5 us)

commit v5 on v4

--- a/solution.py
+++ b/solution.py
@@ -59,8 +59,8 @@
 
 
 def apply_kernel(meta, rows, cols, *refs):
-    pieces, blocks, out = refs[: 2 * REACH], refs[2 * REACH], refs[2 * REACH + 1 : 4 * REACH + 1]
-    everything, window, total, tiles, piece_sems, tile_sems = refs[4 * REACH + 1 :]
+    pieces, blocks, theirs = refs[: 2 * REACH], refs[2 * REACH], refs[2 * REACH + 1 : 2 * REACH + 4]
+    out, (inner, window, total, tiles, piece_sems, tile_sems) = refs[2 * REACH + 4 : -6], refs[-6:]
     used, start, odd, pair_odd = meta[0], meta[1], meta[2], meta[3]
     groups = (used + GROUP - 1) // GROUP
 
@@ -110,10 +110,21 @@
     lax.fori_loop(0, groups, multiply, 0)
     for s, segment in enumerate(out):
         segment[...] = total[pl.ds(2 * s, 2)].astype(segment.dtype)
-    everything[...] = total[...].astype(bf16)
-
-
-def apply_tiles(pieces, blocks, rows, cols, meta):
+
+    size = inner.shape[1]
+    own = jnp.zeros((size, size), f32)
+    other = jnp.zeros((size, size), f32)
+    for s in range(2 * REACH):
+        group, start = GROUPED[s]
+        for t in range(2):
+            mine = total[2 * s + t].astype(bf16)
+            own += dot_nt(mine, window[2 * s + t])
+            other += dot_nt(mine, theirs[group][start + t])
+    inner[pl.ds(0, size), :] = own
+    inner[pl.ds(size, size), :] = other
+
+
+def apply_tiles(pieces, others, blocks, rows, cols, meta):
     size = blocks.shape[1]
     width = pieces[0].shape[1]
     segment, window = (2, width, size), (4 * REACH, width, size)
@@ -121,7 +132,8 @@
         apply_kernel,
         in_specs=[pl.BlockSpec(memory_space=SMEM)] * 3
         + [pl.BlockSpec(memory_space=pl.ANY)] * (2 * REACH)
-        + [pl.BlockSpec(memory_space=pltpu.HBM)],
+        + [pl.BlockSpec(memory_space=pltpu.HBM)]
+        + [pl.BlockSpec(memory_space=VMEM)] * len(others),
         out_specs=[pl.BlockSpec(memory_space=VMEM)] * (2 * REACH + 1),
         scratch_shapes=[
             VMEM(window, bf16),
@@ -130,25 +142,11 @@
             pltpu.SemaphoreType.DMA((2 * REACH,)),
             pltpu.SemaphoreType.DMA((2,)),
         ],
-        out_shape=[shape(kind, *segment) for kind in SEGMENT_KINDS] + [shape(bf16, *window)],
+        out_shape=[shape(kind, *segment) for kind in SEGMENT_KINDS] + [shape(f32, 2 * width, size)],
         compiler_params=pltpu.CompilerParams(vmem_limit_bytes=50 << 20),
         cost_estimate=pl.CostEstimate(flops=4 << 30, bytes_accessed=16 << 20, transcendentals=0),
-    )(meta, rows, cols, *pieces, blocks)
+    )(meta, rows, cols, *pieces, blocks, *others)
     return out[: 2 * REACH : 2], out[1 : 2 * REACH : 2], out[2 * REACH]
-
-
-def inner_kernel(*refs):
-    pieces, theirs, mine, out = refs[: 2 * REACH], refs[2 * REACH : -2], refs[-2], refs[-1]
-    size = out.shape[1]
-    own = jnp.zeros((size, size), f32)
-    other = jnp.zeros((size, size), f32)
-    for s, piece in enumerate(pieces):
-        group, start = GROUPED[s]
-        for t in range(2):
-            own += dot_nt(mine[2 * s + t], piece[t])
-            other += dot_nt(mine[2 * s + t], theirs[group][start + t])
-    out[pl.ds(0, size), :] = own
-    out[pl.ds(size, size), :] = other
 
 
 def update_kernel(rows_total, x, x_other, kept, near, far, two, inner, update, *residual):
@@ -369,17 +367,16 @@
         last = step == STEPS - 1
         pieces, others = reach(u)
         x_other = swap_cores(x)
-        same, cross, everything = apply_tiles(pieces, blocks, block_row, block_col, meta)
-        side_x, far_x, side, own_x = flip(cross[3], 2), flip(cross[2], 1), flip(same[3], 2), flip(cross[0], 1)
-        (inner,) = call(
-            inner_kernel, [shape(f32, 2 * width, width)], pieces + others + [everything], flops=1 << 30
-        )
-        side_x, far_x, inner = together(side_x, far_x, inner)
-        two_x = flip((cross[1] + side_x.astype(f32)).astype(bf16), 1)
-        far = stride((same[2] + far_x.astype(f32)).astype(bf16), True)
+        same, cross, inner = apply_tiles(pieces, others, blocks, block_row, block_col, meta)
+        side_x, far_x, side = flip(cross[3], 2), flip(cross[2], 1), flip(same[3], 2)
+        side_x, far_x = together(side_x, far_x)
+        two_out = (cross[1] + side_x.astype(f32)).astype(bf16)
+        far_out = (same[2] + far_x.astype(f32)).astype(bf16)
+        two_x, far = flip(two_out, 1), stride(far_out, True)
+        near, two_x = together(cross[0], two_x)
         two = (same[1] + (two_x.astype(f32) + side.astype(f32))).astype(bf16)
-        joined = [own_x, far, shift(two, -2)]
-        inner = summed(inner, [(two_x, far), (joined[2],), (own_x,)])
+        joined = [flip(near, 1), far, shift(two, -2)]
+        inner = summed(inner, [(), (two_x, far_out), joined])
         out = [flat] + ([shape(f32, count, width)] if last else [])
         update, *residual = call(
             lambda *refs: update_kernel(rows_total, *refs), out, [x, x_other, same[0], *joined, inner]

time: 304 us -> 299 us (0.984); the launches traced: 309 us -> 298 us
  starting transfers between devices: 140 us -> 126 us
  other arithmetic: 3.77 us -> 11.3 us
  waiting for transfers between devices: 117 us -> 112 us
    ppermute x56, starting transfers between devices: 118 us -> 105 us  [flip(): lax.ppermute(a, 'patch', [(i, i ^ mask) for i in range(lax.axis_size('pat...]
    ppermute x4, waiting for transfers between devices: 9.61 us -> 0.01 us  [stride(): lax.ppermute(a, 'patch', [(d, s) if back else (s, d) for s, d in route if...]
    convert_element_type x4, other arithmetic: 0.94 us -> 4.41 us  [the longest x2 2.21 us: shards(): far_out = (same[2] + far_x.astype(f32)).astype(bf16)]
    ppermute x12, waiting for transfers between devices: 7.24 us -> 10.4 us  [swap_cores(): return lax.ppermute(a, 'vec', [(0, 1), (1, 0)])]
    pallas_call x9 -> x7, Pallas kernels: 31.6 us -> 30.4 us  [call(): pl.pallas_call(kernel, out_shape=out, in_specs=[pl.BlockSpec(memory_space...]
  transfers between devices with their start and end apart: 76 -> 76, of which waited for: 54 -> 49; matrix products, arithmetic and copies ran while one was open for 1% -> 4% of each run, Pallas kernels for 4% -> 0%
where the time goes in v5:
time: 299 us; the launch traced here: 298 us
  starting transfers between devices  126 us (42%)
  waiting for transfers between devices  112 us (37%)
  Pallas kernels  40.1 us (13%)
  other arithmetic  11.3 us (4%)
  local copies, waits for them, and re-layouts  6.9 us (2%)
    ppermute x56, starting transfers between devices, flip(): lax.ppermute(a, 'patch', [(i, i ^ mask) for i in range(lax.axis_size('pat...  105 us
    ppermute x56, waiting for transfers between devices, flip(): lax.ppermute(a, 'patch', [(i, i ^ mask) for i in range(lax.axis_size('pat...  92.7 us
    pallas_call x7, Pallas kernels, call(): pl.pallas_call(kernel, out_shape=out, in_specs=[pl.BlockSpec(memory_space...  30.4 us
    ppermute x4, starting transfers between devices, shift(): lax.ppermute(a, 'patch', [(i - 2 * pairs, i) for i in devices if i - 2 *...  11.6 us
    ppermute x12, waiting for transfers between devices, swap_cores(): return lax.ppermute(a, 'vec', [(0, 1), (1, 0)])  10.4 us
    pallas_call x2, Pallas kernels, apply_tiles(): pl.pallas_call(apply_kernel, in_specs=[pl.BlockSpec(memory_space=SMEM)] *...  9.69 us
    ppermute x4, starting transfers between devices, stride(): lax.ppermute(a, 'patch', [(d, s) if back else (s, d) for s, d in route if...  9.27 us
    ppermute x4, waiting for transfers between devices, shift(): lax.ppermute(a, 'patch', [(i - 2 * pairs, i) for i in devices if i - 2 *...  8.54 us
  transfers between devices with their start and end apart: 76, of which 49 were waited for; matrix products, arithmetic and copies ran while one was open for 4% of the time, Pallas kernels for 0%

profile of v5, /device:TPU:0, one launch (start us, length us, event | category | flops | bytes accessed | tf_op | source)
XLA Modules:
  0.0 297.8 jit_solution(7375592396087094127)
XLA Ops:
  1.9 4.9 %collective-permute-start.1 = (bf16[2,256,256]{2,1,0:T(8,128)(2,1)S(1)}, bf16[2,256,256]{2,1,0:T(8,128)(2,1)S(1)}, u32[]{:S(2)}, u32[]{:S(2)}) collective-permute-start(bf16[2,256,256]{2,1,0:T(8,128)(2,1)S(1)} %get-tuple-element.49.refs_0_), channel_id=1, source_target_pairs={{0,8},{2,10},{4,12},{6,14},{8,16},{10,18},{12,20},{14,22},{16,24},... | collective-permute-start | bytes 786440 | tf_op jit(solution)/shard_map/ppermute | solution.py:287
  8.4 3.4 %collective-permute-start.3 = (bf16[2,256,256]{2,1,0:T(8,128)(2,1)S(1)}, bf16[2,256,256]{2,1,0:T(8,128)(2,1)S(1)}, u32[]{:S(2)}, u32[]{:S(2)}) collective-permute-start(bf16[2,256,256]{2,1,0:T(8,128)(2,1)S(1)} %get-tuple-element.49.refs_0_), channel_id=1, source_target_pairs={{0,4},{2,6},{8,12},{10,14},{4,16},{6,18},{16,20},{18,22},{12,24},{... | collective-permute-start | bytes 786440 | tf_op jit(solution)/shard_map/ppermute | solution.py:293
  12.4 2.3 collective-permute-done.2.refs_1_
  18.6 2.9 collective-permute-done.4.refs_3_
  23.3 2.2 collective-permute-start.7
  26.4 2.7 collective-permute-done.6.refs_5_
  33.2 4.8 %shard_map.69 = (f32[2,256,256]{2,1,0:T(8,128)S(1)}, bf16[2,256,256]{2,1,0:T(8,128)(2,1)S(1)}, f32[2,256,256]{2,1,0:T(8,128)}, f32[2,256,256]{2,1,0:T(8,128)}, f...) custom-call(s32[4]{0:T(128)S(1)} %pad_add_fusion.meta, ...), custom_call_target="tpu_custom_call" | custom-call | flops 4294967296 | bytes 16777216 | tf_op jit(solution)/shard_map/pallas_call | solution.py:131
  38.7 4.8 %collective-permute-start.11 = (bf16[2,256,256]{2,1,0:T(8,128)(2,1)}, bf16[2,256,256]{2,1,0:T(8,128)(2,1)S(1)}, u32[]{:S(2)}, u32[]{:S(2)}) collective-permute-start(bf16[2,256,256]{2,1,0:T(8,128)(2,1)} %get-tuple-element.58), channel_id=1, source_target_pairs={{0,4},{2,6},{4,0},{6,2},{8,12},{10,14},{12,8},{14,10},{16,20},{18,... | collective-permute-start | bytes 786440 | tf_op jit(solution)/shard_map/ppermute | solution.py:282
  46.7 3.0 collective-permute-start.20
  50.9 2.1 collective-permute-start.16
  55.8 2.3 collective-permute-done.20
  63.1 7.0 %collective-permute-start.21 = (f32[128,256]{1,0:T(8,128)S(1)}, f32[128,256]{1,0:T(8,128)S(1)}, u32[]{:S(2)}, u32[]{:S(2)}) collective-permute-start(f32[128,256]{1,0:T(8,128)S(1)} %fusion.3), channel_id=1, source_target_pairs={{0,8},{2,10},{4,12},{6,14},{8,0},{10,2},{12,4},{14,6},{16,24},{18,... | collective-permute-start | bytes 393224 | tf_op jit(solution)/shard_map/ppermute | solution.py:282
  70.0 8.1 %collective-permute-start.22 = (f32[128,256]{1,0:T(8,128)S(1)}, f32[128,256]{1,0:T(8,128)S(1)}, u32[]{:S(2)}, u32[]{:S(2)}) collective-permute-start(f32[128,256]{1,0:T(8,128)S(1)} %fusion.3), channel_id=1, source_target_pairs={{0,16},{2,18},{4,20},{6,22},{8,24},{10,26},{12,28},{14,30},{16,0},... | collective-permute-start | bytes 393224 | tf_op jit(solution)/shard_map/ppermute | solution.py:282
  82.6 10.1 %collective-permute-done.22 = f32[128,256]{1,0:T(8,128)S(1)} collective-permute-done((f32[128,256]{1,0:T(8,128)S(1)}, f32[128,256]{1,0:T(8,128)S(1)}, u32[]{:S(2)}, u32[]{:S(2)}) %collective-permute-start.22) | collective-permute-done | bytes 131104 | tf_op jit(solution)/shard_map/ppermute | solution.py:282
  92.8 2.6 collective-permute-done.17.refs_5_
  95.4 3.0 collective-permute-start.25
  98.8 3.3 %collective-permute-done.24 = f32[128,256]{1,0:T(8,128)S(1)} collective-permute-done((f32[128,256]{1,0:T(8,128)S(1)}, f32[128,256]{1,0:T(8,128)S(1)}, u32[]{:S(2)}, u32[]{:S(2)}) %collective-permute-start.24) | collective-permute-done | bytes 131104 | tf_op jit(solution)/shard_map/ppermute | solution.py:282
  104.2 1.9 collective-permute-done.27.theirs.refs_2_
  110.4 2.0 collective-permute-done.28
  114.5 5.9 %collective-permute-start.31 = (f32[96,256]{1,0:T(8,128)S(1)}, f32[96,256]{1,0:T(8,128)S(1)}, u32[]{:S(2)}, u32[]{:S(2)}) collective-permute-start(f32[96,256]{1,0:T(8,128)S(1)} %fusion.7), channel_id=1, source_target_pairs={{0,8},{2,10},{4,12},{6,14},{8,0},{10,2},{12,4},{14,6},{16,24},{18,... | collective-permute-start | bytes 294920 | tf_op jit(solution)/shard_map/ppermute | solution.py:282
  120.4 2.4 collective-permute-start.33
  124.6 4.7 %collective-permute-done.32 = f32[96,256]{1,0:T(8,128)S(1)} collective-permute-done((f32[96,256]{1,0:T(8,128)S(1)}, f32[96,256]{1,0:T(8,128)S(1)}, u32[]{:S(2)}, u32[]{:S(2)}) %collective-permute-start.32) | collective-permute-done | bytes 98336 | tf_op jit(solution)/shard_map/ppermute | solution.py:282
  132.9 2.1 collective-permute-done.34
  138.9 14.3 %shard_map.72 = (f32[256,512]{1,0:T(8,128)S(1)}, bf16[2,256,256]{2,1,0:T(8,128)(2,1)S(1)}) custom-call(s32[1]{0:T(128)} %bitcast.core.refs_0_, f32[256,512]{1,0:T(8,128)S(1)} %shard_map.70.mine.refs_1_, f32[256,512]{1,0:T(8,128)S(1)} %collective-permute-done.27.theirs.refs_2_, f32[384,256]{1,0:T(8,128)S(1)} %pad_maximum_fusion.8.refs_3_, ...), custom_call_target="tpu_custom_call" | custom-call | flops 17179869184 | bytes 2621444 | tf_op jit(solution)/shard_map/pallas_call | solution.py:38
  153.2 3.8 %collective-permute-start.39 = (bf16[2,256,256]{2,1,0:T(8,128)(2,1)S(1)}, bf16[2,256,256]{2,1,0:T(8,128)(2,1)S(1)}, u32[]{:S(2)}, u32[]{:S(2)}) collective-permute-start(bf16[2,256,256]{2,1,0:T(8,128)(2,1)S(1)} %get-tuple-element.71.refs_0_), channel_id=1, source_target_pairs={{0,8},{2,10},{4,12},{6,14},{8,16},{10,18},{12,20},{14,22},{16,24},... | collective-permute-start | bytes 786440 | tf_op jit(solution)/shard_map/ppermute | solution.py:287
  157.3 3.3 %collective-permute-start.41 = (bf16[2,256,256]{2,1,0:T(8,128)(2,1)S(1)}, bf16[2,256,256]{2,1,0:T(8,128)(2,1)S(1)}, u32[]{:S(2)}, u32[]{:S(2)}) collective-permute-start(bf16[2,256,256]{2,1,0:T(8,128)(2,1)S(1)} %get-tuple-element.71.refs_0_), channel_id=1, source_target_pairs={{0,4},{2,6},{8,12},{10,14},{4,16},{6,18},{16,20},{18,22},{12,24},{... | collective-permute-start | bytes 786440 | tf_op jit(solution)/shard_map/ppermute | solution.py:293
  160.5 2.3 collective-permute-done.39.refs_2_
  162.8 2.3 collective-permute-done.40.refs_1_
  166.9 5.4 %collective-permute-done.42.refs_3_ = bf16[2,256,256]{2,1,0:T(8,128)(2,1)S(1)} collective-permute-done((bf16[2,256,256]{2,1,0:T(8,128)(2,1)S(1)}, bf16[2,256,256]{2,1,0:T(8,128)(2,1)S(1)}, u32[]{:S(2)}, u32[]{:S(2)}) %collective-permute-start.42) | collective-permute-done | bytes 262176 | tf_op jit(solution)/shard_map/ppermute | solution.py:282
  175.0 3.7 %collective-permute-done.44.refs_5_ = bf16[2,256,256]{2,1,0:T(8,128)(2,1)S(1)} collective-permute-done((bf16[2,256,256]{2,1,0:T(8,128)(2,1)S(1)}, bf16[2,256,256]{2,1,0:T(8,128)(2,1)S(1)}, u32[]{:S(2)}, u32[]{:S(2)}) %collective-permute-start.44) | collective-permute-done | bytes 262176 | tf_op jit(solution)/shard_map/ppermute | solution.py:282
  184.1 4.9 %shard_map.73 = (f32[2,256,256]{2,1,0:T(8,128)S(1)}, bf16[2,256,256]{2,1,0:T(8,128)(2,1)S(1)}, f32[2,256,256]{2,1,0:T(8,128)}, f32[2,256,256]{2,1,0:T(8,128)}, f...) custom-call(s32[4]{0:T(128)S(1)} %pad_add_fusion.meta, ...), custom_call_target="tpu_custom_call" | custom-call | flops 4294967296 | bytes 16777216 | tf_op jit(solution)/shard_map/pallas_call | solution.py:131
  189.0 3.7 %collective-permute-start.49 = (bf16[2,256,256]{2,1,0:T(8,128)(2,1)S(1)}, bf16[2,256,256]{2,1,0:T(8,128)(2,1)S(1)}, u32[]{:S(2)}, u32[]{:S(2)}) collective-permute-start(bf16[2,256,256]{2,1,0:T(8,128)(2,1)S(1)} %get-tuple-element.80), channel_id=1, source_target_pairs={{0,4},{2,6},{4,0},{6,2},{8,12},{10,14},{12,8},{14,10},{16,20},{18,... | collective-permute-start | bytes 786440 | tf_op jit(solution)/shard_map/ppermute | solution.py:282
  196.0 2.5 collective-permute-start.58
  199.8 2.1 collective-permute-start.54
  204.7 2.3 collective-permute-done.58
  212.0 3.3 %collective-permute-start.59 = (f32[128,256]{1,0:T(8,128)S(1)}, f32[128,256]{1,0:T(8,128)S(1)}, u32[]{:S(2)}, u32[]{:S(2)}) collective-permute-start(f32[128,256]{1,0:T(8,128)S(1)} %fusion.1), channel_id=1, source_target_pairs={{0,8},{2,10},{4,12},{6,14},{8,0},{10,2},{12,4},{14,6},{16,24},{18,... | collective-permute-start | bytes 393224 | tf_op jit(solution)/shard_map/ppermute | solution.py:282
  215.3 9.0 %collective-permute-start.60 = (f32[128,256]{1,0:T(8,128)S(1)}, f32[128,256]{1,0:T(8,128)S(1)}, u32[]{:S(2)}, u32[]{:S(2)}) collective-permute-start(f32[128,256]{1,0:T(8,128)S(1)} %fusion.1), channel_id=1, source_target_pairs={{0,16},{2,18},{4,20},{6,22},{8,24},{10,26},{12,28},{14,30},{16,0},... | collective-permute-start | bytes 393224 | tf_op jit(solution)/shard_map/ppermute | solution.py:282
  228.7 10.3 %collective-permute-done.60 = f32[128,256]{1,0:T(8,128)S(1)} collective-permute-done((f32[128,256]{1,0:T(8,128)S(1)}, f32[128,256]{1,0:T(8,128)S(1)}, u32[]{:S(2)}, u32[]{:S(2)}) %collective-permute-start.60) | collective-permute-done | bytes 131104 | tf_op jit(solution)/shard_map/ppermute | solution.py:282
  239.0 3.1 %collective-permute-done.55.refs_5_ = bf16[2,256,256]{2,1,0:T(8,128)(2,1)S(1)} collective-permute-done((bf16[2,256,256]{2,1,0:T(8,128)(2,1)S(1)}, bf16[2,256,256]{2,1,0:T(8,128)(2,1)S(1)}, u32[]{:S(2)}, u32[]{:S(2)}) %collective-permute-start.55) | collective-permute-done | bytes 262176 | tf_op jit(solution)/shard_map/ppermute | solution.py:287
  242.2 2.1 collective-permute-start.63
  245.7 3.3 %collective-permute-done.62 = f32[128,256]{1,0:T(8,128)S(1)} collective-permute-done((f32[128,256]{1,0:T(8,128)S(1)}, f32[128,256]{1,0:T(8,128)S(1)}, u32[]{:S(2)}, u32[]{:S(2)}) %collective-permute-start.62) | collective-permute-done | bytes 131104 | tf_op jit(solution)/shard_map/ppermute | solution.py:282
  251.0 1.9 collective-permute-done.65.theirs.refs_2_
  258.5 3.3 %collective-permute-done.67 = f32[96,256]{1,0:T(8,128)S(1)} collective-permute-done((f32[96,256]{1,0:T(8,128)S(1)}, f32[96,256]{1,0:T(8,128)S(1)}, u32[]{:S(2)}, u32[]{:S(2)}) %collective-permute-start.67) | collective-permute-done | bytes 98336 | tf_op jit(solution)/shard_map/ppermute | solution.py:282
  261.8 5.0 %collective-permute-start.69 = (f32[96,256]{1,0:T(8,128)S(1)}, f32[96,256]{1,0:T(8,128)S(1)}, u32[]{:S(2)}, u32[]{:S(2)}) collective-permute-start(f32[96,256]{1,0:T(8,128)S(1)} %fusion.5), channel_id=1, source_target_pairs={{0,8},{2,10},{4,12},{6,14},{8,0},{10,2},{12,4},{14,6},{16,24},{18,... | collective-permute-start | bytes 294920 | tf_op jit(solution)/shard_map/ppermute | solution.py:282
  266.9 2.4 collective-permute-start.71
  270.2 5.6 %collective-permute-done.70 = f32[96,256]{1,0:T(8,128)S(1)} collective-permute-done((f32[96,256]{1,0:T(8,128)S(1)}, f32[96,256]{1,0:T(8,128)S(1)}, u32[]{:S(2)}, u32[]{:S(2)}) %collective-permute-start.70) | collective-permute-done | bytes 98336 | tf_op jit(solution)/shard_map/ppermute | solution.py:282
  279.4 2.1 collective-permute-done.72
  285.3 12.5 %shard_map.76 = f32[512,256]{1,0:T(8,128)} custom-call(s32[1]{0:T(128)} %bitcast.core.refs_0_, f32[256,512]{1,0:T(8,128)S(1)} %get-tuple-element.92.mine.refs_1_, f32[256,512]{1,0:T(8,128)S(1)} %collective-permute-done.65.theirs.refs_2_, f32[384,256]{1,0:T(8,128)S(1)} %pad_maximum_fusion.9.refs_3_, f32[384,256]{1,0:T(8,128)S(1)} %collective-permute-done.75.refs_4_), custom_call_target="tpu_custom_call" | custom-call | flops 17179869184 | bytes 2359300 | tf_op jit(solution)/shard_map/pallas_call | solution.py:38
  (164 shorter events, 93.1 us)
Async XLA Ops:
  1.9 10.5 %collective-permute-start.1 = (bf16[2,256,256]{2,1,0:T(8,128)(2,1)S(1)}, bf16[2,256,256]{2,1,0:T(8,128)(2,1)S(1)}, u32[]{:S(2)}, u32[]{:S(2)}) collective-permute-start(bf16[2,256,256]{2,1,0:T(8,128)(2,1)S(1)} %get-tuple-element.49.refs_0_), channel_id=1, source_target_pairs={{0,8},{2,10},{4,12},{6,14},{8,16},{10,18},{12,20},{14,22},{16,24},... | collective-permute-start | bytes 786440 | tf_op jit(solution)/shard_map/ppermute | solution.py:287
  6.8 7.8 %collective-permute-start.2 = (bf16[2,256,256]{2,1,0:T(8,128)(2,1)S(1)}, bf16[2,256,256]{2,1,0:T(8,128)(2,1)S(1)}, u32[]{:S(2)}, u32[]{:S(2)}) collective-permute-start(bf16[2,256,256]{2,1,0:T(8,128)(2,1)S(1)} %get-tuple-element.49.refs_0_), channel_id=1, source_target_pairs={{0,2},{2,0},{4,6},{6,4},{8,10},{10,8},{12,14},{14,12},{16,18},{18,... | collective-permute-start | bytes 786440 | tf_op jit(solution)/shard_map/ppermute | solution.py:282
  8.4 10.2 %collective-permute-start.3 = (bf16[2,256,256]{2,1,0:T(8,128)(2,1)S(1)}, bf16[2,256,256]{2,1,0:T(8,128)(2,1)S(1)}, u32[]{:S(2)}, u32[]{:S(2)}) collective-permute-start(bf16[2,256,256]{2,1,0:T(8,128)(2,1)S(1)} %get-tuple-element.49.refs_0_), channel_id=1, source_target_pairs={{0,4},{2,6},{8,12},{10,14},{4,16},{6,18},{16,20},{18,22},{12,24},{... | collective-permute-start | bytes 786440 | tf_op jit(solution)/shard_map/ppermute | solution.py:293
  14.7 6.9 %collective-permute-start.4 = (bf16[2,256,256]{2,1,0:T(8,128)(2,1)S(1)}, bf16[2,256,256]{2,1,0:T(8,128)(2,1)S(1)}, u32[]{:S(2)}, u32[]{:S(2)}) collective-permute-start(bf16[2,256,256]{2,1,0:T(8,128)(2,1)S(1)} %collective-permute-done.1.refs_2_), channel_id=1, source_target_pairs={{0,2},{2,0},{4,6},{6,4},{8,10},{10,8},{12,14},{14,12},{16,18},{18,... | collective-permute-start | bytes 786440 | tf_op jit(solution)/shard_map/ppermute | solution.py:282
  18.6 12.0 %collective-permute-start.8 = (bf16[6,256,256]{2,1,0:T(8,128)(2,1)}, bf16[6,256,256]{2,1,0:T(8,128)(2,1)}, u32[]{:S(2)}, u32[]{:S(2)}) collective-permute-start(bf16[6,256,256]{2,1,0:T(8,128)(2,1)} %pad_maximum_fusion), channel_id=1, source_target_pairs={{0,1},{1,0},{2,3},{3,2},{4,5},{5,4},{6,7},{7,6},{8,9},{9,8},{10,11... | collective-permute-start | bytes 2359304 | tf_op jit(solution)/shard_map/ppermute | solution.py:278
  38.7 12.1 %collective-permute-start.11 = (bf16[2,256,256]{2,1,0:T(8,128)(2,1)}, bf16[2,256,256]{2,1,0:T(8,128)(2,1)S(1)}, u32[]{:S(2)}, u32[]{:S(2)}) collective-permute-start(bf16[2,256,256]{2,1,0:T(8,128)(2,1)} %get-tuple-element.58), channel_id=1, source_target_pairs={{0,4},{2,6},{4,0},{6,2},{8,12},{10,14},{12,8},{14,10},{16,20},{18,... | collective-permute-start | bytes 786440 | tf_op jit(solution)/shard_map/ppermute | solution.py:282
  43.6 9.4 %collective-permute-start.12 = (bf16[2,256,256]{2,1,0:T(8,128)(2,1)}, bf16[2,256,256]{2,1,0:T(8,128)(2,1)S(1)}, u32[]{:S(2)}, u32[]{:S(2)}) collective-permute-start(bf16[2,256,256]{2,1,0:T(8,128)(2,1)} %get-tuple-element.59), channel_id=1, source_target_pairs={{0,2},{2,0},{4,6},{6,4},{8,10},{10,8},{12,14},{14,12},{16,18},{18,... | collective-permute-start | bytes 786440 | tf_op jit(solution)/shard_map/ppermute | solution.py:282
  46.1 9.7 %collective-permute-start.18 = (f32[128,256]{1,0:T(8,128)S(1)}, f32[128,256]{1,0:T(8,128)S(1)}, u32[]{:S(2)}, u32[]{:S(2)}) collective-permute-start(f32[128,256]{1,0:T(8,128)S(1)} %get-tuple-element.105), channel_id=1, source_target_pairs={{0,2},{2,0},{4,6},{6,4},{8,10},{10,8},{12,14},{14,12},{16,18},{18,... | collective-permute-start | bytes 393224 | tf_op jit(solution)/shard_map/ppermute | solution.py:282
  46.7 9.1 %collective-permute-start.19 = (f32[128,256]{1,0:T(8,128)S(1)}, f32[128,256]{1,0:T(8,128)S(1)}, u32[]{:S(2)}, u32[]{:S(2)}) collective-permute-start(f32[128,256]{1,0:T(8,128)S(1)} %get-tuple-element.107), channel_id=1, source_target_pairs={{0,4},{2,6},{4,0},{6,2},{8,12},{10,14},{12,8},{14,10},{16,20},{18,... | collective-permute-start | bytes 393224 | tf_op jit(solution)/shard_map/ppermute | solution.py:282
  46.7 11.3 %collective-permute-start.20 = (f32[128,256]{1,0:T(8,128)S(1)}, f32[128,256]{1,0:T(8,128)S(1)}, u32[]{:S(2)}, u32[]{:S(2)}) collective-permute-start(f32[128,256]{1,0:T(8,128)S(1)} %get-tuple-element.106), channel_id=1, source_target_pairs={{0,6},{2,4},{4,2},{6,0},{8,14},{10,12},{12,10},{14,8},{16,22},{18,... | collective-permute-start | bytes 393224 | tf_op jit(solution)/shard_map/ppermute | solution.py:282
  50.9 28.8 %collective-permute-start.16 = (bf16[2,256,256]{2,1,0:T(8,128)(2,1)}, bf16[2,256,256]{2,1,0:T(8,128)(2,1)S(1)}, u32[]{:S(2)}, u32[]{:S(2)}) collective-permute-start(bf16[2,256,256]{2,1,0:T(8,128)(2,1)} %copy-done.1), channel_id=1, source_target_pairs={{0,4},{2,6},{4,0},{6,2},{8,12},{10,14},{12,8},{14,10},{16,20},{18,... | collective-permute-start | bytes 786440 | tf_op jit(solution)/shard_map/ppermute | solution.py:282
  54.1 9.0 %collective-permute-start.13 = (bf16[2,256,256]{2,1,0:T(8,128)(2,1)S(1)}, bf16[2,256,256]{2,1,0:T(8,128)(2,1)S(1)}, u32[]{:S(2)}, u32[]{:S(2)}) collective-permute-start(bf16[2,256,256]{2,1,0:T(8,128)(2,1)S(1)} %add_convert_fusion.5), channel_id=1, source_target_pairs={{0,2},{2,0},{4,6},{6,4},{8,10},{10,8},{12,14},{14,12},{16,18},{18,... | collective-permute-start | bytes 786440 | tf_op jit(solution)/shard_map/ppermute | solution.py:282
  60.1 32.7 %collective-permute-start.15 = (bf16[2,256,256]{2,1,0:T(8,128)(2,1)S(1)}, bf16[2,256,256]{2,1,0:T(8,128)(2,1)S(1)}, u32[]{:S(2)}, u32[]{:S(2)}) collective-permute-start(bf16[2,256,256]{2,1,0:T(8,128)(2,1)S(1)} %add_convert_fusion.4), channel_id=1, source_target_pairs={{4,0},{6,2},{12,8},{14,10},{16,4},{18,6},{20,16},{22,18},{24,12},{... | collective-permute-start | bytes 786440 | tf_op jit(solution)/shard_map/ppermute | solution.py:293
  63.1 19.2 %collective-permute-start.21 = (f32[128,256]{1,0:T(8,128)S(1)}, f32[128,256]{1,0:T(8,128)S(1)}, u32[]{:S(2)}, u32[]{:S(2)}) collective-permute-start(f32[128,256]{1,0:T(8,128)S(1)} %fusion.3), channel_id=1, source_target_pairs={{0,8},{2,10},{4,12},{6,14},{8,0},{10,2},{12,4},{14,6},{16,24},{18,... | collective-permute-start | bytes 393224 | tf_op jit(solution)/shard_map/ppermute | solution.py:282
  70.0 22.7 %collective-permute-start.22 = (f32[128,256]{1,0:T(8,128)S(1)}, f32[128,256]{1,0:T(8,128)S(1)}, u32[]{:S(2)}, u32[]{:S(2)}) collective-permute-start(f32[128,256]{1,0:T(8,128)S(1)} %fusion.3), channel_id=1, source_target_pairs={{0,16},{2,18},{4,20},{6,22},{8,24},{10,26},{12,28},{14,30},{16,0},... | collective-permute-start | bytes 393224 | tf_op jit(solution)/shard_map/ppermute | solution.py:282
  78.1 14.6 %collective-permute-start.23 = (f32[128,256]{1,0:T(8,128)S(1)}, f32[128,256]{1,0:T(8,128)S(1)}, u32[]{:S(2)}, u32[]{:S(2)}) collective-permute-start(f32[128,256]{1,0:T(8,128)S(1)} %fusion.3), channel_id=1, source_target_pairs={{0,24},{2,26},{4,28},{6,30},{8,16},{10,18},{12,20},{14,22},{16,8},... | collective-permute-start | bytes 393224 | tf_op jit(solution)/shard_map/ppermute | solution.py:282
  80.8 14.6 %collective-permute-start.17 = (bf16[2,256,256]{2,1,0:T(8,128)(2,1)S(1)}, bf16[2,256,256]{2,1,0:T(8,128)(2,1)S(1)}, u32[]{:S(2)}, u32[]{:S(2)}) collective-permute-start(bf16[2,256,256]{2,1,0:T(8,128)(2,1)S(1)} %add_convert_fusion.3), channel_id=1, source_target_pairs={{8,0},{10,2},{12,4},{14,6},{16,8},{18,10},{20,12},{22,14},{24,16},... | collective-permute-start | bytes 786440 | tf_op jit(solution)/shard_map/ppermute | solution.py:287
  82.2 13.1 %collective-permute-start.14 = (bf16[2,256,256]{2,1,0:T(8,128)(2,1)S(1)}, bf16[2,256,256]{2,1,0:T(8,128)(2,1)S(1)}, u32[]{:S(2)}, u32[]{:S(2)}) collective-permute-start(bf16[2,256,256]{2,1,0:T(8,128)(2,1)S(1)} %get-tuple-element.61), channel_id=1, source_target_pairs={{0,2},{2,0},{4,6},{6,4},{8,10},{10,8},{12,14},{14,12},{16,18},{18,... | collective-permute-start | bytes 786440 | tf_op jit(solution)/shard_map/ppermute | solution.py:282
  92.7 10.8 %collective-permute-start = (f32[256,512]{1,0:T(8,128)S(1)}, f32[256,512]{1,0:T(8,128)S(1)}, u32[]{:S(2)}, u32[]{:S(2)}) collective-permute-start(f32[256,512]{1,0:T(8,128)S(1)} %get-tuple-element.48.refs_0_), channel_id=1, source_target_pairs={{0,1},{1,0},{2,3},{3,2},{4,5},{5,4},{6,7},{7,6},{8,9},{9,8},{10,11... | collective-permute-start | bytes 1572872 | tf_op jit(solution)/shard_map/ppermute | solution.py:278
  95.4 8.1 %collective-permute-start.25 = (f32[128,256]{1,0:T(8,128)S(1)}, f32[128,256]{1,0:T(8,128)S(1)}, u32[]{:S(2)}, u32[]{:S(2)}) collective-permute-start(f32[128,256]{1,0:T(8,128)S(1)} %add_add_fusion.1), channel_id=1, source_target_pairs={{0,4},{2,6},{4,0},{6,2},{8,12},{10,14},{12,8},{14,10},{16,20},{18,... | collective-permute-start | bytes 393224 | tf_op jit(solution)/shard_map/ppermute | solution.py:282
  114.5 10.0 %collective-permute-start.31 = (f32[96,256]{1,0:T(8,128)S(1)}, f32[96,256]{1,0:T(8,128)S(1)}, u32[]{:S(2)}, u32[]{:S(2)}) collective-permute-start(f32[96,256]{1,0:T(8,128)S(1)} %fusion.7), channel_id=1, source_target_pairs={{0,8},{2,10},{4,12},{6,14},{8,0},{10,2},{12,4},{14,6},{16,24},{18,... | collective-permute-start | bytes 294920 | tf_op jit(solution)/shard_map/ppermute | solution.py:282
  120.4 8.9 %collective-permute-start.32 = (f32[96,256]{1,0:T(8,128)S(1)}, f32[96,256]{1,0:T(8,128)S(1)}, u32[]{:S(2)}, u32[]{:S(2)}) collective-permute-start(f32[96,256]{1,0:T(8,128)S(1)} %fusion.7), channel_id=1, source_target_pairs={{0,16},{2,18},{4,20},{6,22},{8,24},{10,26},{12,28},{14,30},{16,0},... | collective-permute-start | bytes 294920 | tf_op jit(solution)/shard_map/ppermute | solution.py:282
  120.4 8.9 %collective-permute-start.33 = (f32[96,256]{1,0:T(8,128)S(1)}, f32[96,256]{1,0:T(8,128)S(1)}, u32[]{:S(2)}, u32[]{:S(2)}) collective-permute-start(f32[96,256]{1,0:T(8,128)S(1)} %fusion.7), channel_id=1, source_target_pairs={{0,24},{2,26},{4,28},{6,30},{8,16},{10,18},{12,20},{14,22},{16,8},... | collective-permute-start | bytes 294920 | tf_op jit(solution)/shard_map/ppermute | solution.py:282
  153.2 9.7 %collective-permute-start.39 = (bf16[2,256,256]{2,1,0:T(8,128)(2,1)S(1)}, bf16[2,256,256]{2,1,0:T(8,128)(2,1)S(1)}, u32[]{:S(2)}, u32[]{:S(2)}) collective-permute-start(bf16[2,256,256]{2,1,0:T(8,128)(2,1)S(1)} %get-tuple-element.71.refs_0_), channel_id=1, source_target_pairs={{0,8},{2,10},{4,12},{6,14},{8,16},{10,18},{12,20},{14,22},{16,24},... | collective-permute-start | bytes 786440 | tf_op jit(solution)/shard_map/ppermute | solution.py:287
  157.0 8.1 %collective-permute-start.40 = (bf16[2,256,256]{2,1,0:T(8,128)(2,1)S(1)}, bf16[2,256,256]{2,1,0:T(8,128)(2,1)S(1)}, u32[]{:S(2)}, u32[]{:S(2)}) collective-permute-start(bf16[2,256,256]{2,1,0:T(8,128)(2,1)S(1)} %get-tuple-element.71.refs_0_), channel_id=1, source_target_pairs={{0,2},{2,0},{4,6},{6,4},{8,10},{10,8},{12,14},{14,12},{16,18},{18,... | collective-permute-start | bytes 786440 | tf_op jit(solution)/shard_map/ppermute | solution.py:282
  157.3 9.6 %collective-permute-start.41 = (bf16[2,256,256]{2,1,0:T(8,128)(2,1)S(1)}, bf16[2,256,256]{2,1,0:T(8,128)(2,1)S(1)}, u32[]{:S(2)}, u32[]{:S(2)}) collective-permute-start(bf16[2,256,256]{2,1,0:T(8,128)(2,1)S(1)} %get-tuple-element.71.refs_0_), channel_id=1, source_target_pairs={{0,4},{2,6},{8,12},{10,14},{4,16},{6,18},{16,20},{18,22},{12,24},{... | collective-permute-start | bytes 786440 | tf_op jit(solution)/shard_map/ppermute | solution.py:293
  165.1 7.2 %collective-permute-start.42 = (bf16[2,256,256]{2,1,0:T(8,128)(2,1)S(1)}, bf16[2,256,256]{2,1,0:T(8,128)(2,1)S(1)}, u32[]{:S(2)}, u32[]{:S(2)}) collective-permute-start(bf16[2,256,256]{2,1,0:T(8,128)(2,1)S(1)} %collective-permute-done.39.refs_2_), channel_id=1, source_target_pairs={{0,2},{2,0},{4,6},{6,4},{8,10},{10,8},{12,14},{14,12},{16,18},{18,... | collective-permute-start | bytes 786440 | tf_op jit(solution)/shard_map/ppermute | solution.py:282
  165.4 7.0 %collective-permute-start.43 = (bf16[2,256,256]{2,1,0:T(8,128)(2,1)S(1)}, bf16[2,256,256]{2,1,0:T(8,128)(2,1)S(1)}, u32[]{:S(2)}, u32[]{:S(2)}) collective-permute-start(bf16[2,256,256]{2,1,0:T(8,128)(2,1)S(1)} %collective-permute-done.39.refs_2_), channel_id=1, source_target_pairs={{0,4},{2,6},{4,0},{6,2},{8,12},{10,14},{12,8},{14,10},{16,20},{18,... | collective-permute-start | bytes 786440 | tf_op jit(solution)/shard_map/ppermute | solution.py:282
  166.8 13.7 %collective-permute-start.46 = (bf16[6,256,256]{2,1,0:T(8,128)(2,1)S(1)}, bf16[6,256,256]{2,1,0:T(8,128)(2,1)S(1)}, u32[]{:S(2)}, u32[]{:S(2)}) collective-permute-start(bf16[6,256,256]{2,1,0:T(8,128)(2,1)S(1)} %pad_maximum_fusion.2), channel_id=1, source_target_pairs={{0,1},{1,0},{2,3},{3,2},{4,5},{5,4},{6,7},{7,6},{8,9},{9,8},{10,11... | collective-permute-start | bytes 2359304 | tf_op jit(solution)/shard_map/ppermute | solution.py:278
  175.0 7.5 %collective-permute-start.47 = (bf16[6,256,256]{2,1,0:T(8,128)(2,1)S(1)}, bf16[6,256,256]{2,1,0:T(8,128)(2,1)S(1)}, u32[]{:S(2)}, u32[]{:S(2)}) collective-permute-start(bf16[6,256,256]{2,1,0:T(8,128)(2,1)S(1)} %pad_maximum_fusion.3), channel_id=1, source_target_pairs={{0,1},{1,0},{2,3},{3,2},{4,5},{5,4},{6,7},{7,6},{8,9},{9,8},{10,11... | collective-permute-start | bytes 2359304 | tf_op jit(solution)/shard_map/ppermute | solution.py:278
  189.0 10.8 %collective-permute-start.49 = (bf16[2,256,256]{2,1,0:T(8,128)(2,1)S(1)}, bf16[2,256,256]{2,1,0:T(8,128)(2,1)S(1)}, u32[]{:S(2)}, u32[]{:S(2)}) collective-permute-start(bf16[2,256,256]{2,1,0:T(8,128)(2,1)S(1)} %get-tuple-element.80), channel_id=1, source_target_pairs={{0,4},{2,6},{4,0},{6,2},{8,12},{10,14},{12,8},{14,10},{16,20},{18,... | collective-permute-start | bytes 786440 | tf_op jit(solution)/shard_map/ppermute | solution.py:282
  192.7 9.2 %collective-permute-start.50 = (bf16[2,256,256]{2,1,0:T(8,128)(2,1)S(1)}, bf16[2,256,256]{2,1,0:T(8,128)(2,1)S(1)}, u32[]{:S(2)}, u32[]{:S(2)}) collective-permute-start(bf16[2,256,256]{2,1,0:T(8,128)(2,1)S(1)} %get-tuple-element.81), channel_id=1, source_target_pairs={{0,2},{2,0},{4,6},{6,4},{8,10},{10,8},{12,14},{14,12},{16,18},{18,... | collective-permute-start | bytes 786440 | tf_op jit(solution)/shard_map/ppermute | solution.py:282
  194.8 9.9 %collective-permute-start.56 = (f32[128,256]{1,0:T(8,128)S(1)}, f32[128,256]{1,0:T(8,128)S(1)}, u32[]{:S(2)}, u32[]{:S(2)}) collective-permute-start(f32[128,256]{1,0:T(8,128)S(1)} %get-tuple-element.98), channel_id=1, source_target_pairs={{0,2},{2,0},{4,6},{6,4},{8,10},{10,8},{12,14},{14,12},{16,18},{18,... | collective-permute-start | bytes 393224 | tf_op jit(solution)/shard_map/ppermute | solution.py:282
  195.9 8.9 %collective-permute-start.57 = (f32[128,256]{1,0:T(8,128)S(1)}, f32[128,256]{1,0:T(8,128)S(1)}, u32[]{:S(2)}, u32[]{:S(2)}) collective-permute-start(f32[128,256]{1,0:T(8,128)S(1)} %get-tuple-element.100), channel_id=1, source_target_pairs={{0,4},{2,6},{4,0},{6,2},{8,12},{10,14},{12,8},{14,10},{16,20},{18,... | collective-permute-start | bytes 393224 | tf_op jit(solution)/shard_map/ppermute | solution.py:282
  196.0 11.1 %collective-permute-start.58 = (f32[128,256]{1,0:T(8,128)S(1)}, f32[128,256]{1,0:T(8,128)S(1)}, u32[]{:S(2)}, u32[]{:S(2)}) collective-permute-start(f32[128,256]{1,0:T(8,128)S(1)} %get-tuple-element.99), channel_id=1, source_target_pairs={{0,6},{2,4},{4,2},{6,0},{8,14},{10,12},{12,10},{14,8},{16,22},{18,... | collective-permute-start | bytes 393224 | tf_op jit(solution)/shard_map/ppermute | solution.py:282
  199.8 26.0 %collective-permute-start.54 = (bf16[2,256,256]{2,1,0:T(8,128)(2,1)S(1)}, bf16[2,256,256]{2,1,0:T(8,128)(2,1)S(1)}, u32[]{:S(2)}, u32[]{:S(2)}) collective-permute-start(bf16[2,256,256]{2,1,0:T(8,128)(2,1)S(1)} %get-tuple-element.88), channel_id=1, source_target_pairs={{0,4},{2,6},{4,0},{6,2},{8,12},{10,14},{12,8},{14,10},{16,20},{18,... | collective-permute-start | bytes 786440 | tf_op jit(solution)/shard_map/ppermute | solution.py:282
  203.0 9.0 %collective-permute-start.51 = (bf16[2,256,256]{2,1,0:T(8,128)(2,1)S(1)}, bf16[2,256,256]{2,1,0:T(8,128)(2,1)S(1)}, u32[]{:S(2)}, u32[]{:S(2)}) collective-permute-start(bf16[2,256,256]{2,1,0:T(8,128)(2,1)S(1)} %add_convert_fusion.2), channel_id=1, source_target_pairs={{0,2},{2,0},{4,6},{6,4},{8,10},{10,8},{12,14},{14,12},{16,18},{18,... | collective-permute-start | bytes 786440 | tf_op jit(solution)/shard_map/ppermute | solution.py:282
  209.1 29.9 %collective-permute-start.53 = (bf16[2,256,256]{2,1,0:T(8,128)(2,1)S(1)}, bf16[2,256,256]{2,1,0:T(8,128)(2,1)S(1)}, u32[]{:S(2)}, u32[]{:S(2)}) collective-permute-start(bf16[2,256,256]{2,1,0:T(8,128)(2,1)S(1)} %add_convert_fusion.1), channel_id=1, source_target_pairs={{4,0},{6,2},{12,8},{14,10},{16,4},{18,6},{20,16},{22,18},{24,12},{... | collective-permute-start | bytes 786440 | tf_op jit(solution)/shard_map/ppermute | solution.py:293
  212.0 16.2 %collective-permute-start.59 = (f32[128,256]{1,0:T(8,128)S(1)}, f32[128,256]{1,0:T(8,128)S(1)}, u32[]{:S(2)}, u32[]{:S(2)}) collective-permute-start(f32[128,256]{1,0:T(8,128)S(1)} %fusion.1), channel_id=1, source_target_pairs={{0,8},{2,10},{4,12},{6,14},{8,0},{10,2},{12,4},{14,6},{16,24},{18,... | collective-permute-start | bytes 393224 | tf_op jit(solution)/shard_map/ppermute | solution.py:282
  215.3 23.7 %collective-permute-start.60 = (f32[128,256]{1,0:T(8,128)S(1)}, f32[128,256]{1,0:T(8,128)S(1)}, u32[]{:S(2)}, u32[]{:S(2)}) collective-permute-start(f32[128,256]{1,0:T(8,128)S(1)} %fusion.1), channel_id=1, source_target_pairs={{0,16},{2,18},{4,20},{6,22},{8,24},{10,26},{12,28},{14,30},{16,0},... | collective-permute-start | bytes 393224 | tf_op jit(solution)/shard_map/ppermute | solution.py:282
  224.4 14.6 %collective-permute-start.61 = (f32[128,256]{1,0:T(8,128)S(1)}, f32[128,256]{1,0:T(8,128)S(1)}, u32[]{:S(2)}, u32[]{:S(2)}) collective-permute-start(f32[128,256]{1,0:T(8,128)S(1)} %fusion.1), channel_id=1, source_target_pairs={{0,24},{2,26},{4,28},{6,30},{8,16},{10,18},{12,20},{14,22},{16,8},... | collective-permute-start | bytes 393224 | tf_op jit(solution)/shard_map/ppermute | solution.py:282
  227.0 15.2 %collective-permute-start.55 = (bf16[2,256,256]{2,1,0:T(8,128)(2,1)S(1)}, bf16[2,256,256]{2,1,0:T(8,128)(2,1)S(1)}, u32[]{:S(2)}, u32[]{:S(2)}) collective-permute-start(bf16[2,256,256]{2,1,0:T(8,128)(2,1)S(1)} %add_convert_fusion), channel_id=1, source_target_pairs={{8,0},{10,2},{12,4},{14,6},{16,8},{18,10},{20,12},{22,14},{24,16},... | collective-permute-start | bytes 786440 | tf_op jit(solution)/shard_map/ppermute | solution.py:287
  228.3 13.9 %collective-permute-start.52 = (bf16[2,256,256]{2,1,0:T(8,128)(2,1)S(1)}, bf16[2,256,256]{2,1,0:T(8,128)(2,1)S(1)}, u32[]{:S(2)}, u32[]{:S(2)}) collective-permute-start(bf16[2,256,256]{2,1,0:T(8,128)(2,1)S(1)} %get-tuple-element.83), channel_id=1, source_target_pairs={{0,2},{2,0},{4,6},{6,4},{8,10},{10,8},{12,14},{14,12},{16,18},{18,... | collective-permute-start | bytes 786440 | tf_op jit(solution)/shard_map/ppermute | solution.py:282
  239.0 10.5 %collective-permute-start.38 = (f32[256,512]{1,0:T(8,128)S(1)}, f32[256,512]{1,0:T(8,128)S(1)}, u32[]{:S(2)}, u32[]{:S(2)}) collective-permute-start(f32[256,512]{1,0:T(8,128)S(1)} %get-tuple-element.70.refs_0_), channel_id=1, source_target_pairs={{0,1},{1,0},{2,3},{3,2},{4,5},{5,4},{6,7},{7,6},{8,9},{9,8},{10,11... | collective-permute-start | bytes 1572872 | tf_op jit(solution)/shard_map/ppermute | solution.py:278
  242.2 7.2 %collective-permute-start.63 = (f32[128,256]{1,0:T(8,128)S(1)}, f32[128,256]{1,0:T(8,128)S(1)}, u32[]{:S(2)}, u32[]{:S(2)}) collective-permute-start(f32[128,256]{1,0:T(8,128)S(1)} %add_add_fusion), channel_id=1, source_target_pairs={{0,4},{2,6},{4,0},{6,2},{8,12},{10,14},{12,8},{14,10},{16,20},{18,... | collective-permute-start | bytes 393224 | tf_op jit(solution)/shard_map/ppermute | solution.py:282
  261.8 8.3 %collective-permute-start.69 = (f32[96,256]{1,0:T(8,128)S(1)}, f32[96,256]{1,0:T(8,128)S(1)}, u32[]{:S(2)}, u32[]{:S(2)}) collective-permute-start(f32[96,256]{1,0:T(8,128)S(1)} %fusion.5), channel_id=1, source_target_pairs={{0,8},{2,10},{4,12},{6,14},{8,0},{10,2},{12,4},{14,6},{16,24},{18,... | collective-permute-start | bytes 294920 | tf_op jit(solution)/shard_map/ppermute | solution.py:282
  266.9 8.9 %collective-permute-start.70 = (f32[96,256]{1,0:T(8,128)S(1)}, f32[96,256]{1,0:T(8,128)S(1)}, u32[]{:S(2)}, u32[]{:S(2)}) collective-permute-start(f32[96,256]{1,0:T(8,128)S(1)} %fusion.5), channel_id=1, source_target_pairs={{0,16},{2,18},{4,20},{6,22},{8,24},{10,26},{12,28},{14,30},{16,0},... | collective-permute-start | bytes 294920 | tf_op jit(solution)/shard_map/ppermute | solution.py:282
  266.9 8.9 %collective-permute-start.71 = (f32[96,256]{1,0:T(8,128)S(1)}, f32[96,256]{1,0:T(8,128)S(1)}, u32[]{:S(2)}, u32[]{:S(2)}) collective-permute-start(f32[96,256]{1,0:T(8,128)S(1)} %fusion.5), channel_id=1, source_target_pairs={{0,24},{2,26},{4,28},{6,30},{8,16},{10,18},{12,20},{14,22},{16,8},... | collective-permute-start | bytes 294920 | tf_op jit(solution)/shard_map/ppermute | solution.py:282
  (37 other events, 237.6 us)

commit v6 on v5

--- a/solution.py
+++ b/solution.py
@@ -11,7 +11,8 @@
 REACH = 4
 
 f32, bf16 = jnp.float32, jnp.bfloat16
-SEGMENT_KINDS = (f32, bf16, f32, f32, f32, bf16, bf16, bf16)
+SEGMENT_KINDS = (f32, f32, f32, f32, f32, bf16, bf16, bf16)
+TILES_VMEM = 24
 VMEM, SMEM = pltpu.VMEM, pltpu.SMEM
 
 
@@ -58,34 +59,35 @@
         chunk[t] = turned.astype(bf16)
 
 
-def apply_kernel(meta, rows, cols, *refs):
-    pieces, blocks, theirs = refs[: 2 * REACH], refs[2 * REACH], refs[2 * REACH + 1 : 2 * REACH + 4]
-    out, (inner, window, total, tiles, piece_sems, tile_sems) = refs[2 * REACH + 4 : -6], refs[-6:]
-    used, start, odd, pair_odd = meta[0], meta[1], meta[2], meta[3]
+def place(tile, meta):
+    start, odd, pair_odd = meta[1], meta[2], meta[3]
+    w = tile - start
+    back = REACH - 1 - w // 4
+    role = jnp.where(back % 2 == 1, 2 + ((back // 2) ^ pair_odd ^ 1), back // 2)
+    return role * 4 + 2 * (((w % 4) // 2) ^ odd) + w % 2
+
+
+def gather(pieces, window, sems):
+    return [pltpu.make_async_copy(piece, window.at[pl.ds(2 * s, 2)], sems.at[s]) for s, piece in enumerate(pieces)]
+
+
+def each_tile(meta, rows, cols, blocks, tiles, sems, ready, product, total):
+    used = meta[0]
     groups = (used + GROUP - 1) // GROUP
 
     def fetch(group):
         at = group % 2
-        return pltpu.make_async_copy(blocks.at[pl.ds(group * GROUP, GROUP)], tiles.at[at], tile_sems.at[at])
+        return pltpu.make_async_copy(blocks.at[pl.ds(group * GROUP, GROUP)], tiles.at[at], sems.at[at])
 
     @pl.when(groups > 0)
     def _():
         fetch(0).start()
 
-    copies = [
-        pltpu.make_async_copy(piece, window.at[pl.ds(2 * s, 2)], piece_sems.at[s]) for s, piece in enumerate(pieces)
-    ]
-    for copy in copies:
+    for copy in ready:
         copy.start()
     total[...] = jnp.zeros_like(total)
-    for copy in copies:
+    for copy in ready:
         copy.wait()
-
-    def place(tile):
-        w = tile - start
-        back = REACH - 1 - w // 4
-        role = jnp.where(back % 2 == 1, 2 + ((back // 2) ^ pair_odd ^ 1), back // 2)
-        return role * 4 + 2 * (((w % 4) // 2) ^ odd) + w % 2
 
     def multiply(group, carry):
         @pl.when(group + 1 < groups)
@@ -97,63 +99,78 @@
         for k in range(GROUP):
             slot = group * GROUP + k
             row, col = rows[slot], cols[slot]
-            weight = jnp.where(row == col, 0.5, 1.0).astype(f32)
-            r, c = place(row), place(col)
             tile = tiles[group % 2, k]
             tile = jnp.where(slot < used, tile, jnp.zeros_like(tile))
-            found.append((r, dot_nt(window[c], tile), weight))
-            found.append((c, dot_nn(window[r], tile), weight))
-        for at, part, weight in found:
-            total[at] += part * weight
+            found.append(product(tile, place(row, meta), place(col, meta)) + (row == col,))
+        for at, part, diagonal in found:
+            total[at] += part * jnp.where(diagonal, 0.5, 1.0).astype(f32)
         return carry
 
     lax.fori_loop(0, groups, multiply, 0)
+
+
+def mirror_kernel(meta, rows, cols, *refs):
+    pieces, blocks, out = refs[:2], refs[2], refs[3:-5]
+    window, total, tiles, piece_sems, tile_sems = refs[-5:]
+
+    def product(tile, row, col):
+        return col, dot_nn(window[row], tile)
+
+    each_tile(meta, rows, cols, blocks, tiles, tile_sems, gather(pieces, window, piece_sems), product, total)
     for s, segment in enumerate(out):
         segment[...] = total[pl.ds(2 * s, 2)].astype(segment.dtype)
 
+
+def direct_kernel(meta, rows, cols, *refs):
+    pieces, blocks = refs[: 2 * REACH], refs[2 * REACH]
+    x_other, cross_other, kept, near, kept_out, near_out, inner = refs[2 * REACH + 1 : -5]
+    window, total, tiles, piece_sems, tile_sems = refs[-5:]
+
+    def product(tile, row, col):
+        return row, dot_nt(window[col], tile)
+
+    each_tile(meta, rows, cols, blocks, tiles, tile_sems, gather(pieces, window, piece_sems), product, total)
+    kept_out[...] = kept[...] + total[pl.ds(0, 2)]
+    near_out[...] = (near[...] + total[pl.ds(2, 2)]).astype(bf16)
     size = inner.shape[1]
     own = jnp.zeros((size, size), f32)
     other = jnp.zeros((size, size), f32)
-    for s in range(2 * REACH):
-        group, start = GROUPED[s]
-        for t in range(2):
-            mine = total[2 * s + t].astype(bf16)
-            own += dot_nt(mine, window[2 * s + t])
-            other += dot_nt(mine, theirs[group][start + t])
-    inner[pl.ds(0, size), :] = own
+    for s in range(4):
+        mine = total[s].astype(bf16)
+        there = x_other[:, pl.ds(s * size, size)].astype(bf16) if s < 2 else cross_other[s - 2]
+        own += dot_nt(mine, window[s])
+        other += dot_nt(mine, there)
+    inner[pl.ds(0, size), :] = own + own.T
     inner[pl.ds(size, size), :] = other
 
 
-def apply_tiles(pieces, others, blocks, rows, cols, meta):
-    size = blocks.shape[1]
-    width = pieces[0].shape[1]
-    segment, window = (2, width, size), (4 * REACH, width, size)
-    out = pl.pallas_call(
-        apply_kernel,
+def tiles_call(kernel, out, meta, blocks, rows, cols, pieces, more, window, total):
+    size, width = blocks.shape[1], pieces[0].shape[1]
+    return pl.pallas_call(
+        kernel,
         in_specs=[pl.BlockSpec(memory_space=SMEM)] * 3
-        + [pl.BlockSpec(memory_space=pl.ANY)] * (2 * REACH)
+        + [pl.BlockSpec(memory_space=pl.ANY)] * len(pieces)
         + [pl.BlockSpec(memory_space=pltpu.HBM)]
-        + [pl.BlockSpec(memory_space=VMEM)] * len(others),
-        out_specs=[pl.BlockSpec(memory_space=VMEM)] * (2 * REACH + 1),
+        + [pl.BlockSpec(memory_space=VMEM)] * len(more),
+        out_specs=[pl.BlockSpec(memory_space=VMEM)] * len(out),
         scratch_shapes=[
-            VMEM(window, bf16),
-            VMEM(window, f32),
+            VMEM((window, width, size), bf16),
+            VMEM((total, width, size), f32),
             VMEM((2, GROUP, size, size), bf16),
-            pltpu.SemaphoreType.DMA((2 * REACH,)),
+            pltpu.SemaphoreType.DMA((len(pieces),)),
             pltpu.SemaphoreType.DMA((2,)),
         ],
-        out_shape=[shape(kind, *segment) for kind in SEGMENT_KINDS] + [shape(f32, 2 * width, size)],
-        compiler_params=pltpu.CompilerParams(vmem_limit_bytes=50 << 20),
-        cost_estimate=pl.CostEstimate(flops=4 << 30, bytes_accessed=16 << 20, transcendentals=0),
-    )(meta, rows, cols, *pieces, blocks, *others)
-    return out[: 2 * REACH : 2], out[1 : 2 * REACH : 2], out[2 * REACH]
-
-
-def update_kernel(rows_total, x, x_other, kept, near, far, two, inner, update, *residual):
+        out_shape=out,
+        compiler_params=pltpu.CompilerParams(vmem_limit_bytes=TILES_VMEM << 20),
+        cost_estimate=pl.CostEstimate(flops=4 << 30, bytes_accessed=12 << 20, transcendentals=0),
+    )(meta, rows, cols, *pieces, blocks, *more)
+
+
+def update_kernel(rows_total, x, x_other, kept, near, far, two, inner, turned, update, *residual):
     width, count = x.shape
     size = kept.shape[2]
     own = split(inner[pl.ds(0, width), :] / rows_total)
-    other = split(inner[pl.ds(width, width), :] / rows_total)
+    other = split((inner[pl.ds(width, width), :] + turned[...].T) / rows_total)
     for t in range(count // size):
         part = pl.ds(t * size, size)
         applied = kept[t] + near[t].astype(f32) + (far[t].astype(f32) + two[t].astype(f32))
@@ -297,21 +314,12 @@
     return lax.optimization_barrier(arrays)
 
 
-def reach(u):
+def reach(u, own_x, done):
     two = shift(u, 2)
     far = stride(u)
-    own_x = flip(u, 1)
-    two, own_x = together(two, own_x)
     two_x, side = flip(two, 1), flip(two, 2)
-    first = swap_cores(jnp.concatenate([u, own_x, two]))
-    far, two_x, side = together(far, two_x, side)
-    second = swap_cores(jnp.concatenate([far, two_x, side]))
-    far_x, side_x = flip(far, 1), flip(two_x, 2)
-    third = swap_cores(jnp.concatenate([far_x, side_x]))
-    return [u, own_x, two, two_x, far, far_x, side, side_x], [first, second, third]
-
-
-GROUPED = ((0, 0), (0, 2), (0, 4), (1, 2), (1, 0), (2, 0), (1, 4), (2, 2))
+    far, two_x, side, _ = together(far, two_x, side, done)
+    return [u, own_x, two, two_x, far, flip(far, 1), side, flip(two_x, 2)]
 
 
 def place_order(parts, place):
@@ -365,21 +373,34 @@
     x, u = call(pack_kernel, [flat, chunk], [vectors])
     for step in range(STEPS):
         last = step == STEPS - 1
-        pieces, others = reach(u)
+        own_x = flip(u, 1)
         x_other = swap_cores(x)
-        same, cross, inner = apply_tiles(pieces, others, blocks, block_row, block_col, meta)
+        cross_other = swap_cores(own_x)
+        table = (meta, blocks, block_row, block_col)
+        segment = (2, width, size)
+        sums = tiles_call(
+            mirror_kernel, [shape(kind, *segment) for kind in SEGMENT_KINDS], *table, [u, own_x], [], 4, 4 * REACH
+        )
+        same, cross = sums[::2], sums[1::2]
+        kept, near, inner = tiles_call(
+            direct_kernel,
+            [shape(f32, *segment), shape(bf16, *segment), shape(f32, 2 * width, width)],
+            *table,
+            reach(u, own_x, cross[3]),
+            [x_other, cross_other, same[0], cross[0]],
+            4 * REACH,
+            4,
+        )
         side_x, far_x, side = flip(cross[3], 2), flip(cross[2], 1), flip(same[3], 2)
-        side_x, far_x = together(side_x, far_x)
         two_out = (cross[1] + side_x.astype(f32)).astype(bf16)
-        far_out = (same[2] + far_x.astype(f32)).astype(bf16)
-        two_x, far = flip(two_out, 1), stride(far_out, True)
-        near, two_x = together(cross[0], two_x)
-        two = (same[1] + (two_x.astype(f32) + side.astype(f32))).astype(bf16)
-        joined = [flip(near, 1), far, shift(two, -2)]
-        inner = summed(inner, [(), (two_x, far_out), joined])
+        two_x, far = flip(two_out, 1), stride((same[2] + far_x.astype(f32)).astype(bf16), True)
+        two = shift((same[1] + (two_x.astype(f32) + side.astype(f32))).astype(bf16), -2)
+        joined = [flip(near, 1), far, two]
+        inner = summed(inner)
+        turned = swap_cores(inner[width:])
         out = [flat] + ([shape(f32, count, width)] if last else [])
         update, *residual = call(
-            lambda *refs: update_kernel(rows_total, *refs), out, [x, x_other, same[0], *joined, inner]
+            lambda *refs: update_kernel(rows_total, *refs), out, [x, x_other, kept, *joined, inner, turned]
         )
         update_other = swap_cores(update)
         (gram,) = call(

time: 299 us -> 275 us (0.920)
  starting transfers between devices: 126 us -> 106 us
  other arithmetic: 11.3 us -> 1.09 us
  local copies, waits for them, and re-layouts: 6.9 us -> 16.7 us
  waiting for transfers between devices: 112 us -> 109 us
    ppermute x56, starting transfers between devices: 105 us -> 85.8 us  [flip(): lax.ppermute(a, 'patch', [(i, i ^ mask) for i in range(lax.axis_size('pat...]
    unnamed x18 -> x36, local copies, waits for them, and re-layouts: 4.72 us -> 16.6 us
    ppermute x4, waiting for transfers between devices: 8.54 us -> 14.5 us  [shift(): lax.ppermute(a, 'patch', [(i - 2 * pairs, i) for i in devices if i - 2 *...]
    ppermute x56, waiting for transfers between devices: 92.7 us -> 87.3 us  [flip(): lax.ppermute(a, 'patch', [(i, i ^ mask) for i in range(lax.axis_size('pat...]
    convert_element_type x4, other arithmetic: 4.48 us -> 0.31 us  [the longest x2 0.18 us: shards(): (same[1] + (two_x.astype(f32) + side.astype(f32))).astype(bf16)]
    ppermute x12 -> x10, waiting for transfers between devices: 10.4 us -> 7.23 us  [swap_cores(): return lax.ppermute(a, 'vec', [(0, 1), (1, 0)])]
    pallas_call x2 -> x4, Pallas kernels: 9.69 us -> 9.97 us  [tiles_call(): pl.pallas_call(kernel, in_specs=[pl.BlockSpec(memory_space=SMEM)] * 3 + [...]
  transfers between devices with their start and end apart: 76 -> 74, of which waited for: 49 -> 39; matrix products, arithmetic and copies ran while one was open for 4% -> 0% of each run, Pallas kernels for 0% -> 4%
where the time goes in v6:
time: 275 us
  waiting for transfers between devices  109 us (40%)
  starting transfers between devices  106 us (39%)
  Pallas kernels  40.4 us (15%)
  local copies, waits for them, and re-layouts  16.7 us (6%)
    ppermute x56, waiting for transfers between devices, flip(): lax.ppermute(a, 'patch', [(i, i ^ mask) for i in range(lax.axis_size('pat...  87.3 us
    ppermute x56, starting transfers between devices, flip(): lax.ppermute(a, 'patch', [(i, i ^ mask) for i in range(lax.axis_size('pat...  85.8 us
    pallas_call x7, Pallas kernels, call(): pl.pallas_call(kernel, out_shape=out, in_specs=[pl.BlockSpec(memory_space...  30.4 us
    unnamed x36, local copies, waits for them, and re-layouts  16.6 us
    ppermute x4, waiting for transfers between devices, shift(): lax.ppermute(a, 'patch', [(i - 2 * pairs, i) for i in devices if i - 2 *...  14.5 us
    pallas_call x4, Pallas kernels, tiles_call(): pl.pallas_call(kernel, in_specs=[pl.BlockSpec(memory_space=SMEM)] * 3 + [...  9.97 us
    ppermute x4, starting transfers between devices, stride(): lax.ppermute(a, 'patch', [(d, s) if back else (s, d) for s, d in route if...  9.84 us
    ppermute x4, starting transfers between devices, shift(): lax.ppermute(a, 'patch', [(i - 2 * pairs, i) for i in devices if i - 2 *...  9.5 us
  transfers between devices with their start and end apart: 74, of which 39 were waited for; matrix products, arithmetic and copies ran while one was open for 0% of the time, Pallas kernels for 4%

profile of v6, /device:TPU:0, one launch (start us, length us, event | category | flops | bytes accessed | tf_op | source)
XLA Modules:
  0.0 274.6 jit_solution(6035014686894491423)
XLA Ops:
  1.9 4.9 %collective-permute-start.2 = (bf16[2,256,256]{2,1,0:T(8,128)(2,1)S(1)}, bf16[2,256,256]{2,1,0:T(8,128)(2,1)S(1)}, u32[]{:S(2)}, u32[]{:S(2)}) collective-permute-start(bf16[2,256,256]{2,1,0:T(8,128)(2,1)S(1)} %get-tuple-element.37.refs_0_), channel_id=1, source_target_pairs={{0,8},{2,10},{4,12},{6,14},{8,16},{10,18},{12,20},{14,22},{16,24},... | collective-permute-start | bytes 786440 | tf_op jit(solution)/shard_map/ppermute | solution.py:304
  8.4 4.2 %collective-permute-start.3 = (bf16[2,256,256]{2,1,0:T(8,128)(2,1)S(1)}, bf16[2,256,256]{2,1,0:T(8,128)(2,1)}, u32[]{:S(2)}, u32[]{:S(2)}) collective-permute-start(bf16[2,256,256]{2,1,0:T(8,128)(2,1)S(1)} %get-tuple-element.37.refs_0_), channel_id=1, source_target_pairs={{0,4},{2,6},{8,12},{10,14},{4,16},{6,18},{16,20},{18,22},{12,24},{... | collective-permute-start | bytes 786440 | tf_op jit(solution)/shard_map/ppermute | solution.py:310
  13.3 1.9 collective-permute-start.5
  16.5 3.4 %copy-done = bf16[64,256,256]{2,1,0:T(8,128)(2,1)S(1)} copy-done((bf16[64,256,256]{2,1,0:T(8,128)(2,1)S(1)}, bf16[64,256,256]{2,1,0:T(8,128)(2,1)}, u32[]{:S(2)}) %copy-start) | copy-done | bytes 8388632
  21.1 2.0 shard_map.69
  27.6 2.0 collective-permute-start.6
  29.6 2.0 collective-permute-start.10
  31.7 5.3 %collective-permute-done.7.refs_7_ = bf16[2,256,256]{2,1,0:T(8,128)(2,1)} collective-permute-done((bf16[2,256,256]{2,1,0:T(8,128)(2,1)}, bf16[2,256,256]{2,1,0:T(8,128)(2,1)}, u32[]{:S(2)}, u32[]{:S(2)}) %collective-permute-start.7) | collective-permute-done | bytes 262176 | tf_op jit(solution)/shard_map/ppermute | solution.py:299
  37.0 3.4 %copy-done.1 = bf16[64,256,256]{2,1,0:T(8,128)(2,1)S(1)} copy-done((bf16[64,256,256]{2,1,0:T(8,128)(2,1)S(1)}, bf16[64,256,256]{2,1,0:T(8,128)(2,1)}, u32[]{:S(2)}) %copy-start.1) | copy-done | bytes 8388632
  43.4 3.7 %shard_map.70 = (f32[2,256,256]{2,1,0:T(8,128)S(1)}, bf16[2,256,256]{2,1,0:T(8,128)(2,1)S(1)}, f32[512,256]{1,0:T(8,128)S(1)}) custom-call(s32[4]{0:T(128)S(1)} %pad_add_fusion.meta, s32[64]{0:T(128)S(1)} %copy-done.9, s32[64]{0:T(128)S(1)} %copy-done.11, bf16[2,256,256]{2,1,0:T(8,128)(2,1)S(1)} %get-tuple-element.37.refs_0_, ...), custom_call_target="tpu_custom_call" | custom-call | flops 4294967296 | bytes 12582912 | tf_op jit(solution)/shard_map/pallas_call | solution.py:149
  48.6 2.2 collective-permute-start.18
  50.9 2.4 collective-permute-done.16
  54.9 2.5 collective-permute-done.18
  57.5 13.7 %collective-permute-start.21 = (f32[128,256]{1,0:T(8,128)S(1)}, f32[128,256]{1,0:T(8,128)S(1)}, u32[]{:S(2)}, u32[]{:S(2)}) collective-permute-start(f32[128,256]{1,0:T(8,128)S(1)} %fusion.3), channel_id=1, source_target_pairs={{0,24},{2,26},{4,28},{6,30},{8,16},{10,18},{12,20},{14,22},{16,8},... | collective-permute-start | bytes 393224 | tf_op jit(solution)/shard_map/ppermute | solution.py:299
  71.1 2.1 collective-permute-start.20
  75.6 6.9 %collective-permute-done.20 = f32[128,256]{1,0:T(8,128)S(1)} collective-permute-done((f32[128,256]{1,0:T(8,128)S(1)}, f32[128,256]{1,0:T(8,128)S(1)}, u32[]{:S(2)}, u32[]{:S(2)}) %collective-permute-start.20) | collective-permute-done | bytes 131104 | tf_op jit(solution)/shard_map/ppermute | solution.py:299
  82.5 2.1 collective-permute-start.24
  86.3 8.1 %collective-permute-done.24 = f32[128,256]{1,0:T(8,128)S(1)} collective-permute-done((f32[128,256]{1,0:T(8,128)S(1)}, f32[128,256]{1,0:T(8,128)S(1)}, u32[]{:S(2)}, u32[]{:S(2)}) %collective-permute-start.24) | collective-permute-done | bytes 131104 | tf_op jit(solution)/shard_map/ppermute | solution.py:299
  96.1 6.7 %collective-permute-done.15.refs_5_ = bf16[2,256,256]{2,1,0:T(8,128)(2,1)S(1)} collective-permute-done((bf16[2,256,256]{2,1,0:T(8,128)(2,1)S(1)}, bf16[2,256,256]{2,1,0:T(8,128)(2,1)S(1)}, u32[]{:S(2)}, u32[]{:S(2)}) %collective-permute-start.15) | collective-permute-done | bytes 262176 | tf_op jit(solution)/shard_map/ppermute | solution.py:304
  107.5 2.2 collective-permute-start.28
  109.7 2.2 collective-permute-done.27
  114.2 2.6 collective-permute-start.32
  118.7 2.4 collective-permute-done.32
  121.1 5.3 %collective-permute-done.31 = f32[96,256]{1,0:T(8,128)S(1)} collective-permute-done((f32[96,256]{1,0:T(8,128)S(1)}, f32[96,256]{1,0:T(8,128)S(1)}, u32[]{:S(2)}, u32[]{:S(2)}) %collective-permute-start.31) | collective-permute-done | bytes 98336 | tf_op jit(solution)/shard_map/ppermute | solution.py:299
  127.5 2.5 collective-permute-start.33
  130.0 2.0 collective-permute-done.35
  135.2 14.3 %shard_map.73 = (f32[256,512]{1,0:T(8,128)S(1)}, bf16[2,256,256]{2,1,0:T(8,128)(2,1)S(1)}) custom-call(s32[1]{0:T(128)} %bitcast.core.refs_0_, f32[256,512]{1,0:T(8,128)S(1)} %shard_map.71.mine.refs_1_, f32[256,512]{1,0:T(8,128)S(1)} %collective-permute-done.26.theirs.refs_2_, f32[384,256]{1,0:T(8,128)S(1)} %pad_maximum_fusion.2.refs_3_, ...), custom_call_target="tpu_custom_call" | custom-call | flops 17179869184 | bytes 2621444 | tf_op jit(solution)/shard_map/pallas_call | solution.py:39
  153.0 2.9 %collective-permute-start.40 = (bf16[2,256,256]{2,1,0:T(8,128)(2,1)S(1)}, bf16[2,256,256]{2,1,0:T(8,128)(2,1)S(1)}, u32[]{:S(2)}, u32[]{:S(2)}) collective-permute-start(bf16[2,256,256]{2,1,0:T(8,128)(2,1)S(1)} %get-tuple-element.53.refs_0_), channel_id=1, source_target_pairs={{0,4},{2,6},{8,12},{10,14},{4,16},{6,18},{16,20},{18,22},{12,24},{... | collective-permute-start | bytes 786440 | tf_op jit(solution)/shard_map/ppermute | solution.py:310
  157.2 2.7 collective-permute-start.42
  160.4 2.0 shard_map.74
  162.4 4.5 %collective-permute-done.42.refs_6_ = bf16[2,256,256]{2,1,0:T(8,128)(2,1)S(1)} collective-permute-done((bf16[2,256,256]{2,1,0:T(8,128)(2,1)S(1)}, bf16[2,256,256]{2,1,0:T(8,128)(2,1)S(1)}, u32[]{:S(2)}, u32[]{:S(2)}) %collective-permute-start.42) | collective-permute-done | bytes 262176 | tf_op jit(solution)/shard_map/ppermute | solution.py:299
  173.4 4.2 %collective-permute-done.44.refs_7_ = bf16[2,256,256]{2,1,0:T(8,128)(2,1)S(1)} collective-permute-done((bf16[2,256,256]{2,1,0:T(8,128)(2,1)S(1)}, bf16[2,256,256]{2,1,0:T(8,128)(2,1)S(1)}, u32[]{:S(2)}, u32[]{:S(2)}) %collective-permute-start.44) | collective-permute-done | bytes 262176 | tf_op jit(solution)/shard_map/ppermute | solution.py:299
  178.5 2.3 shard_map.75
  181.0 2.4 collective-permute-start.55
  184.5 2.5 collective-permute-done.53
  187.7 2.7 collective-permute-done.55
  190.3 2.3 collective-permute-done.54
  192.7 9.7 %collective-permute-start.58 = (f32[128,256]{1,0:T(8,128)S(1)}, f32[128,256]{1,0:T(8,128)S(1)}, u32[]{:S(2)}, u32[]{:S(2)}) collective-permute-start(f32[128,256]{1,0:T(8,128)S(1)} %fusion.1), channel_id=1, source_target_pairs={{0,24},{2,26},{4,28},{6,30},{8,16},{10,18},{12,20},{14,22},{16,8},... | collective-permute-start | bytes 393224 | tf_op jit(solution)/shard_map/ppermute | solution.py:299
  203.1 2.4 collective-permute-done.58
  207.0 5.6 %collective-permute-done.57 = f32[128,256]{1,0:T(8,128)S(1)} collective-permute-done((f32[128,256]{1,0:T(8,128)S(1)}, f32[128,256]{1,0:T(8,128)S(1)}, u32[]{:S(2)}, u32[]{:S(2)}) %collective-permute-start.57) | collective-permute-done | bytes 131104 | tf_op jit(solution)/shard_map/ppermute | solution.py:299
  214.8 2.3 collective-permute-start.59
  217.1 3.5 %collective-permute-done.61 = f32[128,256]{1,0:T(8,128)S(1)} collective-permute-done((f32[128,256]{1,0:T(8,128)S(1)}, f32[128,256]{1,0:T(8,128)S(1)}, u32[]{:S(2)}, u32[]{:S(2)}) %collective-permute-start.61) | collective-permute-done | bytes 131104 | tf_op jit(solution)/shard_map/ppermute | solution.py:299
  222.3 6.6 %collective-permute-done.52.refs_5_ = bf16[2,256,256]{2,1,0:T(8,128)(2,1)S(1)} collective-permute-done((bf16[2,256,256]{2,1,0:T(8,128)(2,1)S(1)}, bf16[2,256,256]{2,1,0:T(8,128)(2,1)S(1)}, u32[]{:S(2)}, u32[]{:S(2)}) %collective-permute-start.52) | collective-permute-done | bytes 262176 | tf_op jit(solution)/shard_map/ppermute | solution.py:304
  236.6 2.2 collective-permute-done.64
  243.5 2.4 collective-permute-start.67
  246.0 3.1 %collective-permute-done.69 = f32[96,256]{1,0:T(8,128)S(1)} collective-permute-done((f32[96,256]{1,0:T(8,128)S(1)}, f32[96,256]{1,0:T(8,128)S(1)}, u32[]{:S(2)}, u32[]{:S(2)}) %collective-permute-start.69) | collective-permute-done | bytes 98336 | tf_op jit(solution)/shard_map/ppermute | solution.py:299
  249.1 2.8 %collective-permute-done.68 = f32[96,256]{1,0:T(8,128)S(1)} collective-permute-done((f32[96,256]{1,0:T(8,128)S(1)}, f32[96,256]{1,0:T(8,128)S(1)}, u32[]{:S(2)}, u32[]{:S(2)}) %collective-permute-start.68) | collective-permute-done | bytes 98336 | tf_op jit(solution)/shard_map/ppermute | solution.py:299
  262.1 12.5 %shard_map.78 = f32[512,256]{1,0:T(8,128)} custom-call(s32[1]{0:T(128)} %bitcast.core.refs_0_, f32[256,512]{1,0:T(8,128)S(1)} %get-tuple-element.68.mine.refs_1_, f32[256,512]{1,0:T(8,128)S(1)} %collective-permute-done.63.theirs.refs_2_, f32[384,256]{1,0:T(8,128)S(1)} %pad_maximum_fusion.3.refs_3_, f32[384,256]{1,0:T(8,128)S(1)} %collective-permute-done.73.refs_4_), custom_call_target="tpu_custom_call" | custom-call | flops 17179869184 | bytes 2359300 | tf_op jit(solution)/shard_map/pallas_call | solution.py:39
  (177 shorter events, 78.3 us)
Async XLA Ops:
  1.9 11.4 %collective-permute-start.2 = (bf16[2,256,256]{2,1,0:T(8,128)(2,1)S(1)}, bf16[2,256,256]{2,1,0:T(8,128)(2,1)S(1)}, u32[]{:S(2)}, u32[]{:S(2)}) collective-permute-start(bf16[2,256,256]{2,1,0:T(8,128)(2,1)S(1)} %get-tuple-element.37.refs_0_), channel_id=1, source_target_pairs={{0,8},{2,10},{4,12},{6,14},{8,16},{10,18},{12,20},{14,22},{16,24},... | collective-permute-start | bytes 786440 | tf_op jit(solution)/shard_map/ppermute | solution.py:304
  6.8 9.6 %collective-permute-start.1 = (bf16[2,256,256]{2,1,0:T(8,128)(2,1)S(1)}, bf16[2,256,256]{2,1,0:T(8,128)(2,1)S(1)}, u32[]{:S(2)}, u32[]{:S(2)}) collective-permute-start(bf16[2,256,256]{2,1,0:T(8,128)(2,1)S(1)} %get-tuple-element.37.refs_0_), channel_id=1, source_target_pairs={{0,2},{2,0},{4,6},{6,4},{8,10},{10,8},{12,14},{14,12},{16,18},{18,... | collective-permute-start | bytes 786440 | tf_op jit(solution)/shard_map/ppermute | solution.py:299
  8.4 18.4 %collective-permute-start.3 = (bf16[2,256,256]{2,1,0:T(8,128)(2,1)S(1)}, bf16[2,256,256]{2,1,0:T(8,128)(2,1)}, u32[]{:S(2)}, u32[]{:S(2)}) collective-permute-start(bf16[2,256,256]{2,1,0:T(8,128)(2,1)S(1)} %get-tuple-element.37.refs_0_), channel_id=1, source_target_pairs={{0,4},{2,6},{8,12},{10,14},{4,16},{6,18},{16,20},{18,22},{12,24},{... | collective-permute-start | bytes 786440 | tf_op jit(solution)/shard_map/ppermute | solution.py:310
  12.5 19.1 %collective-permute-start = (f32[256,512]{1,0:T(8,128)S(1)}, f32[256,512]{1,0:T(8,128)S(1)}, u32[]{:S(2)}, u32[]{:S(2)}) collective-permute-start(f32[256,512]{1,0:T(8,128)S(1)} %get-tuple-element.36.refs_0_), channel_id=1, source_target_pairs={{0,1},{1,0},{2,3},{3,2},{4,5},{5,4},{6,7},{7,6},{8,9},{9,8},{10,11... | collective-permute-start | bytes 1572872 | tf_op jit(solution)/shard_map/ppermute | solution.py:295
  13.3 13.6 %collective-permute-start.5 = (bf16[2,256,256]{2,1,0:T(8,128)(2,1)S(1)}, bf16[2,256,256]{2,1,0:T(8,128)(2,1)S(1)}, u32[]{:S(2)}, u32[]{:S(2)}) collective-permute-start(bf16[2,256,256]{2,1,0:T(8,128)(2,1)S(1)} %collective-permute-done.2.refs_2_), channel_id=1, source_target_pairs={{0,4},{2,6},{4,0},{6,2},{8,12},{10,14},{12,8},{14,10},{16,20},{18,... | collective-permute-start | bytes 786440 | tf_op jit(solution)/shard_map/ppermute | solution.py:299
  15.2 12.4 %collective-permute-start.4 = (bf16[2,256,256]{2,1,0:T(8,128)(2,1)S(1)}, bf16[2,256,256]{2,1,0:T(8,128)(2,1)}, u32[]{:S(2)}, u32[]{:S(2)}) collective-permute-start(bf16[2,256,256]{2,1,0:T(8,128)(2,1)S(1)} %collective-permute-done.2.refs_2_), channel_id=1, source_target_pairs={{0,2},{2,0},{4,6},{6,4},{8,10},{10,8},{12,14},{14,12},{16,18},{18,... | collective-permute-start | bytes 786440 | tf_op jit(solution)/shard_map/ppermute | solution.py:299
  16.4 13.2 %collective-permute-start.8 = (bf16[2,256,256]{2,1,0:T(8,128)(2,1)S(1)}, bf16[2,256,256]{2,1,0:T(8,128)(2,1)}, u32[]{:S(2)}, u32[]{:S(2)}) collective-permute-start(bf16[2,256,256]{2,1,0:T(8,128)(2,1)S(1)} %collective-permute-done.1.refs_1_), channel_id=1, source_target_pairs={{0,1},{1,0},{2,3},{3,2},{4,5},{5,4},{6,7},{7,6},{8,9},{9,8},{10,11... | collective-permute-start | bytes 786440 | tf_op jit(solution)/shard_map/ppermute | solution.py:295
  27.6 9.4 %collective-permute-start.7 = (bf16[2,256,256]{2,1,0:T(8,128)(2,1)}, bf16[2,256,256]{2,1,0:T(8,128)(2,1)}, u32[]{:S(2)}, u32[]{:S(2)}) collective-permute-start(bf16[2,256,256]{2,1,0:T(8,128)(2,1)} %collective-permute-done.4.refs_3_), channel_id=1, source_target_pairs={{0,4},{2,6},{4,0},{6,2},{8,12},{10,14},{12,8},{14,10},{16,20},{18,... | collective-permute-start | bytes 786440 | tf_op jit(solution)/shard_map/ppermute | solution.py:299
  27.6 9.4 %collective-permute-start.6 = (bf16[2,256,256]{2,1,0:T(8,128)(2,1)}, bf16[2,256,256]{2,1,0:T(8,128)(2,1)}, u32[]{:S(2)}, u32[]{:S(2)}) collective-permute-start(bf16[2,256,256]{2,1,0:T(8,128)(2,1)} %collective-permute-done.3.refs_4_), channel_id=1, source_target_pairs={{0,2},{2,0},{4,6},{6,4},{8,10},{10,8},{12,14},{14,12},{16,18},{18,... | collective-permute-start | bytes 786440 | tf_op jit(solution)/shard_map/ppermute | solution.py:299
  29.6 21.2 %collective-permute-start.12 = (bf16[2,256,256]{2,1,0:T(8,128)(2,1)}, bf16[2,256,256]{2,1,0:T(8,128)(2,1)S(1)}, u32[]{:S(2)}, u32[]{:S(2)}) collective-permute-start(bf16[2,256,256]{2,1,0:T(8,128)(2,1)} %copy-done.5), channel_id=1, source_target_pairs={{0,4},{2,6},{4,0},{6,2},{8,12},{10,14},{12,8},{14,10},{16,20},{18,... | collective-permute-start | bytes 786440 | tf_op jit(solution)/shard_map/ppermute | solution.py:299
  29.6 43.6 %collective-permute-start.10 = (bf16[2,256,256]{2,1,0:T(8,128)(2,1)}, bf16[2,256,256]{2,1,0:T(8,128)(2,1)S(1)}, u32[]{:S(2)}, u32[]{:S(2)}) collective-permute-start(bf16[2,256,256]{2,1,0:T(8,128)(2,1)} %copy-done.4), channel_id=1, source_target_pairs={{0,2},{2,0},{4,6},{6,4},{8,10},{10,8},{12,14},{14,12},{16,18},{18,... | collective-permute-start | bytes 786440 | tf_op jit(solution)/shard_map/ppermute | solution.py:299
  31.6 53.0 %collective-permute-start.14 = (bf16[2,256,256]{2,1,0:T(8,128)(2,1)}, bf16[2,256,256]{2,1,0:T(8,128)(2,1)S(1)}, u32[]{:S(2)}, u32[]{:S(2)}) collective-permute-start(bf16[2,256,256]{2,1,0:T(8,128)(2,1)} %copy-done.3), channel_id=1, source_target_pairs={{0,4},{2,6},{4,0},{6,2},{8,12},{10,14},{12,8},{14,10},{16,20},{18,... | collective-permute-start | bytes 786440 | tf_op jit(solution)/shard_map/ppermute | solution.py:299
  48.6 8.9 %collective-permute-start.18 = (f32[128,256]{1,0:T(8,128)S(1)}, f32[128,256]{1,0:T(8,128)S(1)}, u32[]{:S(2)}, u32[]{:S(2)}) collective-permute-start(f32[128,256]{1,0:T(8,128)S(1)} %get-tuple-element.82), channel_id=1, source_target_pairs={{0,6},{2,4},{4,2},{6,0},{8,14},{10,12},{12,10},{14,8},{16,22},{18,... | collective-permute-start | bytes 393224 | tf_op jit(solution)/shard_map/ppermute | solution.py:299
  53.3 31.7 %collective-permute-start.13 = (bf16[2,256,256]{2,1,0:T(8,128)(2,1)S(1)}, bf16[2,256,256]{2,1,0:T(8,128)(2,1)S(1)}, u32[]{:S(2)}, u32[]{:S(2)}) collective-permute-start(bf16[2,256,256]{2,1,0:T(8,128)(2,1)S(1)} %add_convert_fusion.4), channel_id=1, source_target_pairs={{0,2},{2,0},{4,6},{6,4},{8,10},{10,8},{12,14},{14,12},{16,18},{18,... | collective-permute-start | bytes 786440 | tf_op jit(solution)/shard_map/ppermute | solution.py:299
  57.5 16.9 %collective-permute-start.21 = (f32[128,256]{1,0:T(8,128)S(1)}, f32[128,256]{1,0:T(8,128)S(1)}, u32[]{:S(2)}, u32[]{:S(2)}) collective-permute-start(f32[128,256]{1,0:T(8,128)S(1)} %fusion.3), channel_id=1, source_target_pairs={{0,24},{2,26},{4,28},{6,30},{8,16},{10,18},{12,20},{14,22},{16,8},... | collective-permute-start | bytes 393224 | tf_op jit(solution)/shard_map/ppermute | solution.py:299
  71.1 11.4 %collective-permute-start.20 = (f32[128,256]{1,0:T(8,128)S(1)}, f32[128,256]{1,0:T(8,128)S(1)}, u32[]{:S(2)}, u32[]{:S(2)}) collective-permute-start(f32[128,256]{1,0:T(8,128)S(1)} %fusion.3), channel_id=1, source_target_pairs={{0,16},{2,18},{4,20},{6,22},{8,24},{10,26},{12,28},{14,30},{16,0},... | collective-permute-start | bytes 393224 | tf_op jit(solution)/shard_map/ppermute | solution.py:299
  73.2 9.3 %collective-permute-start.19 = (f32[128,256]{1,0:T(8,128)S(1)}, f32[128,256]{1,0:T(8,128)S(1)}, u32[]{:S(2)}, u32[]{:S(2)}) collective-permute-start(f32[128,256]{1,0:T(8,128)S(1)} %fusion.3), channel_id=1, source_target_pairs={{0,8},{2,10},{4,12},{6,14},{8,0},{10,2},{12,4},{14,6},{16,24},{18,... | collective-permute-start | bytes 393224 | tf_op jit(solution)/shard_map/ppermute | solution.py:299
  74.3 21.8 %collective-permute-start.11 = (bf16[2,256,256]{2,1,0:T(8,128)(2,1)S(1)}, bf16[2,256,256]{2,1,0:T(8,128)(2,1)S(1)}, u32[]{:S(2)}, u32[]{:S(2)}) collective-permute-start(bf16[2,256,256]{2,1,0:T(8,128)(2,1)S(1)} %add_convert_fusion.5), channel_id=1, source_target_pairs={{4,0},{6,2},{12,8},{14,10},{16,4},{18,6},{20,16},{22,18},{24,12},{... | collective-permute-start | bytes 786440 | tf_op jit(solution)/shard_map/ppermute | solution.py:310
  82.5 13.6 %collective-permute-start.9 = (bf16[2,256,256]{2,1,0:T(8,128)(2,1)S(1)}, bf16[2,256,256]{2,1,0:T(8,128)(2,1)S(1)}, u32[]{:S(2)}, u32[]{:S(2)}) collective-permute-start(bf16[2,256,256]{2,1,0:T(8,128)(2,1)S(1)} %get-tuple-element.45), channel_id=1, source_target_pairs={{0,2},{2,0},{4,6},{6,4},{8,10},{10,8},{12,14},{14,12},{16,18},{18,... | collective-permute-start | bytes 786440 | tf_op jit(solution)/shard_map/ppermute | solution.py:299
  82.5 11.9 %collective-permute-start.24 = (f32[128,256]{1,0:T(8,128)S(1)}, f32[128,256]{1,0:T(8,128)S(1)}, u32[]{:S(2)}, u32[]{:S(2)}) collective-permute-start(f32[128,256]{1,0:T(8,128)S(1)} %add_add_fusion.1), channel_id=1, source_target_pairs={{0,2},{2,0},{4,6},{6,4},{8,10},{10,8},{12,14},{14,12},{16,18},{18,... | collective-permute-start | bytes 393224 | tf_op jit(solution)/shard_map/ppermute | solution.py:299
  84.6 11.2 %collective-permute-start.23 = (f32[128,256]{1,0:T(8,128)S(1)}, f32[128,256]{1,0:T(8,128)S(1)}, u32[]{:S(2)}, u32[]{:S(2)}) collective-permute-start(f32[128,256]{1,0:T(8,128)S(1)} %add_add_fusion.1), channel_id=1, source_target_pairs={{0,4},{2,6},{4,0},{6,2},{8,12},{10,14},{12,8},{14,10},{16,20},{18,... | collective-permute-start | bytes 393224 | tf_op jit(solution)/shard_map/ppermute | solution.py:299
  84.9 10.9 %collective-permute-start.22 = (f32[128,256]{1,0:T(8,128)S(1)}, f32[128,256]{1,0:T(8,128)S(1)}, u32[]{:S(2)}, u32[]{:S(2)}) collective-permute-start(f32[128,256]{1,0:T(8,128)S(1)} %add_add_fusion.1), channel_id=1, source_target_pairs={{0,6},{2,4},{4,2},{6,0},{8,14},{10,12},{12,10},{14,8},{16,22},{18,... | collective-permute-start | bytes 393224 | tf_op jit(solution)/shard_map/ppermute | solution.py:299
  94.4 8.4 %collective-permute-start.15 = (bf16[2,256,256]{2,1,0:T(8,128)(2,1)S(1)}, bf16[2,256,256]{2,1,0:T(8,128)(2,1)S(1)}, u32[]{:S(2)}, u32[]{:S(2)}) collective-permute-start(bf16[2,256,256]{2,1,0:T(8,128)(2,1)S(1)} %add_convert_fusion.3), channel_id=1, source_target_pairs={{8,0},{10,2},{12,4},{14,6},{16,8},{18,10},{20,12},{22,14},{24,16},... | collective-permute-start | bytes 786440 | tf_op jit(solution)/shard_map/ppermute | solution.py:304
  116.8 9.7 %collective-permute-start.31 = (f32[96,256]{1,0:T(8,128)S(1)}, f32[96,256]{1,0:T(8,128)S(1)}, u32[]{:S(2)}, u32[]{:S(2)}) collective-permute-start(f32[96,256]{1,0:T(8,128)S(1)} %fusion.7), channel_id=1, source_target_pairs={{0,16},{2,18},{4,20},{6,22},{8,24},{10,26},{12,28},{14,30},{16,0},... | collective-permute-start | bytes 294920 | tf_op jit(solution)/shard_map/ppermute | solution.py:299
  117.9 8.6 %collective-permute-start.30 = (f32[96,256]{1,0:T(8,128)S(1)}, f32[96,256]{1,0:T(8,128)S(1)}, u32[]{:S(2)}, u32[]{:S(2)}) collective-permute-start(f32[96,256]{1,0:T(8,128)S(1)} %fusion.7), channel_id=1, source_target_pairs={{0,8},{2,10},{4,12},{6,14},{8,0},{10,2},{12,4},{14,6},{16,24},{18,... | collective-permute-start | bytes 294920 | tf_op jit(solution)/shard_map/ppermute | solution.py:299
  149.5 7.6 %collective-permute-start.39 = (bf16[2,256,256]{2,1,0:T(8,128)(2,1)S(1)}, bf16[2,256,256]{2,1,0:T(8,128)(2,1)S(1)}, u32[]{:S(2)}, u32[]{:S(2)}) collective-permute-start(bf16[2,256,256]{2,1,0:T(8,128)(2,1)S(1)} %get-tuple-element.53.refs_0_), channel_id=1, source_target_pairs={{0,8},{2,10},{4,12},{6,14},{8,16},{10,18},{12,20},{14,22},{16,24},... | collective-permute-start | bytes 786440 | tf_op jit(solution)/shard_map/ppermute | solution.py:304
  151.3 9.0 %collective-permute-start.38 = (bf16[2,256,256]{2,1,0:T(8,128)(2,1)S(1)}, bf16[2,256,256]{2,1,0:T(8,128)(2,1)S(1)}, u32[]{:S(2)}, u32[]{:S(2)}) collective-permute-start(bf16[2,256,256]{2,1,0:T(8,128)(2,1)S(1)} %get-tuple-element.53.refs_0_), channel_id=1, source_target_pairs={{0,2},{2,0},{4,6},{6,4},{8,10},{10,8},{12,14},{14,12},{16,18},{18,... | collective-permute-start | bytes 786440 | tf_op jit(solution)/shard_map/ppermute | solution.py:299
  153.0 9.4 %collective-permute-start.40 = (bf16[2,256,256]{2,1,0:T(8,128)(2,1)S(1)}, bf16[2,256,256]{2,1,0:T(8,128)(2,1)S(1)}, u32[]{:S(2)}, u32[]{:S(2)}) collective-permute-start(bf16[2,256,256]{2,1,0:T(8,128)(2,1)S(1)} %get-tuple-element.53.refs_0_), channel_id=1, source_target_pairs={{0,4},{2,6},{8,12},{10,14},{4,16},{6,18},{16,20},{18,22},{12,24},{... | collective-permute-start | bytes 786440 | tf_op jit(solution)/shard_map/ppermute | solution.py:310
  155.9 16.4 %collective-permute-start.37 = (f32[256,512]{1,0:T(8,128)S(1)}, f32[256,512]{1,0:T(8,128)S(1)}, u32[]{:S(2)}, u32[]{:S(2)}) collective-permute-start(f32[256,512]{1,0:T(8,128)S(1)} %get-tuple-element.52.refs_0_), channel_id=1, source_target_pairs={{0,1},{1,0},{2,3},{3,2},{4,5},{5,4},{6,7},{7,6},{8,9},{9,8},{10,11... | collective-permute-start | bytes 1572872 | tf_op jit(solution)/shard_map/ppermute | solution.py:295
  157.2 9.7 %collective-permute-start.42 = (bf16[2,256,256]{2,1,0:T(8,128)(2,1)S(1)}, bf16[2,256,256]{2,1,0:T(8,128)(2,1)S(1)}, u32[]{:S(2)}, u32[]{:S(2)}) collective-permute-start(bf16[2,256,256]{2,1,0:T(8,128)(2,1)S(1)} %collective-permute-done.39.refs_2_), channel_id=1, source_target_pairs={{0,4},{2,6},{4,0},{6,2},{8,12},{10,14},{12,8},{14,10},{16,20},{18,... | collective-permute-start | bytes 786440 | tf_op jit(solution)/shard_map/ppermute | solution.py:299
  159.9 8.4 %collective-permute-start.41 = (bf16[2,256,256]{2,1,0:T(8,128)(2,1)S(1)}, bf16[2,256,256]{2,1,0:T(8,128)(2,1)S(1)}, u32[]{:S(2)}, u32[]{:S(2)}) collective-permute-start(bf16[2,256,256]{2,1,0:T(8,128)(2,1)S(1)} %collective-permute-done.39.refs_2_), channel_id=1, source_target_pairs={{0,2},{2,0},{4,6},{6,4},{8,10},{10,8},{12,14},{14,12},{16,18},{18,... | collective-permute-start | bytes 786440 | tf_op jit(solution)/shard_map/ppermute | solution.py:299
  160.4 10.4 %collective-permute-start.45 = (bf16[2,256,256]{2,1,0:T(8,128)(2,1)S(1)}, bf16[2,256,256]{2,1,0:T(8,128)(2,1)S(1)}, u32[]{:S(2)}, u32[]{:S(2)}) collective-permute-start(bf16[2,256,256]{2,1,0:T(8,128)(2,1)S(1)} %collective-permute-done.38.refs_1_), channel_id=1, source_target_pairs={{0,1},{1,0},{2,3},{3,2},{4,5},{5,4},{6,7},{7,6},{8,9},{9,8},{10,11... | collective-permute-start | bytes 786440 | tf_op jit(solution)/shard_map/ppermute | solution.py:295
  168.3 9.3 %collective-permute-start.44 = (bf16[2,256,256]{2,1,0:T(8,128)(2,1)S(1)}, bf16[2,256,256]{2,1,0:T(8,128)(2,1)S(1)}, u32[]{:S(2)}, u32[]{:S(2)}) collective-permute-start(bf16[2,256,256]{2,1,0:T(8,128)(2,1)S(1)} %collective-permute-done.41.refs_3_), channel_id=1, source_target_pairs={{0,4},{2,6},{4,0},{6,2},{8,12},{10,14},{12,8},{14,10},{16,20},{18,... | collective-permute-start | bytes 786440 | tf_op jit(solution)/shard_map/ppermute | solution.py:299
  169.3 9.2 %collective-permute-start.43 = (bf16[2,256,256]{2,1,0:T(8,128)(2,1)S(1)}, bf16[2,256,256]{2,1,0:T(8,128)(2,1)S(1)}, u32[]{:S(2)}, u32[]{:S(2)}) collective-permute-start(bf16[2,256,256]{2,1,0:T(8,128)(2,1)S(1)} %collective-permute-done.40.refs_4_), channel_id=1, source_target_pairs={{0,2},{2,0},{4,6},{6,4},{8,10},{10,8},{12,14},{14,12},{16,18},{18,... | collective-permute-start | bytes 786440 | tf_op jit(solution)/shard_map/ppermute | solution.py:299
  170.1 13.4 %collective-permute-start.49 = (bf16[2,256,256]{2,1,0:T(8,128)(2,1)S(1)}, bf16[2,256,256]{2,1,0:T(8,128)(2,1)S(1)}, u32[]{:S(2)}, u32[]{:S(2)}) collective-permute-start(bf16[2,256,256]{2,1,0:T(8,128)(2,1)S(1)} %get-tuple-element.54), channel_id=1, source_target_pairs={{0,4},{2,6},{4,0},{6,2},{8,12},{10,14},{12,8},{14,10},{16,20},{18,... | collective-permute-start | bytes 786440 | tf_op jit(solution)/shard_map/ppermute | solution.py:299
  170.8 31.6 %collective-permute-start.47 = (bf16[2,256,256]{2,1,0:T(8,128)(2,1)S(1)}, bf16[2,256,256]{2,1,0:T(8,128)(2,1)S(1)}, u32[]{:S(2)}, u32[]{:S(2)}) collective-permute-start(bf16[2,256,256]{2,1,0:T(8,128)(2,1)S(1)} %get-tuple-element.63), channel_id=1, source_target_pairs={{0,2},{2,0},{4,6},{6,4},{8,10},{10,8},{12,14},{14,12},{16,18},{18,... | collective-permute-start | bytes 786440 | tf_op jit(solution)/shard_map/ppermute | solution.py:299
  172.3 42.4 %collective-permute-start.51 = (bf16[2,256,256]{2,1,0:T(8,128)(2,1)S(1)}, bf16[2,256,256]{2,1,0:T(8,128)(2,1)S(1)}, u32[]{:S(2)}, u32[]{:S(2)}) collective-permute-start(bf16[2,256,256]{2,1,0:T(8,128)(2,1)S(1)} %get-tuple-element.66), channel_id=1, source_target_pairs={{0,4},{2,6},{4,0},{6,2},{8,12},{10,14},{12,8},{14,10},{16,20},{18,... | collective-permute-start | bytes 786440 | tf_op jit(solution)/shard_map/ppermute | solution.py:299
  181.0 9.3 %collective-permute-start.55 = (f32[128,256]{1,0:T(8,128)S(1)}, f32[128,256]{1,0:T(8,128)S(1)}, u32[]{:S(2)}, u32[]{:S(2)}) collective-permute-start(f32[128,256]{1,0:T(8,128)S(1)} %get-tuple-element.75), channel_id=1, source_target_pairs={{0,6},{2,4},{4,2},{6,0},{8,14},{10,12},{12,10},{14,8},{16,22},{18,... | collective-permute-start | bytes 393224 | tf_op jit(solution)/shard_map/ppermute | solution.py:299
  183.4 9.2 %collective-permute-start.54 = (f32[128,256]{1,0:T(8,128)S(1)}, f32[128,256]{1,0:T(8,128)S(1)}, u32[]{:S(2)}, u32[]{:S(2)}) collective-permute-start(f32[128,256]{1,0:T(8,128)S(1)} %get-tuple-element.76), channel_id=1, source_target_pairs={{0,4},{2,6},{4,0},{6,2},{8,12},{10,14},{12,8},{14,10},{16,20},{18,... | collective-permute-start | bytes 393224 | tf_op jit(solution)/shard_map/ppermute | solution.py:299
  187.0 27.7 %collective-permute-start.50 = (bf16[2,256,256]{2,1,0:T(8,128)(2,1)S(1)}, bf16[2,256,256]{2,1,0:T(8,128)(2,1)S(1)}, u32[]{:S(2)}, u32[]{:S(2)}) collective-permute-start(bf16[2,256,256]{2,1,0:T(8,128)(2,1)S(1)} %add_convert_fusion.1), channel_id=1, source_target_pairs={{0,2},{2,0},{4,6},{6,4},{8,10},{10,8},{12,14},{14,12},{16,18},{18,... | collective-permute-start | bytes 786440 | tf_op jit(solution)/shard_map/ppermute | solution.py:299
  192.7 12.8 %collective-permute-start.58 = (f32[128,256]{1,0:T(8,128)S(1)}, f32[128,256]{1,0:T(8,128)S(1)}, u32[]{:S(2)}, u32[]{:S(2)}) collective-permute-start(f32[128,256]{1,0:T(8,128)S(1)} %fusion.1), channel_id=1, source_target_pairs={{0,24},{2,26},{4,28},{6,30},{8,16},{10,18},{12,20},{14,22},{16,8},... | collective-permute-start | bytes 393224 | tf_op jit(solution)/shard_map/ppermute | solution.py:299
  202.4 10.2 %collective-permute-start.57 = (f32[128,256]{1,0:T(8,128)S(1)}, f32[128,256]{1,0:T(8,128)S(1)}, u32[]{:S(2)}, u32[]{:S(2)}) collective-permute-start(f32[128,256]{1,0:T(8,128)S(1)} %fusion.1), channel_id=1, source_target_pairs={{0,16},{2,18},{4,20},{6,22},{8,24},{10,26},{12,28},{14,30},{16,0},... | collective-permute-start | bytes 393224 | tf_op jit(solution)/shard_map/ppermute | solution.py:299
  202.4 11.1 %collective-permute-start.56 = (f32[128,256]{1,0:T(8,128)S(1)}, f32[128,256]{1,0:T(8,128)S(1)}, u32[]{:S(2)}, u32[]{:S(2)}) collective-permute-start(f32[128,256]{1,0:T(8,128)S(1)} %fusion.1), channel_id=1, source_target_pairs={{0,8},{2,10},{4,12},{6,14},{8,0},{10,2},{12,4},{14,6},{16,24},{18,... | collective-permute-start | bytes 393224 | tf_op jit(solution)/shard_map/ppermute | solution.py:299
  205.5 16.8 %collective-permute-start.48 = (bf16[2,256,256]{2,1,0:T(8,128)(2,1)S(1)}, bf16[2,256,256]{2,1,0:T(8,128)(2,1)S(1)}, u32[]{:S(2)}, u32[]{:S(2)}) collective-permute-start(bf16[2,256,256]{2,1,0:T(8,128)(2,1)S(1)} %add_convert_fusion.2), channel_id=1, source_target_pairs={{4,0},{6,2},{12,8},{14,10},{16,4},{18,6},{20,16},{22,18},{24,12},{... | collective-permute-start | bytes 786440 | tf_op jit(solution)/shard_map/ppermute | solution.py:310
  212.6 9.7 %collective-permute-start.46 = (bf16[2,256,256]{2,1,0:T(8,128)(2,1)S(1)}, bf16[2,256,256]{2,1,0:T(8,128)(2,1)S(1)}, u32[]{:S(2)}, u32[]{:S(2)}) collective-permute-start(bf16[2,256,256]{2,1,0:T(8,128)(2,1)S(1)} %get-tuple-element.61), channel_id=1, source_target_pairs={{0,2},{2,0},{4,6},{6,4},{8,10},{10,8},{12,14},{14,12},{16,18},{18,... | collective-permute-start | bytes 786440 | tf_op jit(solution)/shard_map/ppermute | solution.py:299
  220.6 8.3 %collective-permute-start.52 = (bf16[2,256,256]{2,1,0:T(8,128)(2,1)S(1)}, bf16[2,256,256]{2,1,0:T(8,128)(2,1)S(1)}, u32[]{:S(2)}, u32[]{:S(2)}) collective-permute-start(bf16[2,256,256]{2,1,0:T(8,128)(2,1)S(1)} %add_convert_fusion), channel_id=1, source_target_pairs={{8,0},{10,2},{12,4},{14,6},{16,8},{18,10},{20,12},{22,14},{24,16},... | collective-permute-start | bytes 786440 | tf_op jit(solution)/shard_map/ppermute | solution.py:304
  241.8 10.1 %collective-permute-start.68 = (f32[96,256]{1,0:T(8,128)S(1)}, f32[96,256]{1,0:T(8,128)S(1)}, u32[]{:S(2)}, u32[]{:S(2)}) collective-permute-start(f32[96,256]{1,0:T(8,128)S(1)} %fusion.5), channel_id=1, source_target_pairs={{0,16},{2,18},{4,20},{6,22},{8,24},{10,26},{12,28},{14,30},{16,0},... | collective-permute-start | bytes 294920 | tf_op jit(solution)/shard_map/ppermute | solution.py:299
  243.5 8.4 %collective-permute-start.67 = (f32[96,256]{1,0:T(8,128)S(1)}, f32[96,256]{1,0:T(8,128)S(1)}, u32[]{:S(2)}, u32[]{:S(2)}) collective-permute-start(f32[96,256]{1,0:T(8,128)S(1)} %fusion.5), channel_id=1, source_target_pairs={{0,8},{2,10},{4,12},{6,14},{8,0},{10,2},{12,4},{14,6},{16,24},{18,... | collective-permute-start | bytes 294920 | tf_op jit(solution)/shard_map/ppermute | solution.py:299
  (44 other events, 288.4 us)

commit v7 on v6

--- a/solution.py
+++ b/solution.py
@@ -166,19 +166,12 @@
     )(meta, rows, cols, *pieces, blocks, *more)
 
 
-def update_kernel(rows_total, x, x_other, kept, near, far, two, inner, turned, update, *residual):
-    width, count = x.shape
+def descend_kernel(x, kept, near, far, two, out):
     size = kept.shape[2]
-    own = split(inner[pl.ds(0, width), :] / rows_total)
-    other = split((inner[pl.ds(width, width), :] + turned[...].T) / rows_total)
-    for t in range(count // size):
+    for t in range(x.shape[1] // size):
         part = pl.ds(t * size, size)
         applied = kept[t] + near[t].astype(f32) + (far[t].astype(f32) + two[t].astype(f32))
-        now = x[:, part]
-        rest = applied - (dot3(dot_nn, own, split(now)) + dot3(dot_nn, other, split(x_other[:, part])))
-        update[:, part] = now - STEP_RATE * rest
-        if residual:
-            residual[0][part, :] = rest.T
+        out[:, part] = x[:, part] - STEP_RATE * applied
 
 
 def gram_kernel(core, mine, theirs, out):
@@ -208,36 +201,68 @@
     scaled = unit * scale
     high[...], low[...] = split(scaled)
 
+    half = n // 2
+    top, bottom = pl.ds(0, half), pl.ds(half, half)
+    small = eye[:half, :half]
+    triangle = (at_row > at_col)[:half, :half]
+
     def lower(e):
-        return jnp.where(at_row > at_col, e, 0.5 * eye * e)
-
-    p = lower(scaled - eye)
-    pb = p.astype(bf16)
-    w[...] = eye - p + dot_nn(pb, pb)
-
-    def improve(e):
-        p = lower(e)
-        pb = p.astype(bf16)
-        first = dot_nn(pb, w[...].astype(bf16))
-        w[...] = w[...] - first + dot_nn(pb, first.astype(bf16))
-        return jnp.sqrt(jnp.sum(p * p))
+        return jnp.where(triangle, e, 0.5 * small * e)
+
+    def read(ref):
+        return ref[top, top], ref[bottom, top], ref[bottom, bottom]
+
+    def product(a, b):
+        return dot_nn(a[0], b[0]), dot_nn(a[1], b[0]) + dot_nn(a[2], b[1]), dot_nn(a[2], b[2])
+
+    def narrow(blocks):
+        return tuple(block.astype(bf16) for block in blocks)
+
+    p = (lower(scaled[:half, :half] - small), scaled[half:, :half], lower(scaled[half:, half:] - small))
+    pb = narrow(p)
+    square = product(pb, pb)
+    w[top, bottom] = jnp.zeros((half, half), f32)
+    w[top, top] = small - p[0] + square[0]
+    w[bottom, top] = square[1] - p[1]
+    w[bottom, bottom] = small - p[2] + square[2]
+
+    def improve(e, old):
+        p = (lower(e[0] - small), e[1], lower(e[2] - small))
+        pb = narrow(p)
+        first = product(pb, narrow(old))
+        second = product(pb, narrow(first))
+        w[top, top] = old[0] - first[0] + second[0]
+        w[bottom, top] = old[1] - first[1] + second[1]
+        w[bottom, bottom] = old[2] - first[2] + second[2]
+        return jnp.sqrt(sum(jnp.sum(block * block) for block in p))
+
+    def congruence(nn, nt, cut, w, s):
+        s00, s10, s11, s01 = s
+        left = nn(w[0], s00)
+        below, right = nn(w[1], s00) + nn(w[2], s10), nn(w[1], s01) + nn(w[2], s11)
+        left, below, right = cut(left), cut(below), cut(right)
+        return nt(left, w[0]), nt(below, w[0]), nt(below, w[1]) + nt(right, w[2])
+
+    def whole(ref):
+        return read(ref) + (ref[top, bottom],)
 
     def rough(state):
-        wb = w[...].astype(bf16)
-        e = dot_nt(dot_nn(wb, high[...]).astype(bf16), wb) - eye
-        return state[0] + 1, improve(e)
+        old = read(w)
+        e = congruence(dot_nn, dot_nt, lambda a: a.astype(bf16), narrow(old), whole(high))
+        return state[0] + 1, improve(e, old)
 
     def fine(state):
-        ws = split(w[...])
-        e = dot3(dot_nt, split(dot3(dot_nn, ws, (high[...], low[...]))), ws) - eye
-        return state[0] + 1, improve(e)
+        old = read(w)
+        nn, nt = (lambda a, b: dot3(dot_nn, a, b)), (lambda a, b: dot3(dot_nt, a, b))
+        e = congruence(nn, nt, split, [split(a) for a in old], list(zip(whole(high), whole(low))))
+        return state[0] + 1, improve(e, old)
 
     def until(bound, most):
         return lambda state: (state[0] < most) & jnp.logical_not(state[1] <= bound)
 
     lax.while_loop(until(0.4, 16), rough, (0, jnp.float32(1e9)))
-    _, error = lax.while_loop(until(2e-3, 6), fine, (0, jnp.float32(1e9)))
-    done = error <= 2e-3
+    _, error = lax.while_loop(until(0.1, 6), fine, (0, jnp.float32(1e9)))
+    done = error <= 0.1
 
     @pl.when(done)
     def _():
@@ -263,29 +288,58 @@
         lax.fori_loop(0, n, eliminate, 0)
 
 
-def factor_kernel(rows_total, last, core, mine, theirs, gram, gram_other, *refs):
-    out, (g, w, high, low, update) = refs[:-5], refs[-5:]
-    width = mine.shape[0]
-    half = width // 2
+def lay_out(out, first, second):
+    width = first.shape[1]
+    out[pl.ds(0, width), pl.ds(0, width)] = first[:width]
+    out[pl.ds(width, width), pl.ds(width, width)] = second[:width]
+    below = jnp.concatenate([first[width:], second[width:]], axis=0)
+    out[pl.ds(width, width), pl.ds(0, width)] = below
+    out[pl.ds(0, width), pl.ds(width, width)] = below.T
+
+
+def factor_kernel(rows_total, first_step, last, core, v, v_other, x, x_other, gram, gram_other, inner, inner_other, *refs):
+    out, (g, w, high, low, update, rayleigh) = refs[:-6], refs[-6:]
+    width, count = v.shape
     ahead = core[0] == 0
-    first = jnp.where(ahead, gram[...], gram_other[...]) / rows_total
-    second = jnp.where(ahead, gram_other[...], gram[...]) / rows_total
-    g[pl.ds(0, width), pl.ds(0, width)] = first[:width]
-    g[pl.ds(width, width), pl.ds(width, width)] = second[:width]
-    below = jnp.concatenate([first[width:], second[width:]], axis=0)
-    g[pl.ds(width, width), pl.ds(0, width)] = below
-    g[pl.ds(0, width), pl.ds(width, width)] = below.T
+
+    def ordered(mine, theirs):
+        mine, theirs = mine / rows_total, theirs / rows_total
+        return jnp.where(ahead, mine, theirs), jnp.where(ahead, theirs, mine)
+
+    first, second = ordered(inner[pl.ds(0, 2 * width), :], inner_other[pl.ds(0, 2 * width), :])
+    rayleigh[pl.ds(0, width), pl.ds(0, width)] = first[:width]
+    rayleigh[pl.ds(width, width), pl.ds(width, width)] = second[:width]
+    across = first[width:] + second[width:].T
+    rayleigh[pl.ds(0, width), pl.ds(width, width)] = across
+    rayleigh[pl.ds(width, width), pl.ds(0, width)] = across.T
+    lay_out(g, *ordered(gram[...], gram_other[...]))
+    r = split(rayleigh[...])
+    if first_step:
+        extra = pl.ds(2 * width, width + width // 2)
+        lay_out(w, *ordered(inner[extra, :], inner_other[extra, :]))
+        turned = dot3(dot_nn, split(w[...]), r)
+        g[...] += STEP_RATE * (turned + turned.T)
+        g[...] += dot3(dot_nn, r, split(STEP_RATE**2 * turned - (2 * STEP_RATE**2) * rayleigh[...]))
+    else:
+        g[...] += 2 * STEP_RATE * rayleigh[...] - STEP_RATE**2 * dot3(dot_nn, r, r)
     inverse_factor(g, w, high, low)
     start = pl.multiple_of(core[0] * width, width)
-    update[pl.ds(start, width), :] = mine[...]
-    update[pl.ds(width - start, width), :] = theirs[...]
+    there = width - start
+    update[pl.ds(start, width), :] = x[...]
+    update[pl.ds(there, width), :] = x_other[...]
     mix = split(w[pl.ds(start, width), :])
-    size = width
-    for t in range(mine.shape[1] // size):
-        part = pl.ds(t * size, size)
+    mine = split(rayleigh[pl.ds(start, width), :])
+    theirs = split(rayleigh[pl.ds(there, width), :])
+    for t in range(count // width):
+        part = pl.ds(t * width, width)
+        old = split(update[:, part])
+        here = v[:, part] + STEP_RATE * dot3(dot_nn, mine, old)
+        update[pl.ds(there, width), part] = v_other[:, part] + STEP_RATE * dot3(dot_nn, theirs, old)
+        update[pl.ds(start, width), part] = here
         solved = dot3(dot_nn, mix, split(update[:, part]))
         if last:
             out[0][part, :] = solved.T
+            out[1][part, :] = ((x[:, part] - here) * (1 / STEP_RATE)).T
         else:
             out[0][:, part] = solved
             out[1][t] = solved.astype(bf16)
@@ -396,30 +450,28 @@
         two_x, far = flip(two_out, 1), stride((same[2] + far_x.astype(f32)).astype(bf16), True)
         two = shift((same[1] + (two_x.astype(f32) + side.astype(f32))).astype(bf16), -2)
         joined = [flip(near, 1), far, two]
-        inner = summed(inner)
-        turned = swap_cores(inner[width:])
-        out = [flat] + ([shape(f32, count, width)] if last else [])
-        update, *residual = call(
-            lambda *refs: update_kernel(rows_total, *refs), out, [x, x_other, kept, *joined, inner, turned]
-        )
-        update_other = swap_cores(update)
-        (gram,) = call(
-            gram_kernel, [shape(f32, width + width // 2, width)], [core, update, update_other], smem=1
-        )
+        inner_out = [inner]
+        if step == 0:
+            inner_out += call(gram_kernel, [shape(f32, width + width // 2, width)], [core, x, x_other], smem=1)
+        inner = summed(jnp.concatenate(inner_out))
+        (v,) = call(descend_kernel, [flat], [x, kept, *joined])
+        v_other = swap_cores(v)
+        (gram,) = call(gram_kernel, [shape(f32, width + width // 2, width)], [core, v, v_other], smem=1)
         gram = summed(gram)
         full = (2 * width, 2 * width)
+        wide = shape(f32, count, width)
         out = call(
-            lambda *refs: factor_kernel(rows_total, last, *refs),
-            [shape(f32, count, width)] if last else [flat, chunk],
-            [core, update, update_other, gram, swap_cores(gram)],
-            scratch=[VMEM(full, f32), VMEM(full, f32), VMEM(full, bf16), VMEM(full, bf16), VMEM((2 * width, count), f32)],
+            lambda *refs: factor_kernel(rows_total, step == 0, last, *refs),
+            [wide, wide] if last else [flat, chunk],
+            [core, v, v_other, x, x_other, gram, swap_cores(gram), inner, swap_cores(inner)],
+            scratch=[VMEM(full, f32), VMEM(full, f32), VMEM(full, bf16), VMEM(full, bf16)]
+            + [VMEM((2 * width, count), f32), VMEM(full, f32)],
             smem=1,
             flops=16 << 30,
             vmem=28,
         )
-        if last:
-            return out[0], residual[0]
         x, u = out
+    return x, u
 
 
 def solution(mesh):

time: 275 us -> 266 us (0.967); the launches traced: 275 us -> 270 us
  starting transfers between devices: 106 us -> 127 us
  waiting for transfers between devices: 109 us -> 90.1 us
  Pallas kernels: 40.4 us -> 33.7 us
    ppermute x56, starting transfers between devices: 85.8 us -> 105 us  [flip(): lax.ppermute(a, 'patch', [(i, i ^ mask) for i in range(lax.axis_size('pat...]
    ppermute x4, waiting for transfers between devices: 14.5 us -> 3.94 us  [shift(): lax.ppermute(a, 'patch', [(i - 2 * pairs, i) for i in devices if i - 2 *...]
    ppermute x56, waiting for transfers between devices: 87.3 us -> 82.7 us  [flip(): lax.ppermute(a, 'patch', [(i, i ^ mask) for i in range(lax.axis_size('pat...]
    pallas_call x7 -> x8, Pallas kernels: 30.4 us -> 26.6 us  [call(): pl.pallas_call(kernel, out_shape=out, in_specs=[pl.BlockSpec(memory_space...]
    ppermute x10, waiting for transfers between devices: 7.23 us -> 3.43 us  [swap_cores(): return lax.ppermute(a, 'vec', [(0, 1), (1, 0)])]
    pallas_call x4, Pallas kernels: 9.97 us -> 7.17 us  [tiles_call(): pl.pallas_call(kernel, in_specs=[pl.BlockSpec(memory_space=SMEM)] * 3 + [...]
    unnamed x36 -> x30, local copies, waits for them, and re-layouts: 16.6 us -> 14.2 us
  transfers between devices with their start and end apart: 74 -> 74, of which waited for: 39 -> 36; matrix products, arithmetic and copies ran while one was open for 0% -> 1% of each run, Pallas kernels for 4% -> 3%
where the time goes in v7:
time: 266 us; the launch traced here: 270 us
  starting transfers between devices  127 us (48%)
  waiting for transfers between devices  90.1 us (34%)
  Pallas kernels  33.7 us (13%)
  local copies, waits for them, and re-layouts  14.4 us (5%)
    ppermute x56, starting transfers between devices, flip(): lax.ppermute(a, 'patch', [(i, i ^ mask) for i in range(lax.axis_size('pat...  105 us
    ppermute x56, waiting for transfers between devices, flip(): lax.ppermute(a, 'patch', [(i, i ^ mask) for i in range(lax.axis_size('pat...  82.7 us
    pallas_call x8, Pallas kernels, call(): pl.pallas_call(kernel, out_shape=out, in_specs=[pl.BlockSpec(memory_space...  26.6 us
    unnamed x30, local copies, waits for them, and re-layouts  14.2 us
    ppermute x4, starting transfers between devices, shift(): lax.ppermute(a, 'patch', [(i - 2 * pairs, i) for i in devices if i - 2 *...  11.2 us
    ppermute x4, starting transfers between devices, stride(): lax.ppermute(a, 'patch', [(d, s) if back else (s, d) for s, d in route if...  10.6 us
    pallas_call x4, Pallas kernels, tiles_call(): pl.pallas_call(kernel, in_specs=[pl.BlockSpec(memory_space=SMEM)] * 3 + [...  7.17 us
  transfers between devices with their start and end apart: 74, of which 36 were waited for; matrix products, arithmetic and copies ran while one was open for 1% of the time, Pallas kernels for 3%

profile of v7, /device:TPU:0, one launch (start us, length us, event | category | flops | bytes accessed | tf_op | source)
XLA Modules:
  0.0 269.5 jit_solution(4754016944030428654)
XLA Ops:
  1.9 4.9 %collective-permute-start.1 = (bf16[2,256,256]{2,1,0:T(8,128)(2,1)S(1)}, bf16[2,256,256]{2,1,0:T(8,128)(2,1)S(1)}, u32[]{:S(2)}, u32[]{:S(2)}) collective-permute-start(bf16[2,256,256]{2,1,0:T(8,128)(2,1)S(1)} %get-tuple-element.35.refs_0_), channel_id=1, source_target_pairs={{0,8},{2,10},{4,12},{6,14},{8,16},{10,18},{12,20},{14,22},{16,24},... | collective-permute-start | bytes 786440 | tf_op jit(solution)/shard_map/ppermute | solution.py:358
  8.4 4.1 %collective-permute-start.2 = (bf16[2,256,256]{2,1,0:T(8,128)(2,1)S(1)}, bf16[2,256,256]{2,1,0:T(8,128)(2,1)}, u32[]{:S(2)}, u32[]{:S(2)}) collective-permute-start(bf16[2,256,256]{2,1,0:T(8,128)(2,1)S(1)} %get-tuple-element.35.refs_0_), channel_id=1, source_target_pairs={{0,4},{2,6},{8,12},{10,14},{4,16},{6,18},{16,20},{18,22},{12,24},{... | collective-permute-start | bytes 786440 | tf_op jit(solution)/shard_map/ppermute | solution.py:364
  13.8 2.6 collective-permute-start.4
  16.4 3.4 %copy-done = bf16[64,256,256]{2,1,0:T(8,128)(2,1)S(1)} copy-done((bf16[64,256,256]{2,1,0:T(8,128)(2,1)S(1)}, bf16[64,256,256]{2,1,0:T(8,128)(2,1)}, u32[]{:S(2)}) %copy-start) | copy-done | bytes 8388632
  28.0 2.4 collective-permute-start.10
  30.4 5.1 %collective-permute-done.12 = bf16[2,256,256]{2,1,0:T(8,128)(2,1)} collective-permute-done((bf16[2,256,256]{2,1,0:T(8,128)(2,1)}, bf16[2,256,256]{2,1,0:T(8,128)(2,1)}, u32[]{:S(2)}, u32[]{:S(2)}) %collective-permute-start.12) | collective-permute-done | bytes 262176 | tf_op jit(solution)/shard_map/ppermute | solution.py:353
  35.5 2.3 collective-permute-start.5
  41.5 3.5 %collective-permute-done.5.refs_5_ = bf16[2,256,256]{2,1,0:T(8,128)(2,1)S(1)} collective-permute-done((bf16[2,256,256]{2,1,0:T(8,128)(2,1)}, bf16[2,256,256]{2,1,0:T(8,128)(2,1)S(1)}, u32[]{:S(2)}, u32[]{:S(2)}) %collective-permute-start.5) | collective-permute-done | bytes 262176 | tf_op jit(solution)/shard_map/ppermute | solution.py:353
  45.0 2.8 %collective-permute-done.6.refs_7_ = bf16[2,256,256]{2,1,0:T(8,128)(2,1)S(1)} collective-permute-done((bf16[2,256,256]{2,1,0:T(8,128)(2,1)}, bf16[2,256,256]{2,1,0:T(8,128)(2,1)S(1)}, u32[]{:S(2)}, u32[]{:S(2)}) %collective-permute-start.6) | collective-permute-done | bytes 262176 | tf_op jit(solution)/shard_map/ppermute | solution.py:353
  47.9 3.4 %copy-done.1 = bf16[64,256,256]{2,1,0:T(8,128)(2,1)S(1)} copy-done((bf16[64,256,256]{2,1,0:T(8,128)(2,1)S(1)}, bf16[64,256,256]{2,1,0:T(8,128)(2,1)}, u32[]{:S(2)}) %copy-start.1) | copy-done | bytes 8388632
  53.3 2.5 shard_map.70
  55.9 2.7 %collective-permute-start.27 = (f32[224,256]{1,0:T(8,128)S(1)}, f32[224,256]{1,0:T(8,128)S(1)}, u32[]{:S(2)}, u32[]{:S(2)}) collective-permute-start(f32[224,256]{1,0:T(8,128)S(1)} %get-tuple-element.70), channel_id=1, source_target_pairs={{0,2},{2,0},{4,6},{6,4},{8,10},{10,8},{12,14},{14,12},{16,18},{18,... | collective-permute-start | bytes 688136 | tf_op jit(solution)/shard_map/ppermute | solution.py:353
  61.8 3.3 %collective-permute-done.27 = f32[224,256]{1,0:T(8,128)S(1)} collective-permute-done((f32[224,256]{1,0:T(8,128)S(1)}, f32[224,256]{1,0:T(8,128)S(1)}, u32[]{:S(2)}, u32[]{:S(2)}) %collective-permute-start.27) | collective-permute-done | bytes 229408 | tf_op jit(solution)/shard_map/ppermute | solution.py:353
  65.1 2.1 collective-permute-start.9
  69.5 15.1 %collective-permute-start.30 = (f32[224,256]{1,0:T(8,128)S(1)}, f32[224,256]{1,0:T(8,128)S(1)}, u32[]{:S(2)}, u32[]{:S(2)}) collective-permute-start(f32[224,256]{1,0:T(8,128)S(1)} %fusion.1), channel_id=1, source_target_pairs={{0,8},{2,10},{4,12},{6,14},{8,0},{10,2},{12,4},{14,6},{16,24},{18,... | collective-permute-start | bytes 688136 | tf_op jit(solution)/shard_map/ppermute | solution.py:353
  84.6 2.4 collective-permute-start.32
  87.2 4.1 %collective-permute-done.30 = f32[224,256]{1,0:T(8,128)S(1)} collective-permute-done((f32[224,256]{1,0:T(8,128)S(1)}, f32[224,256]{1,0:T(8,128)S(1)}, u32[]{:S(2)}, u32[]{:S(2)}) %collective-permute-start.30) | collective-permute-done | bytes 229408 | tf_op jit(solution)/shard_map/ppermute | solution.py:353
  91.4 7.4 %collective-permute-done.31 = f32[224,256]{1,0:T(8,128)S(1)} collective-permute-done((f32[224,256]{1,0:T(8,128)S(1)}, f32[224,256]{1,0:T(8,128)S(1)}, u32[]{:S(2)}, u32[]{:S(2)}) %collective-permute-start.31) | collective-permute-done | bytes 229408 | tf_op jit(solution)/shard_map/ppermute | solution.py:353
  98.8 2.2 collective-permute-start.33
  105.8 2.6 collective-permute-done.33
  108.4 2.1 collective-permute-start.19
  114.0 4.8 %collective-permute-start.20 = (f32[96,256]{1,0:T(8,128)S(1)}, f32[96,256]{1,0:T(8,128)S(1)}, u32[]{:S(2)}, u32[]{:S(2)}) collective-permute-start(f32[96,256]{1,0:T(8,128)S(1)} %fusion.7), channel_id=1, source_target_pairs={{0,8},{2,10},{4,12},{6,14},{8,0},{10,2},{12,4},{14,6},{16,24},{18,... | collective-permute-start | bytes 294920 | tf_op jit(solution)/shard_map/ppermute | solution.py:353
  118.7 2.4 collective-permute-start.22
  123.0 4.6 %collective-permute-done.21 = f32[96,256]{1,0:T(8,128)S(1)} collective-permute-done((f32[96,256]{1,0:T(8,128)S(1)}, f32[96,256]{1,0:T(8,128)S(1)}, u32[]{:S(2)}, u32[]{:S(2)}) %collective-permute-start.21) | collective-permute-done | bytes 98336 | tf_op jit(solution)/shard_map/ppermute | solution.py:353
  136.9 13.1 %shard_map.74 = (f32[256,512]{1,0:T(8,128)S(1)}, bf16[2,256,256]{2,1,0:T(8,128)(2,1)S(1)}) custom-call(s32[1]{0:T(128)} %bitcast.core.refs_0_, f32[256,512]{1,0:T(8,128)S(1)} %shard_map.71.mine.refs_1_, f32[256,512]{1,0:T(8,128)S(1)} %collective-permute-done.16.theirs.refs_2_, f32[256,512]{1,0:T(8,128)S(1)} %get-tuple-element.34.x.mine.refs_3_, ...), custom_call_target="tpu_custom_call" | custom-call | flops 17179869184 | bytes 5505028 | tf_op jit(solution)/shard_map/pallas_call | solution.py:39
  151.0 3.5 %collective-permute-start.38 = (bf16[2,256,256]{2,1,0:T(8,128)(2,1)S(1)}, bf16[2,256,256]{2,1,0:T(8,128)(2,1)S(1)}, u32[]{:S(2)}, u32[]{:S(2)}) collective-permute-start(bf16[2,256,256]{2,1,0:T(8,128)(2,1)S(1)} %get-tuple-element.51.refs_0_), channel_id=1, source_target_pairs={{0,8},{2,10},{4,12},{6,14},{8,16},{10,18},{12,20},{14,22},{16,24},... | collective-permute-start | bytes 786440 | tf_op jit(solution)/shard_map/ppermute | solution.py:358
  154.5 3.9 %collective-permute-start.39 = (bf16[2,256,256]{2,1,0:T(8,128)(2,1)S(1)}, bf16[2,256,256]{2,1,0:T(8,128)(2,1)S(1)}, u32[]{:S(2)}, u32[]{:S(2)}) collective-permute-start(bf16[2,256,256]{2,1,0:T(8,128)(2,1)S(1)} %get-tuple-element.51.refs_0_), channel_id=1, source_target_pairs={{0,4},{2,6},{8,12},{10,14},{4,16},{6,18},{16,20},{18,22},{12,24},{... | collective-permute-start | bytes 786440 | tf_op jit(solution)/shard_map/ppermute | solution.py:364
  159.9 2.0 collective-permute-start.49
  161.9 2.5 collective-permute-start.40
  166.4 4.3 %collective-permute-done.49 = bf16[2,256,256]{2,1,0:T(8,128)(2,1)S(1)} collective-permute-done((bf16[2,256,256]{2,1,0:T(8,128)(2,1)S(1)}, bf16[2,256,256]{2,1,0:T(8,128)(2,1)S(1)}, u32[]{:S(2)}, u32[]{:S(2)}) %collective-permute-start.49) | collective-permute-done | bytes 262176 | tf_op jit(solution)/shard_map/ppermute | solution.py:353
  171.6 2.0 collective-permute-start.50
  173.7 2.8 %collective-permute-done.41.refs_6_ = bf16[2,256,256]{2,1,0:T(8,128)(2,1)S(1)} collective-permute-done((bf16[2,256,256]{2,1,0:T(8,128)(2,1)S(1)}, bf16[2,256,256]{2,1,0:T(8,128)(2,1)S(1)}, u32[]{:S(2)}, u32[]{:S(2)}) %collective-permute-start.41) | collective-permute-done | bytes 262176 | tf_op jit(solution)/shard_map/ppermute | solution.py:353
  176.4 4.2 %collective-permute-done.51 = bf16[2,256,256]{2,1,0:T(8,128)(2,1)S(1)} collective-permute-done((bf16[2,256,256]{2,1,0:T(8,128)(2,1)S(1)}, bf16[2,256,256]{2,1,0:T(8,128)(2,1)S(1)}, u32[]{:S(2)}, u32[]{:S(2)}) %collective-permute-start.51) | collective-permute-done | bytes 262176 | tf_op jit(solution)/shard_map/ppermute | solution.py:353
  187.5 2.9 %collective-permute-done.43.refs_7_ = bf16[2,256,256]{2,1,0:T(8,128)(2,1)S(1)} collective-permute-done((bf16[2,256,256]{2,1,0:T(8,128)(2,1)S(1)}, bf16[2,256,256]{2,1,0:T(8,128)(2,1)S(1)}, u32[]{:S(2)}, u32[]{:S(2)}) %collective-permute-start.43) | collective-permute-done | bytes 262176 | tf_op jit(solution)/shard_map/ppermute | solution.py:353
  191.9 3.4 %collective-permute-start.46 = (bf16[2,256,256]{2,1,0:T(8,128)(2,1)S(1)}, bf16[2,256,256]{2,1,0:T(8,128)(2,1)S(1)}, u32[]{:S(2)}, u32[]{:S(2)}) collective-permute-start(bf16[2,256,256]{2,1,0:T(8,128)(2,1)S(1)} %get-tuple-element.59), channel_id=1, source_target_pairs={{0,2},{2,0},{4,6},{6,4},{8,10},{10,8},{12,14},{14,12},{16,18},{18,... | collective-permute-start | bytes 786440 | tf_op jit(solution)/shard_map/ppermute | solution.py:353
  195.3 3.9 %collective-permute-done.52.two = bf16[2,256,256]{2,1,0:T(8,128)(2,1)S(1)} collective-permute-done((bf16[2,256,256]{2,1,0:T(8,128)(2,1)S(1)}, bf16[2,256,256]{2,1,0:T(8,128)(2,1)S(1)}, u32[]{:S(2)}, u32[]{:S(2)}) %collective-permute-start.52) | collective-permute-done | bytes 262176 | tf_op jit(solution)/shard_map/ppermute | solution.py:358
  199.9 2.1 collective-permute-start.64
  202.0 4.0 %collective-permute-start.65 = (f32[128,256]{1,0:T(8,128)S(1)}, f32[128,256]{1,0:T(8,128)S(1)}, u32[]{:S(2)}, u32[]{:S(2)}) collective-permute-start(f32[128,256]{1,0:T(8,128)S(1)} %get-tuple-element.79), channel_id=1, source_target_pairs={{0,4},{2,6},{4,0},{6,2},{8,12},{10,14},{12,8},{14,10},{16,20},{18,... | collective-permute-start | bytes 393224 | tf_op jit(solution)/shard_map/ppermute | solution.py:353
  206.1 6.5 %collective-permute-done.65 = f32[128,256]{1,0:T(8,128)S(1)} collective-permute-done((f32[128,256]{1,0:T(8,128)S(1)}, f32[128,256]{1,0:T(8,128)S(1)}, u32[]{:S(2)}, u32[]{:S(2)}) %collective-permute-start.65) | collective-permute-done | bytes 131104 | tf_op jit(solution)/shard_map/ppermute | solution.py:353
  212.7 9.5 %collective-permute-start.67 = (f32[128,256]{1,0:T(8,128)S(1)}, f32[128,256]{1,0:T(8,128)S(1)}, u32[]{:S(2)}, u32[]{:S(2)}) collective-permute-start(f32[128,256]{1,0:T(8,128)S(1)} %fusion.3), channel_id=1, source_target_pairs={{0,8},{2,10},{4,12},{6,14},{8,0},{10,2},{12,4},{14,6},{16,24},{18,... | collective-permute-start | bytes 393224 | tf_op jit(solution)/shard_map/ppermute | solution.py:353
  222.1 2.4 collective-permute-start.69
  228.8 4.6 %collective-permute-done.68 = f32[128,256]{1,0:T(8,128)S(1)} collective-permute-done((f32[128,256]{1,0:T(8,128)S(1)}, f32[128,256]{1,0:T(8,128)S(1)}, u32[]{:S(2)}, u32[]{:S(2)}) %collective-permute-start.68) | collective-permute-done | bytes 131104 | tf_op jit(solution)/shard_map/ppermute | solution.py:353
  234.9 2.1 collective-permute-start.72
  237.0 3.3 %collective-permute-start.57 = (f32[96,256]{1,0:T(8,128)S(1)}, f32[96,256]{1,0:T(8,128)S(1)}, u32[]{:S(2)}, u32[]{:S(2)}) collective-permute-start(f32[96,256]{1,0:T(8,128)S(1)} %fusion.5), channel_id=1, source_target_pairs={{0,8},{2,10},{4,12},{6,14},{8,0},{10,2},{12,4},{14,6},{16,24},{18,... | collective-permute-start | bytes 294920 | tf_op jit(solution)/shard_map/ppermute | solution.py:353
  240.8 2.0 collective-permute-start.59
  243.6 6.3 %collective-permute-done.58 = f32[96,256]{1,0:T(8,128)S(1)} collective-permute-done((f32[96,256]{1,0:T(8,128)S(1)}, f32[96,256]{1,0:T(8,128)S(1)}, u32[]{:S(2)}, u32[]{:S(2)}) %collective-permute-start.58) | collective-permute-done | bytes 98336 | tf_op jit(solution)/shard_map/ppermute | solution.py:353
  251.4 2.0 collective-permute-start.62
  258.4 11.1 %shard_map.79 = (f32[512,256]{1,0:T(8,128)}, f32[512,256]{1,0:T(8,128)}) custom-call(s32[1]{0:T(128)} %bitcast.core.refs_0_, f32[256,512]{1,0:T(8,128)S(1)} %shard_map.77.mine.refs_1_, f32[256,512]{1,0:T(8,128)S(1)} %collective-permute-done.53.theirs.refs_2_, f32[256,512]{1,0:T(8,128)S(1)} %get-tuple-element.50.x.refs_3_, ...), custom_call_target="tpu_custom_call" | custom-call | flops 17179869184 | bytes 4980740 | tf_op jit(solution)/shard_map/pallas_call | solution.py:39
  (171 shorter events, 70.4 us)
Async XLA Ops:
  1.9 11.4 %collective-permute-start.1 = (bf16[2,256,256]{2,1,0:T(8,128)(2,1)S(1)}, bf16[2,256,256]{2,1,0:T(8,128)(2,1)S(1)}, u32[]{:S(2)}, u32[]{:S(2)}) collective-permute-start(bf16[2,256,256]{2,1,0:T(8,128)(2,1)S(1)} %get-tuple-element.35.refs_0_), channel_id=1, source_target_pairs={{0,8},{2,10},{4,12},{6,14},{8,16},{10,18},{12,20},{14,22},{16,24},... | collective-permute-start | bytes 786440 | tf_op jit(solution)/shard_map/ppermute | solution.py:358
  6.8 9.6 %collective-permute-start = (bf16[2,256,256]{2,1,0:T(8,128)(2,1)S(1)}, bf16[2,256,256]{2,1,0:T(8,128)(2,1)S(1)}, u32[]{:S(2)}, u32[]{:S(2)}) collective-permute-start(bf16[2,256,256]{2,1,0:T(8,128)(2,1)S(1)} %get-tuple-element.35.refs_0_), channel_id=1, source_target_pairs={{0,2},{2,0},{4,6},{6,4},{8,10},{10,8},{12,14},{14,12},{16,18},{18,... | collective-permute-start | bytes 786440 | tf_op jit(solution)/shard_map/ppermute | solution.py:353
  8.4 18.3 %collective-permute-start.2 = (bf16[2,256,256]{2,1,0:T(8,128)(2,1)S(1)}, bf16[2,256,256]{2,1,0:T(8,128)(2,1)}, u32[]{:S(2)}, u32[]{:S(2)}) collective-permute-start(bf16[2,256,256]{2,1,0:T(8,128)(2,1)S(1)} %get-tuple-element.35.refs_0_), channel_id=1, source_target_pairs={{0,4},{2,6},{8,12},{10,14},{4,16},{6,18},{16,20},{18,22},{12,24},{... | collective-permute-start | bytes 786440 | tf_op jit(solution)/shard_map/ppermute | solution.py:364
  12.5 26.3 %collective-permute-start.7 = (f32[256,512]{1,0:T(8,128)S(1)}, f32[256,512]{1,0:T(8,128)S(1)}, u32[]{:S(2)}, u32[]{:S(2)}) collective-permute-start(f32[256,512]{1,0:T(8,128)S(1)} %get-tuple-element.34.x.mine.refs_3_), channel_id=1, source_target_pairs={{0,1},{1,0},{2,3},{3,2},{4,5},{5,4},{6,7},{7,6},{8,9},{9,8},{10,11... | collective-permute-start | bytes 1572872 | tf_op jit(solution)/shard_map/ppermute | solution.py:349
  13.3 14.7 %collective-permute-start.3 = (bf16[2,256,256]{2,1,0:T(8,128)(2,1)S(1)}, bf16[2,256,256]{2,1,0:T(8,128)(2,1)}, u32[]{:S(2)}, u32[]{:S(2)}) collective-permute-start(bf16[2,256,256]{2,1,0:T(8,128)(2,1)S(1)} %collective-permute-done.1.refs_2_), channel_id=1, source_target_pairs={{0,2},{2,0},{4,6},{6,4},{8,10},{10,8},{12,14},{14,12},{16,18},{18,... | collective-permute-start | bytes 786440 | tf_op jit(solution)/shard_map/ppermute | solution.py:353
  13.8 16.5 %collective-permute-start.4 = (bf16[2,256,256]{2,1,0:T(8,128)(2,1)S(1)}, bf16[2,256,256]{2,1,0:T(8,128)(2,1)}, u32[]{:S(2)}, u32[]{:S(2)}) collective-permute-start(bf16[2,256,256]{2,1,0:T(8,128)(2,1)S(1)} %collective-permute-done.1.refs_2_), channel_id=1, source_target_pairs={{0,4},{2,6},{4,0},{6,2},{8,12},{10,14},{12,8},{14,10},{16,20},{18,... | collective-permute-start | bytes 786440 | tf_op jit(solution)/shard_map/ppermute | solution.py:353
  25.9 9.6 %collective-permute-start.12 = (bf16[2,256,256]{2,1,0:T(8,128)(2,1)}, bf16[2,256,256]{2,1,0:T(8,128)(2,1)}, u32[]{:S(2)}, u32[]{:S(2)}) collective-permute-start(bf16[2,256,256]{2,1,0:T(8,128)(2,1)} %get-tuple-element.36), channel_id=1, source_target_pairs={{0,4},{2,6},{4,0},{6,2},{8,12},{10,14},{12,8},{14,10},{16,20},{18,... | collective-permute-start | bytes 786440 | tf_op jit(solution)/shard_map/ppermute | solution.py:353
  26.7 31.9 %collective-permute-start.14 = (bf16[2,256,256]{2,1,0:T(8,128)(2,1)}, bf16[2,256,256]{2,1,0:T(8,128)(2,1)S(1)}, u32[]{:S(2)}, u32[]{:S(2)}) collective-permute-start(bf16[2,256,256]{2,1,0:T(8,128)(2,1)} %copy-done.3), channel_id=1, source_target_pairs={{0,4},{2,6},{4,0},{6,2},{8,12},{10,14},{12,8},{14,10},{16,20},{18,... | collective-permute-start | bytes 786440 | tf_op jit(solution)/shard_map/ppermute | solution.py:353
  28.0 12.0 %collective-permute-start.10 = (bf16[2,256,256]{2,1,0:T(8,128)(2,1)}, bf16[2,256,256]{2,1,0:T(8,128)(2,1)S(1)}, u32[]{:S(2)}, u32[]{:S(2)}) collective-permute-start(bf16[2,256,256]{2,1,0:T(8,128)(2,1)} %copy-done.4), channel_id=1, source_target_pairs={{0,2},{2,0},{4,6},{6,4},{8,10},{10,8},{12,14},{14,12},{16,18},{18,... | collective-permute-start | bytes 786440 | tf_op jit(solution)/shard_map/ppermute | solution.py:353
  30.4 9.8 %collective-permute-start.8 = (bf16[2,256,256]{2,1,0:T(8,128)(2,1)S(1)}, bf16[2,256,256]{2,1,0:T(8,128)(2,1)S(1)}, u32[]{:S(2)}, u32[]{:S(2)}) collective-permute-start(bf16[2,256,256]{2,1,0:T(8,128)(2,1)S(1)} %collective-permute-done.refs_1_), channel_id=1, source_target_pairs={{0,1},{1,0},{2,3},{3,2},{4,5},{5,4},{6,7},{7,6},{8,9},{9,8},{10,11... | collective-permute-start | bytes 786440 | tf_op jit(solution)/shard_map/ppermute | solution.py:349
  35.5 9.5 %collective-permute-start.5 = (bf16[2,256,256]{2,1,0:T(8,128)(2,1)}, bf16[2,256,256]{2,1,0:T(8,128)(2,1)S(1)}, u32[]{:S(2)}, u32[]{:S(2)}) collective-permute-start(bf16[2,256,256]{2,1,0:T(8,128)(2,1)} %collective-permute-done.2.refs_4_), channel_id=1, source_target_pairs={{0,2},{2,0},{4,6},{6,4},{8,10},{10,8},{12,14},{14,12},{16,18},{18,... | collective-permute-start | bytes 786440 | tf_op jit(solution)/shard_map/ppermute | solution.py:353
  40.0 20.2 %collective-permute-start.13 = (bf16[2,256,256]{2,1,0:T(8,128)(2,1)S(1)}, bf16[2,256,256]{2,1,0:T(8,128)(2,1)S(1)}, u32[]{:S(2)}, u32[]{:S(2)}) collective-permute-start(bf16[2,256,256]{2,1,0:T(8,128)(2,1)S(1)} %add_convert_fusion.4), channel_id=1, source_target_pairs={{0,2},{2,0},{4,6},{6,4},{8,10},{10,8},{12,14},{14,12},{16,18},{18,... | collective-permute-start | bytes 786440 | tf_op jit(solution)/shard_map/ppermute | solution.py:353
  40.2 44.4 %collective-permute-start.11 = (bf16[2,256,256]{2,1,0:T(8,128)(2,1)S(1)}, bf16[2,256,256]{2,1,0:T(8,128)(2,1)S(1)}, u32[]{:S(2)}, u32[]{:S(2)}) collective-permute-start(bf16[2,256,256]{2,1,0:T(8,128)(2,1)S(1)} %add_convert_fusion.5), channel_id=1, source_target_pairs={{4,0},{6,2},{12,8},{14,10},{16,4},{18,6},{20,16},{22,18},{24,12},{... | collective-permute-start | bytes 786440 | tf_op jit(solution)/shard_map/ppermute | solution.py:364
  55.9 9.2 %collective-permute-start.27 = (f32[224,256]{1,0:T(8,128)S(1)}, f32[224,256]{1,0:T(8,128)S(1)}, u32[]{:S(2)}, u32[]{:S(2)}) collective-permute-start(f32[224,256]{1,0:T(8,128)S(1)} %get-tuple-element.70), channel_id=1, source_target_pairs={{0,2},{2,0},{4,6},{6,4},{8,10},{10,8},{12,14},{14,12},{16,18},{18,... | collective-permute-start | bytes 688136 | tf_op jit(solution)/shard_map/ppermute | solution.py:353
  58.7 9.9 %collective-permute-start.28 = (f32[224,256]{1,0:T(8,128)S(1)}, f32[224,256]{1,0:T(8,128)S(1)}, u32[]{:S(2)}, u32[]{:S(2)}) collective-permute-start(f32[224,256]{1,0:T(8,128)S(1)} %get-tuple-element.72), channel_id=1, source_target_pairs={{0,4},{2,6},{4,0},{6,2},{8,12},{10,14},{12,8},{14,10},{16,20},{18,... | collective-permute-start | bytes 688136 | tf_op jit(solution)/shard_map/ppermute | solution.py:353
  58.7 10.7 %collective-permute-start.29 = (f32[224,256]{1,0:T(8,128)S(1)}, f32[224,256]{1,0:T(8,128)S(1)}, u32[]{:S(2)}, u32[]{:S(2)}) collective-permute-start(f32[224,256]{1,0:T(8,128)S(1)} %get-tuple-element.71), channel_id=1, source_target_pairs={{0,6},{2,4},{4,2},{6,0},{8,14},{10,12},{12,10},{14,8},{16,22},{18,... | collective-permute-start | bytes 688136 | tf_op jit(solution)/shard_map/ppermute | solution.py:353
  60.3 26.7 %collective-permute-start.15 = (bf16[2,256,256]{2,1,0:T(8,128)(2,1)S(1)}, bf16[2,256,256]{2,1,0:T(8,128)(2,1)S(1)}, u32[]{:S(2)}, u32[]{:S(2)}) collective-permute-start(bf16[2,256,256]{2,1,0:T(8,128)(2,1)S(1)} %add_convert_fusion.3), channel_id=1, source_target_pairs={{8,0},{10,2},{12,4},{14,6},{16,8},{18,10},{20,12},{22,14},{24,16},... | collective-permute-start | bytes 786440 | tf_op jit(solution)/shard_map/ppermute | solution.py:358
  65.1 21.9 %collective-permute-start.9 = (bf16[2,256,256]{2,1,0:T(8,128)(2,1)S(1)}, bf16[2,256,256]{2,1,0:T(8,128)(2,1)S(1)}, u32[]{:S(2)}, u32[]{:S(2)}) collective-permute-start(bf16[2,256,256]{2,1,0:T(8,128)(2,1)S(1)} %get-tuple-element.43), channel_id=1, source_target_pairs={{0,2},{2,0},{4,6},{6,4},{8,10},{10,8},{12,14},{14,12},{16,18},{18,... | collective-permute-start | bytes 786440 | tf_op jit(solution)/shard_map/ppermute | solution.py:353
  69.5 21.9 %collective-permute-start.30 = (f32[224,256]{1,0:T(8,128)S(1)}, f32[224,256]{1,0:T(8,128)S(1)}, u32[]{:S(2)}, u32[]{:S(2)}) collective-permute-start(f32[224,256]{1,0:T(8,128)S(1)} %fusion.1), channel_id=1, source_target_pairs={{0,8},{2,10},{4,12},{6,14},{8,0},{10,2},{12,4},{14,6},{16,24},{18,... | collective-permute-start | bytes 688136 | tf_op jit(solution)/shard_map/ppermute | solution.py:353
  84.6 14.2 %collective-permute-start.31 = (f32[224,256]{1,0:T(8,128)S(1)}, f32[224,256]{1,0:T(8,128)S(1)}, u32[]{:S(2)}, u32[]{:S(2)}) collective-permute-start(f32[224,256]{1,0:T(8,128)S(1)} %fusion.1), channel_id=1, source_target_pairs={{0,16},{2,18},{4,20},{6,22},{8,24},{10,26},{12,28},{14,30},{16,0},... | collective-permute-start | bytes 688136 | tf_op jit(solution)/shard_map/ppermute | solution.py:353
  84.6 14.2 %collective-permute-start.32 = (f32[224,256]{1,0:T(8,128)S(1)}, f32[224,256]{1,0:T(8,128)S(1)}, u32[]{:S(2)}, u32[]{:S(2)}) collective-permute-start(f32[224,256]{1,0:T(8,128)S(1)} %fusion.1), channel_id=1, source_target_pairs={{0,24},{2,26},{4,28},{6,30},{8,16},{10,18},{12,20},{14,22},{16,8},... | collective-permute-start | bytes 688136 | tf_op jit(solution)/shard_map/ppermute | solution.py:353
  87.2 15.2 %collective-permute-start.16 = (f32[256,512]{1,0:T(8,128)S(1)}, f32[256,512]{1,0:T(8,128)S(1)}, u32[]{:S(2)}, u32[]{:S(2)}) collective-permute-start(f32[256,512]{1,0:T(8,128)S(1)} %shard_map.71.mine.refs_1_), channel_id=1, source_target_pairs={{0,1},{1,0},{2,3},{3,2},{4,5},{5,4},{6,7},{7,6},{8,9},{9,8},{10,11... | collective-permute-start | bytes 1572872 | tf_op jit(solution)/shard_map/ppermute | solution.py:349
  98.8 9.6 %collective-permute-start.33 = (f32[224,256]{1,0:T(8,128)S(1)}, f32[224,256]{1,0:T(8,128)S(1)}, u32[]{:S(2)}, u32[]{:S(2)}) collective-permute-start(f32[224,256]{1,0:T(8,128)S(1)} %add_add_fusion), channel_id=1, source_target_pairs={{0,6},{2,4},{4,2},{6,0},{8,14},{10,12},{12,10},{14,8},{16,22},{18,... | collective-permute-start | bytes 688136 | tf_op jit(solution)/shard_map/ppermute | solution.py:353
  101.0 10.1 %collective-permute-start.34 = (f32[224,256]{1,0:T(8,128)S(1)}, f32[224,256]{1,0:T(8,128)S(1)}, u32[]{:S(2)}, u32[]{:S(2)}) collective-permute-start(f32[224,256]{1,0:T(8,128)S(1)} %add_add_fusion), channel_id=1, source_target_pairs={{0,4},{2,6},{4,0},{6,2},{8,12},{10,14},{12,8},{14,10},{16,20},{18,... | collective-permute-start | bytes 688136 | tf_op jit(solution)/shard_map/ppermute | solution.py:353
  101.3 9.9 %collective-permute-start.35 = (f32[224,256]{1,0:T(8,128)S(1)}, f32[224,256]{1,0:T(8,128)S(1)}, u32[]{:S(2)}, u32[]{:S(2)}) collective-permute-start(f32[224,256]{1,0:T(8,128)S(1)} %add_add_fusion), channel_id=1, source_target_pairs={{0,2},{2,0},{4,6},{6,4},{8,10},{10,8},{12,14},{14,12},{16,18},{18,... | collective-permute-start | bytes 688136 | tf_op jit(solution)/shard_map/ppermute | solution.py:353
  103.1 9.2 %collective-permute-start.17 = (f32[96,256]{1,0:T(8,128)S(1)}, f32[96,256]{1,0:T(8,128)S(1)}, u32[]{:S(2)}, u32[]{:S(2)}) collective-permute-start(f32[96,256]{1,0:T(8,128)S(1)} %get-tuple-element.91), channel_id=1, source_target_pairs={{0,2},{2,0},{4,6},{6,4},{8,10},{10,8},{12,14},{14,12},{16,18},{18,... | collective-permute-start | bytes 294920 | tf_op jit(solution)/shard_map/ppermute | solution.py:353
  121.2 15.7 %collective-permute-start.36 = (f32[896,256]{1,0:T(8,128)S(1)}, f32[896,256]{1,0:T(8,128)S(1)}, u32[]{:S(2)}, u32[]{:S(2)}) collective-permute-start(f32[896,256]{1,0:T(8,128)S(1)} %pad_maximum_fusion.1.refs_7_), channel_id=1, source_target_pairs={{0,1},{1,0},{2,3},{3,2},{4,5},{5,4},{6,7},{7,6},{8,9},{9,8},{10,11... | collective-permute-start | bytes 2752520 | tf_op jit(solution)/shard_map/ppermute | solution.py:349
  151.0 10.9 %collective-permute-start.38 = (bf16[2,256,256]{2,1,0:T(8,128)(2,1)S(1)}, bf16[2,256,256]{2,1,0:T(8,128)(2,1)S(1)}, u32[]{:S(2)}, u32[]{:S(2)}) collective-permute-start(bf16[2,256,256]{2,1,0:T(8,128)(2,1)S(1)} %get-tuple-element.51.refs_0_), channel_id=1, source_target_pairs={{0,8},{2,10},{4,12},{6,14},{8,16},{10,18},{12,20},{14,22},{16,24},... | collective-permute-start | bytes 786440 | tf_op jit(solution)/shard_map/ppermute | solution.py:358
  154.5 11.9 %collective-permute-start.39 = (bf16[2,256,256]{2,1,0:T(8,128)(2,1)S(1)}, bf16[2,256,256]{2,1,0:T(8,128)(2,1)S(1)}, u32[]{:S(2)}, u32[]{:S(2)}) collective-permute-start(bf16[2,256,256]{2,1,0:T(8,128)(2,1)S(1)} %get-tuple-element.51.refs_0_), channel_id=1, source_target_pairs={{0,4},{2,6},{8,12},{10,14},{4,16},{6,18},{16,20},{18,22},{12,24},{... | collective-permute-start | bytes 786440 | tf_op jit(solution)/shard_map/ppermute | solution.py:364
  159.9 10.9 %collective-permute-start.49 = (bf16[2,256,256]{2,1,0:T(8,128)(2,1)S(1)}, bf16[2,256,256]{2,1,0:T(8,128)(2,1)S(1)}, u32[]{:S(2)}, u32[]{:S(2)}) collective-permute-start(bf16[2,256,256]{2,1,0:T(8,128)(2,1)S(1)} %get-tuple-element.52), channel_id=1, source_target_pairs={{0,4},{2,6},{4,0},{6,2},{8,12},{10,14},{12,8},{14,10},{16,20},{18,... | collective-permute-start | bytes 786440 | tf_op jit(solution)/shard_map/ppermute | solution.py:353
  161.9 9.8 %collective-permute-start.40 = (bf16[2,256,256]{2,1,0:T(8,128)(2,1)S(1)}, bf16[2,256,256]{2,1,0:T(8,128)(2,1)S(1)}, u32[]{:S(2)}, u32[]{:S(2)}) collective-permute-start(bf16[2,256,256]{2,1,0:T(8,128)(2,1)S(1)} %collective-permute-done.38.refs_2_), channel_id=1, source_target_pairs={{0,2},{2,0},{4,6},{6,4},{8,10},{10,8},{12,14},{14,12},{16,18},{18,... | collective-permute-start | bytes 786440 | tf_op jit(solution)/shard_map/ppermute | solution.py:353
  164.4 12.0 %collective-permute-start.41 = (bf16[2,256,256]{2,1,0:T(8,128)(2,1)S(1)}, bf16[2,256,256]{2,1,0:T(8,128)(2,1)S(1)}, u32[]{:S(2)}, u32[]{:S(2)}) collective-permute-start(bf16[2,256,256]{2,1,0:T(8,128)(2,1)S(1)} %collective-permute-done.38.refs_2_), channel_id=1, source_target_pairs={{0,4},{2,6},{4,0},{6,2},{8,12},{10,14},{12,8},{14,10},{16,20},{18,... | collective-permute-start | bytes 786440 | tf_op jit(solution)/shard_map/ppermute | solution.py:353
  164.5 16.1 %collective-permute-start.51 = (bf16[2,256,256]{2,1,0:T(8,128)(2,1)S(1)}, bf16[2,256,256]{2,1,0:T(8,128)(2,1)S(1)}, u32[]{:S(2)}, u32[]{:S(2)}) collective-permute-start(bf16[2,256,256]{2,1,0:T(8,128)(2,1)S(1)} %get-tuple-element.64), channel_id=1, source_target_pairs={{0,4},{2,6},{4,0},{6,2},{8,12},{10,14},{12,8},{14,10},{16,20},{18,... | collective-permute-start | bytes 786440 | tf_op jit(solution)/shard_map/ppermute | solution.py:353
  166.4 15.0 %collective-permute-start.47 = (bf16[2,256,256]{2,1,0:T(8,128)(2,1)S(1)}, bf16[2,256,256]{2,1,0:T(8,128)(2,1)S(1)}, u32[]{:S(2)}, u32[]{:S(2)}) collective-permute-start(bf16[2,256,256]{2,1,0:T(8,128)(2,1)S(1)} %get-tuple-element.61), channel_id=1, source_target_pairs={{0,2},{2,0},{4,6},{6,4},{8,10},{10,8},{12,14},{14,12},{16,18},{18,... | collective-permute-start | bytes 786440 | tf_op jit(solution)/shard_map/ppermute | solution.py:353
  170.8 15.4 %collective-permute-start.44 = (f32[256,512]{1,0:T(8,128)S(1)}, f32[256,512]{1,0:T(8,128)S(1)}, u32[]{:S(2)}, u32[]{:S(2)}) collective-permute-start(f32[256,512]{1,0:T(8,128)S(1)} %get-tuple-element.50.x.refs_3_), channel_id=1, source_target_pairs={{0,1},{1,0},{2,3},{3,2},{4,5},{5,4},{6,7},{7,6},{8,9},{9,8},{10,11... | collective-permute-start | bytes 1572872 | tf_op jit(solution)/shard_map/ppermute | solution.py:349
  171.6 11.8 %collective-permute-start.50 = (bf16[2,256,256]{2,1,0:T(8,128)(2,1)S(1)}, bf16[2,256,256]{2,1,0:T(8,128)(2,1)S(1)}, u32[]{:S(2)}, u32[]{:S(2)}) collective-permute-start(bf16[2,256,256]{2,1,0:T(8,128)(2,1)S(1)} %add_convert_fusion.1), channel_id=1, source_target_pairs={{0,2},{2,0},{4,6},{6,4},{8,10},{10,8},{12,14},{14,12},{16,18},{18,... | collective-permute-start | bytes 786440 | tf_op jit(solution)/shard_map/ppermute | solution.py:353
  183.5 11.8 %collective-permute-start.48 = (bf16[2,256,256]{2,1,0:T(8,128)(2,1)S(1)}, bf16[2,256,256]{2,1,0:T(8,128)(2,1)S(1)}, u32[]{:S(2)}, u32[]{:S(2)}) collective-permute-start(bf16[2,256,256]{2,1,0:T(8,128)(2,1)S(1)} %add_convert_fusion.2), channel_id=1, source_target_pairs={{4,0},{6,2},{12,8},{14,10},{16,4},{18,6},{20,16},{22,18},{24,12},{... | collective-permute-start | bytes 786440 | tf_op jit(solution)/shard_map/ppermute | solution.py:364
  184.9 14.4 %collective-permute-start.52 = (bf16[2,256,256]{2,1,0:T(8,128)(2,1)S(1)}, bf16[2,256,256]{2,1,0:T(8,128)(2,1)S(1)}, u32[]{:S(2)}, u32[]{:S(2)}) collective-permute-start(bf16[2,256,256]{2,1,0:T(8,128)(2,1)S(1)} %add_convert_fusion), channel_id=1, source_target_pairs={{8,0},{10,2},{12,4},{14,6},{16,8},{18,10},{20,12},{22,14},{24,16},... | collective-permute-start | bytes 786440 | tf_op jit(solution)/shard_map/ppermute | solution.py:358
  199.8 24.8 %collective-permute-start.53 = (f32[256,512]{1,0:T(8,128)S(1)}, f32[256,512]{1,0:T(8,128)S(1)}, u32[]{:S(2)}, u32[]{:S(2)}) collective-permute-start(f32[256,512]{1,0:T(8,128)S(1)} %shard_map.77.mine.refs_1_), channel_id=1, source_target_pairs={{0,1},{1,0},{2,3},{3,2},{4,5},{5,4},{6,7},{7,6},{8,9},{9,8},{10,11... | collective-permute-start | bytes 1572872 | tf_op jit(solution)/shard_map/ppermute | solution.py:349
  202.0 10.6 %collective-permute-start.65 = (f32[128,256]{1,0:T(8,128)S(1)}, f32[128,256]{1,0:T(8,128)S(1)}, u32[]{:S(2)}, u32[]{:S(2)}) collective-permute-start(f32[128,256]{1,0:T(8,128)S(1)} %get-tuple-element.79), channel_id=1, source_target_pairs={{0,4},{2,6},{4,0},{6,2},{8,12},{10,14},{12,8},{14,10},{16,20},{18,... | collective-permute-start | bytes 393224 | tf_op jit(solution)/shard_map/ppermute | solution.py:353
  212.7 15.0 %collective-permute-start.67 = (f32[128,256]{1,0:T(8,128)S(1)}, f32[128,256]{1,0:T(8,128)S(1)}, u32[]{:S(2)}, u32[]{:S(2)}) collective-permute-start(f32[128,256]{1,0:T(8,128)S(1)} %fusion.3), channel_id=1, source_target_pairs={{0,8},{2,10},{4,12},{6,14},{8,0},{10,2},{12,4},{14,6},{16,24},{18,... | collective-permute-start | bytes 393224 | tf_op jit(solution)/shard_map/ppermute | solution.py:353
  222.1 11.2 %collective-permute-start.68 = (f32[128,256]{1,0:T(8,128)S(1)}, f32[128,256]{1,0:T(8,128)S(1)}, u32[]{:S(2)}, u32[]{:S(2)}) collective-permute-start(f32[128,256]{1,0:T(8,128)S(1)} %fusion.3), channel_id=1, source_target_pairs={{0,16},{2,18},{4,20},{6,22},{8,24},{10,26},{12,28},{14,30},{16,0},... | collective-permute-start | bytes 393224 | tf_op jit(solution)/shard_map/ppermute | solution.py:353
  222.1 11.2 %collective-permute-start.69 = (f32[128,256]{1,0:T(8,128)S(1)}, f32[128,256]{1,0:T(8,128)S(1)}, u32[]{:S(2)}, u32[]{:S(2)}) collective-permute-start(f32[128,256]{1,0:T(8,128)S(1)} %fusion.3), channel_id=1, source_target_pairs={{0,24},{2,26},{4,28},{6,30},{8,16},{10,18},{12,20},{14,22},{16,8},... | collective-permute-start | bytes 393224 | tf_op jit(solution)/shard_map/ppermute | solution.py:353
  225.2 9.7 %collective-permute-start.54 = (f32[96,256]{1,0:T(8,128)S(1)}, f32[96,256]{1,0:T(8,128)S(1)}, u32[]{:S(2)}, u32[]{:S(2)}) collective-permute-start(f32[96,256]{1,0:T(8,128)S(1)} %get-tuple-element.84), channel_id=1, source_target_pairs={{0,2},{2,0},{4,6},{6,4},{8,10},{10,8},{12,14},{14,12},{16,18},{18,... | collective-permute-start | bytes 294920 | tf_op jit(solution)/shard_map/ppermute | solution.py:353
  225.9 11.1 %collective-permute-start.55 = (f32[96,256]{1,0:T(8,128)S(1)}, f32[96,256]{1,0:T(8,128)S(1)}, u32[]{:S(2)}, u32[]{:S(2)}) collective-permute-start(f32[96,256]{1,0:T(8,128)S(1)} %get-tuple-element.86), channel_id=1, source_target_pairs={{0,4},{2,6},{4,0},{6,2},{8,12},{10,14},{12,8},{14,10},{16,20},{18,... | collective-permute-start | bytes 294920 | tf_op jit(solution)/shard_map/ppermute | solution.py:353
  227.6 9.4 %collective-permute-start.56 = (f32[96,256]{1,0:T(8,128)S(1)}, f32[96,256]{1,0:T(8,128)S(1)}, u32[]{:S(2)}, u32[]{:S(2)}) collective-permute-start(f32[96,256]{1,0:T(8,128)S(1)} %get-tuple-element.85), channel_id=1, source_target_pairs={{0,6},{2,4},{4,2},{6,0},{8,14},{10,12},{12,10},{14,8},{16,22},{18,... | collective-permute-start | bytes 294920 | tf_op jit(solution)/shard_map/ppermute | solution.py:353
  240.3 9.5 %collective-permute-start.58 = (f32[96,256]{1,0:T(8,128)S(1)}, f32[96,256]{1,0:T(8,128)S(1)}, u32[]{:S(2)}, u32[]{:S(2)}) collective-permute-start(f32[96,256]{1,0:T(8,128)S(1)} %fusion.5), channel_id=1, source_target_pairs={{0,16},{2,18},{4,20},{6,22},{8,24},{10,26},{12,28},{14,30},{16,0},... | collective-permute-start | bytes 294920 | tf_op jit(solution)/shard_map/ppermute | solution.py:353
  240.8 9.1 %collective-permute-start.59 = (f32[96,256]{1,0:T(8,128)S(1)}, f32[96,256]{1,0:T(8,128)S(1)}, u32[]{:S(2)}, u32[]{:S(2)}) collective-permute-start(f32[96,256]{1,0:T(8,128)S(1)} %fusion.5), channel_id=1, source_target_pairs={{0,24},{2,26},{4,28},{6,30},{8,16},{10,18},{12,20},{14,22},{16,8},... | collective-permute-start | bytes 294920 | tf_op jit(solution)/shard_map/ppermute | solution.py:353
  (41 other events, 300.9 us)
